TPU v7x, 32 devices: a whole 2x2x4 slice. The times are simulated.
32 devices in a mesh: groups: 2 (over y), expert: 8 (over z, x), tensor: 2 (over core).
Axes of the slice: x: 2, y: 2, z: 4, core: 2. Of those that a mesh axis runs over, the one named last changes fastest.
Arguments:
- tokens: bfloat16 [256, 6144], P(('groups', 'expert'), 'tensor'), parts along dimension 0, may hold values from -6 to 6
- grad_out: bfloat16 [256, 6144], P(('groups', 'expert'), 'tensor'), parts along dimension 0, may hold values from -6 to 6
- expert_ids: int32 [256, 4], P(('groups', 'expert')), parts along dimension 0, may hold values from 0 to 15, all different within a row; in each aligned block of 16 rows (0 to 15, 16 to 31, ...) at most 5 rows name the same one
- gate_probs: bfloat16 [256, 4], P(('groups', 'expert')), parts along dimension 0, may hold values from 0.099609375 to 1
- w_gate: bfloat16 [21504, 6144], P(('expert', 'tensor')), may hold values from -0.078125 to 0.078125
- w_up: bfloat16 [21504, 6144], P(('expert', 'tensor')), may hold values from -0.078125 to 0.078125
- w_down: bfloat16 [21504, 6144], P(('expert', 'tensor')), may hold values from -0.0625 to 0.0625
Outputs:
- grad_tokens: bfloat16 [256, 6144], P(('groups', 'expert'), 'tensor'), parts along dimension 0
- grad_gates: float32 [256, 4], P(('groups', 'expert')), parts along dimension 0
- grad_w_gate: bfloat16 [21504, 12288], P(('expert', 'tensor'), 'groups'), parts along dimension 1
- grad_w_up: bfloat16 [21504, 12288], P(('expert', 'tensor'), 'groups'), parts along dimension 1
- grad_w_down: bfloat16 [21504, 12288], P(('expert', 'tensor'), 'groups'), parts along dimension 1
There are 2 independent parts, one for each index of `groups`. A program takes and returns all parts, laid end to end along the dimension named above; an argument that names none is the same for every part. Nothing has to cross between parts.
Inputs may be any that keep to these rules, and one draw needn't show every extreme that they name: `expert_ids`: in each aligned block of 16 rows (the rows of one index of expert) no expert is named by more than 5 rows, a bound that some block reaches.
All inputs are finite; a program needn't handle non-finite values.
Results may differ from a plain program's by a relative error of at most 0.0051.
Values may be sent and summed in bfloat16 or wider, within the bound.
No kernel may reach another device: no remote copies, remote signals or barrier semaphores. Data moves between devices by JAX's collectives and lax.ppermute only.
A program may use at most 192 MiB of HBM per device.

v0:
```python
import jax
import jax.numpy as jnp
from jax import lax
from jax.sharding import PartitionSpec as P

EXPERTS_ON = 2
CAP = 5


def on_device(tokens, grad_out, expert_ids, gate_probs, w_gate, w_up, w_down):
    highest = lax.Precision.HIGHEST
    n_expert = lax.axis_size("expert")
    copies = n_expert // EXPERTS_ON
    tok_rows = expert_ids.shape[0]
    top_count = expert_ids.shape[1]
    capacity = CAP
    slots = tok_rows * top_count
    flat_ids = expert_ids.reshape(slots)
    expert_range = jnp.arange(EXPERTS_ON, dtype=jnp.int32)
    member = (flat_ids[:, None] == expert_range[None, :]).astype(jnp.int32)
    earlier = jnp.cumsum(member, axis=0) - member
    position = jnp.sum(earlier * member, axis=1)
    inside = flat_ids < EXPERTS_ON
    target = flat_ids * capacity + position
    buffer_range = jnp.arange(EXPERTS_ON * capacity, dtype=jnp.int32)
    placing = ((target[None, :] == buffer_range[:, None]) & inside[None, :]).astype(jnp.float32)
    slot_token = jnp.arange(slots, dtype=jnp.int32) // top_count
    owner = (slot_token[:, None] == jnp.arange(tok_rows, dtype=jnp.int32)[None, :]).astype(
        jnp.float32
    )
    select_rows = jnp.dot(placing, owner, precision=highest, preferred_element_type=jnp.float32)
    select_half = select_rows.astype(jnp.bfloat16)
    gate_slots = jnp.dot(
        placing,
        gate_probs.reshape(slots).astype(jnp.float32),
        precision=highest,
        preferred_element_type=jnp.float32,
    ).astype(jnp.bfloat16)

    def spread(block):
        tail = block.shape[1:]
        shaped = block.reshape((EXPERTS_ON, 1, capacity) + tail)
        return jnp.broadcast_to(shaped, (EXPERTS_ON, copies, capacity) + tail).reshape(
            (n_expert, capacity) + tail
        )

    def pick(source):
        return jnp.dot(select_half, source, preferred_element_type=jnp.float32).astype(jnp.bfloat16)

    full_tokens, full_grads = (
        lax.all_gather(tokens, "tensor", axis=1, tiled=True),
        lax.all_gather(grad_out, "tensor", axis=1, tiled=True),
    )
    got_tokens, got_grads, got_gates = (
        lax.all_to_all(
            spread(pick(full_tokens)), "expert", split_axis=0, concat_axis=0, tiled=True
        ),
        lax.all_to_all(spread(pick(full_grads)), "expert", split_axis=0, concat_axis=0, tiled=True),
        lax.all_to_all(spread(gate_slots), "expert", split_axis=0, concat_axis=0, tiled=True),
    )
    width = got_tokens.shape[2]
    row_count = n_expert * capacity
    rows_in = got_tokens.reshape(row_count, width)
    rows_grad = got_grads.reshape(row_count, width)
    factor = got_gates.reshape(row_count).astype(jnp.float32)[:, None]
    contract_cols = (((1,), (1,)), ((), ()))
    contract_rows = (((0,), (0,)), ((), ()))
    hidden = lax.dot_general(rows_in, w_gate, contract_cols, preferred_element_type=jnp.float32)
    upper = lax.dot_general(rows_in, w_up, contract_cols, preferred_element_type=jnp.float32)
    dact = lax.dot_general(rows_grad, w_down, contract_cols, preferred_element_type=jnp.float32)
    sigma = jax.nn.sigmoid(hidden)
    silu = hidden * sigma
    act = silu * upper
    gate_part = jnp.sum(act * dact, axis=1)
    weighted = (factor * act).astype(jnp.bfloat16)
    scaled = factor * dact
    grad_h = (scaled * upper * sigma * (1.0 + hidden * (1.0 - sigma))).astype(jnp.bfloat16)
    grad_u = (scaled * silu).astype(jnp.bfloat16)
    grad_w_down = lax.dot_general(
        weighted, rows_grad, contract_rows, preferred_element_type=jnp.float32
    ).astype(jnp.bfloat16)
    grad_w_gate = lax.dot_general(
        grad_h, rows_in, contract_rows, preferred_element_type=jnp.float32
    ).astype(jnp.bfloat16)
    grad_w_up = lax.dot_general(
        grad_u, rows_in, contract_rows, preferred_element_type=jnp.float32
    ).astype(jnp.bfloat16)
    partial_grad = jnp.dot(grad_h, w_gate, preferred_element_type=jnp.float32) + jnp.dot(
        grad_u, w_up, preferred_element_type=jnp.float32
    )
    partial_rows = partial_grad.reshape(n_expert, capacity, width)
    gate_terms = gate_part.reshape(n_expert, capacity)
    back_rows, back_gates = (
        lax.all_to_all(partial_rows, "expert", split_axis=0, concat_axis=0, tiled=True),
        lax.all_to_all(gate_terms, "expert", split_axis=0, concat_axis=0, tiled=True),
    )
    columns = back_rows.shape[2]
    summed = jnp.sum(back_rows.reshape(EXPERTS_ON, copies, capacity, columns), axis=1).reshape(
        EXPERTS_ON * capacity, columns
    )
    token_grad = lax.psum_scatter(
        jnp.dot(select_rows.T, summed, precision=highest, preferred_element_type=jnp.float32),
        "tensor",
        scatter_dimension=1,
        tiled=True,
    )
    gate_sum = jnp.sum(back_gates.reshape(EXPERTS_ON, copies, capacity), axis=1).reshape(
        EXPERTS_ON * capacity
    )
    gate_local = jnp.dot(
        placing.T, gate_sum, precision=highest, preferred_element_type=jnp.float32
    ).reshape(tok_rows, top_count)
    grad_gates = lax.psum(gate_local, "tensor")
    return (token_grad.astype(jnp.bfloat16), grad_gates, grad_w_gate, grad_w_up, grad_w_down)


def solution(mesh):
    return jax.shard_map(
        on_device,
        mesh=mesh,
        in_specs=(
            P(("groups", "expert"), "tensor"),
            P(("groups", "expert"), "tensor"),
            P(("groups", "expert"), None),
            P(("groups", "expert"), None),
            P(("expert", "tensor"), None),
            P(("expert", "tensor"), None),
            P(("expert", "tensor"), None),
        ),
        out_specs=(
            P(("groups", "expert"), "tensor"),
            P(("groups", "expert"), None),
            P(("expert", "tensor"), "groups"),
            P(("expert", "tensor"), "groups"),
            P(("expert", "tensor"), "groups"),
        ),
        check_vma=False,
    )
```

profile of v0, /device:TPU:0, one launch (start us, length us, event | category | flops | bytes accessed | tf_op | source)
XLA Modules:
  0.0 171.2 jit_solution(610419728009264612)
XLA Ops:
  7.2 0.8 copy.26
  7.9 0.1 reshape.128
  8.0 0.1 fusion.4
  8.1 0.8 copy.27
  8.9 0.1 reshape.140
  9.0 0.1 reduce_window_sum.11
  9.1 0.2 select_reduce_fusion
  9.3 0.1 fusion
  9.4 0.1 broadcast_in_dim.12
  9.5 0.6 copy.28
  10.1 7.3 %all-to-all-start = ((bf16[8,1,5]{2,1,0:T(2,128)(2,1)}), bf16[8,1,5]{2,1,0:T(2,128)(2,1)S(1)}, u32[]{:S(2)}, u32[]{:S(2)}) async-start(bf16[8,1,5]{2,1,0:T(2,128)(2,1)} %copy.28), calls=%async_computation | async-start | bytes 8192 | tf_op jit(solution)/shard_map/all_to_all | solution.py:59
  17.3 0.2 fusion.5
  17.5 2.2 %all_gather.7 = bf16[16,6144]{1,0:T(8,128)(2,1)S(1)} all-gather(bf16[16,3072]{1,0:T(8,128)(2,1)} %param.7), channel_id=1, replica_groups=mesh['groups'=2,'expert'=8,'tensor'=2] {'tensor'}, dimensions={1}, use_global_device_ids=true | all-gather | bytes 294912 | tf_op jit(solution)/shard_map/all_gather | solution.py:51
  19.8 0.2 convolution_convert_fusion.3
  20.0 2.3 %all_gather.6 = bf16[16,6144]{1,0:T(8,128)(2,1)S(1)} all-gather(bf16[16,3072]{1,0:T(8,128)(2,1)} %param.8), channel_id=1, replica_groups=mesh['groups'=2,'expert'=8,'tensor'=2] {'tensor'}, dimensions={1}, use_global_device_ids=true | all-gather | bytes 294912 | tf_op jit(solution)/shard_map/all_gather | solution.py:52
  22.2 0.1 broadcast_in_dim.32
  22.3 1.4 all-to-all-done
  23.7 0.9 broadcast_in_dim.33
  24.7 4.6 %all-to-all-start.2 = ((bf16[8,5,6144]{2,1,0:T(8,128)(2,1)}), bf16[8,5,6144]{2,1,0:T(8,128)(2,1)S(1)}, u32[]{:S(2)}, u32[]{:S(2)}) async-start(bf16[8,5,6144]{2,1,0:T(8,128)(2,1)} %bitcast.3), calls=%async_computation.2 | async-start | bytes 1572864 | tf_op jit(solution)/shard_map/all_to_all | solution.py:55
  29.2 0.2 convolution_convert_fusion.4
  29.4 0.1 reduce_sum.40
  29.5 0.1 copy.29
  29.6 0.1 broadcast_in_dim.14
  29.7 0.7 broadcast_compare_fusion
  30.3 0.7 multiply_add_fusion
  31.1 0.1 reshape.139
  31.1 18.6 %all-to-all-done.2 = bf16[8,5,6144]{2,1,0:T(8,128)(2,1)S(1)} async-done(((bf16[8,5,6144]{2,1,0:T(8,128)(2,1)}), bf16[8,5,6144]{2,1,0:T(8,128)(2,1)S(1)}, u32[]{:S(2)}, u32[]{:S(2)}) %all-to-all-start.2) | async-done | bytes 491552 | tf_op jit(solution)/shard_map/all_to_all | solution.py:55
  49.7 0.9 broadcast_in_dim.15
  50.6 3.6 %all-to-all-start.1 = ((bf16[8,5,6144]{2,1,0:T(8,128)(2,1)}), bf16[8,5,6144]{2,1,0:T(8,128)(2,1)S(1)}, u32[]{:S(2)}, u32[]{:S(2)}) async-start(bf16[8,5,6144]{2,1,0:T(8,128)(2,1)} %bitcast.2), calls=%async_computation.1 | async-start | bytes 1572864 | tf_op jit(solution)/shard_map/all_to_all | solution.py:58
  54.2 0.2 reshape.133
  54.5 10.6 %fusion.21 = f32[40,1344]{1,0:T(8,128)S(1)} fusion(bf16[40,6144]{1,0:T(8,128)(2,1)S(1)} %reshape.133, bf16[1344,6144]{1,0:T(8,128)(2,1)} %param.11), kind=kOutput, calls=%fused_computation.46 | convolution fusion | flops 660602880 | bytes 17221632 | tf_op jit(solution)/shard_map/dot_general | solution.py:68
  65.0 0.0 copy-start
  65.1 10.7 %fusion.20 = f32[40,1344]{1,0:T(8,128)S(1)} fusion(bf16[40,6144]{1,0:T(8,128)(2,1)S(1)} %reshape.133, bf16[1344,6144]{1,0:T(8,128)(2,1)} %param.12), kind=kOutput, calls=%fused_computation.45 | convolution fusion | flops 660602880 | bytes 17221632 | tf_op jit(solution)/shard_map/dot_general | solution.py:69
  75.7 0.0 copy-start.2
  75.7 0.0 all-to-all-done.1
  75.7 0.2 reshape.131
  76.0 10.7 %multiply_reduce_fusion = (f32[40]{0:T(128)S(1)}, bf16[40,1344]{1,0:T(8,128)(2,1)S(1)}, bf16[40,1344]{1,0:T(8,128)(2,1)S(1)}) fusion(f32[40,1344]{1,0:T(8,128)S(1)} %fusion.20, f32[40,1344]{1,0:T(8,128)S(1)} %fusion.21, f32[40]{0:T(128)S(1)} %reshape.139, bf16[40,6144]{1,0:T(8,128)(2,1)S(1)} %reshape.131, bf16[1344,6144]{1,0:T(8,128)(2,1)} %param.13), kind=kOutput, calls=%fused_computation.10 | convolution fusion | flops 661516736 | bytes 17652032 | tf_op jit(solution)/shard_map/dot_general | solution.py:70
  86.7 0.0 copy-done
  86.7 0.0 copy-start.4
  86.7 0.7 all_to_all.26
  87.4 0.0 copy-done.2
  87.4 7.2 %fusion.22 = f32[40,6144]{1,0:T(8,128)S(1)} fusion(bf16[40,1344]{1,0:T(8,128)(2,1)S(1)} %get-tuple-element.6, bf16[1344,6144]{1,0:T(8,128)(2,1)} %param.11), kind=kOutput, calls=%fused_computation.47 | convolution fusion | flops 660602880 | bytes 17605632 | tf_op jit(solution)/shard_map/dot_general | solution.py:88
  94.6 7.3 %convolution_add_fusion = f32[40,6144]{1,0:T(8,128)S(1)} fusion(f32[40,6144]{1,0:T(8,128)S(1)} %fusion.22, bf16[40,1344]{1,0:T(8,128)(2,1)S(1)} %get-tuple-element.7, bf16[1344,6144]{1,0:T(8,128)(2,1)} %param.12), kind=kOutput, calls=%fused_computation.3 | convolution fusion | flops 660848640 | bytes 18588672 | tf_op jit(solution)/shard_map/dot_general | solution.py:88
  101.9 0.0 copy-done.4
  101.9 1.3 reshape.134
  103.2 0.0 copy-start.1
  103.2 6.1 %all-to-all-start.3 = ((f32[8,5,6144]{2,1,0:T(8,128)}), f32[8,5,6144]{2,1,0:T(8,128)S(1)}, u32[]{:S(2)}, u32[]{:S(2)}) async-start(f32[8,5,6144]{2,1,0:T(8,128)} %reshape.134), calls=%async_computation.3 | async-start | bytes 3145728 | tf_op jit(solution)/shard_map/all_to_all | solution.py:94
  109.3 8.4 %convolution_convert_fusion.1 = bf16[1344,6144]{1,0:T(8,128)(2,1)} fusion(bf16[40,1344]{1,0:T(8,128)(2,1)S(1)} %get-tuple-element.7, bf16[40,6144]{1,0:T(8,128)(2,1)S(1)} %reshape.133), kind=kOutput, calls=%fused_computation.1 | convolution fusion | flops 668860416 | bytes 17114112 | tf_op jit(solution)/shard_map/dot_general | solution.py:85
  117.8 0.0 copy-done.1
  117.8 0.0 copy-done.3
  117.8 8.5 %convolution_convert_fusion = bf16[1344,6144]{1,0:T(8,128)(2,1)} fusion(bf16[40,6144]{1,0:T(8,128)(2,1)S(1)} %reshape.131, f32[40]{0:T(128)S(1)} %reshape.139, f32[40,1344]{1,0:T(8,128)S(1)} %copy-done.3, f32[40,1344]{1,0:T(8,128)S(1)} %copy-done.1), kind=kOutput, calls=%fused_computation | convolution fusion | flops 669236736 | bytes 17436832 | tf_op jit(solution)/shard_map/dot_general | solution.py:79
  126.3 19.7 %all-to-all-done.3 = f32[8,5,6144]{2,1,0:T(8,128)S(1)} async-done(((f32[8,5,6144]{2,1,0:T(8,128)}), f32[8,5,6144]{2,1,0:T(8,128)S(1)}, u32[]{:S(2)}, u32[]{:S(2)}) %all-to-all-start.3) | async-done | bytes 983072 | tf_op jit(solution)/shard_map/all_to_all | solution.py:94
  146.0 3.6 %all-to-all-start.4 = ((f32[8,1,5]{2,1,0:T(1,128)}), f32[8,1,5]{2,1,0:T(1,128)S(1)}, u32[]{:S(2)}, u32[]{:S(2)}) async-start(f32[8,1,5]{2,1,0:T(1,128)} %bitcast.6), calls=%async_computation.5 | async-start | bytes 8192 | tf_op jit(solution)/shard_map/all_to_all | solution.py:95
  149.6 0.0 reduce-scatter.2.cloned.1.call-start
  149.7 0.1 bitcast_reduce_fusion
  149.8 1.3 fusion.23
  151.1 0.0 reduce-scatter.2.cloned.1.call-update
  151.1 0.0 copy-done.5
  151.1 8.4 %convolution_convert_fusion.2 = bf16[1344,6144]{1,0:T(8,128)(2,1)} fusion(bf16[40,1344]{1,0:T(8,128)(2,1)S(1)} %copy-done.5, bf16[40,6144]{1,0:T(8,128)(2,1)S(1)} %reshape.133), kind=kOutput, calls=%fused_computation.2 | convolution fusion | flops 668860416 | bytes 17114112 | tf_op jit(solution)/shard_map/dot_general | solution.py:82
  159.5 0.0 all-to-all-done.4
  159.5 0.1 reshape.142
  159.6 0.1 fusion.8
  159.8 3.0 %psum.7 = f32[16,4]{0,1:T(4,128)} all-reduce(f32[16,4]{0,1:T(4,128)S(1)} %bitcast.39), channel_id=1, replica_groups=mesh['groups'=2,'expert'=8,'tensor'=2] {'tensor'}, use_global_device_ids=true, to_apply=%region_6.7 | all-reduce | flops 64 | bytes 512 | tf_op jit(solution)/shard_map/psum | solution.py:113
  162.8 1.6 convert_element_type.58
  (10 shorter events, 0.1 us)
Async XLA Ops:
  10.1 13.6 %all-to-all-start = ((bf16[8,1,5]{2,1,0:T(2,128)(2,1)}), bf16[8,1,5]{2,1,0:T(2,128)(2,1)S(1)}, u32[]{:S(2)}, u32[]{:S(2)}) async-start(bf16[8,1,5]{2,1,0:T(2,128)(2,1)} %copy.28), calls=%async_computation | async-start | bytes 8192 | tf_op jit(solution)/shard_map/all_to_all | solution.py:59
  24.7 25.1 %all-to-all-start.2 = ((bf16[8,5,6144]{2,1,0:T(8,128)(2,1)}), bf16[8,5,6144]{2,1,0:T(8,128)(2,1)S(1)}, u32[]{:S(2)}, u32[]{:S(2)}) async-start(bf16[8,5,6144]{2,1,0:T(8,128)(2,1)} %bitcast.3), calls=%async_computation.2 | async-start | bytes 1572864 | tf_op jit(solution)/shard_map/all_to_all | solution.py:55
  50.6 25.1 %all-to-all-start.1 = ((bf16[8,5,6144]{2,1,0:T(8,128)(2,1)}), bf16[8,5,6144]{2,1,0:T(8,128)(2,1)S(1)}, u32[]{:S(2)}, u32[]{:S(2)}) async-start(bf16[8,5,6144]{2,1,0:T(8,128)(2,1)} %bitcast.2), calls=%async_computation.1 | async-start | bytes 1572864 | tf_op jit(solution)/shard_map/all_to_all | solution.py:58
  65.0 21.7 %copy-start = (f32[40,1344]{1,0:T(8,128)}, f32[40,1344]{1,0:T(8,128)S(1)}, u32[]{:S(2)}) copy-start(f32[40,1344]{1,0:T(8,128)S(1)} %fusion.21) | copy-start | bytes 645124
  75.7 11.7 %copy-start.2 = (f32[40,1344]{1,0:T(8,128)}, f32[40,1344]{1,0:T(8,128)S(1)}, u32[]{:S(2)}) copy-start(f32[40,1344]{1,0:T(8,128)S(1)} %fusion.20) | copy-start | bytes 645124
  86.7 15.2 %copy-start.4 = (bf16[40,1344]{1,0:T(8,128)(2,1)}, bf16[40,1344]{1,0:T(8,128)(2,1)S(1)}, u32[]{:S(2)}) copy-start(bf16[40,1344]{1,0:T(8,128)(2,1)S(1)} %get-tuple-element.6) | copy-start | bytes 322564
  103.2 14.6 %copy-start.1 = (f32[40,1344]{1,0:T(8,128)S(1)}, f32[40,1344]{1,0:T(8,128)}, u32[]{:S(2)}) copy-start(f32[40,1344]{1,0:T(8,128)} %copy-done) | copy-start | bytes 645124
  103.2 14.6 %copy-start.3 = (f32[40,1344]{1,0:T(8,128)S(1)}, f32[40,1344]{1,0:T(8,128)}, u32[]{:S(2)}) copy-start(f32[40,1344]{1,0:T(8,128)} %copy-done.2) | copy-start | bytes 645124
  103.2 42.8 %all-to-all-start.3 = ((f32[8,5,6144]{2,1,0:T(8,128)}), f32[8,5,6144]{2,1,0:T(8,128)S(1)}, u32[]{:S(2)}, u32[]{:S(2)}) async-start(f32[8,5,6144]{2,1,0:T(8,128)} %reshape.134), calls=%async_computation.3 | async-start | bytes 3145728 | tf_op jit(solution)/shard_map/all_to_all | solution.py:94
  117.8 33.3 %copy-start.5 = (bf16[40,1344]{1,0:T(8,128)(2,1)S(1)}, bf16[40,1344]{1,0:T(8,128)(2,1)}, u32[]{:S(2)}) copy-start(bf16[40,1344]{1,0:T(8,128)(2,1)} %copy-done.4) | copy-start | bytes 322564
  146.0 13.6 %all-to-all-start.4 = ((f32[8,1,5]{2,1,0:T(1,128)}), f32[8,1,5]{2,1,0:T(1,128)S(1)}, u32[]{:S(2)}, u32[]{:S(2)}) async-start(f32[8,1,5]{2,1,0:T(1,128)} %bitcast.6), calls=%async_computation.5 | async-start | bytes 8192 | tf_op jit(solution)/shard_map/all_to_all | solution.py:95
  149.6 13.2 %reduce-scatter.2.cloned.1.call-start = ((), (), s32[]{:S(2)}) async-start(), calls=%async_computation.6 | async-start | bytes 589824 | tf_op jit(solution)/shard_map/reduce_scatter | solution.py:101
Sparse Core Ops, SparseCore 0:
  152.7 9.1 reduce-scatter.1
where the time goes:
time: 172 us; the launch traced here: 171 us
  matrix products  73.9 us (43%)
  waiting for transfers between devices  39.7 us (23%)
  starting transfers between devices  25.2 us (15%)
  between operations  14.2 us (8%)
  blocking collectives  7.52 us (4%)
  local copies, waits for them, and re-layouts  7.23 us (4%)
  other arithmetic  3.44 us (2%)
    all_to_all x1, waiting for transfers between devices, on_device(): lax.all_to_all(partial_rows, 'expert', split_axis=0, concat_axis=0, tiled...  19.7 us
    all_to_all x1, waiting for transfers between devices, on_device(): lax.all_to_all(spread(pick(full_tokens)), 'expert', split_axis=0, concat_...  18.6 us
    dot_general x1, matrix products, on_device(): lax.dot_general(rows_grad, w_down, contract_cols, preferred_element_type=...  10.7 us
    dot_general x1, matrix products, on_device(): lax.dot_general(rows_in, w_up, contract_cols, preferred_element_type=jnp....  10.7 us
    dot_general x1, matrix products, on_device(): lax.dot_general(rows_in, w_gate, contract_cols, preferred_element_type=jn...  10.6 us
    dot_general x1, matrix products, on_device(): lax.dot_general(weighted, rows_grad, contract_rows, preferred_element_typ...  8.52 us
    dot_general x1, matrix products, on_device(): lax.dot_general(grad_h, rows_in, contract_rows, preferred_element_type=jn...  8.43 us
    dot_general x1, matrix products, on_device(): lax.dot_general(grad_u, rows_in, contract_rows, preferred_element_type=jn...  8.42 us
  transfers between devices with their start and end apart: 6, of which 3 were waited for; matrix products, arithmetic and copies ran while one was open for 30% of the time, Pallas kernels for 0%

commit v1 on v0

v1 whole, which is shorter than its diff:
```python
import functools
import math

import jax
import jax.numpy as jnp
from jax import lax
from jax.experimental import pallas as pl
from jax.experimental.pallas import tpu as pltpu
from jax.sharding import PartitionSpec as P

EXPERTS_ON = 2
CAP = 5
HALF = 4
MAIN = EXPERTS_ON * HALF
LANES = 128
F32 = jnp.float32
BF16 = jnp.bfloat16
MIB = 1 << 20


def iota(shape, dim):
    return lax.broadcasted_iota(jnp.int32, shape, dim)


def selection(ids, expert, position):
    rows, toks = expert.shape
    hits = [ids[k : k + 1, :] == expert for k in range(ids.shape[0])]
    member = functools.reduce(jnp.logical_or, hits).astype(F32)
    before = (iota((toks, toks), 0) < iota((toks, toks), 1)).astype(F32)
    earlier = jnp.dot(member, before, preferred_element_type=F32)
    chosen = jnp.where(earlier == position.astype(F32), member, 0.0)
    return chosen, hits


def slots(first, toks):
    row = iota((MAIN, toks), 0)
    group = (row >= HALF).astype(jnp.int32)
    expert = jnp.where(group == 0, first, 1 - first)
    return expert, row - HALF * group, jnp.full((MAIN, toks), CAP - 1, jnp.int32)


def pick_body(first_ref, ids_ref, probs_ref, tok_ref, grad_ref, x_ref, g_ref):
    ids = ids_ref[...]
    probs = probs_ref[...].astype(F32)
    toks, width = tok_ref.shape
    quarter = width // HALF
    expert, place, last = slots(first_ref[0], toks)
    main, hits = selection(ids, expert, place)
    tail, _ = selection(ids, expert, last)
    weight = sum(jnp.where(hit, probs[k : k + 1, :], 0.0) for k, hit in enumerate(hits))
    row = iota((MAIN, toks), 0)
    part = jnp.where(row >= HALF, row - HALF, row)
    for src, dst in ((tok_ref, x_ref), (grad_ref, g_ref)):
        dst[:, :width] = jnp.dot(main.astype(BF16), src[...], preferred_element_type=F32).astype(BF16)
        ext = jnp.zeros((MAIN, quarter), F32)
        for s in range(HALF):
            one = jnp.where(part == s, tail, 0.0).astype(BF16)
            ext += jnp.dot(one, src[:, s * quarter : (s + 1) * quarter], preferred_element_type=F32)
        dst[:, width : width + quarter] = ext.astype(BF16)
    base = width + quarter
    for at, chosen in enumerate((main, tail)):
        gate = jnp.sum(chosen * weight, axis=1, keepdims=True)
        x_ref[:, base + at * LANES : base + (at + 1) * LANES] = jnp.broadcast_to(gate, (MAIN, LANES)).astype(BF16)


def pick(first, ids_t, probs_t, tokens, grad_out):
    width = tokens.shape[1]
    packed = width + width // HALF
    return pl.pallas_call(
        pick_body,
        out_shape=(
            jax.ShapeDtypeStruct((MAIN, packed + 2 * LANES), BF16),
            jax.ShapeDtypeStruct((MAIN, packed), BF16),
        ),
        in_specs=[pl.BlockSpec(memory_space=pltpu.SMEM)] + [pl.BlockSpec(memory_space=pltpu.VMEM)] * 4,
        out_specs=[pl.BlockSpec(memory_space=pltpu.VMEM)] * 2,
        name="pick_rows",
    )(first, ids_t, probs_t, tokens, grad_out)


def unpack_maps(e, rows, copies, tensors):
    n_expert = EXPERTS_ON * copies
    senders = n_expert * tensors * MAIN
    r = iota((rows, senders), 0)
    k = iota((rows, senders), 1)
    whole = copies * MAIN
    is_main = r < whole
    rest = r - whole
    c = jnp.where(is_main, r // MAIN, rest // EXPERTS_ON)
    q = jnp.where(is_main, r % MAIN, 0)
    own = jnp.where(is_main, q // HALF, rest % EXPERTS_ON)
    p = q % HALF
    owner = (e * copies + c + (1 - own) * copies) % n_expert
    base = owner * (tensors * MAIN) + e * HALF
    is_tail = jnp.logical_and(r >= whole, rest < copies * EXPERTS_ON)

    def main(t):
        return jnp.logical_and(is_main, k == base + t * MAIN + p).astype(BF16)

    def tail(t, s):
        return jnp.logical_and(is_tail, k == base + t * MAIN + s).astype(BF16)

    return main, tail


def forward_body(copies, tensors, e_ref, xr_ref, gr_ref, wg_ref, wu_ref, wd_ref,
                 x_ref, g_ref, wt_ref, dh_ref, du_ref, back_ref, factor, acc, gates):
    step = pl.program_id(0)
    rows, depth = x_ref.shape
    width = depth // tensors
    quarter = width // HALF
    base = width + quarter

    @pl.when(step == 0)
    def _():
        main, tail = unpack_maps(e_ref[0], rows, copies, tensors)
        for t in range(tensors):
            whole = main(t)
            for s in range(HALF):
                piece = tail(t, s)
                cols = pl.ds(s * quarter, quarter)
                to = pl.ds(t * width + s * quarter, quarter)
                for src, dst in ((xr_ref, x_ref), (gr_ref, g_ref)):
                    dst[:, to] = (
                        jnp.dot(whole, src[:, cols], preferred_element_type=F32)
                        + jnp.dot(piece, src[:, width:base], preferred_element_type=F32)
                    ).astype(BF16)
        factor[...] = jnp.dot(main(0), xr_ref[:, base : base + LANES], preferred_element_type=F32) + jnp.dot(
            tail(0, 0), xr_ref[:, base + LANES : base + 2 * LANES], preferred_element_type=F32
        )
        acc[...] = jnp.zeros_like(acc)
        gates[...] = jnp.zeros_like(gates)

    nt = (((1,), (1,)), ((), ()))
    x = x_ref[...]
    hidden = lax.dot_general(x, wg_ref[...], nt, preferred_element_type=F32)
    upper = lax.dot_general(x, wu_ref[...], nt, preferred_element_type=F32)
    dact = lax.dot_general(g_ref[...], wd_ref[...], nt, preferred_element_type=F32)
    weight = factor[:, :1]
    sigma = 1.0 / (1.0 + jnp.exp(-hidden))
    silu = hidden * sigma
    act = silu * upper
    gates[...] += jnp.sum(act * dact, axis=1, keepdims=True)
    scaled = weight * dact
    wt_ref[0] = (weight * act).astype(BF16)
    dh = (scaled * upper * sigma * (1.0 + hidden * (1.0 - sigma))).astype(BF16)
    du = (scaled * silu).astype(BF16)
    dh_ref[0] = dh
    du_ref[0] = du
    acc[...] += jnp.dot(dh, wg_ref[...], preferred_element_type=F32) + jnp.dot(
        du, wu_ref[...], preferred_element_type=F32
    )

    @pl.when(step == pl.num_programs(0) - 1)
    def _():
        whole = copies * MAIN
        for c in range(copies):
            for t in range(tensors):
                at = (c * tensors + t) * MAIN
                back_ref[at : at + MAIN, :width] = acc[c * MAIN : (c + 1) * MAIN, t * width : (t + 1) * width]
                back_ref[at : at + MAIN, base : base + LANES] = gates[c * MAIN : (c + 1) * MAIN, :]
                for a in range(EXPERTS_ON):
                    r = whole + c * EXPERTS_ON + a
                    back_ref[at + a * HALF : at + (a + 1) * HALF, base + LANES :] = jnp.broadcast_to(
                        gates[r : r + 1, :], (HALF, LANES)
                    )
                    for s in range(HALF):
                        back_ref[at + a * HALF + s : at + a * HALF + s + 1, width:base] = acc[
                            r : r + 1, t * width + s * quarter : t * width + (s + 1) * quarter
                        ]


def tile_of(hidden):
    sizes = [n for n in range(16, 257, 16) if hidden % n == 0]
    return max(sizes) if sizes else hidden


def forward(copies, tensors, e, xr, gr, w_gate, w_up, w_down):
    hidden, depth = w_gate.shape
    width = depth // tensors
    rows = -(-copies * EXPERTS_ON * CAP // 16) * 16
    tile = tile_of(hidden)
    steps = hidden // tile
    back = (copies * tensors * MAIN, width + width // HALF + 2 * LANES)
    held = jax.ShapeDtypeStruct((rows, depth), BF16)
    per_unit = jax.ShapeDtypeStruct((steps, rows, tile), BF16)
    full = lambda shape: pl.BlockSpec(shape, lambda i: (0, 0))
    weights = pl.BlockSpec((tile, depth), lambda i: (i, 0))
    unit = pl.BlockSpec((1, rows, tile), lambda i: (i, 0, 0))
    return pl.pallas_call(
        functools.partial(forward_body, copies, tensors),
        grid=(steps,),
        out_shape=(held, held, per_unit, per_unit, per_unit, jax.ShapeDtypeStruct(back, F32)),
        in_specs=[pl.BlockSpec(memory_space=pltpu.SMEM), full(xr.shape), full(gr.shape), weights, weights, weights],
        out_specs=[full((rows, depth)), full((rows, depth)), unit, unit, unit, full(back)],
        scratch_shapes=[
            pltpu.VMEM((rows, LANES), F32),
            pltpu.VMEM((rows, depth), F32),
            pltpu.VMEM((rows, LANES), F32),
        ],
        compiler_params=pltpu.CompilerParams(vmem_limit_bytes=48 * MIB),
        cost_estimate=pl.CostEstimate(
            flops=10 * rows * hidden * depth, bytes_accessed=6 * hidden * depth, transcendentals=rows * hidden
        ),
        name="hidden_and_inputs",
    )(e, xr, gr, w_gate, w_up, w_down)


def weights_body(x_ref, g_ref, wt_ref, dh_ref, du_ref, og_ref, ou_ref, od_ref):
    tn = (((0,), (0,)), ((), ()))
    for left, right, out in ((dh_ref, x_ref, og_ref), (du_ref, x_ref, ou_ref), (wt_ref, g_ref, od_ref)):
        out[...] = lax.dot_general(left[0], right[...], tn, preferred_element_type=F32).astype(BF16)


def weight_grads(x, g, wt, dh, du):
    rows, depth = x.shape
    steps, _, tile = wt.shape
    hidden = steps * tile
    full = pl.BlockSpec((rows, depth), lambda i: (0, 0))
    unit = pl.BlockSpec((1, rows, tile), lambda i: (i, 0, 0))
    out = pl.BlockSpec((tile, depth), lambda i: (i, 0))
    return pl.pallas_call(
        weights_body,
        grid=(steps,),
        out_shape=[jax.ShapeDtypeStruct((hidden, depth), BF16)] * 3,
        in_specs=[full, full, unit, unit, unit],
        out_specs=[out, out, out],
        compiler_params=pltpu.CompilerParams(vmem_limit_bytes=48 * MIB),
        cost_estimate=pl.CostEstimate(
            flops=6 * rows * hidden * depth, bytes_accessed=6 * hidden * depth, transcendentals=0
        ),
        name="weight_grads",
    )(x, g, wt, dh, du)


def finish_body(first_ref, ids_ref, mine_ref, got_ref, tok_ref, gate_ref):
    ids = ids_ref[...]
    toks, width = tok_ref.shape
    quarter = width // HALF
    base = width + quarter
    expert, place, last = slots(first_ref[0], toks)
    main, hits = selection(ids, expert, place)
    tail, _ = selection(ids, expert, last)
    row = iota((MAIN, toks), 0)
    part = jnp.where(row >= HALF, row - HALF, row)
    tn = (((0,), (0,)), ((), ()))
    exact = dict(precision=lax.Precision.HIGHEST, preferred_element_type=F32)
    data = jnp.concatenate([got_ref[...], mine_ref[HALF:, :]], axis=0)
    for s in range(HALF):
        cols = slice(s * quarter, (s + 1) * quarter)
        one = jnp.where(part == s, tail, 0.0)
        tok_ref[:, cols] = (
            lax.dot_general(main, data[:, cols], tn, **exact)
            + lax.dot_general(one, data[:, width:base], tn, **exact)
        ).astype(BF16)
    term = main * data[:, base : base + 1] + jnp.where(part == 0, tail, 0.0) * data[:, base + LANES : base + LANES + 1]
    for k, hit in enumerate(hits):
        gate_ref[k : k + 1, :] = jnp.sum(jnp.where(hit, term, 0.0), axis=0, keepdims=True)


def finish(first, ids_t, mine, got, width):
    top, toks = ids_t.shape
    return pl.pallas_call(
        finish_body,
        out_shape=(jax.ShapeDtypeStruct((toks, width), BF16), jax.ShapeDtypeStruct((top, toks), F32)),
        in_specs=[pl.BlockSpec(memory_space=pltpu.SMEM)] + [pl.BlockSpec(memory_space=pltpu.VMEM)] * 3,
        out_specs=[pl.BlockSpec(memory_space=pltpu.VMEM)] * 2,
        name="finish_tokens",
    )(first, ids_t, mine, got)


def on_device(tokens, grad_out, expert_ids, gate_probs, w_gate, w_up, w_down):
    n_expert = lax.axis_size("expert")
    tensors = lax.axis_size("tensor")
    copies = n_expert // EXPERTS_ON
    e = (lax.axis_index("expert") // copies).astype(jnp.int32).reshape(1)
    zero = jnp.zeros((1,), jnp.int32)
    ids_t = expert_ids.T
    x_rows, g_rows = pick(zero, ids_t, gate_probs.T, tokens, grad_out)
    axes = ("expert", "tensor")
    xr = lax.all_gather(x_rows, axes, axis=0, tiled=True)
    gr = lax.all_gather(g_rows, axes, axis=0, tiled=True)
    x, g, wt, dh, du, back = forward(copies, tensors, e, xr, gr, w_gate, w_up, w_down)
    size = copies * tensors
    groups = [list(range(n * size, (n + 1) * size)) for n in range(EXPERTS_ON)]
    mine = lax.psum_scatter(back, axes, scatter_dimension=0, axis_index_groups=groups, tiled=True)
    swap = [(i, (i + copies) % n_expert) for i in range(n_expert)]
    got = lax.ppermute(mine[:HALF], "expert", swap)
    grad_w_gate, grad_w_up, grad_w_down = weight_grads(x, g, wt, dh, du)
    token_grad, gate_t = finish(1 - e, ids_t, mine, got, tokens.shape[1])
    return token_grad, gate_t.T, grad_w_gate, grad_w_up, grad_w_down


def solution(mesh):
    return jax.shard_map(
        on_device,
        mesh=mesh,
        in_specs=(
            P(("groups", "expert"), "tensor"),
            P(("groups", "expert"), "tensor"),
            P(("groups", "expert"), None),
            P(("groups", "expert"), None),
            P(("expert", "tensor"), None),
            P(("expert", "tensor"), None),
            P(("expert", "tensor"), None),
        ),
        out_specs=(
            P(("groups", "expert"), "tensor"),
            P(("groups", "expert"), None),
            P(("expert", "tensor"), "groups"),
            P(("expert", "tensor"), "groups"),
            P(("expert", "tensor"), "groups"),
        ),
        check_vma=False,
    )
```

time: 172 us -> 146 us (0.85)
  matrix products: 73.9 us -> 0 us
  Pallas kernels: 0 us -> 55.8 us
  starting transfers between devices: 25.2 us -> 2.61 us
  blocking collectives: 7.52 us -> 26.7 us
  local copies, waits for them, and re-layouts: 7.23 us -> 2.77 us
  waiting for transfers between devices: 39.7 us -> 43.6 us
  other arithmetic: 3.44 us -> 0 us
    dot_general x14 -> x0, matrix products: 73.9 us -> none  [the longest x1 10.7 us: on_device(): lax.dot_general(rows_grad, w_down, contract_cols, preferred_element_type=...]
    pallas_call x0 -> x4, Pallas kernels: none -> 55.8 us  [the longest x1 34.1 us: forward(): pl.pallas_call(functools.partial(forward_body, copies, tensors), grid=(st...]
    all_to_all x5 -> x0, waiting for transfers between devices: 39.7 us -> none  [the longest x1 19.7 us: on_device(): lax.all_to_all(partial_rows, 'expert', split_axis=0, concat_axis=0, tiled...]
    reduce_scatter x1, waiting for transfers between devices: 0.01 us -> 27.4 us  [on_device(): lax.psum_scatter(back, axes, scatter_dimension=0, axis_index_groups=group...]
    all_to_all x5 -> x0, starting transfers between devices: 25.2 us -> none  [the longest x1 7.25 us: on_device(): lax.all_to_all(spread(gate_slots), 'expert', split_axis=0, concat_axis=0,...]
    all_gather x2 -> x1, blocking collectives: 4.5 us -> 26.7 us  [on_device(): gr = lax.all_gather(g_rows, axes, axis=0, tiled=True)]
    all_gather x0 -> x1, waiting for transfers between devices: none -> 16.2 us  [on_device(): xr = lax.all_gather(x_rows, axes, axis=0, tiled=True)]
    psum x1 -> x0, blocking collectives: 3.02 us -> none  [on_device(): grad_gates = lax.psum(gate_local, 'tensor')]
  transfers between devices with their start and end apart: 6 -> 3, of which waited for: 3 -> 2; matrix products, arithmetic and copies ran while one was open for 30% -> 0% of each run, Pallas kernels for 0% -> 12%
where the time goes in v1:
time: 146 us
  Pallas kernels  55.8 us (38%)
  waiting for transfers between devices  43.6 us (30%)
  blocking collectives  26.7 us (18%)
  between operations  14.1 us (10%)
  local copies, waits for them, and re-layouts  2.77 us (2%)
  starting transfers between devices  2.61 us (2%)
    pallas_call x1, Pallas kernels, forward(): pl.pallas_call(functools.partial(forward_body, copies, tensors), grid=(st...  34.1 us
    reduce_scatter x1, waiting for transfers between devices, on_device(): lax.psum_scatter(back, axes, scatter_dimension=0, axis_index_groups=group...  27.4 us
    all_gather x1, blocking collectives, on_device(): gr = lax.all_gather(g_rows, axes, axis=0, tiled=True)  26.7 us
    pallas_call x1, Pallas kernels, weight_grads(): pl.pallas_call(weights_body, grid=(steps,), out_shape=[jax.ShapeDtypeStru...  17.4 us
    all_gather x1, waiting for transfers between devices, on_device(): xr = lax.all_gather(x_rows, axes, axis=0, tiled=True)  16.2 us
  transfers between devices with their start and end apart: 3, of which 2 were waited for; matrix products, arithmetic and copies ran while one was open for 0% of the time, Pallas kernels for 12%

profile of v1, /device:TPU:0, one launch (start us, length us, event | category | flops | bytes accessed | tf_op | source)
XLA Modules:
  0.0 145.5 jit_solution(5183408183356894271)
XLA Ops:
  7.2 0.0 all-gather.2.cloned.1.call-start
  7.2 2.0 %pick_rows.1 = (bf16[8,4096]{1,0:T(8,128)(2,1)}, bf16[8,3840]{1,0:T(8,128)(2,1)}) custom-call(s32[1]{0:T(128)} %constant.25.clone.1.first_ref, s32[4,16]{1,0:T(4,128)} %bitcast.4, bf16[4,16]{1,0:T(4,128)(2,1)} %bitcast.6, bf16[16,3072]{1,0:T(8,128)(2,1)} %tok_ref.1, bf16[16,3072]{1,0:T(8,128)(2,1)} %grad_ref.1), custom_call_target="tpu_custom_call" | custom-call | tf_op jit(solution)/shard_map/pick_rows/pallas_call | solution.py:69
  9.2 0.0 all-gather.2.cloned.1.call-update
  9.2 0.0 reduce-scatter.2.cloned.1.call-start
  9.3 26.7 %all_gather.7.gr_ref = bf16[128,3840]{1,0:T(8,128)(2,1)S(1)} all-gather(bf16[8,3840]{1,0:T(8,128)(2,1)} %get-tuple-element.19), channel_id=1, replica_groups=mesh['groups'=2,'expert'=8,'tensor'=2] {'expert','tensor'}, dimensions={0}, use_global_device_ids=true | all-gather | bytes 1044480 | tf_op jit(solution)/shard_map/all_gather | solution.py:282
  35.9 16.2 %all-gather.2.cloned.1.call-done.xr_ref = bf16[128,4096]{1,0:T(8,128)(2,1)} async-done(((bf16[8,4096]{1,0:T(8,128)(2,1)}), bf16[128,4096]{1,0:T(8,128)(2,1)}) %all-gather.2.cloned.1.call-update) | async-done | bytes 1048592 | tf_op jit(solution)/shard_map/all_gather | solution.py:281
  52.1 0.0 copy-start
  52.1 1.2 copy-done
  53.4 34.1 %hidden_and_inputs.1 = (bf16[48,6144]{1,0:T(8,128)(2,1)S(1)}, bf16[48,6144]{1,0:T(8,128)(2,1)S(1)}, bf16[6,48,224]{2,1,0:T(8,128)(2,1)S(1)}, bf16[6,48,224]{2,1,...) custom-call(s32[1]{0:T(128)} %bitcast.e_ref, bf16[128,4096]{1,0:T(8,128)(2,1)S(1)} %copy-done, ...), custom_call_target="tpu_custom_call" | custom-call | flops 3963617280 | bytes 49545216 | tf_op jit(solution)/shard_map/hidden_and_inputs/pallas_call | solution.py:190
  87.5 0.0 reduce-scatter.2.cloned.1.call-update
  87.5 27.4 %reduce-scatter.2.cloned.1.call-done.mine_ref = f32[8,4096]{1,0:T(8,128)} async-done(((f32[64,4096]{1,0:T(8,128)}), f32[8,4096]{1,0:T(8,128)}) %reduce-scatter.2.cloned.1.call-update) | async-done | bytes 131088 | tf_op jit(solution)/shard_map/reduce_scatter | solution.py:286
  114.9 0.9 slice.4
  115.8 2.5 %collective-permute-start = (f32[4,4096]{1,0:T(4,128)S(1)}, f32[4,4096]{1,0:T(4,128)S(1)}, u32[]{:S(2)}, u32[]{:S(2)}) collective-permute-start(f32[4,4096]{1,0:T(4,128)S(1)} %slice.4), channel_id=1, source_target_pairs={{0,8},{2,10},{4,12},{6,14},{8,0},{10,2},{12,4},{14,6},{1,9},{3,11}... | collective-permute-start | bytes 196616 | tf_op jit(solution)/shard_map/ppermute | solution.py:288
  118.3 17.4 %weight_grads.1 = (bf16[1344,6144]{1,0:T(8,128)(2,1)}, bf16[1344,6144]{1,0:T(8,128)(2,1)}, bf16[1344,6144]{1,0:T(8,128)(2,1)}) custom-call(bf16[48,6144]{1,0:T(8,128)(2,1)S(1)} %get-tuple-element.23.x_ref, bf16[48,6144]{1,0:T(8,128)(2,1)S(1)} %get-tuple-element.24.g_ref, bf16[6,48,224]{2,1,0:T(8,128)(2,1)S(1)} %get-tuple-element.25.wt_ref, ...), custom_call_target="tpu_custom_call" | custom-call | flops 2378170368 | bytes 49545216 | tf_op jit(solution)/shard_map/weight_grads/pallas_call | solution.py:222
  135.7 0.0 collective-permute-done.got_ref
  135.7 0.0 copy-start.1
  135.7 0.6 copy-done.1
  136.3 2.4 %finish_tokens.1 = (bf16[16,3072]{1,0:T(8,128)(2,1)}, f32[4,16]{1,0:T(4,128)}) custom-call(s32[1]{0:T(128)S(6)} %sub.8.first_ref, s32[4,16]{1,0:T(4,128)} %bitcast.5, f32[8,4096]{1,0:T(8,128)} %reduce-scatter.2.cloned.1.call-done.mine_ref, f32[4,4096]{1,0:T(4,128)} %copy-done.1), custom_call_target="tpu_custom_call" | custom-call | tf_op jit(solution)/shard_map/finish_tokens/pallas_call | solution.py:263
Async XLA Ops:
  7.2 45.0 %all-gather.2.cloned.1.call-start = ((), (), s32[]{:S(2)}) async-start(), calls=%async_computation.1 | async-start | bytes 1114112 | tf_op jit(solution)/shard_map/all_gather | solution.py:281
  9.2 105.6 %reduce-scatter.2.cloned.1.call-start = ((), (), s32[]{:S(2)}) async-start(), calls=%async_computation.2 | async-start | bytes 1179648 | tf_op jit(solution)/shard_map/reduce_scatter | solution.py:286
  52.1 1.2 copy-start
  115.8 19.9 %collective-permute-start = (f32[4,4096]{1,0:T(4,128)S(1)}, f32[4,4096]{1,0:T(4,128)S(1)}, u32[]{:S(2)}, u32[]{:S(2)}) collective-permute-start(f32[4,4096]{1,0:T(4,128)S(1)} %slice.4), channel_id=1, source_target_pairs={{0,8},{2,10},{4,12},{6,14},{8,0},{10,2},{12,4},{14,6},{1,9},{3,11}... | collective-permute-start | bytes 196616 | tf_op jit(solution)/shard_map/ppermute | solution.py:288
  135.7 0.6 copy-start.1
Sparse Core Ops, SparseCore 0:
  10.7 41.3 all-gather.1
  87.6 27.2 reduce-scatter.1

commit v2 on v0

v2 whole, which is shorter than its diff:
```python
import functools

import jax
import jax.numpy as jnp
from jax import lax
from jax.experimental import pallas as pl
from jax.experimental.pallas import tpu as pltpu
from jax.sharding import PartitionSpec as P

EXPERTS_ON = 2
CAP = 5
LANES = 128
SUBS = 8
WHOLE = 4
F32 = jnp.float32
BF16 = jnp.bfloat16
MIB = 1 << 20
CHUNK = 512
VMEM = pl.BlockSpec(memory_space=pltpu.VMEM)
SMEM = pl.BlockSpec(memory_space=pltpu.SMEM)


def iota(shape, dim):
    return lax.broadcasted_iota(jnp.int32, shape, dim)


def chosen_rows(ids, expert, position):
    rows, toks = position.shape
    hits = [ids[k : k + 1, :] == expert for k in range(ids.shape[0])]
    member = functools.reduce(jnp.logical_or, hits).astype(F32)
    before = (iota((toks, toks), 0) < iota((toks, toks), 1)).astype(F32)
    earlier = jnp.dot(member, before, preferred_element_type=F32)
    return jnp.where(earlier == position.astype(F32), member, 0.0), hits


def sub_row(rows, toks):
    return iota((rows, toks), 0) % SUBS


def pick_body(e_ref, ids_ref, probs_ref, tok_ref, grad_ref, x_own, x_oth, g_own, g_oth):
    ids = ids_ref[...]
    probs = probs_ref[...].astype(F32)
    toks, width = tok_ref.shape
    half, eighth = width // 2, width // SUBS
    both = 2 * SUBS
    row = iota((both, toks), 0)
    sub = sub_row(both, toks)
    expert = jnp.where(row < SUBS, e_ref[0], 1 - e_ref[0])
    main, hits = chosen_rows(ids, expert, sub % WHOLE)
    tail, _ = chosen_rows(ids, expert, jnp.full((both, toks), WHOLE, jnp.int32))
    plain = jnp.where(sub < WHOLE, main, jnp.where(sub == WHOLE, tail, 0.0))
    for src, own, oth in ((tok_ref, x_own, x_oth), (grad_ref, g_own, g_oth)):
        packed = sum(
            jnp.dot(
                jnp.where(sub // WHOLE == h, main, 0.0).astype(BF16),
                src[:, h * half : (h + 1) * half],
                preferred_element_type=F32,
            )
            for h in range(2)
        ).astype(BF16)
        last = sum(
            jnp.dot(
                jnp.where(sub == s, tail, 0.0).astype(BF16),
                src[:, s * eighth : (s + 1) * eighth],
                preferred_element_type=F32,
            )
            for s in range(SUBS)
        ).astype(BF16)
        for n, dst in enumerate((own, oth)):
            dst[:, :half] = packed[n * SUBS : (n + 1) * SUBS]
            dst[:, half : half + eighth] = last[n * SUBS : (n + 1) * SUBS]
    weight = sum(jnp.where(hit, probs[k : k + 1, :], 0.0) for k, hit in enumerate(hits))
    gate = jnp.broadcast_to(jnp.sum(plain * weight, axis=1, keepdims=True), (both, LANES)).astype(BF16)
    for n, dst in enumerate((x_own, x_oth)):
        dst[:, half + eighth :] = gate[n * SUBS : (n + 1) * SUBS]


def pick(e, ids_t, probs_t, tokens, grad_out):
    width = tokens.shape[1]
    size = width // 2 + width // SUBS
    with_gate = jax.ShapeDtypeStruct((SUBS, size + LANES), BF16)
    without = jax.ShapeDtypeStruct((SUBS, size), BF16)
    return pl.pallas_call(
        pick_body,
        out_shape=(with_gate, with_gate, without, without),
        in_specs=[SMEM] + [VMEM] * 4,
        out_specs=[VMEM] * 4,
        name="pick_rows",
    )(e, ids_t, probs_t, tokens, grad_out)


def assemble_body(count, width, *refs):
    pieces, outs, held = refs[:count], refs[count:-1], refs[-1]
    half, eighth = width // 2, width // SUBS
    held[...] = jnp.zeros_like(held)
    for n, ref in enumerate(pieces):
        piece = ref[...].astype(F32)
        at = n * SUBS
        for h in range(2):
            held[at : at + WHOLE, h * half : (h + 1) * half] = piece[h * WHOLE : (h + 1) * WHOLE, :half]
        for s in range(SUBS):
            held[at + WHOLE : at + WHOLE + 1, s * eighth : (s + 1) * eighth] = piece[s : s + 1, half : half + eighth]
        if len(outs) == 2:
            outs[1][at : at + SUBS, :] = piece[:, half + eighth :]
    outs[0][...] = held[...].astype(BF16)


def assemble(pieces, width, gated):
    count = len(pieces)
    rows = count * SUBS
    shapes = [jax.ShapeDtypeStruct((rows, width), BF16)]
    if gated:
        shapes.append(jax.ShapeDtypeStruct((rows, LANES), F32))
    return pl.pallas_call(
        functools.partial(assemble_body, count, width),
        out_shape=shapes,
        in_specs=[VMEM] * count,
        out_specs=[VMEM] * len(shapes),
        scratch_shapes=[pltpu.VMEM((rows, width), F32)],
        name="assemble_rows",
    )(*pieces)


def tile_of(hidden, most):
    sizes = [n for n in range(16, most + 1, 16) if hidden % n == 0]
    return max(sizes) if sizes else hidden


def column_map(chunks):
    return lambda i, t: jnp.where(i < chunks, t, 1 - t) * chunks + lax.rem(i, chunks)


NT = (((1,), (1,)), ((), ()))


def hidden_body(chunks, t_ref, xa_ref, xb_ref, wg_ref, wu_ref, h_ref, u_ref):
    step = pl.program_id(0)
    x = jnp.where(step < chunks, xa_ref[...], xb_ref[...])

    @pl.when(step == 0)
    def _():
        h_ref[...] = jnp.zeros_like(h_ref)
        u_ref[...] = jnp.zeros_like(u_ref)

    h_ref[...] += lax.dot_general(wg_ref[...], x, NT, preferred_element_type=F32)
    u_ref[...] += lax.dot_general(wu_ref[...], x, NT, preferred_element_type=F32)


def halves_specs(rows, chunk, chunks):
    own = pl.BlockSpec((rows, chunk), lambda i, t: (0, jnp.minimum(i, chunks - 1)))
    oth = pl.BlockSpec((rows, chunk), lambda i, t: (0, jnp.clip(i - chunks, 0, chunks - 1)))
    return [own, oth]


def hidden_units(t, xa, xb, w_gate, w_up):
    hidden, depth = w_gate.shape
    rows, width = xa.shape
    chunk = CHUNK
    chunks = width // chunk
    column = column_map(chunks)
    unit = jax.ShapeDtypeStruct((hidden, rows), F32)
    kept = pl.BlockSpec((hidden, rows), lambda i, t: (0, 0))
    weight = pl.BlockSpec((hidden, chunk), lambda i, t: (0, column(i, t[0])))
    return pl.pallas_call(
        functools.partial(hidden_body, chunks),
        out_shape=(unit, unit),
        grid_spec=pltpu.PrefetchScalarGridSpec(
            num_scalar_prefetch=1,
            grid=(2 * chunks,),
            in_specs=halves_specs(rows, chunk, chunks) + [weight, weight],
            out_specs=[kept, kept],
        ),
        compiler_params=pltpu.CompilerParams(vmem_limit_bytes=32 * MIB),
        cost_estimate=pl.CostEstimate(
            flops=4 * rows * hidden * depth, bytes_accessed=4 * hidden * depth, transcendentals=0
        ),
        name="hidden_units",
    )(t, xa, xb, w_gate, w_up)


def inputs_body(chunks, t_ref, ga_ref, gb_ref, factor_ref, h_ref, u_ref, wd_ref, wg_ref, wu_ref,
                wt_ref, dh_ref, du_ref, dhr_ref, dur_ref, gate_ref, give_ref, dact):
    step = pl.program_id(0)
    last = 2 * chunks - 1
    rows = ga_ref.shape[0]

    @pl.when(step == 0)
    def _():
        dact[...] = jnp.zeros_like(dact)

    @pl.when(step <= last)
    def _():
        g = jnp.where(step < chunks, ga_ref[...], gb_ref[...])
        dact[...] += lax.dot_general(wd_ref[...], g, NT, preferred_element_type=F32)

    @pl.when(step == last)
    def _():
        weight = factor_ref[...].T[:1, :]
        h = h_ref[...]
        u = u_ref[...]
        da = dact[...]
        sigma = 1.0 / (1.0 + jnp.exp(-h))
        silu = h * sigma
        act = silu * u
        scaled = weight * da
        wt_ref[...] = (weight * act).astype(BF16)
        dh = scaled * u * sigma * (1.0 + h * (1.0 - sigma))
        du = scaled * silu
        dh_ref[...] = dh.astype(BF16)
        du_ref[...] = du.astype(BF16)
        dhr_ref[...] = dh.T.astype(BF16)
        dur_ref[...] = du.T.astype(BF16)
        total = jnp.sum(act * da, axis=0, keepdims=True)
        gate_ref[...] = jnp.broadcast_to(total, (LANES, rows)).T

    @pl.when(step > last)
    def _():
        give_ref[...] = jnp.dot(dhr_ref[...], wg_ref[...], preferred_element_type=F32) + jnp.dot(
            dur_ref[...], wu_ref[...], preferred_element_type=F32
        )


def first_input_grads(t, ga, gb, factor, h, u, w_gate, w_up, w_down):
    hidden, depth = w_gate.shape
    rows, width = ga.shape
    chunk = CHUNK
    chunks = width // chunk
    column = column_map(chunks)
    last = 2 * chunks - 1
    full = lambda shape: pl.BlockSpec(shape, lambda i, t: (0, 0))
    down = pl.BlockSpec((hidden, chunk), lambda i, t: (0, column(jnp.minimum(i, last), t[0])))
    later = lambda i: jnp.maximum(i - last - 1, 0)
    other = pl.BlockSpec((hidden, chunk), lambda i, t: (0, column(chunks + later(i), t[0])))
    unit = jax.ShapeDtypeStruct((hidden, rows), BF16)
    turned = jax.ShapeDtypeStruct((rows, hidden), BF16)
    return pl.pallas_call(
        functools.partial(inputs_body, chunks),
        out_shape=(
            unit,
            unit,
            unit,
            turned,
            turned,
            jax.ShapeDtypeStruct((rows, LANES), F32),
            jax.ShapeDtypeStruct((rows, width), F32),
        ),
        grid_spec=pltpu.PrefetchScalarGridSpec(
            num_scalar_prefetch=1,
            grid=(3 * chunks,),
            in_specs=halves_specs(rows, chunk, chunks)
            + [full((rows, LANES)), full((hidden, rows)), full((hidden, rows)), down, other, other],
            out_specs=[full((hidden, rows))] * 3
            + [full((rows, hidden))] * 2
            + [full((rows, LANES)), pl.BlockSpec((rows, chunk), lambda i, t: (0, later(i)))],
            scratch_shapes=[pltpu.VMEM((hidden, rows), F32)],
        ),
        compiler_params=pltpu.CompilerParams(vmem_limit_bytes=40 * MIB),
        cost_estimate=pl.CostEstimate(
            flops=4 * rows * hidden * depth, bytes_accessed=4 * hidden * depth, transcendentals=rows * hidden
        ),
        name="give_half",
    )(t, ga, gb, factor, h, u, w_down, w_gate, w_up)


def keep_body(t_ref, dhr_ref, dur_ref, wg_ref, wu_ref, keep_ref):
    keep_ref[...] = jnp.dot(dhr_ref[...], wg_ref[...], preferred_element_type=F32) + jnp.dot(
        dur_ref[...], wu_ref[...], preferred_element_type=F32
    )


def second_input_grads(t, dhr, dur, w_gate, w_up, width):
    hidden, depth = w_gate.shape
    rows = dhr.shape[0]
    chunk = CHUNK
    chunks = width // chunk
    column = column_map(chunks)
    full = pl.BlockSpec((rows, hidden), lambda i, t: (0, 0))
    own = pl.BlockSpec((hidden, chunk), lambda i, t: (0, column(i, t[0])))
    return pl.pallas_call(
        keep_body,
        out_shape=jax.ShapeDtypeStruct((rows, width), F32),
        grid_spec=pltpu.PrefetchScalarGridSpec(
            num_scalar_prefetch=1,
            grid=(chunks,),
            in_specs=[full, full, own, own],
            out_specs=pl.BlockSpec((rows, chunk), lambda i, t: (0, i)),
        ),
        compiler_params=pltpu.CompilerParams(vmem_limit_bytes=32 * MIB),
        cost_estimate=pl.CostEstimate(
            flops=4 * rows * hidden * width, bytes_accessed=4 * hidden * width, transcendentals=0
        ),
        name="keep_half",
    )(t, dhr, dur, w_gate, w_up)


def weights_body(t_ref, left_ref, own_ref, oth_ref, out_ref):
    width = own_ref.shape[1]
    t = t_ref[0]
    for at, ref in ((t, own_ref), (1 - t, oth_ref)):
        cols = pl.ds(pl.multiple_of(at * width, width), width)
        out_ref[:, cols] = jnp.dot(left_ref[...], ref[...], preferred_element_type=F32).astype(BF16)


def weight_grad(t, left, own, oth, name):
    hidden, rows = left.shape
    width = own.shape[1]
    depth = 2 * width
    tile = tile_of(hidden, 192)
    half = pl.BlockSpec((rows, width), lambda i, t: (0, 0))
    return pl.pallas_call(
        weights_body,
        out_shape=jax.ShapeDtypeStruct((hidden, depth), BF16),
        grid_spec=pltpu.PrefetchScalarGridSpec(
            num_scalar_prefetch=1,
            grid=(hidden // tile,),
            in_specs=[pl.BlockSpec((tile, rows), lambda i, t: (i, 0)), half, half],
            out_specs=pl.BlockSpec((tile, depth), lambda i, t: (i, 0)),
        ),
        compiler_params=pltpu.CompilerParams(vmem_limit_bytes=24 * MIB),
        cost_estimate=pl.CostEstimate(
            flops=2 * rows * hidden * depth, bytes_accessed=2 * hidden * depth, transcendentals=0
        ),
        name=name,
    )(t, left, own, oth)


def fold_body(copies, keep_ref, got_ref, gate_mine, gate_got, *outs):
    width = keep_ref.shape[1]
    half, eighth = width // 2, width // SUBS
    both = 2 * SUBS
    for d in range(copies):
        out = outs[d]
        for a in range(2):
            r = d * both + a * SUBS
            to = a * SUBS
            block = keep_ref[r : r + SUBS, :] + got_ref[r : r + SUBS, :]
            for h in range(2):
                out[to + h * WHOLE : to + (h + 1) * WHOLE, :half] = block[:WHOLE, h * half : (h + 1) * half]
            for s in range(SUBS):
                out[to + s : to + s + 1, half : half + eighth] = block[
                    WHOLE : WHOLE + 1, s * eighth : (s + 1) * eighth
                ]
            out[to : to + SUBS, half + eighth :] = gate_mine[r : r + SUBS, :] + gate_got[r : r + SUBS, :]


def fold(copies, keep, got, gate_mine, gate_got):
    width = keep.shape[1]
    size = width // 2 + width // SUBS + LANES
    return pl.pallas_call(
        functools.partial(fold_body, copies),
        out_shape=[jax.ShapeDtypeStruct((2 * SUBS, size), F32)] * copies,
        in_specs=[VMEM] * 4,
        out_specs=[VMEM] * copies,
        name="fold_cores",
    )(keep, got, gate_mine, gate_got)


def finish_body(e_ref, ids_ref, mine_ref, got_ref, tok_ref, gate_ref):
    ids = ids_ref[...]
    toks, width = tok_ref.shape
    half, eighth = width // 2, width // SUBS
    both = 2 * SUBS
    row = iota((both, toks), 0)
    sub = sub_row(both, toks)
    expert = jnp.where(row < SUBS, e_ref[0], 1 - e_ref[0])
    main, hits = chosen_rows(ids, expert, sub % WHOLE)
    tail, _ = chosen_rows(ids, expert, jnp.full((both, toks), WHOLE, jnp.int32))
    plain = jnp.where(sub < WHOLE, main, jnp.where(sub == WHOLE, tail, 0.0))
    data = jnp.concatenate([mine_ref[...], got_ref[...]], axis=0)
    tn = (((0,), (0,)), ((), ()))
    exact = dict(precision=lax.Precision.HIGHEST, preferred_element_type=F32)
    halves = [
        lax.dot_general(jnp.where(sub // WHOLE == h, main, 0.0), data[:, :half], tn, **exact) for h in range(2)
    ]
    for s in range(SUBS):
        last = lax.dot_general(jnp.where(sub == s, tail, 0.0), data[:, half : half + eighth], tn, **exact)
        h, at = divmod(s * eighth, half)
        tok_ref[:, s * eighth : (s + 1) * eighth] = (halves[h][:, at : at + eighth] + last).astype(BF16)
    term = plain * data[:, half + eighth : half + eighth + 1]
    for k, hit in enumerate(hits):
        gate_ref[k : k + 1, :] = jnp.sum(jnp.where(hit, term, 0.0), axis=0, keepdims=True)


def finish(e, ids_t, mine, got, width):
    top, toks = ids_t.shape
    return pl.pallas_call(
        finish_body,
        out_shape=(jax.ShapeDtypeStruct((toks, width), BF16), jax.ShapeDtypeStruct((top, toks), F32)),
        in_specs=[SMEM] + [VMEM] * 3,
        out_specs=[VMEM] * 2,
        name="finish_tokens",
    )(e, ids_t, mine, got)


def on_device(tokens, grad_out, expert_ids, gate_probs, w_gate, w_up, w_down):
    n_expert = lax.axis_size("expert")
    copies = n_expert // EXPERTS_ON
    place = lax.axis_index("expert")
    e = (place >= copies).astype(jnp.int32).reshape(1)
    t = lax.axis_index("tensor").astype(jnp.int32).reshape(1)
    width = tokens.shape[1]

    def partner(v):
        return lax.ppermute(v, "expert", [(i, (i + copies) % n_expert) for i in range(n_expert)])

    def across(v, d):
        return lax.ppermute(v, "expert", [(i, i ^ d) for i in range(n_expert)])

    def other_core(v):
        return lax.ppermute(v, "tensor", [(0, 1), (1, 0)])

    def spread(own, oth):
        got = partner(oth)
        first = [own if d == 0 else across(own, d) for d in range(copies)]
        second = [got if d == 0 else across(got, d) for d in range(copies)]
        return [piece for pair in zip(first, second) for piece in pair]

    w_gate, w_up, w_down = (pltpu.with_memory_space_constraint(w, pltpu.HBM) for w in (w_gate, w_up, w_down))
    ids_t = expert_ids.T
    x_own, x_oth, g_own, g_oth = pick(e, ids_t, gate_probs.T, tokens, grad_out)
    xa, factor = assemble(spread(x_own, x_oth), width, True)
    xb = other_core(xa)
    (ga,) = assemble(spread(g_own, g_oth), width, False)
    gb = other_core(ga)
    h, u = hidden_units(t, xa, xb, w_gate, w_up)
    wt, dh, du, dhr, dur, gate, give = first_input_grads(t, ga, gb, factor, h, u, w_gate, w_up, w_down)
    got, gate_got = other_core(give), other_core(gate)
    keep = second_input_grads(t, dhr, dur, w_gate, w_up, width)
    keep, got, gate_got = lax.optimization_barrier((keep, got, gate_got))
    blocks = fold(copies, keep, got, gate, gate_got)
    arrived = [across(blocks[d], d) for d in range(1, copies)]
    dh, mine = lax.optimization_barrier((dh, blocks[0]))
    grad_w_gate = weight_grad(t, dh, xa, xb, "grad_w_gate")
    grad_w_gate, du, arrived = lax.optimization_barrier((grad_w_gate, du, arrived))
    summed = functools.reduce(jnp.add, arrived, mine)
    theirs = partner(summed[SUBS:])
    du, summed = lax.optimization_barrier((du, summed))
    grad_w_up = weight_grad(t, du, xa, xb, "grad_w_up")
    grad_w_down = weight_grad(t, wt, ga, gb, "grad_w_down")
    grad_w_up, grad_w_down, theirs = lax.optimization_barrier((grad_w_up, grad_w_down, theirs))
    token_grad, gate_t = finish(e, ids_t, summed[:SUBS], theirs, width)
    return token_grad, gate_t.T, grad_w_gate, grad_w_up, grad_w_down


def solution(mesh):
    return jax.shard_map(
        on_device,
        mesh=mesh,
        in_specs=(
            P(("groups", "expert"), "tensor"),
            P(("groups", "expert"), "tensor"),
            P(("groups", "expert"), None),
            P(("groups", "expert"), None),
            P(("expert", "tensor"), None),
            P(("expert", "tensor"), None),
            P(("expert", "tensor"), None),
        ),
        out_specs=(
            P(("groups", "expert"), "tensor"),
            P(("groups", "expert"), None),
            P(("expert", "tensor"), "groups"),
            P(("expert", "tensor"), "groups"),
            P(("expert", "tensor"), "groups"),
        ),
        check_vma=False,
    )
```

time: 172 us -> 124 us (0.72)
  Pallas kernels: 0 us -> 84.3 us
  matrix products: 73.9 us -> 0 us
  waiting for transfers between devices: 39.7 us -> 6.88 us
  between operations: 14.2 us -> 0.85 us
  blocking collectives: 7.52 us -> 0 us
  other arithmetic: 3.44 us -> 0.03 us
    pallas_call x0 -> x11, Pallas kernels: none -> 84.3 us  [the longest x3 25.9 us: weight_grad(): pl.pallas_call(weights_body, out_shape=jax.ShapeDtypeStruct((hidden, dept...]
    dot_general x14 -> x0, matrix products: 73.9 us -> none  [the longest x1 10.7 us: on_device(): lax.dot_general(rows_grad, w_down, contract_cols, preferred_element_type=...]
    all_to_all x5 -> x0, waiting for transfers between devices: 39.7 us -> none  [the longest x1 19.7 us: on_device(): lax.all_to_all(partial_rows, 'expert', split_axis=0, concat_axis=0, tiled...]
    ppermute x0 -> x22, starting transfers between devices: none -> 25.3 us  [the longest x15 17.4 us: across(): return lax.ppermute(v, 'expert', [(i, i ^ d) for i in range(n_expert)])]
    all_to_all x5 -> x0, starting transfers between devices: 25.2 us -> none  [the longest x1 7.25 us: on_device(): lax.all_to_all(spread(gate_slots), 'expert', split_axis=0, concat_axis=0,...]
    ppermute x0 -> x22, waiting for transfers between devices: none -> 6.88 us  [the longest x15 6.87 us: across(): return lax.ppermute(v, 'expert', [(i, i ^ d) for i in range(n_expert)])]
    all_gather x2 -> x0, blocking collectives: 4.5 us -> none  [the longest x1 2.26 us: on_device(): lax.all_gather(grad_out, 'tensor', axis=1, tiled=True)]
    unnamed x14 -> x48, local copies, waits for them, and re-layouts: 1.58 us -> 5.33 us
  transfers between devices with their start and end apart: 6 -> 22, of which waited for: 3 -> 8; matrix products, arithmetic and copies ran while one was open for 30% -> 0% of each run, Pallas kernels for 0% -> 44%
where the time goes in v2:
time: 124 us; the launch traced here: 123 us
  Pallas kernels  84.3 us (68%)
  starting transfers between devices  25.3 us (20%)
  waiting for transfers between devices  6.88 us (6%)
  local copies, waits for them, and re-layouts  5.96 us (5%)
    pallas_call x3, Pallas kernels, weight_grad(): pl.pallas_call(weights_body, out_shape=jax.ShapeDtypeStruct((hidden, dept...  25.9 us
    pallas_call x1, Pallas kernels, first_input_grads(): pl.pallas_call(functools.partial(inputs_body, chunks), out_shape=(unit, u...  21.9 us
    pallas_call x1, Pallas kernels, hidden_units(): pl.pallas_call(functools.partial(hidden_body, chunks), out_shape=(unit, u...  17.9 us
    ppermute x15, starting transfers between devices, across(): return lax.ppermute(v, 'expert', [(i, i ^ d) for i in range(n_expert)])  17.4 us
    pallas_call x1, Pallas kernels, second_input_grads(): pl.pallas_call(keep_body, out_shape=jax.ShapeDtypeStruct((rows, width), F...  8.46 us
    ppermute x3, starting transfers between devices, partner(): lax.ppermute(v, 'expert', [(i, (i + copies) % n_expert) for i in range(n_...  7.12 us
    ppermute x15, waiting for transfers between devices, across(): return lax.ppermute(v, 'expert', [(i, i ^ d) for i in range(n_expert)])  6.87 us
    unnamed x48, local copies, waits for them, and re-layouts  5.33 us
  transfers between devices with their start and end apart: 22, of which 8 were waited for; matrix products, arithmetic and copies ran while one was open for 0% of the time, Pallas kernels for 44%

profile of v2, /device:TPU:0, one launch (start us, length us, event | category | flops | bytes accessed | tf_op | source)
XLA Modules:
  0.0 123.3 jit_solution(6654640021604508265)
XLA Ops:
  0.6 2.0 %pick_rows.1 = (bf16[8,2048]{1,0:T(8,128)(2,1)}, bf16[8,2048]{1,0:T(8,128)(2,1)}, bf16[8,1920]{1,0:T(8,128)(2,1)}, bf16[8,1920]{1,0:T(8,128)(2,1)}) custom-call(s32[1]{0:T(128)} %bitcast.e_ref, s32[4,16]{1,0:T(4,128)} %bitcast.5, bf16[4,16]{1,0:T(4,128)(2,1)} %bitcast.7, bf16[16,3072]{1,0:T(8,128)(2,1)} %tok_ref.1, bf16[16,3072]{1,0:T(8,128)(2,1)} %grad_ref.1), custom_call_target="tpu_custom_call" | custom-call | tf_op jit(solution)/shard_map/pick_rows/pallas_call | solution.py:83
  2.6 4.0 %collective-permute-start.8 = (bf16[8,2048]{1,0:T(8,128)(2,1)}, bf16[8,2048]{1,0:T(8,128)(2,1)S(1)}, u32[]{:S(2)}, u32[]{:S(2)}) collective-permute-start(bf16[8,2048]{1,0:T(8,128)(2,1)} %get-tuple-element.44), channel_id=1, source_target_pairs={{0,8},{2,10},{4,12},{6,14},{8,0},{10,2},{12,4},{14,6},{1,9},{3,11}... | collective-permute-start | bytes 98312 | tf_op jit(solution)/shard_map/ppermute | solution.py:404
  6.7 2.5 %collective-permute-start.13 = (bf16[8,2048]{1,0:T(8,128)(2,1)}, bf16[8,2048]{1,0:T(8,128)(2,1)S(1)}, u32[]{:S(2)}, u32[]{:S(2)}) collective-permute-start(bf16[8,2048]{1,0:T(8,128)(2,1)} %get-tuple-element.43.refs_0_), channel_id=1, source_target_pairs={{0,6},{2,4},{4,2},{6,0},{8,14},{10,12},{12,10},{14,8},{1,7},{3,5},... | collective-permute-start | bytes 98312 | tf_op jit(solution)/shard_map/ppermute | solution.py:407
  9.2 0.4 collective-permute-start.11
  9.6 0.5 collective-permute-start.9
  10.2 0.0 collective-permute-done.8.refs_1_
  10.2 2.5 %collective-permute-start.14 = (bf16[8,2048]{1,0:T(8,128)(2,1)S(1)}, bf16[8,2048]{1,0:T(8,128)(2,1)S(1)}, u32[]{:S(2)}, u32[]{:S(2)}) collective-permute-start(bf16[8,2048]{1,0:T(8,128)(2,1)S(1)} %collective-permute-done.8.refs_1_), channel_id=1, source_target_pairs={{0,6},{2,4},{4,2},{6,0},{8,14},{10,12},{12,10},{14,8},{1,7},{3,5},... | collective-permute-start | bytes 98312 | tf_op jit(solution)/shard_map/ppermute | solution.py:407
  12.7 0.4 collective-permute-start.12
  13.1 0.0 collective-permute-done.13.refs_6_
  13.1 0.5 collective-permute-start.10
  13.7 0.0 collective-permute-done.11.refs_4_
  13.7 0.1 collective-permute-done.9.refs_2_
  13.8 1.2 collective-permute-done.14.refs_7_
  15.0 1.6 %collective-permute-done.12.refs_5_ = bf16[8,2048]{1,0:T(8,128)(2,1)S(1)} collective-permute-done((bf16[8,2048]{1,0:T(8,128)(2,1)S(1)}, bf16[8,2048]{1,0:T(8,128)(2,1)S(1)}, u32[]{:S(2)}, u32[]{:S(2)}) %collective-permute-start.12) | collective-permute-done | bytes 32800 | tf_op jit(solution)/shard_map/ppermute | solution.py:407
  16.6 0.5 collective-permute-done.10.refs_3_
  17.1 0.1 copy-done.15
  17.2 0.6 copy-done.16
  17.8 1.8 %assemble_rows.3 = (bf16[64,3072]{1,0:T(8,128)(2,1)}, f32[64,128]{1,0:T(8,128)}) custom-call(bf16[8,2048]{1,0:T(8,128)(2,1)} %get-tuple-element.43.refs_0_, bf16[8,2048]{1,0:T(8,128)(2,1)} %copy-done.10, bf16[8,2048]{1,0:T(8,128)(2,1)} %copy-done.13, bf16[8,2048]{1,0:T(8,128)(2,1)} %copy-done.16, bf16[8,2048]{1,0:T(8,128)(2,1)} %copy-done.12, ...), custom_call_target="tpu_custom_call" | custom-call | tf_op jit(solution)/shard_map/assemble_rows/pallas_call | solution.py:114
  19.6 0.0 collective-permute-start.15
  19.6 1.8 %collective-permute-start = (bf16[8,1920]{1,0:T(8,128)(2,1)}, bf16[8,1920]{1,0:T(8,128)(2,1)S(1)}, u32[]{:S(2)}, u32[]{:S(2)}) collective-permute-start(bf16[8,1920]{1,0:T(8,128)(2,1)} %get-tuple-element.42), channel_id=1, source_target_pairs={{0,8},{2,10},{4,12},{6,14},{8,0},{10,2},{12,4},{14,6},{1,9},{3,11}... | collective-permute-start | bytes 92168 | tf_op jit(solution)/shard_map/ppermute | solution.py:404
  21.3 1.5 %collective-permute-start.5 = (bf16[8,1920]{1,0:T(8,128)(2,1)}, bf16[8,1920]{1,0:T(8,128)(2,1)S(1)}, u32[]{:S(2)}, u32[]{:S(2)}) collective-permute-start(bf16[8,1920]{1,0:T(8,128)(2,1)} %get-tuple-element.41.refs_0_), channel_id=1, source_target_pairs={{0,6},{2,4},{4,2},{6,0},{8,14},{10,12},{12,10},{14,8},{1,7},{3,5},... | collective-permute-start | bytes 92168 | tf_op jit(solution)/shard_map/ppermute | solution.py:407
  22.8 0.6 collective-permute-start.3
  23.4 1.5 %collective-permute-start.1 = (bf16[8,1920]{1,0:T(8,128)(2,1)}, bf16[8,1920]{1,0:T(8,128)(2,1)S(1)}, u32[]{:S(2)}, u32[]{:S(2)}) collective-permute-start(bf16[8,1920]{1,0:T(8,128)(2,1)} %get-tuple-element.41.refs_0_), channel_id=1, source_target_pairs={{0,2},{2,0},{4,6},{6,4},{8,10},{10,8},{12,14},{14,12},{1,3},{3,1},... | collective-permute-start | bytes 92168 | tf_op jit(solution)/shard_map/ppermute | solution.py:407
  24.8 0.0 collective-permute-done.refs_1_
  24.8 1.5 %collective-permute-start.6 = (bf16[8,1920]{1,0:T(8,128)(2,1)S(1)}, bf16[8,1920]{1,0:T(8,128)(2,1)S(1)}, u32[]{:S(2)}, u32[]{:S(2)}) collective-permute-start(bf16[8,1920]{1,0:T(8,128)(2,1)S(1)} %collective-permute-done.refs_1_), channel_id=1, source_target_pairs={{0,6},{2,4},{4,2},{6,0},{8,14},{10,12},{12,10},{14,8},{1,7},{3,5},... | collective-permute-start | bytes 92168 | tf_op jit(solution)/shard_map/ppermute | solution.py:407
  26.3 0.1 collective-permute-done.5.refs_6_
  26.4 1.5 %collective-permute-start.4 = (bf16[8,1920]{1,0:T(8,128)(2,1)S(1)}, bf16[8,1920]{1,0:T(8,128)(2,1)S(1)}, u32[]{:S(2)}, u32[]{:S(2)}) collective-permute-start(bf16[8,1920]{1,0:T(8,128)(2,1)S(1)} %collective-permute-done.refs_1_), channel_id=1, source_target_pairs={{0,4},{2,6},{4,0},{6,2},{8,12},{10,14},{12,8},{14,10},{1,5},{3,7},... | collective-permute-start | bytes 92168 | tf_op jit(solution)/shard_map/ppermute | solution.py:407
  27.9 0.0 collective-permute-done.3.refs_4_
  27.9 0.6 collective-permute-start.2
  28.5 0.0 collective-permute-done.1.refs_2_
  28.5 1.2 %collective-permute-done.6.refs_7_ = bf16[8,1920]{1,0:T(8,128)(2,1)S(1)} collective-permute-done((bf16[8,1920]{1,0:T(8,128)(2,1)S(1)}, bf16[8,1920]{1,0:T(8,128)(2,1)S(1)}, u32[]{:S(2)}, u32[]{:S(2)}) %collective-permute-start.6) | collective-permute-done | bytes 30752 | tf_op jit(solution)/shard_map/ppermute | solution.py:407
  29.7 0.6 collective-permute-done.4.refs_5_
  30.3 1.5 %collective-permute-done.2.refs_3_ = bf16[8,1920]{1,0:T(8,128)(2,1)S(1)} collective-permute-done((bf16[8,1920]{1,0:T(8,128)(2,1)S(1)}, bf16[8,1920]{1,0:T(8,128)(2,1)S(1)}, u32[]{:S(2)}, u32[]{:S(2)}) %collective-permute-start.2) | collective-permute-done | bytes 30752 | tf_op jit(solution)/shard_map/ppermute | solution.py:407
  31.9 0.6 copy-done.23
  32.5 1.8 %assemble_rows.2.ga_ref.own_ref = bf16[64,3072]{1,0:T(8,128)(2,1)} custom-call(bf16[8,1920]{1,0:T(8,128)(2,1)} %get-tuple-element.41.refs_0_, bf16[8,1920]{1,0:T(8,128)(2,1)} %copy-done.17, bf16[8,1920]{1,0:T(8,128)(2,1)} %copy-done.20, bf16[8,1920]{1,0:T(8,128)(2,1)} %copy-done.23, bf16[8,1920]{1,0:T(8,128)(2,1)} %copy-done.19, bf16[8,1920]{1,0:T(8,128)(2,1)} %copy-done.22, ...), custom_call_target="tpu_custom_call" | custom-call | tf_op jit(solution)/shard_map/assemble_rows/pallas_call | solution.py:114
  34.2 0.0 collective-permute-start.7
  34.2 0.0 collective-permute-done.15.xb_ref.oth_ref
  34.2 0.0 copy-start.1
  34.2 1.0 copy-done.1
  35.2 17.9 %hidden_units.1 = (f32[1344,64]{1,0:T(8,128)S(1)}, f32[1344,64]{1,0:T(8,128)S(1)}) custom-call(s32[1]{0:T(128)} %bitcast.2.t_ref, bf16[64,3072]{1,0:T(8,128)(2,1)S(1)} %copy-done.1, bf16[64,3072]{1,0:T(8,128)(2,1)S(1)} %collective-permute-done.15.xb_ref.oth_ref, bf16[1344,6144]{1,0:T(8,128)(2,1)} %wg_ref.5, bf16[1344,6144]{1,0:T(8,128)(2,1)} %wu_ref.5), custom_call_target="tpu_custom_call" | custom-call | flops 2113929216 | bytes 33030144 | tf_op jit(solution)/shard_map/hidden_units/pallas_call | solution.py:164
  53.2 0.0 collective-permute-done.7.gb_ref.oth_ref
  53.2 21.9 %give_half.1 = (bf16[1344,64]{1,0:T(8,128)(2,1)S(1)}, bf16[1344,64]{1,0:T(8,128)(2,1)S(1)}, bf16[1344,64]{1,0:T(8,128)(2,1)S(1)}, bf16[64,1344]{1,0:T(8,128)(2,1...) custom-call(s32[1]{0:T(128)} %bitcast.2.t_ref, bf16[64,3072]{1,0:T(8,128)(2,1)S(1)} %copy-done, ...), custom_call_target="tpu_custom_call" | custom-call | flops 2113929216 | bytes 33030144 | tf_op jit(solution)/shard_map/give_half/pallas_call | solution.py:236
  75.1 0.0 copy-start.5
  75.1 0.6 collective-permute-start.16
  75.7 0.1 collective-permute-start.17
  75.8 8.5 %keep_half.1.keep_ref = f32[64,3072]{1,0:T(8,128)S(1)} custom-call(s32[1]{0:T(128)} %bitcast.2.t_ref, bf16[64,1344]{1,0:T(8,128)(2,1)S(1)} %get-tuple-element.50.dhr_ref, bf16[64,1344]{1,0:T(8,128)(2,1)S(1)} %get-tuple-element.51.dur_ref, bf16[1344,6144]{1,0:T(8,128)(2,1)} %wg_ref.5, bf16[1344,6144]{1,0:T(8,128)(2,1)} %wu_ref.5), custom_call_target="tpu_custom_call" | custom-call | flops 1056964608 | bytes 16515072 | tf_op jit(solution)/shard_map/keep_half/pallas_call | solution.py:279
  84.3 0.0 copy-start.3
  84.3 0.9 copy-done.3
  85.1 0.0 collective-permute-done.17.gate_got
  85.1 0.0 collective-permute-done.16.got_ref
  85.1 0.6 copy-done.9
  85.7 0.9 copy-done.6
  86.6 2.2 %fold_cores.1 = (f32[16,2048]{1,0:T(8,128)}, f32[16,2048]{1,0:T(8,128)}, f32[16,2048]{1,0:T(8,128)}, f32[16,2048]{1,0:T(8,128)}) custom-call(f32[64,3072]{1,0:T(8,128)} %copy-done.3, f32[64,3072]{1,0:T(8,128)} %copy-done.6, f32[64,128]{1,0:T(8,128)} %copy-done.5, f32[64,128]{1,0:T(8,128)} %copy-done.9), custom_call_target="tpu_custom_call" | custom-call | tf_op jit(solution)/shard_map/fold_cores/pallas_call | solution.py:349
  88.8 0.5 collective-permute-start.18
  89.3 1.4 %collective-permute-start.19 = (f32[16,2048]{1,0:T(8,128)}, f32[16,2048]{1,0:T(8,128)S(1)}, u32[]{:S(2)}, u32[]{:S(2)}) collective-permute-start(f32[16,2048]{1,0:T(8,128)} %get-tuple-element.61), channel_id=1, source_target_pairs={{0,4},{2,6},{4,0},{6,2},{8,12},{10,14},{12,8},{14,10},{1,5},{3,7},... | collective-permute-start | bytes 393224 | tf_op jit(solution)/shard_map/ppermute | solution.py:407
  90.7 1.6 %collective-permute-start.20 = (f32[16,2048]{1,0:T(8,128)}, f32[16,2048]{1,0:T(8,128)S(1)}, u32[]{:S(2)}, u32[]{:S(2)}) collective-permute-start(f32[16,2048]{1,0:T(8,128)} %get-tuple-element.62), channel_id=1, source_target_pairs={{0,6},{2,4},{4,2},{6,0},{8,14},{10,12},{12,10},{14,8},{1,7},{3,5},... | collective-permute-start | bytes 393224 | tf_op jit(solution)/shard_map/ppermute | solution.py:407
  92.3 8.6 %grad_w_down.1 = bf16[1344,6144]{1,0:T(8,128)(2,1)} custom-call(s32[1]{0:T(128)} %bitcast.2.t_ref, bf16[1344,64]{1,0:T(8,128)(2,1)S(1)} %get-tuple-element.70.left_ref, bf16[64,3072]{1,0:T(8,128)(2,1)S(1)} %copy-done, bf16[64,3072]{1,0:T(8,128)(2,1)S(1)} %collective-permute-done.7.gb_ref.oth_ref), custom_call_target="tpu_custom_call" | custom-call | flops 1056964608 | bytes 16515072 | tf_op jit(solution)/shard_map/grad_w_down/pallas_call | solution.py:310
  100.9 8.6 %grad_w_gate.1 = bf16[1344,6144]{1,0:T(8,128)(2,1)} custom-call(s32[1]{0:T(128)} %bitcast.2.t_ref, bf16[1344,64]{1,0:T(8,128)(2,1)S(1)} %get-tuple-element.58.left_ref, bf16[64,3072]{1,0:T(8,128)(2,1)S(1)} %copy-done.2, bf16[64,3072]{1,0:T(8,128)(2,1)S(1)} %collective-permute-done.15.xb_ref.oth_ref), custom_call_target="tpu_custom_call" | custom-call | flops 1056964608 | bytes 16515072 | tf_op jit(solution)/shard_map/grad_w_gate/pallas_call | solution.py:310
  109.6 0.6 slice.6.mine_ref
  110.3 1.3 %collective-permute-start.21 = (f32[8,2048]{1,0:T(8,128)S(1)}, f32[8,2048]{1,0:T(8,128)S(1)}, u32[]{:S(2)}, u32[]{:S(2)}) collective-permute-start(f32[8,2048]{1,0:T(8,128)S(1)} %slice.8), channel_id=1, source_target_pairs={{0,8},{2,10},{4,12},{6,14},{8,0},{10,2},{12,4},{14,6},{1,9},{3,11}... | collective-permute-start | bytes 196616 | tf_op jit(solution)/shard_map/ppermute | solution.py:404
  111.6 8.6 %grad_w_up.1 = bf16[1344,6144]{1,0:T(8,128)(2,1)} custom-call(s32[1]{0:T(128)} %bitcast.2.t_ref, bf16[1344,64]{1,0:T(8,128)(2,1)S(1)} %get-tuple-element.69.left_ref, bf16[64,3072]{1,0:T(8,128)(2,1)S(1)} %copy-done.2, bf16[64,3072]{1,0:T(8,128)(2,1)S(1)} %collective-permute-done.15.xb_ref.oth_ref), custom_call_target="tpu_custom_call" | custom-call | flops 1056964608 | bytes 16515072 | tf_op jit(solution)/shard_map/grad_w_up/pallas_call | solution.py:310
  120.2 0.0 collective-permute-done.21.got_ref
  120.2 0.6 copy-done.8
  120.8 2.4 %finish_tokens.1 = (bf16[16,3072]{1,0:T(8,128)(2,1)}, f32[4,16]{1,0:T(4,128)}) custom-call(s32[1]{0:T(128)} %bitcast.e_ref, s32[4,16]{1,0:T(4,128)} %bitcast.6, f32[8,2048]{1,0:T(8,128)} %slice.6.mine_ref, f32[8,2048]{1,0:T(8,128)} %copy-done.8), custom_call_target="tpu_custom_call" | custom-call | tf_op jit(solution)/shard_map/finish_tokens/pallas_call | solution.py:386
  (42 shorter events, 0.1 us)
Async XLA Ops:
  2.6 7.5 %collective-permute-start.8 = (bf16[8,2048]{1,0:T(8,128)(2,1)}, bf16[8,2048]{1,0:T(8,128)(2,1)S(1)}, u32[]{:S(2)}, u32[]{:S(2)}) collective-permute-start(bf16[8,2048]{1,0:T(8,128)(2,1)} %get-tuple-element.44), channel_id=1, source_target_pairs={{0,8},{2,10},{4,12},{6,14},{8,0},{10,2},{12,4},{14,6},{1,9},{3,11}... | collective-permute-start | bytes 98312 | tf_op jit(solution)/shard_map/ppermute | solution.py:404
  6.7 6.5 %collective-permute-start.13 = (bf16[8,2048]{1,0:T(8,128)(2,1)}, bf16[8,2048]{1,0:T(8,128)(2,1)S(1)}, u32[]{:S(2)}, u32[]{:S(2)}) collective-permute-start(bf16[8,2048]{1,0:T(8,128)(2,1)} %get-tuple-element.43.refs_0_), channel_id=1, source_target_pairs={{0,6},{2,4},{4,2},{6,0},{8,14},{10,12},{12,10},{14,8},{1,7},{3,5},... | collective-permute-start | bytes 98312 | tf_op jit(solution)/shard_map/ppermute | solution.py:407
  9.2 4.5 %collective-permute-start.11 = (bf16[8,2048]{1,0:T(8,128)(2,1)}, bf16[8,2048]{1,0:T(8,128)(2,1)S(1)}, u32[]{:S(2)}, u32[]{:S(2)}) collective-permute-start(bf16[8,2048]{1,0:T(8,128)(2,1)} %get-tuple-element.43.refs_0_), channel_id=1, source_target_pairs={{0,4},{2,6},{4,0},{6,2},{8,12},{10,14},{12,8},{14,10},{1,5},{3,7},... | collective-permute-start | bytes 98312 | tf_op jit(solution)/shard_map/ppermute | solution.py:407
  9.6 4.1 %collective-permute-start.9 = (bf16[8,2048]{1,0:T(8,128)(2,1)}, bf16[8,2048]{1,0:T(8,128)(2,1)S(1)}, u32[]{:S(2)}, u32[]{:S(2)}) collective-permute-start(bf16[8,2048]{1,0:T(8,128)(2,1)} %get-tuple-element.43.refs_0_), channel_id=1, source_target_pairs={{0,2},{2,0},{4,6},{6,4},{8,10},{10,8},{12,14},{14,12},{1,3},{3,1},... | collective-permute-start | bytes 98312 | tf_op jit(solution)/shard_map/ppermute | solution.py:407
  10.2 6.9 %copy-start.10 = (bf16[8,2048]{1,0:T(8,128)(2,1)}, bf16[8,2048]{1,0:T(8,128)(2,1)S(1)}, u32[]{:S(2)}) copy-start(bf16[8,2048]{1,0:T(8,128)(2,1)S(1)} %collective-permute-done.8.refs_1_) | copy-start | bytes 98308
  10.2 4.8 %collective-permute-start.14 = (bf16[8,2048]{1,0:T(8,128)(2,1)S(1)}, bf16[8,2048]{1,0:T(8,128)(2,1)S(1)}, u32[]{:S(2)}, u32[]{:S(2)}) collective-permute-start(bf16[8,2048]{1,0:T(8,128)(2,1)S(1)} %collective-permute-done.8.refs_1_), channel_id=1, source_target_pairs={{0,6},{2,4},{4,2},{6,0},{8,14},{10,12},{12,10},{14,8},{1,7},{3,5},... | collective-permute-start | bytes 98312 | tf_op jit(solution)/shard_map/ppermute | solution.py:407
  12.7 3.9 %collective-permute-start.12 = (bf16[8,2048]{1,0:T(8,128)(2,1)S(1)}, bf16[8,2048]{1,0:T(8,128)(2,1)S(1)}, u32[]{:S(2)}, u32[]{:S(2)}) collective-permute-start(bf16[8,2048]{1,0:T(8,128)(2,1)S(1)} %collective-permute-done.8.refs_1_), channel_id=1, source_target_pairs={{0,4},{2,6},{4,0},{6,2},{8,12},{10,14},{12,8},{14,10},{1,5},{3,7},... | collective-permute-start | bytes 98312 | tf_op jit(solution)/shard_map/ppermute | solution.py:407
  13.1 3.9 %copy-start.11 = (bf16[8,2048]{1,0:T(8,128)(2,1)}, bf16[8,2048]{1,0:T(8,128)(2,1)S(1)}, u32[]{:S(2)}) copy-start(bf16[8,2048]{1,0:T(8,128)(2,1)S(1)} %collective-permute-done.13.refs_6_) | copy-start | bytes 98308
  13.1 3.9 %collective-permute-start.10 = (bf16[8,2048]{1,0:T(8,128)(2,1)S(1)}, bf16[8,2048]{1,0:T(8,128)(2,1)S(1)}, u32[]{:S(2)}, u32[]{:S(2)}) collective-permute-start(bf16[8,2048]{1,0:T(8,128)(2,1)S(1)} %collective-permute-done.8.refs_1_), channel_id=1, source_target_pairs={{0,2},{2,0},{4,6},{6,4},{8,10},{10,8},{12,14},{14,12},{1,3},{3,1},... | collective-permute-start | bytes 98312 | tf_op jit(solution)/shard_map/ppermute | solution.py:407
  13.7 3.4 %copy-start.12 = (bf16[8,2048]{1,0:T(8,128)(2,1)}, bf16[8,2048]{1,0:T(8,128)(2,1)S(1)}, u32[]{:S(2)}) copy-start(bf16[8,2048]{1,0:T(8,128)(2,1)S(1)} %collective-permute-done.11.refs_4_) | copy-start | bytes 98308
  13.8 3.3 %copy-start.13 = (bf16[8,2048]{1,0:T(8,128)(2,1)}, bf16[8,2048]{1,0:T(8,128)(2,1)S(1)}, u32[]{:S(2)}) copy-start(bf16[8,2048]{1,0:T(8,128)(2,1)S(1)} %collective-permute-done.9.refs_2_) | copy-start | bytes 98308
  15.0 2.1 %copy-start.14 = (bf16[8,2048]{1,0:T(8,128)(2,1)}, bf16[8,2048]{1,0:T(8,128)(2,1)S(1)}, u32[]{:S(2)}) copy-start(bf16[8,2048]{1,0:T(8,128)(2,1)S(1)} %collective-permute-done.14.refs_7_) | copy-start | bytes 98308
  16.6 0.6 copy-start.15
  17.2 0.6 copy-start.16
  19.6 14.7 %collective-permute-start.15 = (bf16[64,3072]{1,0:T(8,128)(2,1)}, bf16[64,3072]{1,0:T(8,128)(2,1)S(1)}, u32[]{:S(2)}, u32[]{:S(2)}) collective-permute-start(bf16[64,3072]{1,0:T(8,128)(2,1)} %get-tuple-element.46.xa_ref.own_ref), channel_id=1, source_target_pairs={{0,1},{1,0},{2,3},{3,2},{4,5},{5,4},{6,7},{7,6},{8,9},{9,8},{10,11... | collective-permute-start | bytes 1179656 | tf_op jit(solution)/shard_map/ppermute | solution.py:410
  19.6 5.3 %collective-permute-start = (bf16[8,1920]{1,0:T(8,128)(2,1)}, bf16[8,1920]{1,0:T(8,128)(2,1)S(1)}, u32[]{:S(2)}, u32[]{:S(2)}) collective-permute-start(bf16[8,1920]{1,0:T(8,128)(2,1)} %get-tuple-element.42), channel_id=1, source_target_pairs={{0,8},{2,10},{4,12},{6,14},{8,0},{10,2},{12,4},{14,6},{1,9},{3,11}... | collective-permute-start | bytes 92168 | tf_op jit(solution)/shard_map/ppermute | solution.py:404
  21.3 5.1 %collective-permute-start.5 = (bf16[8,1920]{1,0:T(8,128)(2,1)}, bf16[8,1920]{1,0:T(8,128)(2,1)S(1)}, u32[]{:S(2)}, u32[]{:S(2)}) collective-permute-start(bf16[8,1920]{1,0:T(8,128)(2,1)} %get-tuple-element.41.refs_0_), channel_id=1, source_target_pairs={{0,6},{2,4},{4,2},{6,0},{8,14},{10,12},{12,10},{14,8},{1,7},{3,5},... | collective-permute-start | bytes 92168 | tf_op jit(solution)/shard_map/ppermute | solution.py:407
  22.8 5.1 %collective-permute-start.3 = (bf16[8,1920]{1,0:T(8,128)(2,1)}, bf16[8,1920]{1,0:T(8,128)(2,1)S(1)}, u32[]{:S(2)}, u32[]{:S(2)}) collective-permute-start(bf16[8,1920]{1,0:T(8,128)(2,1)} %get-tuple-element.41.refs_0_), channel_id=1, source_target_pairs={{0,4},{2,6},{4,0},{6,2},{8,12},{10,14},{12,8},{14,10},{1,5},{3,7},... | collective-permute-start | bytes 92168 | tf_op jit(solution)/shard_map/ppermute | solution.py:407
  23.4 5.1 %collective-permute-start.1 = (bf16[8,1920]{1,0:T(8,128)(2,1)}, bf16[8,1920]{1,0:T(8,128)(2,1)S(1)}, u32[]{:S(2)}, u32[]{:S(2)}) collective-permute-start(bf16[8,1920]{1,0:T(8,128)(2,1)} %get-tuple-element.41.refs_0_), channel_id=1, source_target_pairs={{0,2},{2,0},{4,6},{6,4},{8,10},{10,8},{12,14},{14,12},{1,3},{3,1},... | collective-permute-start | bytes 92168 | tf_op jit(solution)/shard_map/ppermute | solution.py:407
  24.8 7.0 %copy-start.17 = (bf16[8,1920]{1,0:T(8,128)(2,1)}, bf16[8,1920]{1,0:T(8,128)(2,1)S(1)}, u32[]{:S(2)}) copy-start(bf16[8,1920]{1,0:T(8,128)(2,1)S(1)} %collective-permute-done.refs_1_) | copy-start | bytes 92164
  24.8 4.9 %collective-permute-start.6 = (bf16[8,1920]{1,0:T(8,128)(2,1)S(1)}, bf16[8,1920]{1,0:T(8,128)(2,1)S(1)}, u32[]{:S(2)}, u32[]{:S(2)}) collective-permute-start(bf16[8,1920]{1,0:T(8,128)(2,1)S(1)} %collective-permute-done.refs_1_), channel_id=1, source_target_pairs={{0,6},{2,4},{4,2},{6,0},{8,14},{10,12},{12,10},{14,8},{1,7},{3,5},... | collective-permute-start | bytes 92168 | tf_op jit(solution)/shard_map/ppermute | solution.py:407
  26.4 5.4 %copy-start.18 = (bf16[8,1920]{1,0:T(8,128)(2,1)}, bf16[8,1920]{1,0:T(8,128)(2,1)S(1)}, u32[]{:S(2)}) copy-start(bf16[8,1920]{1,0:T(8,128)(2,1)S(1)} %collective-permute-done.5.refs_6_) | copy-start | bytes 92164
  26.4 3.9 %collective-permute-start.4 = (bf16[8,1920]{1,0:T(8,128)(2,1)S(1)}, bf16[8,1920]{1,0:T(8,128)(2,1)S(1)}, u32[]{:S(2)}, u32[]{:S(2)}) collective-permute-start(bf16[8,1920]{1,0:T(8,128)(2,1)S(1)} %collective-permute-done.refs_1_), channel_id=1, source_target_pairs={{0,4},{2,6},{4,0},{6,2},{8,12},{10,14},{12,8},{14,10},{1,5},{3,7},... | collective-permute-start | bytes 92168 | tf_op jit(solution)/shard_map/ppermute | solution.py:407
  27.9 3.9 %copy-start.19 = (bf16[8,1920]{1,0:T(8,128)(2,1)}, bf16[8,1920]{1,0:T(8,128)(2,1)S(1)}, u32[]{:S(2)}) copy-start(bf16[8,1920]{1,0:T(8,128)(2,1)S(1)} %collective-permute-done.3.refs_4_) | copy-start | bytes 92164
  27.9 3.9 %collective-permute-start.2 = (bf16[8,1920]{1,0:T(8,128)(2,1)S(1)}, bf16[8,1920]{1,0:T(8,128)(2,1)S(1)}, u32[]{:S(2)}, u32[]{:S(2)}) collective-permute-start(bf16[8,1920]{1,0:T(8,128)(2,1)S(1)} %collective-permute-done.refs_1_), channel_id=1, source_target_pairs={{0,2},{2,0},{4,6},{6,4},{8,10},{10,8},{12,14},{14,12},{1,3},{3,1},... | collective-permute-start | bytes 92168 | tf_op jit(solution)/shard_map/ppermute | solution.py:407
  28.5 3.4 %copy-start.20 = (bf16[8,1920]{1,0:T(8,128)(2,1)}, bf16[8,1920]{1,0:T(8,128)(2,1)S(1)}, u32[]{:S(2)}) copy-start(bf16[8,1920]{1,0:T(8,128)(2,1)S(1)} %collective-permute-done.1.refs_2_) | copy-start | bytes 92164
  29.7 2.1 %copy-start.21 = (bf16[8,1920]{1,0:T(8,128)(2,1)}, bf16[8,1920]{1,0:T(8,128)(2,1)S(1)}, u32[]{:S(2)}) copy-start(bf16[8,1920]{1,0:T(8,128)(2,1)S(1)} %collective-permute-done.6.refs_7_) | copy-start | bytes 92164
  30.3 1.5 %copy-start.22 = (bf16[8,1920]{1,0:T(8,128)(2,1)}, bf16[8,1920]{1,0:T(8,128)(2,1)S(1)}, u32[]{:S(2)}) copy-start(bf16[8,1920]{1,0:T(8,128)(2,1)S(1)} %collective-permute-done.4.refs_5_) | copy-start | bytes 92164
  31.9 0.6 copy-start.23
  34.2 18.9 %collective-permute-start.7 = (bf16[64,3072]{1,0:T(8,128)(2,1)}, bf16[64,3072]{1,0:T(8,128)(2,1)S(1)}, u32[]{:S(2)}, u32[]{:S(2)}) collective-permute-start(bf16[64,3072]{1,0:T(8,128)(2,1)} %assemble_rows.2.ga_ref.own_ref), channel_id=1, source_target_pairs={{0,1},{1,0},{2,3},{3,2},{4,5},{5,4},{6,7},{7,6},{8,9},{9,8},{10,11... | collective-permute-start | bytes 1179656 | tf_op jit(solution)/shard_map/ppermute | solution.py:410
  34.2 1.0 copy-start.1
  35.2 17.9 %copy-start = (bf16[64,3072]{1,0:T(8,128)(2,1)S(1)}, bf16[64,3072]{1,0:T(8,128)(2,1)}, u32[]{:S(2)}) copy-start(bf16[64,3072]{1,0:T(8,128)(2,1)} %assemble_rows.2.ga_ref.own_ref) | copy-start | bytes 1179652
  35.2 17.9 %copy-start.4 = (f32[64,128]{1,0:T(8,128)S(1)}, f32[64,128]{1,0:T(8,128)}, u32[]{:S(2)}) copy-start(f32[64,128]{1,0:T(8,128)} %get-tuple-element.45.factor_ref) | copy-start | bytes 98308
  75.1 9.2 %copy-start.5 = (f32[64,128]{1,0:T(8,128)}, f32[64,128]{1,0:T(8,128)S(1)}, u32[]{:S(2)}) copy-start(f32[64,128]{1,0:T(8,128)S(1)} %get-tuple-element.53.gate_mine) | copy-start | bytes 98308
  75.1 10.1 %collective-permute-start.16 = (f32[64,3072]{1,0:T(8,128)S(1)}, f32[64,3072]{1,0:T(8,128)S(1)}, u32[]{:S(2)}, u32[]{:S(2)}) collective-permute-start(f32[64,3072]{1,0:T(8,128)S(1)} %get-tuple-element.52), channel_id=1, source_target_pairs={{0,1},{1,0},{2,3},{3,2},{4,5},{5,4},{6,7},{7,6},{8,9},{9,8},{10,11... | collective-permute-start | bytes 2359304 | tf_op jit(solution)/shard_map/ppermute | solution.py:410
  75.7 9.4 %collective-permute-start.17 = (f32[64,128]{1,0:T(8,128)S(1)}, f32[64,128]{1,0:T(8,128)S(1)}, u32[]{:S(2)}, u32[]{:S(2)}) collective-permute-start(f32[64,128]{1,0:T(8,128)S(1)} %get-tuple-element.53.gate_mine), channel_id=1, source_target_pairs={{0,1},{1,0},{2,3},{3,2},{4,5},{5,4},{6,7},{7,6},{8,9},{9,8},{10,11... | collective-permute-start | bytes 98312 | tf_op jit(solution)/shard_map/ppermute | solution.py:410
  84.3 0.9 copy-start.3
  85.1 15.8 %copy-start.2 = (bf16[64,3072]{1,0:T(8,128)(2,1)S(1)}, bf16[64,3072]{1,0:T(8,128)(2,1)}, u32[]{:S(2)}) copy-start(bf16[64,3072]{1,0:T(8,128)(2,1)} %get-tuple-element.46.xa_ref.own_ref) | copy-start | bytes 1179652
  85.1 0.6 copy-start.9
  85.7 0.9 copy-start.6
  88.8 20.7 %collective-permute-start.18 = (f32[16,2048]{1,0:T(8,128)}, f32[16,2048]{1,0:T(8,128)S(1)}, u32[]{:S(2)}, u32[]{:S(2)}) collective-permute-start(f32[16,2048]{1,0:T(8,128)} %get-tuple-element.60), channel_id=1, source_target_pairs={{0,2},{2,0},{4,6},{6,4},{8,10},{10,8},{12,14},{14,12},{1,3},{3,1},... | collective-permute-start | bytes 393224 | tf_op jit(solution)/shard_map/ppermute | solution.py:407
  89.3 20.2 %collective-permute-start.19 = (f32[16,2048]{1,0:T(8,128)}, f32[16,2048]{1,0:T(8,128)S(1)}, u32[]{:S(2)}, u32[]{:S(2)}) collective-permute-start(f32[16,2048]{1,0:T(8,128)} %get-tuple-element.61), channel_id=1, source_target_pairs={{0,4},{2,6},{4,0},{6,2},{8,12},{10,14},{12,8},{14,10},{1,5},{3,7},... | collective-permute-start | bytes 393224 | tf_op jit(solution)/shard_map/ppermute | solution.py:407
  90.7 18.9 %collective-permute-start.20 = (f32[16,2048]{1,0:T(8,128)}, f32[16,2048]{1,0:T(8,128)S(1)}, u32[]{:S(2)}, u32[]{:S(2)}) collective-permute-start(f32[16,2048]{1,0:T(8,128)} %get-tuple-element.62), channel_id=1, source_target_pairs={{0,6},{2,4},{4,2},{6,0},{8,14},{10,12},{12,10},{14,8},{1,7},{3,5},... | collective-permute-start | bytes 393224 | tf_op jit(solution)/shard_map/ppermute | solution.py:407
  92.3 17.3 %copy-start.7 = (f32[16,2048]{1,0:T(8,128)S(1)}, f32[16,2048]{1,0:T(8,128)}, u32[]{:S(2)}) copy-start(f32[16,2048]{1,0:T(8,128)} %get-tuple-element.64) | copy-start | bytes 393220
  110.3 9.9 %collective-permute-start.21 = (f32[8,2048]{1,0:T(8,128)S(1)}, f32[8,2048]{1,0:T(8,128)S(1)}, u32[]{:S(2)}, u32[]{:S(2)}) collective-permute-start(f32[8,2048]{1,0:T(8,128)S(1)} %slice.8), channel_id=1, source_target_pairs={{0,8},{2,10},{4,12},{6,14},{8,0},{10,2},{12,4},{14,6},{1,9},{3,11}... | collective-permute-start | bytes 196616 | tf_op jit(solution)/shard_map/ppermute | solution.py:404
  120.2 0.6 copy-start.8

commit v3 on v0

v3 whole, which is shorter than its diff:
```python
import functools

import jax
import jax.numpy as jnp
from jax import lax
from jax.experimental import pallas as pl
from jax.experimental.pallas import tpu as pltpu
from jax.sharding import PartitionSpec as P

EXPERTS_ON = 2
CAP = 5
LANES = 128
SUBS = 8
WHOLE = 4
F32 = jnp.float32
BF16 = jnp.bfloat16
MIB = 1 << 20
VMEM = pl.BlockSpec(memory_space=pltpu.VMEM)
SMEM = pl.BlockSpec(memory_space=pltpu.SMEM)
HBM = pl.BlockSpec(memory_space=pltpu.HBM)


def iota(shape, dim):
    return lax.broadcasted_iota(jnp.int32, shape, dim)


def chosen_rows(ids, expert, position):
    rows, toks = position.shape
    hits = [ids[k : k + 1, :] == expert for k in range(ids.shape[0])]
    member = functools.reduce(jnp.logical_or, hits).astype(F32)
    before = (iota((toks, toks), 0) < iota((toks, toks), 1)).astype(F32)
    earlier = jnp.dot(member, before, preferred_element_type=F32)
    return jnp.where(earlier == position.astype(F32), member, 0.0), hits


def sub_row(rows, toks):
    return iota((rows, toks), 0) % SUBS


def tile_of(hidden, most):
    sizes = [n for n in range(16, most + 1, 16) if hidden % n == 0]
    return max(sizes) if sizes else hidden


def pick_body(e_ref, ids_ref, probs_ref, tok_ref, grad_ref, own_ref, oth_ref):
    ids = ids_ref[...]
    probs = probs_ref[...].astype(F32)
    toks, width = tok_ref.shape
    half, eighth = width // 2, width // SUBS
    size = half + eighth
    both = 2 * SUBS
    row = iota((both, toks), 0)
    sub = sub_row(both, toks)
    expert = jnp.where(row < SUBS, e_ref[0], 1 - e_ref[0])
    main, hits = chosen_rows(ids, expert, sub % WHOLE)
    tail, _ = chosen_rows(ids, expert, jnp.full((both, toks), WHOLE, jnp.int32))
    plain = jnp.where(sub < WHOLE, main, jnp.where(sub == WHOLE, tail, 0.0))
    halves = [jnp.where(sub // WHOLE == h, main, 0.0).astype(BF16) for h in range(2)]
    eighths = [jnp.where(sub == s, tail, 0.0).astype(BF16) for s in range(SUBS)]
    for at, src in enumerate((tok_ref, grad_ref)):
        packed = sum(
            jnp.dot(one, src[:, h * half : (h + 1) * half], preferred_element_type=F32)
            for h, one in enumerate(halves)
        ).astype(BF16)
        last = sum(
            jnp.dot(one, src[:, s * eighth : (s + 1) * eighth], preferred_element_type=F32)
            for s, one in enumerate(eighths)
        ).astype(BF16)
        for n, dst in enumerate((own_ref, oth_ref)):
            dst[:, at * size : at * size + half] = packed[n * SUBS : (n + 1) * SUBS]
            dst[:, at * size + half : (at + 1) * size] = last[n * SUBS : (n + 1) * SUBS]
    weight = sum(jnp.where(hit, probs[k : k + 1, :], 0.0) for k, hit in enumerate(hits))
    gate = jnp.broadcast_to(jnp.sum(plain * weight, axis=1, keepdims=True), (both, LANES)).astype(BF16)
    for n, dst in enumerate((own_ref, oth_ref)):
        dst[:, 2 * size :] = gate[n * SUBS : (n + 1) * SUBS]


def pick(e, ids_t, probs_t, tokens, grad_out):
    width = tokens.shape[1]
    size = width // 2 + width // SUBS
    piece = jax.ShapeDtypeStruct((SUBS, 2 * size + LANES), BF16)
    return pl.pallas_call(
        pick_body,
        out_shape=(piece, piece),
        in_specs=[SMEM] + [VMEM] * 4,
        out_specs=[VMEM] * 2,
        name="pick_rows",
    )(e, ids_t, probs_t, tokens, grad_out)


def assemble_body(count, *refs):
    pieces, (x_ref, g_ref, factor_ref, held) = refs[:count], refs[count:]
    width = x_ref.shape[1]
    half, eighth = width // 2, width // SUBS
    size = half + eighth
    held[...] = jnp.zeros_like(held)
    for side, out in enumerate((x_ref, g_ref)):
        base = side * size
        for n, ref in enumerate(pieces):
            at = n * SUBS
            piece = ref[:, base : base + size].astype(F32)
            for h in range(2):
                held[at : at + WHOLE, h * half : (h + 1) * half] = piece[h * WHOLE : (h + 1) * WHOLE, :half]
            for s in range(SUBS):
                held[at + WHOLE : at + WHOLE + 1, s * eighth : (s + 1) * eighth] = piece[s : s + 1, half:]
        out[...] = held[...].astype(BF16)
    for n, ref in enumerate(pieces):
        factor_ref[n * SUBS : (n + 1) * SUBS, :] = ref[:, 2 * size :].astype(F32)


def assemble(pieces, width):
    count = len(pieces)
    rows = count * SUBS
    held = jax.ShapeDtypeStruct((rows, width), BF16)
    return pl.pallas_call(
        functools.partial(assemble_body, count),
        out_shape=(held, held, jax.ShapeDtypeStruct((rows, LANES), F32)),
        in_specs=[VMEM] * count,
        out_specs=[VMEM] * 3,
        scratch_shapes=[pltpu.VMEM((rows, width), F32)],
        name="assemble_rows",
    )(*pieces)


NT = (((1,), (1,)), ((), ()))


def chunk_of(width, most):
    return max(n for n in range(LANES, most + 1, LANES) if width % n == 0)


def place_of(step, chunks, chunk, t):
    side = jnp.where(step < chunks, t, 1 - t)
    return pl.multiple_of((side * chunks + lax.rem(step, chunks)) * chunk, chunk)


def half_grad(part, wg_ref, wu_ref, dhr_ref, dur_ref, base, chunk):
    def step(c, carry):
        at = pl.multiple_of(c * chunk, chunk)
        cols = pl.ds(base + at, chunk)
        part[:, pl.ds(at, chunk)] = jnp.dot(dhr_ref[...], wg_ref[:, cols], preferred_element_type=F32) + jnp.dot(
            dur_ref[...], wu_ref[:, cols], preferred_element_type=F32
        )
        return carry

    lax.fori_loop(0, part.shape[1] // chunk, step, 0)


def pack_rows(part, gates, out):
    rows, width = part.shape
    half, eighth = width // 2, width // SUBS
    for at in range(0, rows, SUBS):
        for h in range(2):
            out[at + h * WHOLE : at + (h + 1) * WHOLE, :half] = part[at : at + WHOLE, h * half : (h + 1) * half]
        for s in range(SUBS):
            out[at + s : at + s + 1, half : half + eighth] = part[
                at + WHOLE : at + WHOLE + 1, s * eighth : (s + 1) * eighth
            ]
    out[:, half + eighth :] = gates


def experts_body(chunk, t_ref, xa_ref, xb_ref, ga_ref, gb_ref, factor_ref, wg_hbm, wu_hbm, wd_hbm,
                 wt_ref, dh_ref, du_ref, give_ref, keep_ref,
                 wg_ref, wu_ref, ring, h_ref, u_ref, da_ref, dhr_ref, dur_ref, part, landed, ring_landed):
    rows, width = xa_ref.shape
    chunks = width // chunk
    depth = ring.shape[0]
    steps = 2 * chunks
    t = t_ref[0]

    def load(i, n):
        cols = pl.ds(place_of(i, chunks, chunk, t), chunk)
        src, dst = ((wg_hbm, wg_ref), (wu_hbm, wu_ref))[n]
        return pltpu.make_async_copy(src.at[:, cols], dst.at[:, cols], landed.at[i, n])

    def load_down(i):
        cols = pl.ds(place_of(i, chunks, chunk, t), chunk)
        slot = lax.rem(i, depth)
        return pltpu.make_async_copy(wd_hbm.at[:, cols], ring.at[slot], ring_landed.at[slot])

    for i in range(steps):
        for n in range(2):
            load(i, n).start()
    for i in range(min(steps, depth)):
        load_down(i).start()

    def add_to(out, i, w, x):
        more = lax.dot_general(w, x, NT, preferred_element_type=F32)
        out[...] = jnp.where(i == 0, more, out[...] + more)

    for side, x_ref in enumerate((xa_ref, xb_ref)):

        def up_step(c, carry):
            i = side * chunks + c
            x = x_ref[:, pl.ds(pl.multiple_of(c * chunk, chunk), chunk)]
            cols = pl.ds(place_of(i, chunks, chunk, t), chunk)
            for n, (w, out) in enumerate(((wg_ref, h_ref), (wu_ref, u_ref))):
                load(i, n).wait()
                add_to(out, i, w[:, cols], x)
            return carry

        lax.fori_loop(0, chunks, up_step, 0)

    for side, g_ref in enumerate((ga_ref, gb_ref)):

        def down_step(c, carry):
            i = side * chunks + c
            g = g_ref[:, pl.ds(pl.multiple_of(c * chunk, chunk), chunk)]
            load_down(i).wait()
            add_to(da_ref, i, ring[lax.rem(i, depth)], g)

            @pl.when(i + depth < steps)
            def _():
                load_down(i + depth).start()

            return carry

        lax.fori_loop(0, chunks, down_step, 0)

    weight = factor_ref[...].T[:1, :]
    h = h_ref[...]
    u = u_ref[...]
    da = da_ref[...]
    sigma = 1.0 / (1.0 + jnp.exp(-h))
    silu = h * sigma
    act = silu * u
    scaled = weight * da
    wt_ref[...] = (weight * act).astype(BF16)
    dh = scaled * u * sigma * (1.0 + h * (1.0 - sigma))
    du = scaled * silu
    dh_ref[...] = dh.astype(BF16)
    du_ref[...] = du.astype(BF16)
    dhr_ref[...] = dh.T.astype(BF16)
    dur_ref[...] = du.T.astype(BF16)
    total = jnp.sum(act * da, axis=0, keepdims=True)
    gates = jnp.broadcast_to(total, (LANES, rows)).T
    for at, out in ((1 - t, give_ref), (t, keep_ref)):
        base = pl.multiple_of(at * width, width)
        half_grad(part, wg_ref, wu_ref, dhr_ref, dur_ref, base, chunk_of(width, 512))
        pack_rows(part, gates, out)


def expert_units(t, xa, xb, ga, gb, factor, w_gate, w_up, w_down):
    hidden, depth = w_gate.shape
    rows, width = xa.shape
    chunk = chunk_of(width, 1024)
    steps = depth // chunk
    ring = min(3, steps)
    unit = jax.ShapeDtypeStruct((hidden, rows), BF16)
    packed = jax.ShapeDtypeStruct((rows, width // 2 + width // SUBS + LANES), F32)
    return pl.pallas_call(
        functools.partial(experts_body, chunk),
        out_shape=(unit, unit, unit, packed, packed),
        in_specs=[SMEM] + [VMEM] * 5 + [HBM] * 3,
        out_specs=[VMEM] * 5,
        scratch_shapes=[
            pltpu.VMEM((hidden, depth), BF16),
            pltpu.VMEM((hidden, depth), BF16),
            pltpu.VMEM((ring, hidden, chunk), BF16),
            pltpu.VMEM((hidden, rows), F32),
            pltpu.VMEM((hidden, rows), F32),
            pltpu.VMEM((hidden, rows), F32),
            pltpu.VMEM((rows, hidden), BF16),
            pltpu.VMEM((rows, hidden), BF16),
            pltpu.VMEM((rows, width), F32),
            pltpu.SemaphoreType.DMA((steps, 2)),
            pltpu.SemaphoreType.DMA((ring,)),
        ],
        compiler_params=pltpu.CompilerParams(vmem_limit_bytes=48 * MIB),
        cost_estimate=pl.CostEstimate(
            flops=10 * rows * hidden * depth, bytes_accessed=6 * hidden * depth, transcendentals=rows * hidden
        ),
        name="expert_units",
    )(t, xa, xb, ga, gb, factor, w_gate, w_up, w_down)


def weights_body(chunk, t_ref, left_ref, own_ref, oth_ref, out_ref, ring, sent):
    width = own_ref.shape[1]
    chunks = width // chunk
    depth = ring.shape[0]
    hidden = left_ref.shape[0]
    tile = tile_of(hidden, 448)
    t = t_ref[0]

    def store(i):
        cols = pl.ds(place_of(i, chunks, chunk, t), chunk)
        slot = lax.rem(i, depth)
        return pltpu.make_async_copy(ring.at[slot], out_ref.at[:, cols], sent.at[slot])

    for side, x_ref in enumerate((own_ref, oth_ref)):

        def step(c, carry):
            i = side * chunks + c
            slot = lax.rem(i, depth)

            @pl.when(i >= depth)
            def _():
                store(i - depth).wait()

            x = x_ref[:, pl.ds(pl.multiple_of(c * chunk, chunk), chunk)]
            for at in range(0, hidden, tile):
                ring[slot, at : at + tile, :] = jnp.dot(
                    left_ref[at : at + tile, :], x, preferred_element_type=F32
                ).astype(BF16)
            store(i).start()
            return carry

        lax.fori_loop(0, chunks, step, 0)
    for i in range(max(0, 2 * chunks - depth), 2 * chunks):
        store(i).wait()


def weight_grad(t, left, own, oth, name):
    hidden, rows = left.shape
    width = own.shape[1]
    depth = 2 * width
    chunk = chunk_of(width, 512)
    ring = min(4, depth // chunk)
    return pl.pallas_call(
        functools.partial(weights_body, chunk),
        out_shape=jax.ShapeDtypeStruct((hidden, depth), BF16),
        in_specs=[SMEM] + [VMEM] * 3,
        out_specs=HBM,
        scratch_shapes=[pltpu.VMEM((ring, hidden, chunk), BF16), pltpu.SemaphoreType.DMA((ring,))],
        compiler_params=pltpu.CompilerParams(vmem_limit_bytes=24 * MIB),
        cost_estimate=pl.CostEstimate(
            flops=2 * rows * hidden * depth, bytes_accessed=2 * hidden * depth, transcendentals=0
        ),
        name=name,
    )(t, left, own, oth)


def finish_body(e_ref, ids_ref, mine_ref, got_ref, tok_ref, gate_ref):
    ids = ids_ref[...]
    toks, width = tok_ref.shape
    half, eighth = width // 2, width // SUBS
    both = 2 * SUBS
    row = iota((both, toks), 0)
    sub = sub_row(both, toks)
    expert = jnp.where(row < SUBS, e_ref[0], 1 - e_ref[0])
    main, hits = chosen_rows(ids, expert, sub % WHOLE)
    tail, _ = chosen_rows(ids, expert, jnp.full((both, toks), WHOLE, jnp.int32))
    plain = jnp.where(sub < WHOLE, main, jnp.where(sub == WHOLE, tail, 0.0))
    data = jnp.concatenate([mine_ref[...], got_ref[...]], axis=0)
    tn = (((0,), (0,)), ((), ()))
    exact = dict(precision=lax.Precision.HIGHEST, preferred_element_type=F32)
    halves = [
        lax.dot_general(jnp.where(sub // WHOLE == h, main, 0.0), data[:, :half], tn, **exact) for h in range(2)
    ]
    for s in range(SUBS):
        last = lax.dot_general(jnp.where(sub == s, tail, 0.0), data[:, half : half + eighth], tn, **exact)
        h, at = divmod(s * eighth, half)
        tok_ref[:, s * eighth : (s + 1) * eighth] = (halves[h][:, at : at + eighth] + last).astype(BF16)
    term = plain * data[:, half + eighth : half + eighth + 1]
    for k, hit in enumerate(hits):
        gate_ref[k : k + 1, :] = jnp.sum(jnp.where(hit, term, 0.0), axis=0, keepdims=True)


def finish(e, ids_t, mine, got, width):
    top, toks = ids_t.shape
    return pl.pallas_call(
        finish_body,
        out_shape=(jax.ShapeDtypeStruct((toks, width), BF16), jax.ShapeDtypeStruct((top, toks), F32)),
        in_specs=[SMEM] + [VMEM] * 3,
        out_specs=[VMEM] * 2,
        name="finish_tokens",
    )(e, ids_t, mine, got)


def on_device(tokens, grad_out, expert_ids, gate_probs, w_gate, w_up, w_down):
    n_expert = lax.axis_size("expert")
    copies = n_expert // EXPERTS_ON
    place = lax.axis_index("expert")
    e = (place >= copies).astype(jnp.int32).reshape(1)
    t = lax.axis_index("tensor").astype(jnp.int32).reshape(1)
    width = tokens.shape[1]

    def partner(v):
        return lax.ppermute(v, "expert", [(i, (i + copies) % n_expert) for i in range(n_expert)])

    def across(v, d):
        return lax.ppermute(v, "expert", [(i, i ^ d) for i in range(n_expert)])

    def other_core(v):
        return lax.ppermute(v, "tensor", [(0, 1), (1, 0)])

    ids_t = expert_ids.T
    own, oth = pick(e, ids_t, gate_probs.T, tokens, grad_out)
    first, second = [own], [partner(oth)]
    d = 1
    while d < copies:
        first += [across(piece, d) for piece in first]
        second += [across(piece, d) for piece in second]
        d *= 2
    xa, ga, factor = assemble([piece for pair in zip(first, second) for piece in pair], width)
    xb = other_core(xa)
    gb = other_core(ga)
    wt, dh, du, give, keep = expert_units(t, xa, xb, ga, gb, factor, w_gate, w_up, w_down)
    total = keep + other_core(give)
    grads = []
    jobs = [(dh, xa, xb, "grad_w_gate"), (du, xa, xb, "grad_w_up"), (wt, ga, gb, "grad_w_down")]
    d = copies // 2
    while d:
        rows = d * 2 * SUBS
        coming = across(total[rows:], d)
        if len(jobs) > 1:
            left, a, b, name = jobs.pop(0)
            left, total = lax.optimization_barrier((left, total))
            grads.append(weight_grad(t, left, a, b, name))
            grads[-1], coming = lax.optimization_barrier((grads[-1], coming))
        total = total[:rows] + coming
        d //= 2
    theirs = partner(total[SUBS:])
    for left, a, b, name in jobs:
        left, total = lax.optimization_barrier((left, total))
        grads.append(weight_grad(t, left, a, b, name))
    grads, theirs = lax.optimization_barrier((grads, theirs))
    token_grad, gate_t = finish(e, ids_t, total[:SUBS], theirs, width)
    return token_grad, gate_t.T, *grads


def solution(mesh):
    return jax.shard_map(
        on_device,
        mesh=mesh,
        in_specs=(
            P(("groups", "expert"), "tensor"),
            P(("groups", "expert"), "tensor"),
            P(("groups", "expert"), None),
            P(("groups", "expert"), None),
            P(("expert", "tensor"), None),
            P(("expert", "tensor"), None),
            P(("expert", "tensor"), None),
        ),
        out_specs=(
            P(("groups", "expert"), "tensor"),
            P(("groups", "expert"), None),
            P(("expert", "tensor"), "groups"),
            P(("expert", "tensor"), "groups"),
            P(("expert", "tensor"), "groups"),
        ),
        check_vma=False,
    )
```

time: 172 us -> 94.6 us (0.55)
  matrix products: 73.9 us -> 0 us
  Pallas kernels: 0 us -> 62.3 us
  waiting for transfers between devices: 39.7 us -> 9.01 us
  between operations: 14.2 us -> 0.8 us
  starting transfers between devices: 25.2 us -> 17.3 us
  blocking collectives: 7.52 us -> 0 us
  other arithmetic: 3.44 us -> 0.1 us
  local copies, waits for them, and re-layouts: 7.23 us -> 4.65 us
    dot_general x14 -> x0, matrix products: 73.9 us -> none  [the longest x1 10.7 us: on_device(): lax.dot_general(rows_grad, w_down, contract_cols, preferred_element_type=...]
    pallas_call x0 -> x7, Pallas kernels: none -> 62.3 us  [the longest x1 34.3 us: expert_units(): pl.pallas_call(functools.partial(experts_body, chunk), out_shape=(unit, u...]
    all_to_all x5 -> x0, waiting for transfers between devices: 39.7 us -> none  [the longest x1 19.7 us: on_device(): lax.all_to_all(partial_rows, 'expert', split_axis=0, concat_axis=0, tiled...]
    all_to_all x5 -> x0, starting transfers between devices: 25.2 us -> none  [the longest x1 7.25 us: on_device(): lax.all_to_all(spread(gate_slots), 'expert', split_axis=0, concat_axis=0,...]
    ppermute x0 -> x13, starting transfers between devices: none -> 17.3 us  [the longest x8 10 us: across(): return lax.ppermute(v, 'expert', [(i, i ^ d) for i in range(n_expert)])]
    ppermute x0 -> x13, waiting for transfers between devices: none -> 9.01 us  [the longest x3 3.76 us: other_core(): return lax.ppermute(v, 'tensor', [(0, 1), (1, 0)])]
    all_gather x2 -> x0, blocking collectives: 4.5 us -> none  [the longest x1 2.26 us: on_device(): lax.all_gather(grad_out, 'tensor', axis=1, tiled=True)]
    psum x1 -> x0, blocking collectives: 3.02 us -> none  [on_device(): grad_gates = lax.psum(gate_local, 'tensor')]
  transfers between devices with their start and end apart: 6 -> 13, of which waited for: 3 -> 9; matrix products, arithmetic and copies ran while one was open for 30% -> 0% of each run, Pallas kernels for 0% -> 23%
where the time goes in v3:
time: 94.6 us; the launch traced here: 94.2 us
  Pallas kernels  62.3 us (66%)
  starting transfers between devices  17.3 us (18%)
  waiting for transfers between devices  9.01 us (10%)
  local copies, waits for them, and re-layouts  4.65 us (5%)
    pallas_call x1, Pallas kernels, expert_units(): pl.pallas_call(functools.partial(experts_body, chunk), out_shape=(unit, u...  34.3 us
    pallas_call x3, Pallas kernels, weight_grad(): pl.pallas_call(functools.partial(weights_body, chunk), out_shape=jax.Shap...  21.4 us
    ppermute x8, starting transfers between devices, across(): return lax.ppermute(v, 'expert', [(i, i ^ d) for i in range(n_expert)])  10 us
    ppermute x2, starting transfers between devices, partner(): lax.ppermute(v, 'expert', [(i, (i + copies) % n_expert) for i in range(n_...  6.55 us
    unnamed x22, local copies, waits for them, and re-layouts  3.99 us
    ppermute x3, waiting for transfers between devices, other_core(): return lax.ppermute(v, 'tensor', [(0, 1), (1, 0)])  3.76 us
    ppermute x8, waiting for transfers between devices, across(): return lax.ppermute(v, 'expert', [(i, i ^ d) for i in range(n_expert)])  2.95 us
    pallas_call x1, Pallas kernels, finish(): pl.pallas_call(finish_body, out_shape=(jax.ShapeDtypeStruct((toks, width)...  2.43 us
  transfers between devices with their start and end apart: 13, of which 9 were waited for; matrix products, arithmetic and copies ran while one was open for 0% of the time, Pallas kernels for 23%

profile of v3, /device:TPU:0, one launch (start us, length us, event | category | flops | bytes accessed | tf_op | source)
XLA Modules:
  0.0 94.2 jit_solution(3936878059042599705)
XLA Ops:
  0.6 2.0 %pick_rows.1 = (bf16[8,3968]{1,0:T(8,128)(2,1)}, bf16[8,3968]{1,0:T(8,128)(2,1)}) custom-call(s32[1]{0:T(128)} %bitcast.e_ref, s32[4,16]{1,0:T(4,128)} %bitcast.5, bf16[4,16]{1,0:T(4,128)(2,1)} %bitcast.7, bf16[16,3072]{1,0:T(8,128)(2,1)} %tok_ref.1, bf16[16,3072]{1,0:T(8,128)(2,1)} %grad_ref.1), custom_call_target="tpu_custom_call" | custom-call | tf_op jit(solution)/shard_map/pick_rows/pallas_call | solution.py:82
  2.7 4.0 %collective-permute-start = (bf16[8,3968]{1,0:T(8,128)(2,1)}, bf16[8,3968]{1,0:T(8,128)(2,1)S(1)}, u32[]{:S(2)}, u32[]{:S(2)}) collective-permute-start(bf16[8,3968]{1,0:T(8,128)(2,1)} %get-tuple-element.32), channel_id=1, source_target_pairs={{0,8},{2,10},{4,12},{6,14},{8,0},{10,2},{12,4},{14,6},{1,9},{3,11}... | collective-permute-start | bytes 190472 | tf_op jit(solution)/shard_map/ppermute | solution.py:379
  6.7 1.5 %collective-permute-start.1 = (bf16[8,3968]{1,0:T(8,128)(2,1)}, bf16[8,3968]{1,0:T(8,128)(2,1)S(1)}, u32[]{:S(2)}, u32[]{:S(2)}) collective-permute-start(bf16[8,3968]{1,0:T(8,128)(2,1)} %get-tuple-element.31.refs_0_), channel_id=1, source_target_pairs={{0,2},{2,0},{4,6},{6,4},{8,10},{10,8},{12,14},{14,12},{1,3},{3,1},... | collective-permute-start | bytes 190472 | tf_op jit(solution)/shard_map/ppermute | solution.py:382
  8.2 2.3 %collective-permute-done.refs_1_ = bf16[8,3968]{1,0:T(8,128)(2,1)S(1)} collective-permute-done((bf16[8,3968]{1,0:T(8,128)(2,1)}, bf16[8,3968]{1,0:T(8,128)(2,1)S(1)}, u32[]{:S(2)}, u32[]{:S(2)}) %collective-permute-start) | collective-permute-done | bytes 63520 | tf_op jit(solution)/shard_map/ppermute | solution.py:379
  10.5 0.0 copy-start.4
  10.5 1.7 %collective-permute-start.2 = (bf16[8,3968]{1,0:T(8,128)(2,1)S(1)}, bf16[8,3968]{1,0:T(8,128)(2,1)S(1)}, u32[]{:S(2)}, u32[]{:S(2)}) collective-permute-start(bf16[8,3968]{1,0:T(8,128)(2,1)S(1)} %collective-permute-done.refs_1_), channel_id=1, source_target_pairs={{0,2},{2,0},{4,6},{6,4},{8,10},{10,8},{12,14},{14,12},{1,3},{3,1},... | collective-permute-start | bytes 190472 | tf_op jit(solution)/shard_map/ppermute | solution.py:382
  12.2 0.4 collective-permute-start.3
  12.6 1.6 %collective-permute-start.4 = (bf16[8,3968]{1,0:T(8,128)(2,1)S(1)}, bf16[8,3968]{1,0:T(8,128)(2,1)S(1)}, u32[]{:S(2)}, u32[]{:S(2)}) collective-permute-start(bf16[8,3968]{1,0:T(8,128)(2,1)S(1)} %collective-permute-done.refs_1_), channel_id=1, source_target_pairs={{0,4},{2,6},{4,0},{6,2},{8,12},{10,14},{12,8},{14,10},{1,5},{3,7},... | collective-permute-start | bytes 190472 | tf_op jit(solution)/shard_map/ppermute | solution.py:382
  14.2 0.0 collective-permute-done.1.refs_2_
  14.2 0.0 copy-start.5
  14.2 0.4 collective-permute-start.5
  14.7 0.1 collective-permute-done.2.refs_3_
  14.7 0.0 copy-start.6
  14.7 1.5 %collective-permute-start.6 = (bf16[8,3968]{1,0:T(8,128)(2,1)S(1)}, bf16[8,3968]{1,0:T(8,128)(2,1)S(1)}, u32[]{:S(2)}, u32[]{:S(2)}) collective-permute-start(bf16[8,3968]{1,0:T(8,128)(2,1)S(1)} %collective-permute-done.2.refs_3_), channel_id=1, source_target_pairs={{0,4},{2,6},{4,0},{6,2},{8,12},{10,14},{12,8},{14,10},{1,5},{3,7},... | collective-permute-start | bytes 190472 | tf_op jit(solution)/shard_map/ppermute | solution.py:382
  16.3 0.8 collective-permute-done.3.refs_4_
  17.0 0.0 copy-start.7
  17.0 0.7 collective-permute-done.4.refs_5_
  17.7 0.0 copy-start.8
  17.7 0.8 collective-permute-done.5.refs_6_
  18.5 0.0 copy-start.9
  18.5 0.7 collective-permute-done.6.refs_7_
  19.1 0.0 copy-done.4
  19.2 0.0 copy-done.5
  19.2 0.0 copy-done.6
  19.2 0.0 copy-done.7
  19.2 0.0 copy-done.8
  19.2 0.0 copy-done.9
  19.2 0.0 copy-start.10
  19.2 0.6 copy-done.10
  19.8 2.2 %assemble_rows.1 = (bf16[64,3072]{1,0:T(8,128)(2,1)}, bf16[64,3072]{1,0:T(8,128)(2,1)}, f32[64,128]{1,0:T(8,128)}) custom-call(bf16[8,3968]{1,0:T(8,128)(2,1)} %get-tuple-element.31.refs_0_, bf16[8,3968]{1,0:T(8,128)(2,1)} %copy-done.4, bf16[8,3968]{1,0:T(8,128)(2,1)} %copy-done.5, bf16[8,3968]{1,0:T(8,128)(2,1)} %copy-done.6, bf16[8,3968]{1,0:T(8,128)(2,1)} %copy-done.7, ...), custom_call_target="tpu_custom_call" | custom-call | tf_op jit(solution)/shard_map/assemble_rows/pallas_call | solution.py:115
  22.0 0.0 collective-permute-start.8
  22.0 0.5 collective-permute-start.7
  22.5 1.4 %collective-permute-done.8.gb_ref.oth_ref = bf16[64,3072]{1,0:T(8,128)(2,1)S(1)} collective-permute-done((bf16[64,3072]{1,0:T(8,128)(2,1)}, bf16[64,3072]{1,0:T(8,128)(2,1)S(1)}, u32[]{:S(2)}, u32[]{:S(2)}) %collective-permute-start.8) | collective-permute-done | bytes 393248 | tf_op jit(solution)/shard_map/ppermute | solution.py:385
  23.9 0.6 collective-permute-done.7.xb_ref.oth_ref
  24.5 0.0 copy-start
  24.5 1.0 %copy-done = bf16[64,3072]{1,0:T(8,128)(2,1)S(1)} copy-done((bf16[64,3072]{1,0:T(8,128)(2,1)S(1)}, bf16[64,3072]{1,0:T(8,128)(2,1)}, u32[]{:S(2)}) %copy-start) | copy-done | bytes 393240
  25.5 0.0 copy-start.1
  25.5 1.0 %copy-done.1 = bf16[64,3072]{1,0:T(8,128)(2,1)S(1)} copy-done((bf16[64,3072]{1,0:T(8,128)(2,1)S(1)}, bf16[64,3072]{1,0:T(8,128)(2,1)}, u32[]{:S(2)}) %copy-start.1) | copy-done | bytes 393240
  26.5 0.0 copy-start.2
  26.5 0.8 copy-done.2
  27.3 34.3 %expert_units.1 = (bf16[1344,64]{1,0:T(8,128)(2,1)S(1)}, bf16[1344,64]{1,0:T(8,128)(2,1)S(1)}, bf16[1344,64]{1,0:T(8,128)(2,1)S(1)}, f32[64,2048]{1,0:T(8,128)S(1)}, f32[64,2048]{1,0:T(8,128)S(1)}) custom-call(s32[1]{0:T(128)} %bitcast.2.t_ref, bf16[64,3072]{1,0:T(8,128)(2,1)S(1)} %copy-done, bf16[64,3072]{1,0:T(8,128)(2,1)S(1)} %collective-permute-done.7.xb_ref.oth_ref, ...), custom_call_target="tpu_custom_call" | custom-call | flops 5284823040 | bytes 49545216 | tf_op jit(solution)/shard_map/expert_units/pallas_call | solution.py:251
  61.5 0.2 collective-permute-start.9
  61.7 1.8 %collective-permute-done.9 = f32[64,2048]{1,0:T(8,128)S(1)} collective-permute-done((f32[64,2048]{1,0:T(8,128)S(1)}, f32[64,2048]{1,0:T(8,128)S(1)}, u32[]{:S(2)}, u32[]{:S(2)}) %collective-permute-start.9) | collective-permute-done | bytes 524320 | tf_op jit(solution)/shard_map/ppermute | solution.py:385
  63.5 0.1 add.9
  63.6 1.4 %collective-permute-start.10 = (f32[32,2048]{1,0:T(8,128)S(1)}, f32[32,2048]{1,0:T(8,128)S(1)}, u32[]{:S(2)}, u32[]{:S(2)}) collective-permute-start(f32[32,2048]{1,0:T(8,128)S(1)} %slice.24), channel_id=1, source_target_pairs={{0,4},{2,6},{4,0},{6,2},{8,12},{10,14},{12,8},{14,10},{1,5},{3,7},... | collective-permute-start | bytes 786440 | tf_op jit(solution)/shard_map/ppermute | solution.py:382
  65.0 7.1 %grad_w_gate.1 = bf16[1344,6144]{1,0:T(8,128)(2,1)} custom-call(s32[1]{0:T(128)} %bitcast.2.t_ref, bf16[1344,64]{1,0:T(8,128)(2,1)S(1)} %get-tuple-element.42.left_ref, bf16[64,3072]{1,0:T(8,128)(2,1)S(1)} %copy-done, bf16[64,3072]{1,0:T(8,128)(2,1)S(1)} %collective-permute-done.7.xb_ref.oth_ref), custom_call_target="tpu_custom_call" | custom-call | flops 1056964608 | bytes 16515072 | tf_op jit(solution)/shard_map/grad_w_gate/pallas_call | solution.py:319
  72.2 0.0 collective-permute-done.10
  72.2 1.4 %collective-permute-start.11 = (f32[16,2048]{1,0:T(8,128)S(1)}, f32[16,2048]{1,0:T(8,128)S(1)}, u32[]{:S(2)}, u32[]{:S(2)}) collective-permute-start(f32[16,2048]{1,0:T(8,128)S(1)} %slice.25), channel_id=1, source_target_pairs={{0,2},{2,0},{4,6},{6,4},{8,10},{10,8},{12,14},{14,12},{1,3},{3,1},... | collective-permute-start | bytes 393224 | tf_op jit(solution)/shard_map/ppermute | solution.py:382
  73.7 7.1 %grad_w_up.1 = bf16[1344,6144]{1,0:T(8,128)(2,1)} custom-call(s32[1]{0:T(128)} %bitcast.2.t_ref, bf16[1344,64]{1,0:T(8,128)(2,1)S(1)} %get-tuple-element.45.left_ref, bf16[64,3072]{1,0:T(8,128)(2,1)S(1)} %copy-done, bf16[64,3072]{1,0:T(8,128)(2,1)S(1)} %collective-permute-done.7.xb_ref.oth_ref), custom_call_target="tpu_custom_call" | custom-call | flops 1056964608 | bytes 16515072 | tf_op jit(solution)/shard_map/grad_w_up/pallas_call | solution.py:319
  80.8 0.0 collective-permute-done.11
  80.8 0.6 slice.22.mine_ref
  81.5 2.5 %collective-permute-start.12 = (f32[8,2048]{1,0:T(8,128)S(1)}, f32[8,2048]{1,0:T(8,128)S(1)}, u32[]{:S(2)}, u32[]{:S(2)}) collective-permute-start(f32[8,2048]{1,0:T(8,128)S(1)} %slice.26), channel_id=1, source_target_pairs={{0,8},{2,10},{4,12},{6,14},{8,0},{10,2},{12,4},{14,6},{1,9},{3,11}... | collective-permute-start | bytes 196616 | tf_op jit(solution)/shard_map/ppermute | solution.py:379
  84.0 7.1 %grad_w_down.1 = bf16[1344,6144]{1,0:T(8,128)(2,1)} custom-call(s32[1]{0:T(128)} %bitcast.2.t_ref, bf16[1344,64]{1,0:T(8,128)(2,1)S(1)} %get-tuple-element.50.left_ref, bf16[64,3072]{1,0:T(8,128)(2,1)S(1)} %copy-done.1, bf16[64,3072]{1,0:T(8,128)(2,1)S(1)} %collective-permute-done.8.gb_ref.oth_ref), custom_call_target="tpu_custom_call" | custom-call | flops 1056964608 | bytes 16515072 | tf_op jit(solution)/shard_map/grad_w_down/pallas_call | solution.py:319
  91.1 0.0 collective-permute-done.12.got_ref
  91.1 0.0 copy-start.3
  91.2 0.6 copy-done.3
  91.8 2.4 %finish_tokens.1 = (bf16[16,3072]{1,0:T(8,128)(2,1)}, f32[4,16]{1,0:T(4,128)}) custom-call(s32[1]{0:T(128)} %bitcast.e_ref, s32[4,16]{1,0:T(4,128)} %bitcast.6, f32[8,2048]{1,0:T(8,128)} %slice.22.mine_ref, f32[8,2048]{1,0:T(8,128)} %copy-done.3), custom_call_target="tpu_custom_call" | custom-call | tf_op jit(solution)/shard_map/finish_tokens/pallas_call | solution.py:361
  (5 shorter events, 0.1 us)
Async XLA Ops:
  2.7 7.8 %collective-permute-start = (bf16[8,3968]{1,0:T(8,128)(2,1)}, bf16[8,3968]{1,0:T(8,128)(2,1)S(1)}, u32[]{:S(2)}, u32[]{:S(2)}) collective-permute-start(bf16[8,3968]{1,0:T(8,128)(2,1)} %get-tuple-element.32), channel_id=1, source_target_pairs={{0,8},{2,10},{4,12},{6,14},{8,0},{10,2},{12,4},{14,6},{1,9},{3,11}... | collective-permute-start | bytes 190472 | tf_op jit(solution)/shard_map/ppermute | solution.py:379
  6.7 7.5 %collective-permute-start.1 = (bf16[8,3968]{1,0:T(8,128)(2,1)}, bf16[8,3968]{1,0:T(8,128)(2,1)S(1)}, u32[]{:S(2)}, u32[]{:S(2)}) collective-permute-start(bf16[8,3968]{1,0:T(8,128)(2,1)} %get-tuple-element.31.refs_0_), channel_id=1, source_target_pairs={{0,2},{2,0},{4,6},{6,4},{8,10},{10,8},{12,14},{14,12},{1,3},{3,1},... | collective-permute-start | bytes 190472 | tf_op jit(solution)/shard_map/ppermute | solution.py:382
  10.5 8.7 %copy-start.4 = (bf16[8,3968]{1,0:T(8,128)(2,1)}, bf16[8,3968]{1,0:T(8,128)(2,1)S(1)}, u32[]{:S(2)}) copy-start(bf16[8,3968]{1,0:T(8,128)(2,1)S(1)} %collective-permute-done.refs_1_) | copy-start | bytes 190468
  10.5 4.2 %collective-permute-start.2 = (bf16[8,3968]{1,0:T(8,128)(2,1)S(1)}, bf16[8,3968]{1,0:T(8,128)(2,1)S(1)}, u32[]{:S(2)}, u32[]{:S(2)}) collective-permute-start(bf16[8,3968]{1,0:T(8,128)(2,1)S(1)} %collective-permute-done.refs_1_), channel_id=1, source_target_pairs={{0,2},{2,0},{4,6},{6,4},{8,10},{10,8},{12,14},{14,12},{1,3},{3,1},... | collective-permute-start | bytes 190472 | tf_op jit(solution)/shard_map/ppermute | solution.py:382
  12.2 4.8 %collective-permute-start.3 = (bf16[8,3968]{1,0:T(8,128)(2,1)}, bf16[8,3968]{1,0:T(8,128)(2,1)S(1)}, u32[]{:S(2)}, u32[]{:S(2)}) collective-permute-start(bf16[8,3968]{1,0:T(8,128)(2,1)} %get-tuple-element.31.refs_0_), channel_id=1, source_target_pairs={{0,4},{2,6},{4,0},{6,2},{8,12},{10,14},{12,8},{14,10},{1,5},{3,7},... | collective-permute-start | bytes 190472 | tf_op jit(solution)/shard_map/ppermute | solution.py:382
  12.6 5.1 %collective-permute-start.4 = (bf16[8,3968]{1,0:T(8,128)(2,1)S(1)}, bf16[8,3968]{1,0:T(8,128)(2,1)S(1)}, u32[]{:S(2)}, u32[]{:S(2)}) collective-permute-start(bf16[8,3968]{1,0:T(8,128)(2,1)S(1)} %collective-permute-done.refs_1_), channel_id=1, source_target_pairs={{0,4},{2,6},{4,0},{6,2},{8,12},{10,14},{12,8},{14,10},{1,5},{3,7},... | collective-permute-start | bytes 190472 | tf_op jit(solution)/shard_map/ppermute | solution.py:382
  14.2 4.9 %copy-start.5 = (bf16[8,3968]{1,0:T(8,128)(2,1)}, bf16[8,3968]{1,0:T(8,128)(2,1)S(1)}, u32[]{:S(2)}) copy-start(bf16[8,3968]{1,0:T(8,128)(2,1)S(1)} %collective-permute-done.1.refs_2_) | copy-start | bytes 190468
  14.2 4.2 %collective-permute-start.5 = (bf16[8,3968]{1,0:T(8,128)(2,1)S(1)}, bf16[8,3968]{1,0:T(8,128)(2,1)S(1)}, u32[]{:S(2)}, u32[]{:S(2)}) collective-permute-start(bf16[8,3968]{1,0:T(8,128)(2,1)S(1)} %collective-permute-done.1.refs_2_), channel_id=1, source_target_pairs={{0,4},{2,6},{4,0},{6,2},{8,12},{10,14},{12,8},{14,10},{1,5},{3,7},... | collective-permute-start | bytes 190472 | tf_op jit(solution)/shard_map/ppermute | solution.py:382
  14.7 4.4 %copy-start.6 = (bf16[8,3968]{1,0:T(8,128)(2,1)}, bf16[8,3968]{1,0:T(8,128)(2,1)S(1)}, u32[]{:S(2)}) copy-start(bf16[8,3968]{1,0:T(8,128)(2,1)S(1)} %collective-permute-done.2.refs_3_) | copy-start | bytes 190468
  14.7 4.4 %collective-permute-start.6 = (bf16[8,3968]{1,0:T(8,128)(2,1)S(1)}, bf16[8,3968]{1,0:T(8,128)(2,1)S(1)}, u32[]{:S(2)}, u32[]{:S(2)}) collective-permute-start(bf16[8,3968]{1,0:T(8,128)(2,1)S(1)} %collective-permute-done.2.refs_3_), channel_id=1, source_target_pairs={{0,4},{2,6},{4,0},{6,2},{8,12},{10,14},{12,8},{14,10},{1,5},{3,7},... | collective-permute-start | bytes 190472 | tf_op jit(solution)/shard_map/ppermute | solution.py:382
  17.0 2.1 %copy-start.7 = (bf16[8,3968]{1,0:T(8,128)(2,1)}, bf16[8,3968]{1,0:T(8,128)(2,1)S(1)}, u32[]{:S(2)}) copy-start(bf16[8,3968]{1,0:T(8,128)(2,1)S(1)} %collective-permute-done.3.refs_4_) | copy-start | bytes 190468
  17.7 1.5 %copy-start.8 = (bf16[8,3968]{1,0:T(8,128)(2,1)}, bf16[8,3968]{1,0:T(8,128)(2,1)S(1)}, u32[]{:S(2)}) copy-start(bf16[8,3968]{1,0:T(8,128)(2,1)S(1)} %collective-permute-done.4.refs_5_) | copy-start | bytes 190468
  18.5 0.7 copy-start.9
  19.2 0.6 copy-start.10
  22.0 1.9 %collective-permute-start.8 = (bf16[64,3072]{1,0:T(8,128)(2,1)}, bf16[64,3072]{1,0:T(8,128)(2,1)S(1)}, u32[]{:S(2)}, u32[]{:S(2)}) collective-permute-start(bf16[64,3072]{1,0:T(8,128)(2,1)} %get-tuple-element.34.ga_ref.own_ref), channel_id=1, source_target_pairs={{0,1},{1,0},{2,3},{3,2},{4,5},{5,4},{6,7},{7,6},{8,9},{9,8},{10,11... | collective-permute-start | bytes 1179656 | tf_op jit(solution)/shard_map/ppermute | solution.py:385
  22.0 2.5 %collective-permute-start.7 = (bf16[64,3072]{1,0:T(8,128)(2,1)}, bf16[64,3072]{1,0:T(8,128)(2,1)S(1)}, u32[]{:S(2)}, u32[]{:S(2)}) collective-permute-start(bf16[64,3072]{1,0:T(8,128)(2,1)} %get-tuple-element.33.xa_ref.own_ref), channel_id=1, source_target_pairs={{0,1},{1,0},{2,3},{3,2},{4,5},{5,4},{6,7},{7,6},{8,9},{9,8},{10,11... | collective-permute-start | bytes 1179656 | tf_op jit(solution)/shard_map/ppermute | solution.py:385
  24.5 1.0 %copy-start = (bf16[64,3072]{1,0:T(8,128)(2,1)S(1)}, bf16[64,3072]{1,0:T(8,128)(2,1)}, u32[]{:S(2)}) copy-start(bf16[64,3072]{1,0:T(8,128)(2,1)} %get-tuple-element.33.xa_ref.own_ref) | copy-start | bytes 1179652
  25.5 1.0 %copy-start.1 = (bf16[64,3072]{1,0:T(8,128)(2,1)S(1)}, bf16[64,3072]{1,0:T(8,128)(2,1)}, u32[]{:S(2)}) copy-start(bf16[64,3072]{1,0:T(8,128)(2,1)} %get-tuple-element.34.ga_ref.own_ref) | copy-start | bytes 1179652
  26.5 0.8 copy-start.2
  61.5 2.0 %collective-permute-start.9 = (f32[64,2048]{1,0:T(8,128)S(1)}, f32[64,2048]{1,0:T(8,128)S(1)}, u32[]{:S(2)}, u32[]{:S(2)}) collective-permute-start(f32[64,2048]{1,0:T(8,128)S(1)} %get-tuple-element.40), channel_id=1, source_target_pairs={{0,1},{1,0},{2,3},{3,2},{4,5},{5,4},{6,7},{7,6},{8,9},{9,8},{10,11... | collective-permute-start | bytes 1572872 | tf_op jit(solution)/shard_map/ppermute | solution.py:385
  63.6 8.6 %collective-permute-start.10 = (f32[32,2048]{1,0:T(8,128)S(1)}, f32[32,2048]{1,0:T(8,128)S(1)}, u32[]{:S(2)}, u32[]{:S(2)}) collective-permute-start(f32[32,2048]{1,0:T(8,128)S(1)} %slice.24), channel_id=1, source_target_pairs={{0,4},{2,6},{4,0},{6,2},{8,12},{10,14},{12,8},{14,10},{1,5},{3,7},... | collective-permute-start | bytes 786440 | tf_op jit(solution)/shard_map/ppermute | solution.py:382
  72.2 8.6 %collective-permute-start.11 = (f32[16,2048]{1,0:T(8,128)S(1)}, f32[16,2048]{1,0:T(8,128)S(1)}, u32[]{:S(2)}, u32[]{:S(2)}) collective-permute-start(f32[16,2048]{1,0:T(8,128)S(1)} %slice.25), channel_id=1, source_target_pairs={{0,2},{2,0},{4,6},{6,4},{8,10},{10,8},{12,14},{14,12},{1,3},{3,1},... | collective-permute-start | bytes 393224 | tf_op jit(solution)/shard_map/ppermute | solution.py:382
  81.5 9.7 %collective-permute-start.12 = (f32[8,2048]{1,0:T(8,128)S(1)}, f32[8,2048]{1,0:T(8,128)S(1)}, u32[]{:S(2)}, u32[]{:S(2)}) collective-permute-start(f32[8,2048]{1,0:T(8,128)S(1)} %slice.26), channel_id=1, source_target_pairs={{0,8},{2,10},{4,12},{6,14},{8,0},{10,2},{12,4},{14,6},{1,9},{3,11}... | collective-permute-start | bytes 196616 | tf_op jit(solution)/shard_map/ppermute | solution.py:379
  91.1 0.6 copy-start.3

commit v4 on v3

--- a/solution.py
+++ b/solution.py
@@ -134,18 +134,6 @@
     return pl.multiple_of((side * chunks + lax.rem(step, chunks)) * chunk, chunk)
 
 
-def half_grad(part, wg_ref, wu_ref, dhr_ref, dur_ref, base, chunk):
-    def step(c, carry):
-        at = pl.multiple_of(c * chunk, chunk)
-        cols = pl.ds(base + at, chunk)
-        part[:, pl.ds(at, chunk)] = jnp.dot(dhr_ref[...], wg_ref[:, cols], preferred_element_type=F32) + jnp.dot(
-            dur_ref[...], wu_ref[:, cols], preferred_element_type=F32
-        )
-        return carry
-
-    lax.fori_loop(0, part.shape[1] // chunk, step, 0)
-
-
 def pack_rows(part, gates, out):
     rows, width = part.shape
     half, eighth = width // 2, width // SUBS
@@ -159,47 +147,136 @@
     out[:, half + eighth :] = gates
 
 
-def experts_body(chunk, t_ref, xa_ref, xb_ref, ga_ref, gb_ref, factor_ref, wg_hbm, wu_hbm, wd_hbm,
-                 wt_ref, dh_ref, du_ref, give_ref, keep_ref,
-                 wg_ref, wu_ref, ring, h_ref, u_ref, da_ref, dhr_ref, dur_ref, part, landed, ring_landed):
-    rows, width = xa_ref.shape
+def stream_body(chunk, t_ref, xa_ref, xb_ref, w_hbm, out_ref, held, landed):
+    chunks = xa_ref.shape[1] // chunk
+    t = t_ref[0]
+
+    def load(i):
+        cols = pl.ds(place_of(i, chunks, chunk, t), chunk)
+        return pltpu.make_async_copy(w_hbm.at[:, cols], held.at[i], landed.at[i])
+
+    for i in range(2 * chunks):
+        load(i).start()
+    for side, x_ref in enumerate((xa_ref, xb_ref)):
+
+        def step(c, carry):
+            i = side * chunks + c
+            x = x_ref[:, pl.ds(pl.multiple_of(c * chunk, chunk), chunk)]
+            load(i).wait()
+            more = lax.dot_general(held[i], x, NT, preferred_element_type=F32)
+            out_ref[...] = jnp.where(i == 0, more, out_ref[...] + more)
+            return carry
+
+        lax.fori_loop(0, chunks, step, 0)
+
+
+def stream_units(t, xa, xb, w, name):
+    hidden, depth = w.shape
+    rows, width = xa.shape
+    chunk = chunk_of(width, 1024)
+    steps = depth // chunk
+    return pl.pallas_call(
+        functools.partial(stream_body, chunk),
+        out_shape=jax.ShapeDtypeStruct((hidden, rows), F32),
+        in_specs=[SMEM, VMEM, VMEM, HBM],
+        out_specs=VMEM,
+        scratch_shapes=[pltpu.VMEM((steps, hidden, chunk), BF16), pltpu.SemaphoreType.DMA((steps,))],
+        compiler_params=pltpu.CompilerParams(vmem_limit_bytes=32 * MIB),
+        cost_estimate=pl.CostEstimate(
+            flops=2 * rows * hidden * depth, bytes_accessed=2 * hidden * depth, transcendentals=0
+        ),
+        name=name,
+    )(t, xa, xb, w)
+
+
+def rows_body(tile, t_ref, xa_ref, xb_ref, w_hbm, out_ref, held, x, landed):
+    width = xa_ref.shape[1]
+    steps = w_hbm.shape[0] // tile
+    t = t_ref[0]
+
+    def load(i):
+        rows = pl.ds(pl.multiple_of(i * tile, tile), tile)
+        return pltpu.make_async_copy(w_hbm.at[rows, :], held.at[i], landed.at[i])
+
+    for i in range(steps):
+        load(i).start()
+    for at, ref in ((t, xa_ref), (1 - t, xb_ref)):
+        x[:, pl.ds(pl.multiple_of(at * width, width), width)] = ref[...]
+
+    def step(i, carry):
+        rows = pl.ds(pl.multiple_of(i * tile, tile), tile)
+        load(i).wait()
+        out_ref[rows, :] = lax.dot_general(x[...], held[i], NT, preferred_element_type=F32).T
+        return carry
+
+    lax.fori_loop(0, steps, step, 0)
+
+
+def row_units(t, xa, xb, w, name):
+    hidden, depth = w.shape
+    rows, width = xa.shape
+    tile = tile_of(hidden, 256)
+    steps = hidden // tile
+    return pl.pallas_call(
+        functools.partial(rows_body, tile),
+        out_shape=jax.ShapeDtypeStruct((hidden, rows), F32),
+        in_specs=[SMEM, VMEM, VMEM, HBM],
+        out_specs=VMEM,
+        scratch_shapes=[
+            pltpu.VMEM((steps, tile, depth), BF16),
+            pltpu.VMEM((rows, depth), BF16),
+            pltpu.SemaphoreType.DMA((steps,)),
+        ],
+        compiler_params=pltpu.CompilerParams(vmem_limit_bytes=32 * MIB),
+        cost_estimate=pl.CostEstimate(
+            flops=2 * rows * hidden * depth, bytes_accessed=2 * hidden * depth, transcendentals=0
+        ),
+        name=name,
+    )(t, xa, xb, w)
+
+
+def half_loads(t, chunk, width, wg_hbm, wu_hbm, held, landed, own):
+    base = pl.multiple_of((t if own else 1 - t) * width, width)
+
+    def load(c, n):
+        cols = pl.ds(base + pl.multiple_of(c * chunk, chunk), chunk)
+        return pltpu.make_async_copy((wg_hbm, wu_hbm)[n].at[:, cols], held.at[c, n], landed.at[c, n])
+
+    return load
+
+
+def half_grad(part, load, held, dhr_ref, dur_ref, chunk):
+    def step(c, carry):
+        for n in range(2):
+            load(c, n).wait()
+        part[:, pl.ds(pl.multiple_of(c * chunk, chunk), chunk)] = jnp.dot(
+            dhr_ref[...], held[c, 0], preferred_element_type=F32
+        ) + jnp.dot(dur_ref[...], held[c, 1], preferred_element_type=F32)
+        return carry
+
+    lax.fori_loop(0, part.shape[1] // chunk, step, 0)
+
+
+def give_body(chunk, small, t_ref, ga_ref, gb_ref, factor_ref, h_ref, u_ref, wg_hbm, wu_hbm, wd_hbm,
+              wt_ref, dh_ref, du_ref, dhr_ref, dur_ref, gate_ref, give_ref,
+              ring, held, da_ref, part, ring_landed, landed):
+    rows, width = ga_ref.shape
     chunks = width // chunk
     depth = ring.shape[0]
     steps = 2 * chunks
     t = t_ref[0]
 
-    def load(i, n):
-        cols = pl.ds(place_of(i, chunks, chunk, t), chunk)
-        src, dst = ((wg_hbm, wg_ref), (wu_hbm, wu_ref))[n]
-        return pltpu.make_async_copy(src.at[:, cols], dst.at[:, cols], landed.at[i, n])
-
     def load_down(i):
         cols = pl.ds(place_of(i, chunks, chunk, t), chunk)
         slot = lax.rem(i, depth)
         return pltpu.make_async_copy(wd_hbm.at[:, cols], ring.at[slot], ring_landed.at[slot])
 
-    for i in range(steps):
-        for n in range(2):
-            load(i, n).start()
+    load = half_loads(t, small, width, wg_hbm, wu_hbm, held, landed, False)
     for i in range(min(steps, depth)):
         load_down(i).start()
-
-    def add_to(out, i, w, x):
-        more = lax.dot_general(w, x, NT, preferred_element_type=F32)
-        out[...] = jnp.where(i == 0, more, out[...] + more)
-
-    for side, x_ref in enumerate((xa_ref, xb_ref)):
-
-        def up_step(c, carry):
-            i = side * chunks + c
-            x = x_ref[:, pl.ds(pl.multiple_of(c * chunk, chunk), chunk)]
-            cols = pl.ds(place_of(i, chunks, chunk, t), chunk)
-            for n, (w, out) in enumerate(((wg_ref, h_ref), (wu_ref, u_ref))):
-                load(i, n).wait()
-                add_to(out, i, w[:, cols], x)
-            return carry
-
-        lax.fori_loop(0, chunks, up_step, 0)
+    for c in range(width // small):
+        for n in range(2):
+            load(c, n).start()
 
     for side, g_ref in enumerate((ga_ref, gb_ref)):
 
@@ -207,7 +284,8 @@
             i = side * chunks + c
             g = g_ref[:, pl.ds(pl.multiple_of(c * chunk, chunk), chunk)]
             load_down(i).wait()
-            add_to(da_ref, i, ring[lax.rem(i, depth)], g)
+            more = lax.dot_general(ring[lax.rem(i, depth)], g, NT, preferred_element_type=F32)
+            da_ref[...] = jnp.where(i == 0, more, da_ref[...] + more)
 
             @pl.when(i + depth < steps)
             def _():
@@ -233,53 +311,77 @@
     dhr_ref[...] = dh.T.astype(BF16)
     dur_ref[...] = du.T.astype(BF16)
     total = jnp.sum(act * da, axis=0, keepdims=True)
-    gates = jnp.broadcast_to(total, (LANES, rows)).T
-    for at, out in ((1 - t, give_ref), (t, keep_ref)):
-        base = pl.multiple_of(at * width, width)
-        half_grad(part, wg_ref, wu_ref, dhr_ref, dur_ref, base, chunk_of(width, 512))
-        pack_rows(part, gates, out)
-
-
-def expert_units(t, xa, xb, ga, gb, factor, w_gate, w_up, w_down):
+    gate_ref[...] = jnp.broadcast_to(total, (LANES, rows)).T
+    half_grad(part, load, held, dhr_ref, dur_ref, small)
+    pack_rows(part, gate_ref[...], give_ref)
+
+
+def give_half(t, ga, gb, factor, h, u, w_gate, w_up, w_down):
     hidden, depth = w_gate.shape
-    rows, width = xa.shape
+    rows, width = ga.shape
     chunk = chunk_of(width, 1024)
-    steps = depth // chunk
-    ring = min(3, steps)
+    small = chunk_of(width, 512)
+    ring = min(4, depth // chunk)
     unit = jax.ShapeDtypeStruct((hidden, rows), BF16)
+    turned = jax.ShapeDtypeStruct((rows, hidden), BF16)
     packed = jax.ShapeDtypeStruct((rows, width // 2 + width // SUBS + LANES), F32)
     return pl.pallas_call(
-        functools.partial(experts_body, chunk),
-        out_shape=(unit, unit, unit, packed, packed),
+        functools.partial(give_body, chunk, small),
+        out_shape=(unit, unit, unit, turned, turned, jax.ShapeDtypeStruct((rows, LANES), F32), packed),
         in_specs=[SMEM] + [VMEM] * 5 + [HBM] * 3,
-        out_specs=[VMEM] * 5,
+        out_specs=[VMEM] * 7,
         scratch_shapes=[
-            pltpu.VMEM((hidden, depth), BF16),
-            pltpu.VMEM((hidden, depth), BF16),
             pltpu.VMEM((ring, hidden, chunk), BF16),
+            pltpu.VMEM((width // small, 2, hidden, small), BF16),
             pltpu.VMEM((hidden, rows), F32),
-            pltpu.VMEM((hidden, rows), F32),
-            pltpu.VMEM((hidden, rows), F32),
-            pltpu.VMEM((rows, hidden), BF16),
-            pltpu.VMEM((rows, hidden), BF16),
             pltpu.VMEM((rows, width), F32),
-            pltpu.SemaphoreType.DMA((steps, 2)),
             pltpu.SemaphoreType.DMA((ring,)),
+            pltpu.SemaphoreType.DMA((width // small, 2)),
         ],
-        compiler_params=pltpu.CompilerParams(vmem_limit_bytes=48 * MIB),
+        compiler_params=pltpu.CompilerParams(vmem_limit_bytes=44 * MIB),
         cost_estimate=pl.CostEstimate(
-            flops=10 * rows * hidden * depth, bytes_accessed=6 * hidden * depth, transcendentals=rows * hidden
-        ),
-        name="expert_units",
-    )(t, xa, xb, ga, gb, factor, w_gate, w_up, w_down)
-
-
-def weights_body(chunk, t_ref, left_ref, own_ref, oth_ref, out_ref, ring, sent):
+            flops=4 * rows * hidden * depth, bytes_accessed=4 * hidden * depth, transcendentals=rows * hidden
+        ),
+        name="give_half",
+    )(t, ga, gb, factor, h, u, w_gate, w_up, w_down)
+
+
+def keep_body(small, t_ref, gate_ref, dhr_ref, dur_ref, wg_hbm, wu_hbm, keep_ref, held, part, landed):
+    width = part.shape[1]
+    load = half_loads(t_ref[0], small, width, wg_hbm, wu_hbm, held, landed, True)
+    for c in range(width // small):
+        for n in range(2):
+            load(c, n).start()
+    half_grad(part, load, held, dhr_ref, dur_ref, small)
+    pack_rows(part, gate_ref[...], keep_ref)
+
+
+def keep_half(t, gate, dhr, dur, w_gate, w_up, width):
+    rows, hidden = dhr.shape
+    small = chunk_of(width, 512)
+    return pl.pallas_call(
+        functools.partial(keep_body, small),
+        out_shape=jax.ShapeDtypeStruct((rows, width // 2 + width // SUBS + LANES), F32),
+        in_specs=[SMEM] + [VMEM] * 3 + [HBM] * 2,
+        out_specs=VMEM,
+        scratch_shapes=[
+            pltpu.VMEM((width // small, 2, hidden, small), BF16),
+            pltpu.VMEM((rows, width), F32),
+            pltpu.SemaphoreType.DMA((width // small, 2)),
+        ],
+        compiler_params=pltpu.CompilerParams(vmem_limit_bytes=32 * MIB),
+        cost_estimate=pl.CostEstimate(
+            flops=4 * rows * hidden * width, bytes_accessed=4 * hidden * width, transcendentals=0
+        ),
+        name="keep_half",
+    )(t, gate, dhr, dur, w_gate, w_up)
+
+
+def column_body(chunk, tile, t_ref, left_ref, own_ref, oth_ref, out_ref, ring, sent):
     width = own_ref.shape[1]
     chunks = width // chunk
     depth = ring.shape[0]
     hidden = left_ref.shape[0]
-    tile = tile_of(hidden, 448)
     t = t_ref[0]
 
     def store(i):
@@ -310,18 +412,69 @@
         store(i).wait()
 
 
-def weight_grad(t, left, own, oth, name):
+def weight_grad_columns(t, left, own, oth, name, most, tile):
     hidden, rows = left.shape
     width = own.shape[1]
     depth = 2 * width
-    chunk = chunk_of(width, 512)
+    chunk = chunk_of(width, most)
+    tile = tile_of(hidden, tile)
     ring = min(4, depth // chunk)
     return pl.pallas_call(
-        functools.partial(weights_body, chunk),
+        functools.partial(column_body, chunk, tile),
         out_shape=jax.ShapeDtypeStruct((hidden, depth), BF16),
         in_specs=[SMEM] + [VMEM] * 3,
         out_specs=HBM,
         scratch_shapes=[pltpu.VMEM((ring, hidden, chunk), BF16), pltpu.SemaphoreType.DMA((ring,))],
+        compiler_params=pltpu.CompilerParams(vmem_limit_bytes=24 * MIB),
+        cost_estimate=pl.CostEstimate(
+            flops=2 * rows * hidden * depth, bytes_accessed=2 * hidden * depth, transcendentals=0
+        ),
+        name=name,
+    )(t, left, own, oth)
+
+
+def tile_body(t_ref, left_ref, own_ref, oth_ref, out_ref, ring, sent):
+    width = own_ref.shape[1]
+    depth, tile, _ = ring.shape
+    steps = left_ref.shape[0] // tile
+    t = t_ref[0]
+
+    def store(i):
+        slot = lax.rem(i, depth)
+        rows = pl.ds(pl.multiple_of(i * tile, tile), tile)
+        return pltpu.make_async_copy(ring.at[slot], out_ref.at[rows, :], sent.at[slot])
+
+    def step(i, carry):
+        slot = lax.rem(i, depth)
+
+        @pl.when(i >= depth)
+        def _():
+            store(i - depth).wait()
+
+        left = left_ref[pl.ds(pl.multiple_of(i * tile, tile), tile), :]
+        for at, ref in ((t, own_ref), (1 - t, oth_ref)):
+            cols = pl.ds(pl.multiple_of(at * width, width), width)
+            ring[slot, :, cols] = jnp.dot(left, ref[...], preferred_element_type=F32).astype(BF16)
+        store(i).start()
+        return carry
+
+    lax.fori_loop(0, steps, step, 0)
+    for i in range(max(0, steps - depth), steps):
+        store(i).wait()
+
+
+def weight_grad_tiles(t, left, own, oth, name):
+    hidden, rows = left.shape
+    width = own.shape[1]
+    depth = 2 * width
+    tile = tile_of(hidden, 256)
+    ring = min(4, hidden // tile)
+    return pl.pallas_call(
+        tile_body,
+        out_shape=jax.ShapeDtypeStruct((hidden, depth), BF16),
+        in_specs=[SMEM] + [VMEM] * 3,
+        out_specs=HBM,
+        scratch_shapes=[pltpu.VMEM((ring, tile, depth), BF16), pltpu.SemaphoreType.DMA((ring,))],
         compiler_params=pltpu.CompilerParams(vmem_limit_bytes=24 * MIB),
         cost_estimate=pl.CostEstimate(
             flops=2 * rows * hidden * depth, bytes_accessed=2 * hidden * depth, transcendentals=0
@@ -384,6 +537,7 @@
     def other_core(v):
         return lax.ppermute(v, "tensor", [(0, 1), (1, 0)])
 
+    w_gate, w_up, w_down = (pltpu.with_memory_space_constraint(w, pltpu.HBM) for w in (w_gate, w_up, w_down))
     ids_t = expert_ids.T
     own, oth = pick(e, ids_t, gate_probs.T, tokens, grad_out)
     first, second = [own], [partner(oth)]
@@ -395,25 +549,35 @@
     xa, ga, factor = assemble([piece for pair in zip(first, second) for piece in pair], width)
     xb = other_core(xa)
     gb = other_core(ga)
-    wt, dh, du, give, keep = expert_units(t, xa, xb, ga, gb, factor, w_gate, w_up, w_down)
-    total = keep + other_core(give)
+    h = stream_units(t, xa, xb, w_gate, "gate_units")
+    u = row_units(t, xa, xb, w_up, "up_units")
+    wt, dh, du, dhr, dur, gate, give = give_half(t, ga, gb, factor, h, u, w_gate, w_up, w_down)
+    got = other_core(give)
+    keep = keep_half(t, gate, dhr, dur, w_gate, w_up, width)
+    keep, got = lax.optimization_barrier((keep, got))
+    total = keep + got
     grads = []
-    jobs = [(dh, xa, xb, "grad_w_gate"), (du, xa, xb, "grad_w_up"), (wt, ga, gb, "grad_w_down")]
+    forms = (
+        functools.partial(weight_grad_tiles, name="grad_w_gate"),
+        functools.partial(weight_grad_columns, name="grad_w_up", most=512, tile=1344),
+        functools.partial(weight_grad_columns, name="grad_w_down", most=1024, tile=448),
+    )
+    jobs = [(dh, xa, xb, forms[0]), (du, xa, xb, forms[1]), (wt, ga, gb, forms[2])]
     d = copies // 2
     while d:
         rows = d * 2 * SUBS
         coming = across(total[rows:], d)
         if len(jobs) > 1:
-            left, a, b, name = jobs.pop(0)
+            left, a, b, job = jobs.pop(0)
             left, total = lax.optimization_barrier((left, total))
-            grads.append(weight_grad(t, left, a, b, name))
+            grads.append(job(t, left, a, b))
             grads[-1], coming = lax.optimization_barrier((grads[-1], coming))
         total = total[:rows] + coming
         d //= 2
     theirs = partner(total[SUBS:])
-    for left, a, b, name in jobs:
+    for left, a, b, job in jobs:
         left, total = lax.optimization_barrier((left, total))
-        grads.append(weight_grad(t, left, a, b, name))
+        grads.append(job(t, left, a, b))
     grads, theirs = lax.optimization_barrier((grads, theirs))
     token_grad, gate_t = finish(e, ids_t, total[:SUBS], theirs, width)
     return token_grad, gate_t.T, *grads

time: 94.6 us -> 94.3 us (level)
  Pallas kernels: 62.3 us -> 65.8 us
  waiting for transfers between devices: 9.01 us -> 7.17 us
  local copies, waits for them, and re-layouts: 4.65 us -> 2.94 us
    pallas_call x4 -> x7, Pallas kernels: 55.7 us -> 59.1 us  [the longest x1 16.5 us: give_half(): pl.pallas_call(functools.partial(give_body, chunk, small), out_shape=(uni...]
    ppermute x3, waiting for transfers between devices: 3.76 us -> 1.43 us  [other_core(): return lax.ppermute(v, 'tensor', [(0, 1), (1, 0)])]
    unnamed x22 -> x24, local copies, waits for them, and re-layouts: 3.99 us -> 2.28 us
  transfers between devices with their start and end apart: 13 -> 13, of which waited for: 9 -> 8; matrix products, arithmetic and copies ran while one was open for 0% -> 0% of each run, Pallas kernels for 23% -> 45%
where the time goes in v4:
time: 94.3 us; the launch traced here: 94 us
  Pallas kernels  65.8 us (70%)
  starting transfers between devices  17.2 us (18%)
  waiting for transfers between devices  7.17 us (8%)
  local copies, waits for them, and re-layouts  2.94 us (3%)
    pallas_call x1, Pallas kernels, give_half(): pl.pallas_call(functools.partial(give_body, chunk, small), out_shape=(uni...  16.5 us
    pallas_call x2, Pallas kernels, weight_grad_columns(): pl.pallas_call(functools.partial(column_body, chunk, tile), out_shape=jax...  13.8 us
    ppermute x8, starting transfers between devices, across(): return lax.ppermute(v, 'expert', [(i, i ^ d) for i in range(n_expert)])  10.2 us
    pallas_call x1, Pallas kernels, row_units(): pl.pallas_call(functools.partial(rows_body, tile), out_shape=jax.ShapeDty...  8.24 us
    pallas_call x1, Pallas kernels, stream_units(): pl.pallas_call(functools.partial(stream_body, chunk), out_shape=jax.Shape...  7.08 us
    pallas_call x1, Pallas kernels, keep_half(): pl.pallas_call(functools.partial(keep_body, small), out_shape=jax.ShapeDt...  6.73 us
    pallas_call x1, Pallas kernels, weight_grad_tiles(): pl.pallas_call(tile_body, out_shape=jax.ShapeDtypeStruct((hidden, depth),...  6.71 us
    ppermute x2, starting transfers between devices, partner(): lax.ppermute(v, 'expert', [(i, (i + copies) % n_expert) for i in range(n_...  6.24 us
  transfers between devices with their start and end apart: 13, of which 8 were waited for; matrix products, arithmetic and copies ran while one was open for 0% of the time, Pallas kernels for 45%

profile of v4, /device:TPU:0, one launch (start us, length us, event | category | flops | bytes accessed | tf_op | source)
XLA Modules:
  0.0 94.0 jit_solution(16188782509634295091)
XLA Ops:
  0.6 2.0 %pick_rows.1 = (bf16[8,3968]{1,0:T(8,128)(2,1)}, bf16[8,3968]{1,0:T(8,128)(2,1)}) custom-call(s32[1]{0:T(128)} %bitcast.e_ref, s32[4,16]{1,0:T(4,128)} %bitcast.5, bf16[4,16]{1,0:T(4,128)(2,1)} %bitcast.7, bf16[16,3072]{1,0:T(8,128)(2,1)} %tok_ref.1, bf16[16,3072]{1,0:T(8,128)(2,1)} %grad_ref.1), custom_call_target="tpu_custom_call" | custom-call | tf_op jit(solution)/shard_map/pick_rows/pallas_call | solution.py:82
  2.7 4.0 %collective-permute-start = (bf16[8,3968]{1,0:T(8,128)(2,1)}, bf16[8,3968]{1,0:T(8,128)(2,1)S(1)}, u32[]{:S(2)}, u32[]{:S(2)}) collective-permute-start(bf16[8,3968]{1,0:T(8,128)(2,1)} %get-tuple-element.36), channel_id=1, source_target_pairs={{0,8},{2,10},{4,12},{6,14},{8,0},{10,2},{12,4},{14,6},{1,9},{3,11}... | collective-permute-start | bytes 190472 | tf_op jit(solution)/shard_map/ppermute | solution.py:532
  6.7 1.5 %collective-permute-start.1 = (bf16[8,3968]{1,0:T(8,128)(2,1)}, bf16[8,3968]{1,0:T(8,128)(2,1)S(1)}, u32[]{:S(2)}, u32[]{:S(2)}) collective-permute-start(bf16[8,3968]{1,0:T(8,128)(2,1)} %get-tuple-element.35.refs_0_), channel_id=1, source_target_pairs={{0,2},{2,0},{4,6},{6,4},{8,10},{10,8},{12,14},{14,12},{1,3},{3,1},... | collective-permute-start | bytes 190472 | tf_op jit(solution)/shard_map/ppermute | solution.py:535
  8.2 2.3 %collective-permute-done.refs_1_ = bf16[8,3968]{1,0:T(8,128)(2,1)S(1)} collective-permute-done((bf16[8,3968]{1,0:T(8,128)(2,1)}, bf16[8,3968]{1,0:T(8,128)(2,1)S(1)}, u32[]{:S(2)}, u32[]{:S(2)}) %collective-permute-start) | collective-permute-done | bytes 63520 | tf_op jit(solution)/shard_map/ppermute | solution.py:532
  10.5 0.0 copy-start.5
  10.5 1.7 %collective-permute-start.2 = (bf16[8,3968]{1,0:T(8,128)(2,1)S(1)}, bf16[8,3968]{1,0:T(8,128)(2,1)S(1)}, u32[]{:S(2)}, u32[]{:S(2)}) collective-permute-start(bf16[8,3968]{1,0:T(8,128)(2,1)S(1)} %collective-permute-done.refs_1_), channel_id=1, source_target_pairs={{0,2},{2,0},{4,6},{6,4},{8,10},{10,8},{12,14},{14,12},{1,3},{3,1},... | collective-permute-start | bytes 190472 | tf_op jit(solution)/shard_map/ppermute | solution.py:535
  12.2 0.4 collective-permute-start.3
  12.6 1.6 %collective-permute-start.4 = (bf16[8,3968]{1,0:T(8,128)(2,1)S(1)}, bf16[8,3968]{1,0:T(8,128)(2,1)S(1)}, u32[]{:S(2)}, u32[]{:S(2)}) collective-permute-start(bf16[8,3968]{1,0:T(8,128)(2,1)S(1)} %collective-permute-done.refs_1_), channel_id=1, source_target_pairs={{0,4},{2,6},{4,0},{6,2},{8,12},{10,14},{12,8},{14,10},{1,5},{3,7},... | collective-permute-start | bytes 190472 | tf_op jit(solution)/shard_map/ppermute | solution.py:535
  14.2 0.0 collective-permute-done.1.refs_2_
  14.2 0.0 copy-start.6
  14.2 0.4 collective-permute-start.5
  14.7 0.1 collective-permute-done.2.refs_3_
  14.7 0.0 copy-start.7
  14.7 1.5 %collective-permute-start.6 = (bf16[8,3968]{1,0:T(8,128)(2,1)S(1)}, bf16[8,3968]{1,0:T(8,128)(2,1)S(1)}, u32[]{:S(2)}, u32[]{:S(2)}) collective-permute-start(bf16[8,3968]{1,0:T(8,128)(2,1)S(1)} %collective-permute-done.2.refs_3_), channel_id=1, source_target_pairs={{0,4},{2,6},{4,0},{6,2},{8,12},{10,14},{12,8},{14,10},{1,5},{3,7},... | collective-permute-start | bytes 190472 | tf_op jit(solution)/shard_map/ppermute | solution.py:535
  16.3 0.8 collective-permute-done.3.refs_4_
  17.0 0.0 copy-start.8
  17.0 0.7 collective-permute-done.4.refs_5_
  17.7 0.0 copy-start.9
  17.7 0.8 collective-permute-done.5.refs_6_
  18.5 0.0 copy-start.10
  18.5 0.7 collective-permute-done.6.refs_7_
  19.1 0.0 copy-done.5
  19.2 0.0 copy-done.6
  19.2 0.0 copy-done.7
  19.2 0.0 copy-done.8
  19.2 0.0 copy-done.9
  19.2 0.0 copy-done.10
  19.2 0.0 copy-start.11
  19.2 0.6 copy-done.11
  19.8 2.2 %assemble_rows.1 = (bf16[64,3072]{1,0:T(8,128)(2,1)}, bf16[64,3072]{1,0:T(8,128)(2,1)}, f32[64,128]{1,0:T(8,128)}) custom-call(bf16[8,3968]{1,0:T(8,128)(2,1)} %get-tuple-element.35.refs_0_, bf16[8,3968]{1,0:T(8,128)(2,1)} %copy-done.5, bf16[8,3968]{1,0:T(8,128)(2,1)} %copy-done.6, bf16[8,3968]{1,0:T(8,128)(2,1)} %copy-done.7, bf16[8,3968]{1,0:T(8,128)(2,1)} %copy-done.8, ...), custom_call_target="tpu_custom_call" | custom-call | tf_op jit(solution)/shard_map/assemble_rows/pallas_call | solution.py:115
  22.0 0.0 collective-permute-start.8
  22.0 0.5 collective-permute-start.7
  22.5 1.4 %collective-permute-done.8.xb_ref.oth_ref = bf16[64,3072]{1,0:T(8,128)(2,1)S(1)} collective-permute-done((bf16[64,3072]{1,0:T(8,128)(2,1)}, bf16[64,3072]{1,0:T(8,128)(2,1)S(1)}, u32[]{:S(2)}, u32[]{:S(2)}) %collective-permute-start.8) | collective-permute-done | bytes 393248 | tf_op jit(solution)/shard_map/ppermute | solution.py:538
  23.9 0.0 copy-start
  24.0 1.0 %copy-done = bf16[64,3072]{1,0:T(8,128)(2,1)S(1)} copy-done((bf16[64,3072]{1,0:T(8,128)(2,1)S(1)}, bf16[64,3072]{1,0:T(8,128)(2,1)}, u32[]{:S(2)}) %copy-start) | copy-done | bytes 393240
  24.9 0.0 copy-start.2
  24.9 0.0 copy-start.3
  25.0 8.2 %up_units.1.u_ref = f32[1344,64]{1,0:T(8,128)S(1)} custom-call(s32[1]{0:T(128)} %bitcast.2.t_ref, bf16[64,3072]{1,0:T(8,128)(2,1)S(1)} %copy-done, bf16[64,3072]{1,0:T(8,128)(2,1)S(1)} %collective-permute-done.8.xb_ref.oth_ref, bf16[1344,6144]{1,0:T(8,128)(2,1)} %wu_hbm.3), custom_call_target="tpu_custom_call" | custom-call | flops 1056964608 | bytes 16515072 | tf_op jit(solution)/shard_map/up_units/pallas_call | solution.py:220
  33.2 7.1 %gate_units.1.h_ref = f32[1344,64]{1,0:T(8,128)S(1)} custom-call(s32[1]{0:T(128)} %bitcast.2.t_ref, bf16[64,3072]{1,0:T(8,128)(2,1)S(1)} %copy-done, bf16[64,3072]{1,0:T(8,128)(2,1)S(1)} %collective-permute-done.8.xb_ref.oth_ref, bf16[1344,6144]{1,0:T(8,128)(2,1)} %wg_hbm.3), custom_call_target="tpu_custom_call" | custom-call | flops 1056964608 | bytes 16515072 | tf_op jit(solution)/shard_map/gate_units/pallas_call | solution.py:178
  40.3 0.0 collective-permute-done.7.gb_ref.oth_ref
  40.3 0.0 copy-done.2
  40.3 0.0 copy-done.3
  40.3 16.5 %give_half.1 = (bf16[1344,64]{1,0:T(8,128)(2,1)S(1)}, bf16[1344,64]{1,0:T(8,128)(2,1)S(1)}, bf16[1344,64]{1,0:T(8,128)(2,1)S(1)}, bf16[64,1344]{1,0:T(8,128)(2,1...) custom-call(s32[1]{0:T(128)} %bitcast.2.t_ref, ...), custom_call_target="tpu_custom_call" | custom-call | flops 2113929216 | bytes 33030144 | tf_op jit(solution)/shard_map/give_half/pallas_call | solution.py:328
  56.8 0.2 collective-permute-start.9
  57.1 0.0 copy-start.1
  57.1 6.7 %keep_half.1 = f32[64,2048]{1,0:T(8,128)S(1)} custom-call(s32[1]{0:T(128)} %bitcast.2.t_ref, f32[64,128]{1,0:T(8,128)S(1)} %get-tuple-element.43.gate_ref, bf16[64,1344]{1,0:T(8,128)(2,1)S(1)} %get-tuple-element.44.dhr_ref, bf16[64,1344]{1,0:T(8,128)(2,1)S(1)} %get-tuple-element.45.dur_ref, bf16[1344,6144]{1,0:T(8,128)(2,1)} %wg_hbm.3, bf16[1344,6144]{1,0:T(8,128)(2,1)} %wu_hbm.3), custom_call_target="tpu_custom_call" | custom-call | flops 1056964608 | bytes 16515072 | tf_op jit(solution)/shard_map/keep_half/pallas_call | solution.py:362
  63.8 0.0 collective-permute-done.9
  63.8 0.1 add.9
  63.9 1.4 %collective-permute-start.10 = (f32[32,2048]{1,0:T(8,128)S(1)}, f32[32,2048]{1,0:T(8,128)S(1)}, u32[]{:S(2)}, u32[]{:S(2)}) collective-permute-start(f32[32,2048]{1,0:T(8,128)S(1)} %slice.24), channel_id=1, source_target_pairs={{0,4},{2,6},{4,0},{6,2},{8,12},{10,14},{12,8},{14,10},{1,5},{3,7},... | collective-permute-start | bytes 786440 | tf_op jit(solution)/shard_map/ppermute | solution.py:535
  65.3 0.0 copy-done.1
  65.3 6.7 %grad_w_gate.1 = bf16[1344,6144]{1,0:T(8,128)(2,1)} custom-call(s32[1]{0:T(128)} %bitcast.2.t_ref, bf16[1344,64]{1,0:T(8,128)(2,1)S(1)} %get-tuple-element.50.left_ref, bf16[64,3072]{1,0:T(8,128)(2,1)S(1)} %copy-done.1, bf16[64,3072]{1,0:T(8,128)(2,1)S(1)} %collective-permute-done.8.xb_ref.oth_ref), custom_call_target="tpu_custom_call" | custom-call | flops 1056964608 | bytes 16515072 | tf_op jit(solution)/shard_map/grad_w_gate/pallas_call | solution.py:472
  72.1 0.5 collective-permute-done.10
  72.6 1.6 %collective-permute-start.11 = (f32[16,2048]{1,0:T(8,128)S(1)}, f32[16,2048]{1,0:T(8,128)S(1)}, u32[]{:S(2)}, u32[]{:S(2)}) collective-permute-start(f32[16,2048]{1,0:T(8,128)S(1)} %slice.25), channel_id=1, source_target_pairs={{0,2},{2,0},{4,6},{6,4},{8,10},{10,8},{12,14},{14,12},{1,3},{3,1},... | collective-permute-start | bytes 393224 | tf_op jit(solution)/shard_map/ppermute | solution.py:535
  74.2 7.1 %grad_w_up.1 = bf16[1344,6144]{1,0:T(8,128)(2,1)} custom-call(s32[1]{0:T(128)} %bitcast.2.t_ref, bf16[1344,64]{1,0:T(8,128)(2,1)S(1)} %get-tuple-element.53.left_ref, bf16[64,3072]{1,0:T(8,128)(2,1)S(1)} %copy-done.1, bf16[64,3072]{1,0:T(8,128)(2,1)S(1)} %collective-permute-done.8.xb_ref.oth_ref), custom_call_target="tpu_custom_call" | custom-call | flops 1056964608 | bytes 16515072 | tf_op jit(solution)/shard_map/grad_w_up/pallas_call | solution.py:422
  81.3 0.0 collective-permute-done.11
  81.4 0.6 slice.22.mine_ref
  82.0 2.2 %collective-permute-start.12 = (f32[8,2048]{1,0:T(8,128)S(1)}, f32[8,2048]{1,0:T(8,128)S(1)}, u32[]{:S(2)}, u32[]{:S(2)}) collective-permute-start(f32[8,2048]{1,0:T(8,128)S(1)} %slice.26), channel_id=1, source_target_pairs={{0,8},{2,10},{4,12},{6,14},{8,0},{10,2},{12,4},{14,6},{1,9},{3,11}... | collective-permute-start | bytes 196616 | tf_op jit(solution)/shard_map/ppermute | solution.py:532
  84.2 6.7 %grad_w_down.1 = bf16[1344,6144]{1,0:T(8,128)(2,1)} custom-call(s32[1]{0:T(128)} %bitcast.2.t_ref, bf16[1344,64]{1,0:T(8,128)(2,1)S(1)} %get-tuple-element.58.left_ref, bf16[64,3072]{1,0:T(8,128)(2,1)S(1)} %copy-done.2, bf16[64,3072]{1,0:T(8,128)(2,1)S(1)} %collective-permute-done.7.gb_ref.oth_ref), custom_call_target="tpu_custom_call" | custom-call | flops 1056964608 | bytes 16515072 | tf_op jit(solution)/shard_map/grad_w_down/pallas_call | solution.py:422
  90.9 0.0 collective-permute-done.12.got_ref
  91.0 0.0 copy-start.4
  91.0 0.6 copy-done.4
  91.6 2.4 %finish_tokens.1 = (bf16[16,3072]{1,0:T(8,128)(2,1)}, f32[4,16]{1,0:T(4,128)}) custom-call(s32[1]{0:T(128)} %bitcast.e_ref, s32[4,16]{1,0:T(4,128)} %bitcast.6, f32[8,2048]{1,0:T(8,128)} %slice.22.mine_ref, f32[8,2048]{1,0:T(8,128)} %copy-done.4), custom_call_target="tpu_custom_call" | custom-call | tf_op jit(solution)/shard_map/finish_tokens/pallas_call | solution.py:514
  (5 shorter events, 0.1 us)
Async XLA Ops:
  2.7 7.8 %collective-permute-start = (bf16[8,3968]{1,0:T(8,128)(2,1)}, bf16[8,3968]{1,0:T(8,128)(2,1)S(1)}, u32[]{:S(2)}, u32[]{:S(2)}) collective-permute-start(bf16[8,3968]{1,0:T(8,128)(2,1)} %get-tuple-element.36), channel_id=1, source_target_pairs={{0,8},{2,10},{4,12},{6,14},{8,0},{10,2},{12,4},{14,6},{1,9},{3,11}... | collective-permute-start | bytes 190472 | tf_op jit(solution)/shard_map/ppermute | solution.py:532
  6.7 7.5 %collective-permute-start.1 = (bf16[8,3968]{1,0:T(8,128)(2,1)}, bf16[8,3968]{1,0:T(8,128)(2,1)S(1)}, u32[]{:S(2)}, u32[]{:S(2)}) collective-permute-start(bf16[8,3968]{1,0:T(8,128)(2,1)} %get-tuple-element.35.refs_0_), channel_id=1, source_target_pairs={{0,2},{2,0},{4,6},{6,4},{8,10},{10,8},{12,14},{14,12},{1,3},{3,1},... | collective-permute-start | bytes 190472 | tf_op jit(solution)/shard_map/ppermute | solution.py:535
  10.5 8.7 %copy-start.5 = (bf16[8,3968]{1,0:T(8,128)(2,1)}, bf16[8,3968]{1,0:T(8,128)(2,1)S(1)}, u32[]{:S(2)}) copy-start(bf16[8,3968]{1,0:T(8,128)(2,1)S(1)} %collective-permute-done.refs_1_) | copy-start | bytes 190468
  10.5 4.2 %collective-permute-start.2 = (bf16[8,3968]{1,0:T(8,128)(2,1)S(1)}, bf16[8,3968]{1,0:T(8,128)(2,1)S(1)}, u32[]{:S(2)}, u32[]{:S(2)}) collective-permute-start(bf16[8,3968]{1,0:T(8,128)(2,1)S(1)} %collective-permute-done.refs_1_), channel_id=1, source_target_pairs={{0,2},{2,0},{4,6},{6,4},{8,10},{10,8},{12,14},{14,12},{1,3},{3,1},... | collective-permute-start | bytes 190472 | tf_op jit(solution)/shard_map/ppermute | solution.py:535
  12.2 4.8 %collective-permute-start.3 = (bf16[8,3968]{1,0:T(8,128)(2,1)}, bf16[8,3968]{1,0:T(8,128)(2,1)S(1)}, u32[]{:S(2)}, u32[]{:S(2)}) collective-permute-start(bf16[8,3968]{1,0:T(8,128)(2,1)} %get-tuple-element.35.refs_0_), channel_id=1, source_target_pairs={{0,4},{2,6},{4,0},{6,2},{8,12},{10,14},{12,8},{14,10},{1,5},{3,7},... | collective-permute-start | bytes 190472 | tf_op jit(solution)/shard_map/ppermute | solution.py:535
  12.6 5.1 %collective-permute-start.4 = (bf16[8,3968]{1,0:T(8,128)(2,1)S(1)}, bf16[8,3968]{1,0:T(8,128)(2,1)S(1)}, u32[]{:S(2)}, u32[]{:S(2)}) collective-permute-start(bf16[8,3968]{1,0:T(8,128)(2,1)S(1)} %collective-permute-done.refs_1_), channel_id=1, source_target_pairs={{0,4},{2,6},{4,0},{6,2},{8,12},{10,14},{12,8},{14,10},{1,5},{3,7},... | collective-permute-start | bytes 190472 | tf_op jit(solution)/shard_map/ppermute | solution.py:535
  14.2 4.9 %copy-start.6 = (bf16[8,3968]{1,0:T(8,128)(2,1)}, bf16[8,3968]{1,0:T(8,128)(2,1)S(1)}, u32[]{:S(2)}) copy-start(bf16[8,3968]{1,0:T(8,128)(2,1)S(1)} %collective-permute-done.1.refs_2_) | copy-start | bytes 190468
  14.2 4.2 %collective-permute-start.5 = (bf16[8,3968]{1,0:T(8,128)(2,1)S(1)}, bf16[8,3968]{1,0:T(8,128)(2,1)S(1)}, u32[]{:S(2)}, u32[]{:S(2)}) collective-permute-start(bf16[8,3968]{1,0:T(8,128)(2,1)S(1)} %collective-permute-done.1.refs_2_), channel_id=1, source_target_pairs={{0,4},{2,6},{4,0},{6,2},{8,12},{10,14},{12,8},{14,10},{1,5},{3,7},... | collective-permute-start | bytes 190472 | tf_op jit(solution)/shard_map/ppermute | solution.py:535
  14.7 4.4 %copy-start.7 = (bf16[8,3968]{1,0:T(8,128)(2,1)}, bf16[8,3968]{1,0:T(8,128)(2,1)S(1)}, u32[]{:S(2)}) copy-start(bf16[8,3968]{1,0:T(8,128)(2,1)S(1)} %collective-permute-done.2.refs_3_) | copy-start | bytes 190468
  14.7 4.4 %collective-permute-start.6 = (bf16[8,3968]{1,0:T(8,128)(2,1)S(1)}, bf16[8,3968]{1,0:T(8,128)(2,1)S(1)}, u32[]{:S(2)}, u32[]{:S(2)}) collective-permute-start(bf16[8,3968]{1,0:T(8,128)(2,1)S(1)} %collective-permute-done.2.refs_3_), channel_id=1, source_target_pairs={{0,4},{2,6},{4,0},{6,2},{8,12},{10,14},{12,8},{14,10},{1,5},{3,7},... | collective-permute-start | bytes 190472 | tf_op jit(solution)/shard_map/ppermute | solution.py:535
  17.0 2.1 %copy-start.8 = (bf16[8,3968]{1,0:T(8,128)(2,1)}, bf16[8,3968]{1,0:T(8,128)(2,1)S(1)}, u32[]{:S(2)}) copy-start(bf16[8,3968]{1,0:T(8,128)(2,1)S(1)} %collective-permute-done.3.refs_4_) | copy-start | bytes 190468
  17.7 1.5 %copy-start.9 = (bf16[8,3968]{1,0:T(8,128)(2,1)}, bf16[8,3968]{1,0:T(8,128)(2,1)S(1)}, u32[]{:S(2)}) copy-start(bf16[8,3968]{1,0:T(8,128)(2,1)S(1)} %collective-permute-done.4.refs_5_) | copy-start | bytes 190468
  18.5 0.7 copy-start.10
  19.2 0.6 copy-start.11
  22.0 1.9 %collective-permute-start.8 = (bf16[64,3072]{1,0:T(8,128)(2,1)}, bf16[64,3072]{1,0:T(8,128)(2,1)S(1)}, u32[]{:S(2)}, u32[]{:S(2)}) collective-permute-start(bf16[64,3072]{1,0:T(8,128)(2,1)} %get-tuple-element.39.xa_ref.own_ref), channel_id=1, source_target_pairs={{0,1},{1,0},{2,3},{3,2},{4,5},{5,4},{6,7},{7,6},{8,9},{9,8},{10,11... | collective-permute-start | bytes 1179656 | tf_op jit(solution)/shard_map/ppermute | solution.py:538
  22.0 18.3 %collective-permute-start.7 = (bf16[64,3072]{1,0:T(8,128)(2,1)}, bf16[64,3072]{1,0:T(8,128)(2,1)S(1)}, u32[]{:S(2)}, u32[]{:S(2)}) collective-permute-start(bf16[64,3072]{1,0:T(8,128)(2,1)} %get-tuple-element.37.ga_ref.own_ref), channel_id=1, source_target_pairs={{0,1},{1,0},{2,3},{3,2},{4,5},{5,4},{6,7},{7,6},{8,9},{9,8},{10,11... | collective-permute-start | bytes 1179656 | tf_op jit(solution)/shard_map/ppermute | solution.py:538
  23.9 1.0 %copy-start = (bf16[64,3072]{1,0:T(8,128)(2,1)S(1)}, bf16[64,3072]{1,0:T(8,128)(2,1)}, u32[]{:S(2)}) copy-start(bf16[64,3072]{1,0:T(8,128)(2,1)} %get-tuple-element.39.xa_ref.own_ref) | copy-start | bytes 1179652
  24.9 15.3 %copy-start.2 = (bf16[64,3072]{1,0:T(8,128)(2,1)S(1)}, bf16[64,3072]{1,0:T(8,128)(2,1)}, u32[]{:S(2)}) copy-start(bf16[64,3072]{1,0:T(8,128)(2,1)} %get-tuple-element.37.ga_ref.own_ref) | copy-start | bytes 1179652
  24.9 15.4 %copy-start.3 = (f32[64,128]{1,0:T(8,128)S(1)}, f32[64,128]{1,0:T(8,128)}, u32[]{:S(2)}) copy-start(f32[64,128]{1,0:T(8,128)} %get-tuple-element.38.factor_ref) | copy-start | bytes 98308
  56.8 6.9 %collective-permute-start.9 = (f32[64,2048]{1,0:T(8,128)S(1)}, f32[64,2048]{1,0:T(8,128)S(1)}, u32[]{:S(2)}, u32[]{:S(2)}) collective-permute-start(f32[64,2048]{1,0:T(8,128)S(1)} %get-tuple-element.46), channel_id=1, source_target_pairs={{0,1},{1,0},{2,3},{3,2},{4,5},{5,4},{6,7},{7,6},{8,9},{9,8},{10,11... | collective-permute-start | bytes 1572872 | tf_op jit(solution)/shard_map/ppermute | solution.py:538
  57.1 8.3 %copy-start.1 = (bf16[64,3072]{1,0:T(8,128)(2,1)S(1)}, bf16[64,3072]{1,0:T(8,128)(2,1)}, u32[]{:S(2)}) copy-start(bf16[64,3072]{1,0:T(8,128)(2,1)} %get-tuple-element.39.xa_ref.own_ref) | copy-start | bytes 1179652
  63.9 8.6 %collective-permute-start.10 = (f32[32,2048]{1,0:T(8,128)S(1)}, f32[32,2048]{1,0:T(8,128)S(1)}, u32[]{:S(2)}, u32[]{:S(2)}) collective-permute-start(f32[32,2048]{1,0:T(8,128)S(1)} %slice.24), channel_id=1, source_target_pairs={{0,4},{2,6},{4,0},{6,2},{8,12},{10,14},{12,8},{14,10},{1,5},{3,7},... | collective-permute-start | bytes 786440 | tf_op jit(solution)/shard_map/ppermute | solution.py:535
  72.6 8.7 %collective-permute-start.11 = (f32[16,2048]{1,0:T(8,128)S(1)}, f32[16,2048]{1,0:T(8,128)S(1)}, u32[]{:S(2)}, u32[]{:S(2)}) collective-permute-start(f32[16,2048]{1,0:T(8,128)S(1)} %slice.25), channel_id=1, source_target_pairs={{0,2},{2,0},{4,6},{6,4},{8,10},{10,8},{12,14},{14,12},{1,3},{3,1},... | collective-permute-start | bytes 393224 | tf_op jit(solution)/shard_map/ppermute | solution.py:535
  82.0 8.9 %collective-permute-start.12 = (f32[8,2048]{1,0:T(8,128)S(1)}, f32[8,2048]{1,0:T(8,128)S(1)}, u32[]{:S(2)}, u32[]{:S(2)}) collective-permute-start(f32[8,2048]{1,0:T(8,128)S(1)} %slice.26), channel_id=1, source_target_pairs={{0,8},{2,10},{4,12},{6,14},{8,0},{10,2},{12,4},{14,6},{1,9},{3,11}... | collective-permute-start | bytes 196616 | tf_op jit(solution)/shard_map/ppermute | solution.py:532
  91.0 0.6 copy-start.4

commit v5 on v3

--- a/solution.py
+++ b/solution.py
@@ -118,6 +118,7 @@
         in_specs=[VMEM] * count,
         out_specs=[VMEM] * 3,
         scratch_shapes=[pltpu.VMEM((rows, width), F32)],
+        compiler_params=pltpu.CompilerParams(vmem_limit_bytes=6 * MIB),
         name="assemble_rows",
     )(*pieces)
 
@@ -218,21 +219,32 @@
         lax.fori_loop(0, chunks, down_step, 0)
 
     weight = factor_ref[...].T[:1, :]
-    h = h_ref[...]
-    u = u_ref[...]
-    da = da_ref[...]
-    sigma = 1.0 / (1.0 + jnp.exp(-h))
-    silu = h * sigma
-    act = silu * u
-    scaled = weight * da
-    wt_ref[...] = (weight * act).astype(BF16)
-    dh = scaled * u * sigma * (1.0 + h * (1.0 - sigma))
-    du = scaled * silu
-    dh_ref[...] = dh.astype(BF16)
-    du_ref[...] = du.astype(BF16)
-    dhr_ref[...] = dh.T.astype(BF16)
-    dur_ref[...] = du.T.astype(BF16)
-    total = jnp.sum(act * da, axis=0, keepdims=True)
+
+    def units(start, size, total):
+        at = pl.ds(start, size)
+        h = h_ref[at, :]
+        u = u_ref[at, :]
+        da = da_ref[at, :]
+        sigma = 1.0 / (1.0 + jnp.exp(-h))
+        silu = h * sigma
+        act = silu * u
+        scaled = weight * da
+        wt_ref[at, :] = (weight * act).astype(BF16)
+        dh = scaled * u * sigma * (1.0 + h * (1.0 - sigma))
+        du = scaled * silu
+        dh_ref[at, :] = dh.astype(BF16)
+        du_ref[at, :] = du.astype(BF16)
+        dhr_ref[:, at] = dh.T.astype(BF16)
+        dur_ref[:, at] = du.T.astype(BF16)
+        return total + jnp.sum(act * da, axis=0, keepdims=True)
+
+    hidden = h_ref.shape[0]
+    whole = hidden // LANES
+    total = lax.fori_loop(
+        0, whole, lambda i, v: units(pl.multiple_of(i * LANES, LANES), LANES, v), jnp.zeros((1, rows), F32)
+    )
+    if hidden % LANES:
+        total = units(whole * LANES, hidden % LANES, total)
     gates = jnp.broadcast_to(total, (LANES, rows)).T
     for at, out in ((1 - t, give_ref), (t, keep_ref)):
         base = pl.multiple_of(at * width, width)
@@ -274,60 +286,103 @@
     )(t, xa, xb, ga, gb, factor, w_gate, w_up, w_down)
 
 
-def weights_body(chunk, t_ref, left_ref, own_ref, oth_ref, out_ref, ring, sent):
+def weights_body(count, chunk, t_ref, *refs):
+    lefts, (own_ref, oth_ref), outs = refs[:count], refs[count : count + 2], refs[count + 2 : 2 * count + 2]
+    ring, sent = refs[2 * count + 2 :]
     width = own_ref.shape[1]
     chunks = width // chunk
-    depth = ring.shape[0]
-    hidden = left_ref.shape[0]
+    depth = ring.shape[1]
+    hidden = lefts[0].shape[0]
     tile = tile_of(hidden, 448)
     t = t_ref[0]
 
-    def store(i):
+    def store(i, n):
         cols = pl.ds(place_of(i, chunks, chunk, t), chunk)
         slot = lax.rem(i, depth)
-        return pltpu.make_async_copy(ring.at[slot], out_ref.at[:, cols], sent.at[slot])
+        return pltpu.make_async_copy(ring.at[n, slot], outs[n].at[:, cols], sent.at[n, slot])
 
     for side, x_ref in enumerate((own_ref, oth_ref)):
 
         def step(c, carry):
             i = side * chunks + c
             slot = lax.rem(i, depth)
-
-            @pl.when(i >= depth)
-            def _():
-                store(i - depth).wait()
-
             x = x_ref[:, pl.ds(pl.multiple_of(c * chunk, chunk), chunk)]
-            for at in range(0, hidden, tile):
-                ring[slot, at : at + tile, :] = jnp.dot(
-                    left_ref[at : at + tile, :], x, preferred_element_type=F32
-                ).astype(BF16)
-            store(i).start()
+            for n in range(count):
+
+                @pl.when(i >= depth)
+                def _():
+                    store(i - depth, n).wait()
+
+                for at in range(0, hidden, tile):
+                    ring[n, slot, at : at + tile, :] = jnp.dot(
+                        lefts[n][at : at + tile, :], x, preferred_element_type=F32
+                    ).astype(BF16)
+                store(i, n).start()
             return carry
 
         lax.fori_loop(0, chunks, step, 0)
     for i in range(max(0, 2 * chunks - depth), 2 * chunks):
-        store(i).wait()
-
-
-def weight_grad(t, left, own, oth, name):
-    hidden, rows = left.shape
+        for n in range(count):
+            store(i, n).wait()
+
+
+def weight_grads(t, lefts, own, oth, name):
+    count = len(lefts)
+    hidden, rows = lefts[0].shape
     width = own.shape[1]
     depth = 2 * width
     chunk = chunk_of(width, 512)
     ring = min(4, depth // chunk)
     return pl.pallas_call(
-        functools.partial(weights_body, chunk),
-        out_shape=jax.ShapeDtypeStruct((hidden, depth), BF16),
-        in_specs=[SMEM] + [VMEM] * 3,
-        out_specs=HBM,
-        scratch_shapes=[pltpu.VMEM((ring, hidden, chunk), BF16), pltpu.SemaphoreType.DMA((ring,))],
+        functools.partial(weights_body, count, chunk),
+        out_shape=[jax.ShapeDtypeStruct((hidden, depth), BF16)] * count,
+        in_specs=[SMEM] + [VMEM] * (count + 2),
+        out_specs=[HBM] * count,
+        scratch_shapes=[pltpu.VMEM((count, ring, hidden, chunk), BF16), pltpu.SemaphoreType.DMA((count, ring))],
         compiler_params=pltpu.CompilerParams(vmem_limit_bytes=24 * MIB),
         cost_estimate=pl.CostEstimate(
-            flops=2 * rows * hidden * depth, bytes_accessed=2 * hidden * depth, transcendentals=0
+            flops=2 * count * rows * hidden * depth, bytes_accessed=2 * count * hidden * depth, transcendentals=0
         ),
         name=name,
-    )(t, left, own, oth)
+    )(t, *lefts, own, oth)
+
+
+def fold_body(copies, keep_ref, got_ref, *outs):
+    for d, out in enumerate(outs):
+        rows = slice(d * 2 * SUBS, (d + 1) * 2 * SUBS)
+        out[...] = keep_ref[rows, :] + got_ref[rows, :]
+
+
+def fold(copies, keep, got):
+    return pl.pallas_call(
+        functools.partial(fold_body, copies),
+        out_shape=[jax.ShapeDtypeStruct((2 * SUBS, keep.shape[1]), F32)] * copies,
+        in_specs=[VMEM] * 2,
+        out_specs=[VMEM] * copies,
+        compiler_params=pltpu.CompilerParams(vmem_limit_bytes=6 * MIB),
+        name="fold_cores",
+    )(keep, got)
+
+
+def merge_body(*refs):
+    blocks, (mine_ref, other_ref) = refs[:-2], refs[-2:]
+    for at, out in ((0, mine_ref), (SUBS, other_ref)):
+        total = blocks[0][at : at + SUBS, :]
+        for block in blocks[1:]:
+            total += block[at : at + SUBS, :]
+        out[...] = total
+
+
+def merge(blocks):
+    part = jax.ShapeDtypeStruct((SUBS, blocks[0].shape[1]), F32)
+    return pl.pallas_call(
+        merge_body,
+        out_shape=(part, part),
+        in_specs=[VMEM] * len(blocks),
+        out_specs=[VMEM] * 2,
+        compiler_params=pltpu.CompilerParams(vmem_limit_bytes=6 * MIB),
+        name="merge_chips",
+    )(*blocks)
 
 
 def finish_body(e_ref, ids_ref, mine_ref, got_ref, tok_ref, gate_ref):
@@ -363,6 +418,7 @@
         out_shape=(jax.ShapeDtypeStruct((toks, width), BF16), jax.ShapeDtypeStruct((top, toks), F32)),
         in_specs=[SMEM] + [VMEM] * 3,
         out_specs=[VMEM] * 2,
+        compiler_params=pltpu.CompilerParams(vmem_limit_bytes=6 * MIB),
         name="finish_tokens",
     )(e, ids_t, mine, got)
 
@@ -384,38 +440,28 @@
     def other_core(v):
         return lax.ppermute(v, "tensor", [(0, 1), (1, 0)])
 
+    w_gate, w_up, w_down = (pltpu.with_memory_space_constraint(w, pltpu.HBM) for w in (w_gate, w_up, w_down))
     ids_t = expert_ids.T
     own, oth = pick(e, ids_t, gate_probs.T, tokens, grad_out)
-    first, second = [own], [partner(oth)]
-    d = 1
-    while d < copies:
-        first += [across(piece, d) for piece in first]
-        second += [across(piece, d) for piece in second]
-        d *= 2
-    xa, ga, factor = assemble([piece for pair in zip(first, second) for piece in pair], width)
+    far_first = sorted(range(1, copies), key=lambda d: (-d.bit_count(), d))
+    got = partner(oth)
+    first = {0: own} | {d: across(own, d) for d in far_first}
+    second = {0: got} | {d: across(got, d) for d in far_first}
+    xa, ga, factor = assemble([piece for d in range(copies) for piece in (first[d], second[d])], width)
     xb = other_core(xa)
     gb = other_core(ga)
     wt, dh, du, give, keep = expert_units(t, xa, xb, ga, gb, factor, w_gate, w_up, w_down)
-    total = keep + other_core(give)
-    grads = []
-    jobs = [(dh, xa, xb, "grad_w_gate"), (du, xa, xb, "grad_w_up"), (wt, ga, gb, "grad_w_down")]
-    d = copies // 2
-    while d:
-        rows = d * 2 * SUBS
-        coming = across(total[rows:], d)
-        if len(jobs) > 1:
-            left, a, b, name = jobs.pop(0)
-            left, total = lax.optimization_barrier((left, total))
-            grads.append(weight_grad(t, left, a, b, name))
-            grads[-1], coming = lax.optimization_barrier((grads[-1], coming))
-        total = total[:rows] + coming
-        d //= 2
-    theirs = partner(total[SUBS:])
-    for left, a, b, name in jobs:
-        left, total = lax.optimization_barrier((left, total))
-        grads.append(weight_grad(t, left, a, b, name))
+    blocks = list(fold(copies, keep, other_core(give)))
+    arrived = {d: across(blocks[d], d) for d in far_first}
+    dh, mine = lax.optimization_barrier((dh, blocks[0]))
+    grads = weight_grads(t, (dh, du), xa, xb, "grads_gate_up")
+    grads, arrived = lax.optimization_barrier((grads, arrived))
+    mine, others = merge([mine] + [arrived[d] for d in range(1, copies)])
+    theirs = partner(others)
+    wt, mine = lax.optimization_barrier((wt, mine))
+    grads = [*grads, *weight_grads(t, (wt,), ga, gb, "grad_down")]
     grads, theirs = lax.optimization_barrier((grads, theirs))
-    token_grad, gate_t = finish(e, ids_t, total[:SUBS], theirs, width)
+    token_grad, gate_t = finish(e, ids_t, mine, theirs, width)
     return token_grad, gate_t.T, *grads
 
 

time: 94.6 us -> 85.8 us (0.907)
  local copies, waits for them, and re-layouts: 4.65 us -> 0.84 us
  Pallas kernels: 62.3 us -> 59 us
  waiting for transfers between devices: 9.01 us -> 6.66 us
  starting transfers between devices: 17.3 us -> 18.4 us
    unnamed x22 -> x4, local copies, waits for them, and re-layouts: 3.99 us -> 0.84 us
    ppermute x2, waiting for transfers between devices: 2.3 us -> 0.01 us  [partner(): lax.ppermute(v, 'expert', [(i, (i + copies) % n_expert) for i in range(n_...]
    pallas_call x1, Pallas kernels: 2.2 us -> 0.26 us  [assemble(): pl.pallas_call(functools.partial(assemble_body, count), out_shape=(held,...]
    pallas_call x3 -> x4, Pallas kernels: 21.4 us -> 20.2 us  [the longest x2 20.1 us: weight_grads(): pl.pallas_call(functools.partial(weights_body, count, chunk), out_shape=[...]
    ppermute x8 -> x9, starting transfers between devices: 10 us -> 11.2 us  [across(): return lax.ppermute(v, 'expert', [(i, i ^ d) for i in range(n_expert)])]
    ppermute x8 -> x9, waiting for transfers between devices: 2.95 us -> 3.11 us  [across(): return lax.ppermute(v, 'expert', [(i, i ^ d) for i in range(n_expert)])]
  transfers between devices with their start and end apart: 13 -> 14, of which waited for: 9 -> 7; matrix products, arithmetic and copies ran while one was open for 0% -> 0% of each run, Pallas kernels for 23% -> 24%
where the time goes in v5:
time: 85.8 us; the launch traced here: 85.6 us
  Pallas kernels  59 us (69%)
  starting transfers between devices  18.4 us (21%)
  waiting for transfers between devices  6.66 us (8%)
    pallas_call x1, Pallas kernels, expert_units(): pl.pallas_call(functools.partial(experts_body, chunk), out_shape=(unit, u...  34.9 us
    pallas_call x2, Pallas kernels, weight_grads(): pl.pallas_call(functools.partial(weights_body, count, chunk), out_shape=[...  20.1 us
    ppermute x9, starting transfers between devices, across(): return lax.ppermute(v, 'expert', [(i, i ^ d) for i in range(n_expert)])  11.2 us
    ppermute x2, starting transfers between devices, partner(): lax.ppermute(v, 'expert', [(i, (i + copies) % n_expert) for i in range(n_...  6.48 us
    ppermute x3, waiting for transfers between devices, other_core(): return lax.ppermute(v, 'tensor', [(0, 1), (1, 0)])  3.54 us
    ppermute x9, waiting for transfers between devices, across(): return lax.ppermute(v, 'expert', [(i, i ^ d) for i in range(n_expert)])  3.11 us
    pallas_call x1, Pallas kernels, pick(): pl.pallas_call(pick_body, out_shape=(piece, piece), in_specs=[SMEM] + [VM...  2.02 us
  transfers between devices with their start and end apart: 14, of which 7 were waited for; matrix products, arithmetic and copies ran while one was open for 0% of the time, Pallas kernels for 24%

profile of v5, /device:TPU:0, one launch (start us, length us, event | category | flops | bytes accessed | tf_op | source)
XLA Modules:
  0.0 85.6 jit_solution(17749050321756015266)
XLA Ops:
  0.6 2.0 %pick_rows.1 = (bf16[8,3968]{1,0:T(8,128)(2,1)}, bf16[8,3968]{1,0:T(8,128)(2,1)}) custom-call(s32[1]{0:T(128)} %bitcast.e_ref, s32[4,16]{1,0:T(4,128)} %bitcast.5, bf16[4,16]{1,0:T(4,128)(2,1)} %bitcast.7, bf16[16,3072]{1,0:T(8,128)(2,1)} %tok_ref.1, bf16[16,3072]{1,0:T(8,128)(2,1)} %grad_ref.1), custom_call_target="tpu_custom_call" | custom-call | tf_op jit(solution)/shard_map/pick_rows/pallas_call | solution.py:82
  2.7 4.0 %collective-permute-start = (bf16[8,3968]{1,0:T(8,128)(2,1)}, bf16[8,3968]{1,0:T(8,128)(2,1)S(1)}, u32[]{:S(2)}, u32[]{:S(2)}) collective-permute-start(bf16[8,3968]{1,0:T(8,128)(2,1)} %get-tuple-element.39), channel_id=1, source_target_pairs={{0,8},{2,10},{4,12},{6,14},{8,0},{10,2},{12,4},{14,6},{1,9},{3,11}... | collective-permute-start | bytes 190472 | tf_op jit(solution)/shard_map/ppermute | solution.py:435
  6.7 2.5 %collective-permute-start.5 = (bf16[8,3968]{1,0:T(8,128)(2,1)}, bf16[8,3968]{1,0:T(8,128)(2,1)S(1)}, u32[]{:S(2)}, u32[]{:S(2)}) collective-permute-start(bf16[8,3968]{1,0:T(8,128)(2,1)} %get-tuple-element.38.refs_0_), channel_id=1, source_target_pairs={{0,6},{2,4},{4,2},{6,0},{8,14},{10,12},{12,10},{14,8},{1,7},{3,5},... | collective-permute-start | bytes 190472 | tf_op jit(solution)/shard_map/ppermute | solution.py:438
  9.2 0.5 collective-permute-start.3
  9.7 0.5 collective-permute-start.1
  10.2 0.0 collective-permute-done.refs_1_
  10.2 2.5 %collective-permute-start.6 = (bf16[8,3968]{1,0:T(8,128)(2,1)S(1)}, bf16[8,3968]{1,0:T(8,128)(2,1)S(1)}, u32[]{:S(2)}, u32[]{:S(2)}) collective-permute-start(bf16[8,3968]{1,0:T(8,128)(2,1)S(1)} %collective-permute-done.refs_1_), channel_id=1, source_target_pairs={{0,6},{2,4},{4,2},{6,0},{8,14},{10,12},{12,10},{14,8},{1,7},{3,5},... | collective-permute-start | bytes 190472 | tf_op jit(solution)/shard_map/ppermute | solution.py:438
  12.7 0.5 collective-permute-start.4
  13.2 0.0 collective-permute-done.5.refs_6_
  13.2 1.1 %collective-permute-start.2 = (bf16[8,3968]{1,0:T(8,128)(2,1)S(1)}, bf16[8,3968]{1,0:T(8,128)(2,1)S(1)}, u32[]{:S(2)}, u32[]{:S(2)}) collective-permute-start(bf16[8,3968]{1,0:T(8,128)(2,1)S(1)} %collective-permute-done.refs_1_), channel_id=1, source_target_pairs={{0,2},{2,0},{4,6},{6,4},{8,10},{10,8},{12,14},{14,12},{1,3},{3,1},... | collective-permute-start | bytes 190472 | tf_op jit(solution)/shard_map/ppermute | solution.py:438
  14.3 0.0 collective-permute-done.3.refs_4_
  14.3 0.3 collective-permute-done.1.refs_2_
  14.6 0.8 collective-permute-done.6.refs_7_
  15.4 1.5 %collective-permute-done.4.refs_5_ = bf16[8,3968]{1,0:T(8,128)(2,1)S(1)} collective-permute-done((bf16[8,3968]{1,0:T(8,128)(2,1)S(1)}, bf16[8,3968]{1,0:T(8,128)(2,1)S(1)}, u32[]{:S(2)}, u32[]{:S(2)}) %collective-permute-start.4) | collective-permute-done | bytes 63520 | tf_op jit(solution)/shard_map/ppermute | solution.py:438
  16.9 0.5 collective-permute-done.2.refs_3_
  17.4 0.0 copy-start
  17.4 0.8 copy-done
  18.3 0.3 assemble_rows.1
  18.5 0.1 collective-permute-start.7
  18.6 0.5 collective-permute-start.8
  19.1 1.2 %collective-permute-done.7.xb_ref.refs_3_ = bf16[64,3072]{1,0:T(8,128)(2,1)S(1)} collective-permute-done((bf16[64,3072]{1,0:T(8,128)(2,1)S(1)}, bf16[64,3072]{1,0:T(8,128)(2,1)S(1)}, u32[]{:S(2)}, u32[]{:S(2)}) %collective-permute-start.7) | collective-permute-done | bytes 393248 | tf_op jit(solution)/shard_map/ppermute | solution.py:441
  20.3 0.6 collective-permute-done.8.gb_ref.refs_2_
  20.9 34.9 %expert_units.1 = (bf16[1344,64]{1,0:T(8,128)(2,1)S(1)}, bf16[1344,64]{1,0:T(8,128)(2,1)S(1)}, bf16[1344,64]{1,0:T(8,128)(2,1)S(1)}, f32[64,2048]{1,0:T(8,128)S(1)}, f32[64,2048]{1,0:T(8,128)S(1)}) custom-call(s32[1]{0:T(128)} %bitcast.2.t_ref, bf16[64,3072]{1,0:T(8,128)(2,1)S(1)} %get-tuple-element.40.xa_ref.refs_2_, ...), custom_call_target="tpu_custom_call" | custom-call | flops 5284823040 | bytes 49545216 | tf_op jit(solution)/shard_map/expert_units/pallas_call | solution.py:263
  55.8 0.0 copy-start.1
  55.8 0.2 collective-permute-start.9
  56.0 1.8 %collective-permute-done.9.got_ref = f32[64,2048]{1,0:T(8,128)S(1)} collective-permute-done((f32[64,2048]{1,0:T(8,128)S(1)}, f32[64,2048]{1,0:T(8,128)S(1)}, u32[]{:S(2)}, u32[]{:S(2)}) %collective-permute-start.9) | collective-permute-done | bytes 524320 | tf_op jit(solution)/shard_map/ppermute | solution.py:441
  57.8 0.1 fold_cores.1
  57.9 1.2 %collective-permute-start.10 = (f32[16,2048]{1,0:T(8,128)S(1)}, f32[16,2048]{1,0:T(8,128)S(1)}, u32[]{:S(2)}, u32[]{:S(2)}) collective-permute-start(f32[16,2048]{1,0:T(8,128)S(1)} %get-tuple-element.53), channel_id=1, source_target_pairs={{0,2},{2,0},{4,6},{6,4},{8,10},{10,8},{12,14},{14,12},{1,3},{3,1},... | collective-permute-start | bytes 393224 | tf_op jit(solution)/shard_map/ppermute | solution.py:438
  59.1 0.9 %collective-permute-start.11 = (f32[16,2048]{1,0:T(8,128)S(1)}, f32[16,2048]{1,0:T(8,128)S(1)}, u32[]{:S(2)}, u32[]{:S(2)}) collective-permute-start(f32[16,2048]{1,0:T(8,128)S(1)} %get-tuple-element.54), channel_id=1, source_target_pairs={{0,4},{2,6},{4,0},{6,2},{8,12},{10,14},{12,8},{14,10},{1,5},{3,7},... | collective-permute-start | bytes 393224 | tf_op jit(solution)/shard_map/ppermute | solution.py:438
  60.0 1.4 %collective-permute-start.12 = (f32[16,2048]{1,0:T(8,128)S(1)}, f32[16,2048]{1,0:T(8,128)S(1)}, u32[]{:S(2)}, u32[]{:S(2)}) collective-permute-start(f32[16,2048]{1,0:T(8,128)S(1)} %get-tuple-element.55), channel_id=1, source_target_pairs={{0,6},{2,4},{4,2},{6,0},{8,14},{10,12},{12,10},{14,8},{1,7},{3,5},... | collective-permute-start | bytes 393224 | tf_op jit(solution)/shard_map/ppermute | solution.py:438
  61.4 13.0 %grads_gate_up.1 = (bf16[1344,6144]{1,0:T(8,128)(2,1)}, bf16[1344,6144]{1,0:T(8,128)(2,1)}) custom-call(s32[1]{0:T(128)} %bitcast.2.t_ref, bf16[1344,64]{1,0:T(8,128)(2,1)S(1)} %get-tuple-element.49.refs_0_, bf16[1344,64]{1,0:T(8,128)(2,1)S(1)} %get-tuple-element.50.refs_1_, bf16[64,3072]{1,0:T(8,128)(2,1)S(1)} %get-tuple-element.40.xa_ref.refs_2_, ...), custom_call_target="tpu_custom_call" | custom-call | flops 2113929216 | bytes 33030144 | tf_op jit(solution)/shard_map/grads_gate_up/pallas_call | solution.py:336
  74.4 0.0 collective-permute-done.10.refs_1_
  74.5 0.0 collective-permute-done.11.refs_2_
  74.5 0.0 collective-permute-done.12.refs_3_
  74.5 2.4 %collective-permute-start.13 = (f32[8,2048]{1,0:T(8,128)S(1)}, f32[8,2048]{1,0:T(8,128)S(1)}, u32[]{:S(2)}, u32[]{:S(2)}) collective-permute-start(f32[8,2048]{1,0:T(8,128)S(1)} %get-tuple-element.64), channel_id=1, source_target_pairs={{0,8},{2,10},{4,12},{6,14},{8,0},{10,2},{12,4},{14,6},{1,9},{3,11}... | collective-permute-start | bytes 196616 | tf_op jit(solution)/shard_map/ppermute | solution.py:435
  77.0 7.1 %grad_down.1 = bf16[1344,6144]{1,0:T(8,128)(2,1)} custom-call(s32[1]{0:T(128)} %bitcast.2.t_ref, bf16[1344,64]{1,0:T(8,128)(2,1)S(1)} %get-tuple-element.63.refs_0_, bf16[64,3072]{1,0:T(8,128)(2,1)S(1)} %get-tuple-element.41.ga_ref.refs_1_, bf16[64,3072]{1,0:T(8,128)(2,1)S(1)} %collective-permute-done.8.gb_ref.refs_2_), custom_call_target="tpu_custom_call" | custom-call | flops 1056964608 | bytes 16515072 | tf_op jit(solution)/shard_map/grad_down/pallas_call | solution.py:336
  84.1 0.0 collective-permute-done.13.got_ref
  84.1 0.0 copy-done.1
  84.1 1.5 %finish_tokens.1 = (bf16[16,3072]{1,0:T(8,128)(2,1)}, f32[4,16]{1,0:T(4,128)}) custom-call(s32[1]{0:T(128)} %bitcast.e_ref, s32[4,16]{1,0:T(4,128)S(1)} %bitcast.6, f32[8,2048]{1,0:T(8,128)S(1)} %get-tuple-element.60.mine_ref, f32[8,2048]{1,0:T(8,128)S(1)} %collective-permute-done.13.got_ref), custom_call_target="tpu_custom_call" | custom-call | tf_op jit(solution)/shard_map/finish_tokens/pallas_call | solution.py:416
  (1 shorter events, 0.0 us)
Async XLA Ops:
  2.7 7.5 %collective-permute-start = (bf16[8,3968]{1,0:T(8,128)(2,1)}, bf16[8,3968]{1,0:T(8,128)(2,1)S(1)}, u32[]{:S(2)}, u32[]{:S(2)}) collective-permute-start(bf16[8,3968]{1,0:T(8,128)(2,1)} %get-tuple-element.39), channel_id=1, source_target_pairs={{0,8},{2,10},{4,12},{6,14},{8,0},{10,2},{12,4},{14,6},{1,9},{3,11}... | collective-permute-start | bytes 190472 | tf_op jit(solution)/shard_map/ppermute | solution.py:435
  6.7 6.5 %collective-permute-start.5 = (bf16[8,3968]{1,0:T(8,128)(2,1)}, bf16[8,3968]{1,0:T(8,128)(2,1)S(1)}, u32[]{:S(2)}, u32[]{:S(2)}) collective-permute-start(bf16[8,3968]{1,0:T(8,128)(2,1)} %get-tuple-element.38.refs_0_), channel_id=1, source_target_pairs={{0,6},{2,4},{4,2},{6,0},{8,14},{10,12},{12,10},{14,8},{1,7},{3,5},... | collective-permute-start | bytes 190472 | tf_op jit(solution)/shard_map/ppermute | solution.py:438
  9.2 5.1 %collective-permute-start.3 = (bf16[8,3968]{1,0:T(8,128)(2,1)}, bf16[8,3968]{1,0:T(8,128)(2,1)S(1)}, u32[]{:S(2)}, u32[]{:S(2)}) collective-permute-start(bf16[8,3968]{1,0:T(8,128)(2,1)} %get-tuple-element.38.refs_0_), channel_id=1, source_target_pairs={{0,4},{2,6},{4,0},{6,2},{8,12},{10,14},{12,8},{14,10},{1,5},{3,7},... | collective-permute-start | bytes 190472 | tf_op jit(solution)/shard_map/ppermute | solution.py:438
  9.7 5.0 %collective-permute-start.1 = (bf16[8,3968]{1,0:T(8,128)(2,1)}, bf16[8,3968]{1,0:T(8,128)(2,1)S(1)}, u32[]{:S(2)}, u32[]{:S(2)}) collective-permute-start(bf16[8,3968]{1,0:T(8,128)(2,1)} %get-tuple-element.38.refs_0_), channel_id=1, source_target_pairs={{0,2},{2,0},{4,6},{6,4},{8,10},{10,8},{12,14},{14,12},{1,3},{3,1},... | collective-permute-start | bytes 190472 | tf_op jit(solution)/shard_map/ppermute | solution.py:438
  10.2 5.3 %collective-permute-start.6 = (bf16[8,3968]{1,0:T(8,128)(2,1)S(1)}, bf16[8,3968]{1,0:T(8,128)(2,1)S(1)}, u32[]{:S(2)}, u32[]{:S(2)}) collective-permute-start(bf16[8,3968]{1,0:T(8,128)(2,1)S(1)} %collective-permute-done.refs_1_), channel_id=1, source_target_pairs={{0,6},{2,4},{4,2},{6,0},{8,14},{10,12},{12,10},{14,8},{1,7},{3,5},... | collective-permute-start | bytes 190472 | tf_op jit(solution)/shard_map/ppermute | solution.py:438
  12.7 4.2 %collective-permute-start.4 = (bf16[8,3968]{1,0:T(8,128)(2,1)S(1)}, bf16[8,3968]{1,0:T(8,128)(2,1)S(1)}, u32[]{:S(2)}, u32[]{:S(2)}) collective-permute-start(bf16[8,3968]{1,0:T(8,128)(2,1)S(1)} %collective-permute-done.refs_1_), channel_id=1, source_target_pairs={{0,4},{2,6},{4,0},{6,2},{8,12},{10,14},{12,8},{14,10},{1,5},{3,7},... | collective-permute-start | bytes 190472 | tf_op jit(solution)/shard_map/ppermute | solution.py:438
  13.2 4.2 %collective-permute-start.2 = (bf16[8,3968]{1,0:T(8,128)(2,1)S(1)}, bf16[8,3968]{1,0:T(8,128)(2,1)S(1)}, u32[]{:S(2)}, u32[]{:S(2)}) collective-permute-start(bf16[8,3968]{1,0:T(8,128)(2,1)S(1)} %collective-permute-done.refs_1_), channel_id=1, source_target_pairs={{0,2},{2,0},{4,6},{6,4},{8,10},{10,8},{12,14},{14,12},{1,3},{3,1},... | collective-permute-start | bytes 190472 | tf_op jit(solution)/shard_map/ppermute | solution.py:438
  17.4 0.8 copy-start
  18.5 1.8 %collective-permute-start.7 = (bf16[64,3072]{1,0:T(8,128)(2,1)S(1)}, bf16[64,3072]{1,0:T(8,128)(2,1)S(1)}, u32[]{:S(2)}, u32[]{:S(2)}) collective-permute-start(bf16[64,3072]{1,0:T(8,128)(2,1)S(1)} %get-tuple-element.40.xa_ref.refs_2_), channel_id=1, source_target_pairs={{0,1},{1,0},{2,3},{3,2},{4,5},{5,4},{6,7},{7,6},{8,9},{9,8},{10,11... | collective-permute-start | bytes 1179656 | tf_op jit(solution)/shard_map/ppermute | solution.py:441
  18.6 2.3 %collective-permute-start.8 = (bf16[64,3072]{1,0:T(8,128)(2,1)S(1)}, bf16[64,3072]{1,0:T(8,128)(2,1)S(1)}, u32[]{:S(2)}, u32[]{:S(2)}) collective-permute-start(bf16[64,3072]{1,0:T(8,128)(2,1)S(1)} %get-tuple-element.41.ga_ref.refs_1_), channel_id=1, source_target_pairs={{0,1},{1,0},{2,3},{3,2},{4,5},{5,4},{6,7},{7,6},{8,9},{9,8},{10,11... | collective-permute-start | bytes 1179656 | tf_op jit(solution)/shard_map/ppermute | solution.py:441
  55.8 28.3 %copy-start.1 = (s32[16,4]{0,1:T(4,128)S(1)}, s32[16,4]{0,1:T(4,128)}, u32[]{:S(2)}) copy-start(s32[16,4]{0,1:T(4,128)} %param.9) | copy-start | bytes 772
  55.8 2.0 %collective-permute-start.9 = (f32[64,2048]{1,0:T(8,128)S(1)}, f32[64,2048]{1,0:T(8,128)S(1)}, u32[]{:S(2)}, u32[]{:S(2)}) collective-permute-start(f32[64,2048]{1,0:T(8,128)S(1)} %get-tuple-element.46), channel_id=1, source_target_pairs={{0,1},{1,0},{2,3},{3,2},{4,5},{5,4},{6,7},{7,6},{8,9},{9,8},{10,11... | collective-permute-start | bytes 1572872 | tf_op jit(solution)/shard_map/ppermute | solution.py:441
  57.9 16.6 %collective-permute-start.10 = (f32[16,2048]{1,0:T(8,128)S(1)}, f32[16,2048]{1,0:T(8,128)S(1)}, u32[]{:S(2)}, u32[]{:S(2)}) collective-permute-start(f32[16,2048]{1,0:T(8,128)S(1)} %get-tuple-element.53), channel_id=1, source_target_pairs={{0,2},{2,0},{4,6},{6,4},{8,10},{10,8},{12,14},{14,12},{1,3},{3,1},... | collective-permute-start | bytes 393224 | tf_op jit(solution)/shard_map/ppermute | solution.py:438
  59.1 15.4 %collective-permute-start.11 = (f32[16,2048]{1,0:T(8,128)S(1)}, f32[16,2048]{1,0:T(8,128)S(1)}, u32[]{:S(2)}, u32[]{:S(2)}) collective-permute-start(f32[16,2048]{1,0:T(8,128)S(1)} %get-tuple-element.54), channel_id=1, source_target_pairs={{0,4},{2,6},{4,0},{6,2},{8,12},{10,14},{12,8},{14,10},{1,5},{3,7},... | collective-permute-start | bytes 393224 | tf_op jit(solution)/shard_map/ppermute | solution.py:438
  60.0 14.5 %collective-permute-start.12 = (f32[16,2048]{1,0:T(8,128)S(1)}, f32[16,2048]{1,0:T(8,128)S(1)}, u32[]{:S(2)}, u32[]{:S(2)}) collective-permute-start(f32[16,2048]{1,0:T(8,128)S(1)} %get-tuple-element.55), channel_id=1, source_target_pairs={{0,6},{2,4},{4,2},{6,0},{8,14},{10,12},{12,10},{14,8},{1,7},{3,5},... | collective-permute-start | bytes 393224 | tf_op jit(solution)/shard_map/ppermute | solution.py:438
  74.5 9.6 %collective-permute-start.13 = (f32[8,2048]{1,0:T(8,128)S(1)}, f32[8,2048]{1,0:T(8,128)S(1)}, u32[]{:S(2)}, u32[]{:S(2)}) collective-permute-start(f32[8,2048]{1,0:T(8,128)S(1)} %get-tuple-element.64), channel_id=1, source_target_pairs={{0,8},{2,10},{4,12},{6,14},{8,0},{10,2},{12,4},{14,6},{1,9},{3,11}... | collective-permute-start | bytes 196616 | tf_op jit(solution)/shard_map/ppermute | solution.py:435

commit v6 on v5

v6 whole, which is shorter than its diff:
```python
import functools

import jax
import jax.numpy as jnp
from jax import lax
from jax.experimental import pallas as pl
from jax.experimental.pallas import tpu as pltpu
from jax.sharding import PartitionSpec as P

EXPERTS_ON = 2
CAP = 5
LANES = 128
SUBS = 8
WHOLE = 4
F32 = jnp.float32
BF16 = jnp.bfloat16
MIB = 1 << 20
VMEM = pl.BlockSpec(memory_space=pltpu.VMEM)
SMEM = pl.BlockSpec(memory_space=pltpu.SMEM)
HBM = pl.BlockSpec(memory_space=pltpu.HBM)


def iota(shape, dim):
    return lax.broadcasted_iota(jnp.int32, shape, dim)


def chosen_rows(ids, expert, position):
    rows, toks = position.shape
    hits = [ids[k : k + 1, :] == expert for k in range(ids.shape[0])]
    member = functools.reduce(jnp.logical_or, hits).astype(F32)
    before = (iota((toks, toks), 0) < iota((toks, toks), 1)).astype(F32)
    earlier = jnp.dot(member, before, preferred_element_type=F32)
    return jnp.where(earlier == position.astype(F32), member, 0.0), hits


def sub_row(rows, toks):
    return iota((rows, toks), 0) % SUBS


def tile_of(hidden, most):
    sizes = [n for n in range(16, most + 1, 16) if hidden % n == 0]
    return max(sizes) if sizes else hidden


def pick_body(e_ref, ids_any, probs_any, tok_any, grad_any, own_ref, oth_ref, ids_ref, probs_ref, tok_ref, grad_ref, landed):
    copies = [
        pltpu.make_async_copy(src, dst, landed.at[n])
        for n, (src, dst) in enumerate(
            ((ids_any, ids_ref), (probs_any, probs_ref), (tok_any, tok_ref), (grad_any, grad_ref))
        )
    ]
    for copy in copies:
        copy.start()
    for copy in copies[:2]:
        copy.wait()
    ids = ids_ref[...]
    probs = probs_ref[...].astype(F32)
    toks, width = tok_ref.shape
    half, eighth = width // 2, width // SUBS
    size = half + eighth
    both = 2 * SUBS
    row = iota((both, toks), 0)
    sub = sub_row(both, toks)
    expert = jnp.where(row < SUBS, e_ref[0], 1 - e_ref[0])
    main, hits = chosen_rows(ids, expert, sub % WHOLE)
    tail, _ = chosen_rows(ids, expert, jnp.full((both, toks), WHOLE, jnp.int32))
    plain = jnp.where(sub < WHOLE, main, jnp.where(sub == WHOLE, tail, 0.0))
    halves = [jnp.where(sub // WHOLE == h, main, 0.0).astype(BF16) for h in range(2)]
    eighths = [jnp.where(sub == s, tail, 0.0).astype(BF16) for s in range(SUBS)]
    for at, src in enumerate((tok_ref, grad_ref)):
        copies[2 + at].wait()
        packed = sum(
            jnp.dot(one, src[:, h * half : (h + 1) * half], preferred_element_type=F32)
            for h, one in enumerate(halves)
        ).astype(BF16)
        last = sum(
            jnp.dot(one, src[:, s * eighth : (s + 1) * eighth], preferred_element_type=F32)
            for s, one in enumerate(eighths)
        ).astype(BF16)
        for n, dst in enumerate((own_ref, oth_ref)):
            dst[:, at * size : at * size + half] = packed[n * SUBS : (n + 1) * SUBS]
            dst[:, at * size + half : (at + 1) * size] = last[n * SUBS : (n + 1) * SUBS]
    weight = sum(jnp.where(hit, probs[k : k + 1, :], 0.0) for k, hit in enumerate(hits))
    gate = jnp.broadcast_to(jnp.sum(plain * weight, axis=1, keepdims=True), (both, LANES)).astype(BF16)
    for n, dst in enumerate((own_ref, oth_ref)):
        dst[:, 2 * size :] = gate[n * SUBS : (n + 1) * SUBS]


def pick(e, ids_t, probs_t, tokens, grad_out):
    width = tokens.shape[1]
    size = width // 2 + width // SUBS
    piece = jax.ShapeDtypeStruct((SUBS, 2 * size + LANES), BF16)
    return pl.pallas_call(
        pick_body,
        out_shape=(piece, piece),
        in_specs=[SMEM] + [HBM] * 4,
        out_specs=[VMEM] * 2,
        scratch_shapes=[pltpu.VMEM(v.shape, v.dtype) for v in (ids_t, probs_t, tokens, grad_out)]
        + [pltpu.SemaphoreType.DMA((4,))],
        compiler_params=pltpu.CompilerParams(vmem_limit_bytes=6 * MIB),
        name="pick_rows",
    )(e, ids_t, probs_t, tokens, grad_out)


NT = (((1,), (1,)), ((), ()))


def chunk_of(width, most):
    return max(n for n in range(LANES, most + 1, LANES) if width % n == 0)


def assemble(pieces, held, out, base, side):
    width = held.shape[1]
    half, eighth = width // 2, width // SUBS
    size = half + eighth
    for n, ref in enumerate(pieces):
        at = n * CAP
        piece = ref[:, side * size : (side + 1) * size].astype(F32)
        for h in range(2):
            held[at : at + WHOLE, h * half : (h + 1) * half] = piece[h * WHOLE : (h + 1) * WHOLE, :half]
        for s in range(SUBS):
            held[at + WHOLE : at + CAP, s * eighth : (s + 1) * eighth] = piece[s : s + 1, half:]
    out[:, pl.ds(base, width)] = held[...].astype(BF16)


def pack(part, gates, out, pieces):
    width = part.shape[1]
    half, eighth = width // 2, width // SUBS
    size = half + eighth
    for n in range(pieces):
        at, to = n * CAP, n * SUBS
        for h in range(2):
            out[to + h * WHOLE : to + (h + 1) * WHOLE, :half] = part[at : at + WHOLE, h * half : (h + 1) * half]
        for s in range(SUBS):
            out[to + s : to + s + 1, half:size] = part[at + WHOLE : at + CAP, s * eighth : (s + 1) * eighth]
        out[to : to + CAP, size:] = gates[at : at + CAP, :]
        out[to + CAP : to + SUBS, size:] = jnp.zeros((SUBS - CAP, LANES), F32)


def experts_body(pieces, t_ref, *refs):
    mine, theirs = refs[:pieces], refs[pieces : 2 * pieces]
    (wg_hbm, wu_hbm, wd_hbm, x_ref, g_ref, wt_ref, dh_ref, du_ref, give_ref, keep_ref,
     ring, held, acc, factor, gates, landed) = refs[2 * pieces :]
    rows, depth = x_ref.shape
    width = depth // 2
    slots, _, tile, _ = ring.shape
    steps = wg_hbm.shape[0] // tile
    t = t_ref[0]

    def load(i, n):
        at = pl.ds(pl.multiple_of(i * tile, tile), tile)
        slot = lax.rem(i, slots)
        return pltpu.make_async_copy((wg_hbm, wu_hbm, wd_hbm)[n].at[at, :], ring.at[slot, n], landed.at[slot, n])

    for i in range(min(steps, slots)):
        for n in range(3):
            load(i, n).start()

    held[...] = jnp.zeros_like(held)
    factor[...] = jnp.zeros_like(factor)
    for n, ref in enumerate(mine):
        factor[n * CAP : (n + 1) * CAP, :] = ref[:CAP, ref.shape[1] - LANES :].astype(F32)
    for group, at in ((mine, t), (theirs, 1 - t)):
        base = pl.multiple_of(at * width, width)
        for side, out in enumerate((x_ref, g_ref)):
            assemble(group, held, out, base, side)
    acc[...] = jnp.zeros_like(acc)
    gates[...] = jnp.zeros_like(gates)

    def step(i, carry):
        slot = lax.rem(i, slots)
        at = pl.ds(pl.multiple_of(i * tile, tile), tile)
        load(i, 0).wait()
        hidden = lax.dot_general(x_ref[...], ring[slot, 0], NT, preferred_element_type=F32)
        load(i, 1).wait()
        upper = lax.dot_general(x_ref[...], ring[slot, 1], NT, preferred_element_type=F32)
        load(i, 2).wait()
        dact = lax.dot_general(g_ref[...], ring[slot, 2], NT, preferred_element_type=F32)
        weight = factor[:, :1]
        sigma = 1.0 / (1.0 + jnp.exp(-hidden))
        silu = hidden * sigma
        act = silu * upper
        gates[...] += jnp.sum(act * dact, axis=1, keepdims=True)
        scaled = weight * dact
        dh = scaled * upper * sigma * (1.0 + hidden * (1.0 - sigma))
        du = scaled * silu
        wt_ref[at, :] = (weight * act).T.astype(BF16)
        dh_ref[at, :] = dh.T.astype(BF16)
        du_ref[at, :] = du.T.astype(BF16)
        acc[...] += jnp.dot(dh.astype(BF16), ring[slot, 0], preferred_element_type=F32) + jnp.dot(
            du.astype(BF16), ring[slot, 1], preferred_element_type=F32
        )

        @pl.when(i + slots < steps)
        def _():
            for n in range(3):
                load(i + slots, n).start()

        return carry

    lax.fori_loop(0, steps, step, 0)
    for at, out in ((1 - t, give_ref), (t, keep_ref)):
        held[...] = acc[:, pl.ds(pl.multiple_of(at * width, width), width)]
        pack(held, gates, out, pieces)


def expert_units(t, mine, theirs, w_gate, w_up, w_down, width):
    hidden, depth = w_gate.shape
    pieces = len(mine)
    rows = -(-pieces * CAP // 16) * 16
    tile = tile_of(hidden, 256)
    slots = min(3, hidden // tile)
    held = jax.ShapeDtypeStruct((rows, depth), BF16)
    unit = jax.ShapeDtypeStruct((hidden, rows), BF16)
    packed = jax.ShapeDtypeStruct((pieces * SUBS, width // 2 + width // SUBS + LANES), F32)
    return pl.pallas_call(
        functools.partial(experts_body, pieces),
        out_shape=(held, held, unit, unit, unit, packed, packed),
        in_specs=[SMEM] + [VMEM] * (2 * pieces) + [HBM] * 3,
        out_specs=[VMEM] * 7,
        scratch_shapes=[
            pltpu.VMEM((slots, 3, tile, depth), BF16),
            pltpu.VMEM((rows, width), F32),
            pltpu.VMEM((rows, depth), F32),
            pltpu.VMEM((rows, LANES), F32),
            pltpu.VMEM((rows, LANES), F32),
            pltpu.SemaphoreType.DMA((slots, 3)),
        ],
        compiler_params=pltpu.CompilerParams(vmem_limit_bytes=36 * MIB),
        cost_estimate=pl.CostEstimate(
            flops=10 * rows * hidden * depth, bytes_accessed=6 * hidden * depth, transcendentals=rows * hidden
        ),
        name="expert_units",
    )(t, *mine, *theirs, w_gate, w_up, w_down)


def weights_body(count, chunk, *refs):
    lefts, x_ref, outs, (ring, sent) = refs[:count], refs[count], refs[count + 1 : 2 * count + 1], refs[2 * count + 1 :]
    slots = ring.shape[1]
    hidden = lefts[0].shape[0]
    steps = x_ref.shape[1] // chunk
    tile = tile_of(hidden, 448)

    def store(i, n):
        cols = pl.ds(pl.multiple_of(i * chunk, chunk), chunk)
        slot = lax.rem(i, slots)
        return pltpu.make_async_copy(ring.at[n, slot], outs[n].at[:, cols], sent.at[n, slot])

    def step(i, carry):
        slot = lax.rem(i, slots)
        x = x_ref[:, pl.ds(pl.multiple_of(i * chunk, chunk), chunk)]
        for n in range(count):

            @pl.when(i >= slots)
            def _():
                store(i - slots, n).wait()

            for at in range(0, hidden, tile):
                ring[n, slot, at : at + tile, :] = jnp.dot(
                    lefts[n][at : at + tile, :], x, preferred_element_type=F32
                ).astype(BF16)
            store(i, n).start()
        return carry

    lax.fori_loop(0, steps, step, 0)
    for i in range(max(0, steps - slots), steps):
        for n in range(count):
            store(i, n).wait()


def weight_grads(lefts, right, name):
    count = len(lefts)
    hidden, rows = lefts[0].shape
    depth = right.shape[1]
    chunk = chunk_of(depth, 512)
    slots = min(4, depth // chunk)
    return pl.pallas_call(
        functools.partial(weights_body, count, chunk),
        out_shape=[jax.ShapeDtypeStruct((hidden, depth), BF16)] * count,
        in_specs=[VMEM] * (count + 1),
        out_specs=[HBM] * count,
        scratch_shapes=[pltpu.VMEM((count, slots, hidden, chunk), BF16), pltpu.SemaphoreType.DMA((count, slots))],
        compiler_params=pltpu.CompilerParams(vmem_limit_bytes=24 * MIB),
        cost_estimate=pl.CostEstimate(
            flops=2 * count * rows * hidden * depth, bytes_accessed=2 * count * hidden * depth, transcendentals=0
        ),
        name=name,
    )(*lefts, right)


def fold_body(copies, keep_ref, got_ref, *outs):
    for d, out in enumerate(outs):
        rows = slice(d * 2 * SUBS, (d + 1) * 2 * SUBS)
        out[...] = keep_ref[rows, :] + got_ref[rows, :]


def fold(copies, keep, got):
    return pl.pallas_call(
        functools.partial(fold_body, copies),
        out_shape=[jax.ShapeDtypeStruct((2 * SUBS, keep.shape[1]), F32)] * copies,
        in_specs=[VMEM] * 2,
        out_specs=[VMEM] * copies,
        compiler_params=pltpu.CompilerParams(vmem_limit_bytes=6 * MIB),
        name="fold_cores",
    )(keep, got)


def merge_body(*refs):
    blocks, (mine_ref, other_ref) = refs[:-2], refs[-2:]
    for at, out in ((0, mine_ref), (SUBS, other_ref)):
        total = blocks[0][at : at + SUBS, :]
        for block in blocks[1:]:
            total += block[at : at + SUBS, :]
        out[...] = total


def merge(blocks):
    part = jax.ShapeDtypeStruct((SUBS, blocks[0].shape[1]), F32)
    return pl.pallas_call(
        merge_body,
        out_shape=(part, part),
        in_specs=[VMEM] * len(blocks),
        out_specs=[VMEM] * 2,
        compiler_params=pltpu.CompilerParams(vmem_limit_bytes=6 * MIB),
        name="merge_chips",
    )(*blocks)


def finish_body(e_ref, ids_ref, mine_ref, got_ref, tok_ref, gate_ref):
    ids = ids_ref[...]
    toks, width = tok_ref.shape
    half, eighth = width // 2, width // SUBS
    both = 2 * SUBS
    row = iota((both, toks), 0)
    sub = sub_row(both, toks)
    expert = jnp.where(row < SUBS, e_ref[0], 1 - e_ref[0])
    main, hits = chosen_rows(ids, expert, sub % WHOLE)
    tail, _ = chosen_rows(ids, expert, jnp.full((both, toks), WHOLE, jnp.int32))
    plain = jnp.where(sub < WHOLE, main, jnp.where(sub == WHOLE, tail, 0.0))
    data = jnp.concatenate([mine_ref[...], got_ref[...]], axis=0)
    tn = (((0,), (0,)), ((), ()))
    exact = dict(precision=lax.Precision.HIGHEST, preferred_element_type=F32)
    halves = [
        lax.dot_general(jnp.where(sub // WHOLE == h, main, 0.0), data[:, :half], tn, **exact) for h in range(2)
    ]
    for s in range(SUBS):
        last = lax.dot_general(jnp.where(sub == s, tail, 0.0), data[:, half : half + eighth], tn, **exact)
        h, at = divmod(s * eighth, half)
        tok_ref[:, s * eighth : (s + 1) * eighth] = (halves[h][:, at : at + eighth] + last).astype(BF16)
    term = plain * data[:, half + eighth : half + eighth + 1]
    for k, hit in enumerate(hits):
        gate_ref[k : k + 1, :] = jnp.sum(jnp.where(hit, term, 0.0), axis=0, keepdims=True)


def finish(e, ids_t, mine, got, width):
    top, toks = ids_t.shape
    return pl.pallas_call(
        finish_body,
        out_shape=(jax.ShapeDtypeStruct((toks, width), BF16), jax.ShapeDtypeStruct((top, toks), F32)),
        in_specs=[SMEM] + [VMEM] * 3,
        out_specs=[VMEM] * 2,
        compiler_params=pltpu.CompilerParams(vmem_limit_bytes=6 * MIB),
        name="finish_tokens",
    )(e, ids_t, mine, got)


def on_device(tokens, grad_out, expert_ids, gate_probs, w_gate, w_up, w_down):
    n_expert = lax.axis_size("expert")
    copies = n_expert // EXPERTS_ON
    place = lax.axis_index("expert")
    e = (place >= copies).astype(jnp.int32).reshape(1)
    t = lax.axis_index("tensor").astype(jnp.int32).reshape(1)
    width = tokens.shape[1]

    def partner(v):
        return lax.ppermute(v, "expert", [(i, (i + copies) % n_expert) for i in range(n_expert)])

    def across(v, d):
        return lax.ppermute(v, "expert", [(i, i ^ d) for i in range(n_expert)])

    def other_core(v):
        return lax.ppermute(v, "tensor", [(0, 1), (1, 0)])

    w_gate, w_up, w_down = (pltpu.with_memory_space_constraint(w, pltpu.HBM) for w in (w_gate, w_up, w_down))
    ids_t = expert_ids.T
    here = (pltpu.with_memory_space_constraint(v, pltpu.HBM) for v in (ids_t, gate_probs.T, tokens, grad_out))
    own, oth = pick(e, *here)
    far_first = sorted(range(1, copies), key=lambda d: (-d.bit_count(), d))
    got = partner(oth)
    first = {0: own} | {d: across(own, d) for d in far_first}
    second = {0: got} | {d: across(got, d) for d in far_first}
    mine = [piece for d in range(copies) for piece in (first[d], second[d])]
    theirs = [other_core(piece) for piece in mine]
    x, g, wt, dh, du, give, keep = expert_units(t, mine, theirs, w_gate, w_up, w_down, width)
    blocks = list(fold(copies, keep, other_core(give)))
    arrived = {d: across(blocks[d], d) for d in far_first}
    dh, mine = lax.optimization_barrier((dh, blocks[0]))
    grads = weight_grads((dh, du), x, "grads_gate_up")
    grads, arrived = lax.optimization_barrier((grads, arrived))
    mine, others = merge([mine] + [arrived[d] for d in range(1, copies)])
    theirs = partner(others)
    wt, mine = lax.optimization_barrier((wt, mine))
    grads = [*grads, *weight_grads((wt,), g, "grad_down")]
    grads, theirs = lax.optimization_barrier((grads, theirs))
    token_grad, gate_t = finish(e, ids_t, mine, theirs, width)
    return token_grad, gate_t.T, *grads


def solution(mesh):
    return jax.shard_map(
        on_device,
        mesh=mesh,
        in_specs=(
            P(("groups", "expert"), "tensor"),
            P(("groups", "expert"), "tensor"),
            P(("groups", "expert"), None),
            P(("groups", "expert"), None),
            P(("expert", "tensor"), None),
            P(("expert", "tensor"), None),
            P(("expert", "tensor"), None),
        ),
        out_specs=(
            P(("groups", "expert"), "tensor"),
            P(("groups", "expert"), None),
            P(("expert", "tensor"), "groups"),
            P(("expert", "tensor"), "groups"),
            P(("expert", "tensor"), "groups"),
        ),
        check_vma=False,
    )
```

time: 85.8 us -> 87.3 us (1.017)
  Pallas kernels: 59 us -> 62.1 us
  waiting for transfers between devices: 6.66 us -> 4.73 us
  starting transfers between devices: 18.4 us -> 19.6 us
    pallas_call x3 -> x2, Pallas kernels: 37.2 us -> 40.4 us  [the longest x1 39.1 us: expert_units(): pl.pallas_call(functools.partial(experts_body, pieces), out_shape=(held,...]
    ppermute x9, starting transfers between devices: 11.2 us -> 12.3 us  [across(): return lax.ppermute(v, 'expert', [(i, i ^ d) for i in range(n_expert)])]
    ppermute x3 -> x9, waiting for transfers between devices: 3.54 us -> 2.46 us  [other_core(): return lax.ppermute(v, 'tensor', [(0, 1), (1, 0)])]
    ppermute x9, waiting for transfers between devices: 3.11 us -> 2.18 us  [across(): return lax.ppermute(v, 'expert', [(i, i ^ d) for i in range(n_expert)])]
  transfers between devices with their start and end apart: 14 -> 20, of which waited for: 7 -> 6; matrix products, arithmetic and copies ran while one was open for 0% -> 0% of each run, Pallas kernels for 24% -> 23%
where the time goes in v6:
time: 87.3 us; the launch traced here: 87.2 us
  Pallas kernels  62.1 us (71%)
  starting transfers between devices  19.6 us (22%)
  waiting for transfers between devices  4.73 us (5%)
    pallas_call x1, Pallas kernels, expert_units(): pl.pallas_call(functools.partial(experts_body, pieces), out_shape=(held,...  39.1 us
    pallas_call x2, Pallas kernels, weight_grads(): pl.pallas_call(functools.partial(weights_body, count, chunk), out_shape=[...  20 us
    ppermute x9, starting transfers between devices, across(): return lax.ppermute(v, 'expert', [(i, i ^ d) for i in range(n_expert)])  12.3 us
    ppermute x2, starting transfers between devices, partner(): lax.ppermute(v, 'expert', [(i, (i + copies) % n_expert) for i in range(n_...  5.8 us
    ppermute x9, waiting for transfers between devices, other_core(): return lax.ppermute(v, 'tensor', [(0, 1), (1, 0)])  2.46 us
    ppermute x9, waiting for transfers between devices, across(): return lax.ppermute(v, 'expert', [(i, i ^ d) for i in range(n_expert)])  2.18 us
  transfers between devices with their start and end apart: 20, of which 6 were waited for; matrix products, arithmetic and copies ran while one was open for 0% of the time, Pallas kernels for 23%

profile of v6, /device:TPU:0, one launch (start us, length us, event | category | flops | bytes accessed | tf_op | source)
XLA Modules:
  0.0 87.2 jit_solution(11746869626075929354)
XLA Ops:
  0.6 1.4 %pick_rows.1 = (bf16[8,3968]{1,0:T(8,128)(2,1)S(1)}, bf16[8,3968]{1,0:T(8,128)(2,1)S(1)}) custom-call(s32[1]{0:T(128)} %bitcast.e_ref, s32[4,16]{1,0:T(4,128)} %bitcast.5, bf16[4,16]{1,0:T(4,128)(2,1)} %bitcast.7, bf16[16,3072]{1,0:T(8,128)(2,1)} %tok_any.1, bf16[16,3072]{1,0:T(8,128)(2,1)} %grad_any.1), custom_call_target="tpu_custom_call" | custom-call | tf_op jit(solution)/shard_map/pick_rows/pallas_call | solution.py:93
  2.0 4.1 %collective-permute-start = (bf16[8,3968]{1,0:T(8,128)(2,1)S(1)}, bf16[8,3968]{1,0:T(8,128)(2,1)S(1)}, u32[]{:S(2)}, u32[]{:S(2)}) collective-permute-start(bf16[8,3968]{1,0:T(8,128)(2,1)S(1)} %get-tuple-element.38), channel_id=1, source_target_pairs={{0,8},{2,10},{4,12},{6,14},{8,0},{10,2},{12,4},{14,6},{1,9},{3,11}... | collective-permute-start | bytes 190472 | tf_op jit(solution)/shard_map/ppermute | solution.py:376
  6.1 0.0 collective-permute-start.7
  6.1 2.5 %collective-permute-start.5 = (bf16[8,3968]{1,0:T(8,128)(2,1)S(1)}, bf16[8,3968]{1,0:T(8,128)(2,1)S(1)}, u32[]{:S(2)}, u32[]{:S(2)}) collective-permute-start(bf16[8,3968]{1,0:T(8,128)(2,1)S(1)} %get-tuple-element.37.refs_0_), channel_id=1, source_target_pairs={{0,6},{2,4},{4,2},{6,0},{8,14},{10,12},{12,10},{14,8},{1,7},{3,5},... | collective-permute-start | bytes 190472 | tf_op jit(solution)/shard_map/ppermute | solution.py:379
  8.6 0.5 collective-permute-start.3
  9.1 0.5 collective-permute-start.1
  9.6 0.1 collective-permute-done.refs_1_
  9.7 0.0 collective-permute-start.8
  9.7 0.0 collective-permute-done.7.refs_8_
  9.7 2.5 %collective-permute-start.6 = (bf16[8,3968]{1,0:T(8,128)(2,1)S(1)}, bf16[8,3968]{1,0:T(8,128)(2,1)S(1)}, u32[]{:S(2)}, u32[]{:S(2)}) collective-permute-start(bf16[8,3968]{1,0:T(8,128)(2,1)S(1)} %collective-permute-done.refs_1_), channel_id=1, source_target_pairs={{0,6},{2,4},{4,2},{6,0},{8,14},{10,12},{12,10},{14,8},{1,7},{3,5},... | collective-permute-start | bytes 190472 | tf_op jit(solution)/shard_map/ppermute | solution.py:379
  12.2 0.0 collective-permute-done.5.refs_6_
  12.2 1.3 %collective-permute-start.4 = (bf16[8,3968]{1,0:T(8,128)(2,1)S(1)}, bf16[8,3968]{1,0:T(8,128)(2,1)S(1)}, u32[]{:S(2)}, u32[]{:S(2)}) collective-permute-start(bf16[8,3968]{1,0:T(8,128)(2,1)S(1)} %collective-permute-done.refs_1_), channel_id=1, source_target_pairs={{0,4},{2,6},{4,0},{6,2},{8,12},{10,14},{12,8},{14,10},{1,5},{3,7},... | collective-permute-start | bytes 190472 | tf_op jit(solution)/shard_map/ppermute | solution.py:379
  13.4 0.0 collective-permute-done.3.refs_4_
  13.4 1.5 %collective-permute-start.2 = (bf16[8,3968]{1,0:T(8,128)(2,1)S(1)}, bf16[8,3968]{1,0:T(8,128)(2,1)S(1)}, u32[]{:S(2)}, u32[]{:S(2)}) collective-permute-start(bf16[8,3968]{1,0:T(8,128)(2,1)S(1)} %collective-permute-done.refs_1_), channel_id=1, source_target_pairs={{0,2},{2,0},{4,6},{6,4},{8,10},{10,8},{12,14},{14,12},{1,3},{3,1},... | collective-permute-start | bytes 190472 | tf_op jit(solution)/shard_map/ppermute | solution.py:379
  14.9 0.0 collective-permute-done.1.refs_2_
  14.9 0.0 collective-permute-start.13
  14.9 0.0 collective-permute-done.8.refs_9_
  14.9 0.5 collective-permute-start.11
  15.4 0.0 collective-permute-done.6.refs_7_
  15.5 0.1 collective-permute-start.9
  15.5 0.9 %collective-permute-done.4.refs_5_ = bf16[8,3968]{1,0:T(8,128)(2,1)S(1)} collective-permute-done((bf16[8,3968]{1,0:T(8,128)(2,1)S(1)}, bf16[8,3968]{1,0:T(8,128)(2,1)S(1)}, u32[]{:S(2)}, u32[]{:S(2)}) %collective-permute-start.4) | collective-permute-done | bytes 63520 | tf_op jit(solution)/shard_map/ppermute | solution.py:379
  16.4 0.0 collective-permute-start.14
  16.4 1.3 %collective-permute-done.2.refs_3_ = bf16[8,3968]{1,0:T(8,128)(2,1)S(1)} collective-permute-done((bf16[8,3968]{1,0:T(8,128)(2,1)S(1)}, bf16[8,3968]{1,0:T(8,128)(2,1)S(1)}, u32[]{:S(2)}, u32[]{:S(2)}) %collective-permute-start.2) | collective-permute-done | bytes 63520 | tf_op jit(solution)/shard_map/ppermute | solution.py:379
  17.7 0.0 collective-permute-start.12
  17.7 0.0 collective-permute-done.13.refs_14_
  17.7 0.5 collective-permute-start.10
  18.2 0.0 collective-permute-done.11.refs_12_
  18.2 0.0 collective-permute-done.9.refs_10_
  18.2 0.0 collective-permute-done.14.refs_15_
  18.2 0.7 collective-permute-done.12.refs_13_
  18.9 0.2 collective-permute-done.10.refs_11_
  19.1 39.1 %expert_units.1 = (bf16[48,6144]{1,0:T(8,128)(2,1)S(1)}, bf16[48,6144]{1,0:T(8,128)(2,1)S(1)}, bf16[1344,48]{1,0:T(8,128)(2,1)S(1)}, bf16[1344,48]{1,0:T(8,128)(...) custom-call(s32[1]{0:T(128)} %bitcast.2.t_ref, ...), custom_call_target="tpu_custom_call" | custom-call | flops 3963617280 | bytes 49545216 | tf_op jit(solution)/shard_map/expert_units/pallas_call | solution.py:216
  58.2 0.0 copy-start
  58.2 0.4 collective-permute-start.15
  58.6 1.6 %collective-permute-done.15.got_ref = f32[64,2048]{1,0:T(8,128)S(1)} collective-permute-done((f32[64,2048]{1,0:T(8,128)S(1)}, f32[64,2048]{1,0:T(8,128)S(1)}, u32[]{:S(2)}, u32[]{:S(2)}) %collective-permute-start.15) | collective-permute-done | bytes 524320 | tf_op jit(solution)/shard_map/ppermute | solution.py:382
  60.2 0.1 fold_cores.1
  60.2 1.6 %collective-permute-start.16 = (f32[16,2048]{1,0:T(8,128)S(1)}, f32[16,2048]{1,0:T(8,128)S(1)}, u32[]{:S(2)}, u32[]{:S(2)}) collective-permute-start(f32[16,2048]{1,0:T(8,128)S(1)} %get-tuple-element.50), channel_id=1, source_target_pairs={{0,2},{2,0},{4,6},{6,4},{8,10},{10,8},{12,14},{14,12},{1,3},{3,1},... | collective-permute-start | bytes 393224 | tf_op jit(solution)/shard_map/ppermute | solution.py:379
  61.8 0.4 collective-permute-start.17
  62.1 1.6 %collective-permute-start.18 = (f32[16,2048]{1,0:T(8,128)S(1)}, f32[16,2048]{1,0:T(8,128)S(1)}, u32[]{:S(2)}, u32[]{:S(2)}) collective-permute-start(f32[16,2048]{1,0:T(8,128)S(1)} %get-tuple-element.52), channel_id=1, source_target_pairs={{0,6},{2,4},{4,2},{6,0},{8,14},{10,12},{12,10},{14,8},{1,7},{3,5},... | collective-permute-start | bytes 393224 | tf_op jit(solution)/shard_map/ppermute | solution.py:379
  63.8 13.0 %grads_gate_up.1 = (bf16[1344,6144]{1,0:T(8,128)(2,1)}, bf16[1344,6144]{1,0:T(8,128)(2,1)}) custom-call(bf16[1344,48]{1,0:T(8,128)(2,1)S(1)} %get-tuple-element.45.refs_0_, bf16[1344,48]{1,0:T(8,128)(2,1)S(1)} %get-tuple-element.46.refs_1_, bf16[48,6144]{1,0:T(8,128)(2,1)S(1)} %get-tuple-element.47.refs_2_), custom_call_target="tpu_custom_call" | custom-call | flops 1585446912 | bytes 33030144 | tf_op jit(solution)/shard_map/grads_gate_up/pallas_call | solution.py:277
  76.8 0.0 collective-permute-done.16.refs_1_
  76.8 0.0 collective-permute-done.17.refs_2_
  76.8 0.0 collective-permute-done.18.refs_3_
  76.8 1.7 %collective-permute-start.19 = (f32[8,2048]{1,0:T(8,128)S(1)}, f32[8,2048]{1,0:T(8,128)S(1)}, u32[]{:S(2)}, u32[]{:S(2)}) collective-permute-start(f32[8,2048]{1,0:T(8,128)S(1)} %get-tuple-element.62), channel_id=1, source_target_pairs={{0,8},{2,10},{4,12},{6,14},{8,0},{10,2},{12,4},{14,6},{1,9},{3,11}... | collective-permute-start | bytes 196616 | tf_op jit(solution)/shard_map/ppermute | solution.py:376
  78.5 7.0 %grad_down.1 = bf16[1344,6144]{1,0:T(8,128)(2,1)} custom-call(bf16[1344,48]{1,0:T(8,128)(2,1)S(1)} %get-tuple-element.60.refs_0_, bf16[48,6144]{1,0:T(8,128)(2,1)S(1)} %get-tuple-element.61.refs_1_), custom_call_target="tpu_custom_call" | custom-call | flops 792723456 | bytes 16515072 | tf_op jit(solution)/shard_map/grad_down/pallas_call | solution.py:277
  85.6 0.0 collective-permute-done.19.got_ref
  85.6 0.0 copy-done
  85.6 1.5 %finish_tokens.1 = (bf16[16,3072]{1,0:T(8,128)(2,1)}, f32[4,16]{1,0:T(4,128)}) custom-call(s32[1]{0:T(128)} %bitcast.e_ref, s32[4,16]{1,0:T(4,128)S(1)} %bitcast.6, f32[8,2048]{1,0:T(8,128)S(1)} %get-tuple-element.57.mine_ref, f32[8,2048]{1,0:T(8,128)S(1)} %collective-permute-done.19.got_ref), custom_call_target="tpu_custom_call" | custom-call | tf_op jit(solution)/shard_map/finish_tokens/pallas_call | solution.py:357
  (1 shorter events, 0.0 us)
Async XLA Ops:
  2.0 7.7 %collective-permute-start = (bf16[8,3968]{1,0:T(8,128)(2,1)S(1)}, bf16[8,3968]{1,0:T(8,128)(2,1)S(1)}, u32[]{:S(2)}, u32[]{:S(2)}) collective-permute-start(bf16[8,3968]{1,0:T(8,128)(2,1)S(1)} %get-tuple-element.38), channel_id=1, source_target_pairs={{0,8},{2,10},{4,12},{6,14},{8,0},{10,2},{12,4},{14,6},{1,9},{3,11}... | collective-permute-start | bytes 190472 | tf_op jit(solution)/shard_map/ppermute | solution.py:376
  6.1 3.6 %collective-permute-start.7 = (bf16[8,3968]{1,0:T(8,128)(2,1)S(1)}, bf16[8,3968]{1,0:T(8,128)(2,1)S(1)}, u32[]{:S(2)}, u32[]{:S(2)}) collective-permute-start(bf16[8,3968]{1,0:T(8,128)(2,1)S(1)} %get-tuple-element.37.refs_0_), channel_id=1, source_target_pairs={{0,1},{1,0},{2,3},{3,2},{4,5},{5,4},{6,7},{7,6},{8,9},{9,8},{10,11... | collective-permute-start | bytes 190472 | tf_op jit(solution)/shard_map/ppermute | solution.py:382
  6.1 6.1 %collective-permute-start.5 = (bf16[8,3968]{1,0:T(8,128)(2,1)S(1)}, bf16[8,3968]{1,0:T(8,128)(2,1)S(1)}, u32[]{:S(2)}, u32[]{:S(2)}) collective-permute-start(bf16[8,3968]{1,0:T(8,128)(2,1)S(1)} %get-tuple-element.37.refs_0_), channel_id=1, source_target_pairs={{0,6},{2,4},{4,2},{6,0},{8,14},{10,12},{12,10},{14,8},{1,7},{3,5},... | collective-permute-start | bytes 190472 | tf_op jit(solution)/shard_map/ppermute | solution.py:379
  8.6 4.8 %collective-permute-start.3 = (bf16[8,3968]{1,0:T(8,128)(2,1)S(1)}, bf16[8,3968]{1,0:T(8,128)(2,1)S(1)}, u32[]{:S(2)}, u32[]{:S(2)}) collective-permute-start(bf16[8,3968]{1,0:T(8,128)(2,1)S(1)} %get-tuple-element.37.refs_0_), channel_id=1, source_target_pairs={{0,4},{2,6},{4,0},{6,2},{8,12},{10,14},{12,8},{14,10},{1,5},{3,7},... | collective-permute-start | bytes 190472 | tf_op jit(solution)/shard_map/ppermute | solution.py:379
  9.1 5.9 %collective-permute-start.1 = (bf16[8,3968]{1,0:T(8,128)(2,1)S(1)}, bf16[8,3968]{1,0:T(8,128)(2,1)S(1)}, u32[]{:S(2)}, u32[]{:S(2)}) collective-permute-start(bf16[8,3968]{1,0:T(8,128)(2,1)S(1)} %get-tuple-element.37.refs_0_), channel_id=1, source_target_pairs={{0,2},{2,0},{4,6},{6,4},{8,10},{10,8},{12,14},{14,12},{1,3},{3,1},... | collective-permute-start | bytes 190472 | tf_op jit(solution)/shard_map/ppermute | solution.py:379
  9.7 5.2 %collective-permute-start.8 = (bf16[8,3968]{1,0:T(8,128)(2,1)S(1)}, bf16[8,3968]{1,0:T(8,128)(2,1)S(1)}, u32[]{:S(2)}, u32[]{:S(2)}) collective-permute-start(bf16[8,3968]{1,0:T(8,128)(2,1)S(1)} %collective-permute-done.refs_1_), channel_id=1, source_target_pairs={{0,1},{1,0},{2,3},{3,2},{4,5},{5,4},{6,7},{7,6},{8,9},{9,8},{10,11... | collective-permute-start | bytes 190472 | tf_op jit(solution)/shard_map/ppermute | solution.py:382
  9.7 5.7 %collective-permute-start.6 = (bf16[8,3968]{1,0:T(8,128)(2,1)S(1)}, bf16[8,3968]{1,0:T(8,128)(2,1)S(1)}, u32[]{:S(2)}, u32[]{:S(2)}) collective-permute-start(bf16[8,3968]{1,0:T(8,128)(2,1)S(1)} %collective-permute-done.refs_1_), channel_id=1, source_target_pairs={{0,6},{2,4},{4,2},{6,0},{8,14},{10,12},{12,10},{14,8},{1,7},{3,5},... | collective-permute-start | bytes 190472 | tf_op jit(solution)/shard_map/ppermute | solution.py:379
  12.2 4.2 %collective-permute-start.4 = (bf16[8,3968]{1,0:T(8,128)(2,1)S(1)}, bf16[8,3968]{1,0:T(8,128)(2,1)S(1)}, u32[]{:S(2)}, u32[]{:S(2)}) collective-permute-start(bf16[8,3968]{1,0:T(8,128)(2,1)S(1)} %collective-permute-done.refs_1_), channel_id=1, source_target_pairs={{0,4},{2,6},{4,0},{6,2},{8,12},{10,14},{12,8},{14,10},{1,5},{3,7},... | collective-permute-start | bytes 190472 | tf_op jit(solution)/shard_map/ppermute | solution.py:379
  13.4 4.2 %collective-permute-start.2 = (bf16[8,3968]{1,0:T(8,128)(2,1)S(1)}, bf16[8,3968]{1,0:T(8,128)(2,1)S(1)}, u32[]{:S(2)}, u32[]{:S(2)}) collective-permute-start(bf16[8,3968]{1,0:T(8,128)(2,1)S(1)} %collective-permute-done.refs_1_), channel_id=1, source_target_pairs={{0,2},{2,0},{4,6},{6,4},{8,10},{10,8},{12,14},{14,12},{1,3},{3,1},... | collective-permute-start | bytes 190472 | tf_op jit(solution)/shard_map/ppermute | solution.py:379
  14.9 2.8 %collective-permute-start.13 = (bf16[8,3968]{1,0:T(8,128)(2,1)S(1)}, bf16[8,3968]{1,0:T(8,128)(2,1)S(1)}, u32[]{:S(2)}, u32[]{:S(2)}) collective-permute-start(bf16[8,3968]{1,0:T(8,128)(2,1)S(1)} %collective-permute-done.5.refs_6_), channel_id=1, source_target_pairs={{0,1},{1,0},{2,3},{3,2},{4,5},{5,4},{6,7},{7,6},{8,9},{9,8},{10,11... | collective-permute-start | bytes 190472 | tf_op jit(solution)/shard_map/ppermute | solution.py:382
  14.9 3.3 %collective-permute-start.11 = (bf16[8,3968]{1,0:T(8,128)(2,1)S(1)}, bf16[8,3968]{1,0:T(8,128)(2,1)S(1)}, u32[]{:S(2)}, u32[]{:S(2)}) collective-permute-start(bf16[8,3968]{1,0:T(8,128)(2,1)S(1)} %collective-permute-done.3.refs_4_), channel_id=1, source_target_pairs={{0,1},{1,0},{2,3},{3,2},{4,5},{5,4},{6,7},{7,6},{8,9},{9,8},{10,11... | collective-permute-start | bytes 190472 | tf_op jit(solution)/shard_map/ppermute | solution.py:382
  15.5 2.8 %collective-permute-start.9 = (bf16[8,3968]{1,0:T(8,128)(2,1)S(1)}, bf16[8,3968]{1,0:T(8,128)(2,1)S(1)}, u32[]{:S(2)}, u32[]{:S(2)}) collective-permute-start(bf16[8,3968]{1,0:T(8,128)(2,1)S(1)} %collective-permute-done.1.refs_2_), channel_id=1, source_target_pairs={{0,1},{1,0},{2,3},{3,2},{4,5},{5,4},{6,7},{7,6},{8,9},{9,8},{10,11... | collective-permute-start | bytes 190472 | tf_op jit(solution)/shard_map/ppermute | solution.py:382
  16.4 1.8 %collective-permute-start.14 = (bf16[8,3968]{1,0:T(8,128)(2,1)S(1)}, bf16[8,3968]{1,0:T(8,128)(2,1)S(1)}, u32[]{:S(2)}, u32[]{:S(2)}) collective-permute-start(bf16[8,3968]{1,0:T(8,128)(2,1)S(1)} %collective-permute-done.6.refs_7_), channel_id=1, source_target_pairs={{0,1},{1,0},{2,3},{3,2},{4,5},{5,4},{6,7},{7,6},{8,9},{9,8},{10,11... | collective-permute-start | bytes 190472 | tf_op jit(solution)/shard_map/ppermute | solution.py:382
  17.7 1.3 %collective-permute-start.12 = (bf16[8,3968]{1,0:T(8,128)(2,1)S(1)}, bf16[8,3968]{1,0:T(8,128)(2,1)S(1)}, u32[]{:S(2)}, u32[]{:S(2)}) collective-permute-start(bf16[8,3968]{1,0:T(8,128)(2,1)S(1)} %collective-permute-done.4.refs_5_), channel_id=1, source_target_pairs={{0,1},{1,0},{2,3},{3,2},{4,5},{5,4},{6,7},{7,6},{8,9},{9,8},{10,11... | collective-permute-start | bytes 190472 | tf_op jit(solution)/shard_map/ppermute | solution.py:382
  17.7 1.4 %collective-permute-start.10 = (bf16[8,3968]{1,0:T(8,128)(2,1)S(1)}, bf16[8,3968]{1,0:T(8,128)(2,1)S(1)}, u32[]{:S(2)}, u32[]{:S(2)}) collective-permute-start(bf16[8,3968]{1,0:T(8,128)(2,1)S(1)} %collective-permute-done.2.refs_3_), channel_id=1, source_target_pairs={{0,1},{1,0},{2,3},{3,2},{4,5},{5,4},{6,7},{7,6},{8,9},{9,8},{10,11... | collective-permute-start | bytes 190472 | tf_op jit(solution)/shard_map/ppermute | solution.py:382
  58.2 27.4 %copy-start = (s32[16,4]{0,1:T(4,128)S(1)}, s32[16,4]{0,1:T(4,128)}, u32[]{:S(2)}) copy-start(s32[16,4]{0,1:T(4,128)} %param.9) | copy-start | bytes 772
  58.2 2.0 %collective-permute-start.15 = (f32[64,2048]{1,0:T(8,128)S(1)}, f32[64,2048]{1,0:T(8,128)S(1)}, u32[]{:S(2)}, u32[]{:S(2)}) collective-permute-start(f32[64,2048]{1,0:T(8,128)S(1)} %get-tuple-element.42), channel_id=1, source_target_pairs={{0,1},{1,0},{2,3},{3,2},{4,5},{5,4},{6,7},{7,6},{8,9},{9,8},{10,11... | collective-permute-start | bytes 1572872 | tf_op jit(solution)/shard_map/ppermute | solution.py:382
  60.2 16.5 %collective-permute-start.16 = (f32[16,2048]{1,0:T(8,128)S(1)}, f32[16,2048]{1,0:T(8,128)S(1)}, u32[]{:S(2)}, u32[]{:S(2)}) collective-permute-start(f32[16,2048]{1,0:T(8,128)S(1)} %get-tuple-element.50), channel_id=1, source_target_pairs={{0,2},{2,0},{4,6},{6,4},{8,10},{10,8},{12,14},{14,12},{1,3},{3,1},... | collective-permute-start | bytes 393224 | tf_op jit(solution)/shard_map/ppermute | solution.py:379
  61.8 15.0 %collective-permute-start.17 = (f32[16,2048]{1,0:T(8,128)S(1)}, f32[16,2048]{1,0:T(8,128)S(1)}, u32[]{:S(2)}, u32[]{:S(2)}) collective-permute-start(f32[16,2048]{1,0:T(8,128)S(1)} %get-tuple-element.51), channel_id=1, source_target_pairs={{0,4},{2,6},{4,0},{6,2},{8,12},{10,14},{12,8},{14,10},{1,5},{3,7},... | collective-permute-start | bytes 393224 | tf_op jit(solution)/shard_map/ppermute | solution.py:379
  62.1 14.7 %collective-permute-start.18 = (f32[16,2048]{1,0:T(8,128)S(1)}, f32[16,2048]{1,0:T(8,128)S(1)}, u32[]{:S(2)}, u32[]{:S(2)}) collective-permute-start(f32[16,2048]{1,0:T(8,128)S(1)} %get-tuple-element.52), channel_id=1, source_target_pairs={{0,6},{2,4},{4,2},{6,0},{8,14},{10,12},{12,10},{14,8},{1,7},{3,5},... | collective-permute-start | bytes 393224 | tf_op jit(solution)/shard_map/ppermute | solution.py:379
  76.8 8.8 %collective-permute-start.19 = (f32[8,2048]{1,0:T(8,128)S(1)}, f32[8,2048]{1,0:T(8,128)S(1)}, u32[]{:S(2)}, u32[]{:S(2)}) collective-permute-start(f32[8,2048]{1,0:T(8,128)S(1)} %get-tuple-element.62), channel_id=1, source_target_pairs={{0,8},{2,10},{4,12},{6,14},{8,0},{10,2},{12,4},{14,6},{1,9},{3,11}... | collective-permute-start | bytes 196616 | tf_op jit(solution)/shard_map/ppermute | solution.py:376

commit v7 on v6

--- a/solution.py
+++ b/solution.py
@@ -137,98 +137,183 @@
         out[to + CAP : to + SUBS, size:] = jnp.zeros((SUBS - CAP, LANES), F32)
 
 
-def experts_body(pieces, t_ref, *refs):
+def experts_body(pieces, chunk, ahead, t_ref, *refs):
     mine, theirs = refs[:pieces], refs[pieces : 2 * pieces]
-    (wg_hbm, wu_hbm, wd_hbm, x_ref, g_ref, wt_ref, dh_ref, du_ref, give_ref, keep_ref,
-     ring, held, acc, factor, gates, landed) = refs[2 * pieces :]
+    (wg_hbm, wu_hbm, wd_hbm, x_ref, dh_ref, du_ref, give_ref, keep_ref, down_ref,
+     wg_ref, wu_ref, ring, g_ref, wt_ref, h_ref, u_ref, da_ref, dhr_ref, dur_ref, acc,
+     held, factor, landed, ring_landed, sent) = refs[2 * pieces :]
     rows, depth = x_ref.shape
+    hidden = wg_ref.shape[0]
     width = depth // 2
-    slots, _, tile, _ = ring.shape
-    steps = wg_hbm.shape[0] // tile
+    slots = ring.shape[0]
+    steps = depth // chunk
     t = t_ref[0]
 
+    def columns(i):
+        return pl.ds(pl.multiple_of(i * chunk, chunk), chunk)
+
     def load(i, n):
-        at = pl.ds(pl.multiple_of(i * tile, tile), tile)
+        src, dst = ((wg_hbm, wg_ref), (wu_hbm, wu_ref))[n]
+        return pltpu.make_async_copy(src.at[:, columns(i)], dst.at[:, columns(i)], landed.at[i, n])
+
+    def load_down(i):
         slot = lax.rem(i, slots)
-        return pltpu.make_async_copy((wg_hbm, wu_hbm, wd_hbm)[n].at[at, :], ring.at[slot, n], landed.at[slot, n])
-
-    for i in range(min(steps, slots)):
-        for n in range(3):
-            load(i, n).start()
-
+        return pltpu.make_async_copy(wd_hbm.at[:, columns(i)], ring.at[slot], ring_landed.at[slot])
+
+    def store_down(i):
+        slot = lax.rem(i, slots)
+        return pltpu.make_async_copy(ring.at[slot], down_ref.at[:, columns(i)], sent.at[slot])
+
+    for n in range(2):
+        load(0, n).start()
     held[...] = jnp.zeros_like(held)
     factor[...] = jnp.zeros_like(factor)
     for n, ref in enumerate(mine):
         factor[n * CAP : (n + 1) * CAP, :] = ref[:CAP, ref.shape[1] - LANES :].astype(F32)
-    for group, at in ((mine, t), (theirs, 1 - t)):
-        base = pl.multiple_of(at * width, width)
-        for side, out in enumerate((x_ref, g_ref)):
-            assemble(group, held, out, base, side)
-    acc[...] = jnp.zeros_like(acc)
-    gates[...] = jnp.zeros_like(gates)
-
-    def step(i, carry):
+    for side, out in enumerate((x_ref, g_ref)):
+        for group, at in ((mine, t), (theirs, 1 - t)):
+            assemble(group, held, out, pl.multiple_of(at * width, width), side)
+        if side == 0:
+            for i in range(1, min(ahead, steps)):
+                for n in range(2):
+                    load(i, n).start()
+
+    def add_to(out, i, w, x):
+        more = lax.dot_general(w, x, NT, preferred_element_type=F32)
+        out[...] = jnp.where(i == 0, more, out[...] + more)
+
+    def up_step(i, carry):
+        x = x_ref[:, columns(i)]
+        load(i, 0).wait()
+        add_to(h_ref, i, wg_ref[:, columns(i)], x)
+        load(i, 1).wait()
+
+        @pl.when(i + ahead < steps)
+        def _():
+            for n in range(2):
+                load(i + ahead, n).start()
+
+        @pl.when(i + ahead >= steps)
+        def _():
+            load_down(i + ahead - steps).start()
+
+        add_to(u_ref, i, wu_ref[:, columns(i)], x)
+        return carry
+
+    lax.fori_loop(0, steps, up_step, 0)
+
+    def down_step(i, carry):
+        g = g_ref[:, columns(i)]
+        load_down(i).wait()
+
+        @pl.when(i + ahead < steps)
+        def _():
+            load_down(i + ahead).start()
+
+        add_to(da_ref, i, ring[lax.rem(i, slots)], g)
+        return carry
+
+    lax.fori_loop(0, steps, down_step, 0)
+
+    weight = factor[...].T[:1, :]
+
+    def units(start, size, total):
+        at = pl.ds(start, size)
+        h = h_ref[at, :]
+        u = u_ref[at, :]
+        da = da_ref[at, :]
+        sigma = 1.0 / (1.0 + jnp.exp(-h))
+        silu = h * sigma
+        act = silu * u
+        scaled = weight * da
+        wt_ref[at, :] = (weight * act).astype(BF16)
+        dh = scaled * u * sigma * (1.0 + h * (1.0 - sigma))
+        du = scaled * silu
+        dh_ref[at, :] = dh.astype(BF16)
+        du_ref[at, :] = du.astype(BF16)
+        dhr_ref[:, at] = dh.T.astype(BF16)
+        dur_ref[:, at] = du.T.astype(BF16)
+        return total + jnp.sum(act * da, axis=0, keepdims=True)
+
+    whole = hidden // LANES
+    total = lax.fori_loop(
+        0, whole, lambda i, v: units(pl.multiple_of(i * LANES, LANES), LANES, v), jnp.zeros((1, rows), F32)
+    )
+    if hidden % LANES:
+        total = units(whole * LANES, hidden % LANES, total)
+    gates = jnp.broadcast_to(total, (LANES, rows)).T
+    tile = tile_of(hidden, 448)
+
+    def grad_step(i, carry):
         slot = lax.rem(i, slots)
-        at = pl.ds(pl.multiple_of(i * tile, tile), tile)
-        load(i, 0).wait()
-        hidden = lax.dot_general(x_ref[...], ring[slot, 0], NT, preferred_element_type=F32)
-        load(i, 1).wait()
-        upper = lax.dot_general(x_ref[...], ring[slot, 1], NT, preferred_element_type=F32)
-        load(i, 2).wait()
-        dact = lax.dot_general(g_ref[...], ring[slot, 2], NT, preferred_element_type=F32)
-        weight = factor[:, :1]
-        sigma = 1.0 / (1.0 + jnp.exp(-hidden))
-        silu = hidden * sigma
-        act = silu * upper
-        gates[...] += jnp.sum(act * dact, axis=1, keepdims=True)
-        scaled = weight * dact
-        dh = scaled * upper * sigma * (1.0 + hidden * (1.0 - sigma))
-        du = scaled * silu
-        wt_ref[at, :] = (weight * act).T.astype(BF16)
-        dh_ref[at, :] = dh.T.astype(BF16)
-        du_ref[at, :] = du.T.astype(BF16)
-        acc[...] += jnp.dot(dh.astype(BF16), ring[slot, 0], preferred_element_type=F32) + jnp.dot(
-            du.astype(BF16), ring[slot, 1], preferred_element_type=F32
+        cols = columns(i)
+
+        @pl.when(i >= slots)
+        def _():
+            store_down(i - slots).wait()
+
+        g = g_ref[:, cols]
+        for at in range(0, hidden, tile):
+            ring[slot, at : at + tile, :] = jnp.dot(
+                wt_ref[at : at + tile, :], g, preferred_element_type=F32
+            ).astype(BF16)
+        store_down(i).start()
+        acc[:, cols] = jnp.dot(dhr_ref[...], wg_ref[:, cols], preferred_element_type=F32) + jnp.dot(
+            dur_ref[...], wu_ref[:, cols], preferred_element_type=F32
         )
-
-        @pl.when(i + slots < steps)
-        def _():
-            for n in range(3):
-                load(i + slots, n).start()
-
         return carry
 
-    lax.fori_loop(0, steps, step, 0)
+    lax.fori_loop(0, steps, grad_step, 0)
     for at, out in ((1 - t, give_ref), (t, keep_ref)):
         held[...] = acc[:, pl.ds(pl.multiple_of(at * width, width), width)]
         pack(held, gates, out, pieces)
+    for i in range(max(0, steps - slots), steps):
+        store_down(i).wait()
 
 
 def expert_units(t, mine, theirs, w_gate, w_up, w_down, width):
     hidden, depth = w_gate.shape
     pieces = len(mine)
     rows = -(-pieces * CAP // 16) * 16
-    tile = tile_of(hidden, 256)
-    slots = min(3, hidden // tile)
-    held = jax.ShapeDtypeStruct((rows, depth), BF16)
+    chunk = chunk_of(width, 768)
+    steps = depth // chunk
+    ahead = 2
+    slots = 4
     unit = jax.ShapeDtypeStruct((hidden, rows), BF16)
     packed = jax.ShapeDtypeStruct((pieces * SUBS, width // 2 + width // SUBS + LANES), F32)
     return pl.pallas_call(
-        functools.partial(experts_body, pieces),
-        out_shape=(held, held, unit, unit, unit, packed, packed),
+        functools.partial(experts_body, pieces, chunk, ahead),
+        out_shape=(
+            jax.ShapeDtypeStruct((rows, depth), BF16),
+            unit,
+            unit,
+            packed,
+            packed,
+            jax.ShapeDtypeStruct((hidden, depth), BF16),
+        ),
         in_specs=[SMEM] + [VMEM] * (2 * pieces) + [HBM] * 3,
-        out_specs=[VMEM] * 7,
+        out_specs=[VMEM] * 5 + [HBM],
         scratch_shapes=[
-            pltpu.VMEM((slots, 3, tile, depth), BF16),
+            pltpu.VMEM((hidden, depth), BF16),
+            pltpu.VMEM((hidden, depth), BF16),
+            pltpu.VMEM((slots, hidden, chunk), BF16),
+            pltpu.VMEM((rows, depth), BF16),
+            pltpu.VMEM((hidden, rows), BF16),
+            pltpu.VMEM((hidden, rows), F32),
+            pltpu.VMEM((hidden, rows), F32),
+            pltpu.VMEM((hidden, rows), F32),
+            pltpu.VMEM((rows, hidden), BF16),
+            pltpu.VMEM((rows, hidden), BF16),
+            pltpu.VMEM((rows, depth), F32),
             pltpu.VMEM((rows, width), F32),
-            pltpu.VMEM((rows, depth), F32),
             pltpu.VMEM((rows, LANES), F32),
-            pltpu.VMEM((rows, LANES), F32),
-            pltpu.SemaphoreType.DMA((slots, 3)),
+            pltpu.SemaphoreType.DMA((steps, 2)),
+            pltpu.SemaphoreType.DMA((slots,)),
+            pltpu.SemaphoreType.DMA((slots,)),
         ],
-        compiler_params=pltpu.CompilerParams(vmem_limit_bytes=36 * MIB),
+        compiler_params=pltpu.CompilerParams(vmem_limit_bytes=50 * MIB),
         cost_estimate=pl.CostEstimate(
-            flops=10 * rows * hidden * depth, bytes_accessed=6 * hidden * depth, transcendentals=rows * hidden
+            flops=12 * rows * hidden * depth, bytes_accessed=8 * hidden * depth, transcendentals=rows * hidden
         ),
         name="expert_units",
     )(t, *mine, *theirs, w_gate, w_up, w_down)
@@ -391,19 +476,19 @@
     second = {0: got} | {d: across(got, d) for d in far_first}
     mine = [piece for d in range(copies) for piece in (first[d], second[d])]
     theirs = [other_core(piece) for piece in mine]
-    x, g, wt, dh, du, give, keep = expert_units(t, mine, theirs, w_gate, w_up, w_down, width)
+    x, dh, du, give, keep, grad_w_down = expert_units(t, mine, theirs, w_gate, w_up, w_down, width)
     blocks = list(fold(copies, keep, other_core(give)))
     arrived = {d: across(blocks[d], d) for d in far_first}
-    dh, mine = lax.optimization_barrier((dh, blocks[0]))
-    grads = weight_grads((dh, du), x, "grads_gate_up")
-    grads, arrived = lax.optimization_barrier((grads, arrived))
-    mine, others = merge([mine] + [arrived[d] for d in range(1, copies)])
-    theirs = partner(others)
-    wt, mine = lax.optimization_barrier((wt, mine))
-    grads = [*grads, *weight_grads((wt,), g, "grad_down")]
-    grads, theirs = lax.optimization_barrier((grads, theirs))
-    token_grad, gate_t = finish(e, ids_t, mine, theirs, width)
-    return token_grad, gate_t.T, *grads
+    dh, local = lax.optimization_barrier((dh, blocks[0]))
+    (grad_w_gate,) = weight_grads((dh,), x, "grad_gate")
+    grad_w_gate, arrived = lax.optimization_barrier((grad_w_gate, arrived))
+    kept, others = merge([local] + [arrived[d] for d in range(1, copies)])
+    back = partner(others)
+    du, kept = lax.optimization_barrier((du, kept))
+    (grad_w_up,) = weight_grads((du,), x, "grad_up")
+    grad_w_up, back = lax.optimization_barrier((grad_w_up, back))
+    token_grad, gate_t = finish(e, ids_t, kept, back, width)
+    return token_grad, gate_t.T, grad_w_gate, grad_w_up, grad_w_down
 
 
 def solution(mesh):

time: 87.3 us -> 83.4 us (0.955)
  Pallas kernels: 62.1 us -> 58.2 us
    pallas_call x2, Pallas kernels: 20 us -> 14 us  [weight_grads(): pl.pallas_call(functools.partial(weights_body, count, chunk), out_shape=[...]
    pallas_call x1, Pallas kernels: 39.1 us -> 41.1 us  [expert_units(): pl.pallas_call(functools.partial(experts_body, pieces, chunk, ahead), out...]
  transfers between devices with their start and end apart: 20 -> 20, of which waited for: 6 -> 6; matrix products, arithmetic and copies ran while one was open for 0% -> 0% of each run, Pallas kernels for 23% -> 17%
where the time goes in v7:
time: 83.4 us; the launch traced here: 83.2 us
  Pallas kernels  58.2 us (70%)
  starting transfers between devices  19.6 us (24%)
  waiting for transfers between devices  4.74 us (6%)
    pallas_call x1, Pallas kernels, expert_units(): pl.pallas_call(functools.partial(experts_body, pieces, chunk, ahead), out...  41.1 us
    pallas_call x2, Pallas kernels, weight_grads(): pl.pallas_call(functools.partial(weights_body, count, chunk), out_shape=[...  14 us
    ppermute x9, starting transfers between devices, across(): return lax.ppermute(v, 'expert', [(i, i ^ d) for i in range(n_expert)])  12.3 us
    ppermute x2, starting transfers between devices, partner(): lax.ppermute(v, 'expert', [(i, (i + copies) % n_expert) for i in range(n_...  5.81 us
    ppermute x9, waiting for transfers between devices, other_core(): return lax.ppermute(v, 'tensor', [(0, 1), (1, 0)])  2.46 us
    ppermute x9, waiting for transfers between devices, across(): return lax.ppermute(v, 'expert', [(i, i ^ d) for i in range(n_expert)])  2.18 us
  transfers between devices with their start and end apart: 20, of which 6 were waited for; matrix products, arithmetic and copies ran while one was open for 0% of the time, Pallas kernels for 17%

profile of v7, /device:TPU:0, one launch (start us, length us, event | category | flops | bytes accessed | tf_op | source)
XLA Modules:
  0.0 83.2 jit_solution(12035738540360123765)
XLA Ops:
  0.6 1.4 %pick_rows.1 = (bf16[8,3968]{1,0:T(8,128)(2,1)S(1)}, bf16[8,3968]{1,0:T(8,128)(2,1)S(1)}) custom-call(s32[1]{0:T(128)} %bitcast.e_ref, s32[4,16]{1,0:T(4,128)} %bitcast.5, bf16[4,16]{1,0:T(4,128)(2,1)} %bitcast.7, bf16[16,3072]{1,0:T(8,128)(2,1)} %tok_any.1, bf16[16,3072]{1,0:T(8,128)(2,1)} %grad_any.1), custom_call_target="tpu_custom_call" | custom-call | tf_op jit(solution)/shard_map/pick_rows/pallas_call | solution.py:93
  2.0 4.1 %collective-permute-start = (bf16[8,3968]{1,0:T(8,128)(2,1)S(1)}, bf16[8,3968]{1,0:T(8,128)(2,1)S(1)}, u32[]{:S(2)}, u32[]{:S(2)}) collective-permute-start(bf16[8,3968]{1,0:T(8,128)(2,1)S(1)} %get-tuple-element.32), channel_id=1, source_target_pairs={{0,8},{2,10},{4,12},{6,14},{8,0},{10,2},{12,4},{14,6},{1,9},{3,11}... | collective-permute-start | bytes 190472 | tf_op jit(solution)/shard_map/ppermute | solution.py:461
  6.1 0.0 collective-permute-start.7
  6.1 2.5 %collective-permute-start.5 = (bf16[8,3968]{1,0:T(8,128)(2,1)S(1)}, bf16[8,3968]{1,0:T(8,128)(2,1)S(1)}, u32[]{:S(2)}, u32[]{:S(2)}) collective-permute-start(bf16[8,3968]{1,0:T(8,128)(2,1)S(1)} %get-tuple-element.31.refs_0_), channel_id=1, source_target_pairs={{0,6},{2,4},{4,2},{6,0},{8,14},{10,12},{12,10},{14,8},{1,7},{3,5},... | collective-permute-start | bytes 190472 | tf_op jit(solution)/shard_map/ppermute | solution.py:464
  8.6 0.5 collective-permute-start.3
  9.1 0.5 collective-permute-start.1
  9.6 0.1 collective-permute-done.refs_1_
  9.7 0.0 collective-permute-start.8
  9.7 0.0 collective-permute-done.7.refs_8_
  9.7 2.5 %collective-permute-start.6 = (bf16[8,3968]{1,0:T(8,128)(2,1)S(1)}, bf16[8,3968]{1,0:T(8,128)(2,1)S(1)}, u32[]{:S(2)}, u32[]{:S(2)}) collective-permute-start(bf16[8,3968]{1,0:T(8,128)(2,1)S(1)} %collective-permute-done.refs_1_), channel_id=1, source_target_pairs={{0,6},{2,4},{4,2},{6,0},{8,14},{10,12},{12,10},{14,8},{1,7},{3,5},... | collective-permute-start | bytes 190472 | tf_op jit(solution)/shard_map/ppermute | solution.py:464
  12.2 0.0 collective-permute-done.5.refs_6_
  12.2 1.3 %collective-permute-start.4 = (bf16[8,3968]{1,0:T(8,128)(2,1)S(1)}, bf16[8,3968]{1,0:T(8,128)(2,1)S(1)}, u32[]{:S(2)}, u32[]{:S(2)}) collective-permute-start(bf16[8,3968]{1,0:T(8,128)(2,1)S(1)} %collective-permute-done.refs_1_), channel_id=1, source_target_pairs={{0,4},{2,6},{4,0},{6,2},{8,12},{10,14},{12,8},{14,10},{1,5},{3,7},... | collective-permute-start | bytes 190472 | tf_op jit(solution)/shard_map/ppermute | solution.py:464
  13.4 0.0 collective-permute-done.3.refs_4_
  13.4 1.5 %collective-permute-start.2 = (bf16[8,3968]{1,0:T(8,128)(2,1)S(1)}, bf16[8,3968]{1,0:T(8,128)(2,1)S(1)}, u32[]{:S(2)}, u32[]{:S(2)}) collective-permute-start(bf16[8,3968]{1,0:T(8,128)(2,1)S(1)} %collective-permute-done.refs_1_), channel_id=1, source_target_pairs={{0,2},{2,0},{4,6},{6,4},{8,10},{10,8},{12,14},{14,12},{1,3},{3,1},... | collective-permute-start | bytes 190472 | tf_op jit(solution)/shard_map/ppermute | solution.py:464
  14.9 0.0 collective-permute-done.1.refs_2_
  14.9 0.0 collective-permute-start.13
  14.9 0.0 collective-permute-done.8.refs_9_
  14.9 0.5 collective-permute-start.11
  15.5 0.0 collective-permute-done.6.refs_7_
  15.5 0.1 collective-permute-start.9
  15.5 0.9 %collective-permute-done.4.refs_5_ = bf16[8,3968]{1,0:T(8,128)(2,1)S(1)} collective-permute-done((bf16[8,3968]{1,0:T(8,128)(2,1)S(1)}, bf16[8,3968]{1,0:T(8,128)(2,1)S(1)}, u32[]{:S(2)}, u32[]{:S(2)}) %collective-permute-start.4) | collective-permute-done | bytes 63520 | tf_op jit(solution)/shard_map/ppermute | solution.py:464
  16.4 0.0 collective-permute-start.14
  16.4 1.3 %collective-permute-done.2.refs_3_ = bf16[8,3968]{1,0:T(8,128)(2,1)S(1)} collective-permute-done((bf16[8,3968]{1,0:T(8,128)(2,1)S(1)}, bf16[8,3968]{1,0:T(8,128)(2,1)S(1)}, u32[]{:S(2)}, u32[]{:S(2)}) %collective-permute-start.2) | collective-permute-done | bytes 63520 | tf_op jit(solution)/shard_map/ppermute | solution.py:464
  17.7 0.0 collective-permute-start.12
  17.7 0.0 collective-permute-done.13.refs_14_
  17.7 0.5 collective-permute-start.10
  18.2 0.0 collective-permute-done.11.refs_12_
  18.2 0.0 collective-permute-done.9.refs_10_
  18.2 0.0 collective-permute-done.14.refs_15_
  18.2 0.7 collective-permute-done.12.refs_13_
  18.9 0.2 collective-permute-done.10.refs_11_
  19.1 41.1 %expert_units.1 = (bf16[48,6144]{1,0:T(8,128)(2,1)S(1)}, bf16[1344,48]{1,0:T(8,128)(2,1)S(1)}, bf16[1344,48]{1,0:T(8,128)(2,1)S(1)}, f32[64,2048]{1,0:T(8,128)S(...) custom-call(s32[1]{0:T(128)} %bitcast.2.t_ref, bf16[8,3968]{1,0:T(8,128)(2,1)S(1)} %get-tuple-element.31.refs_0_, ...), custom_call_target="tpu_custom_call" | custom-call | flops 4756340736 | bytes 66060288 | tf_op jit(solution)/shard_map/expert_units/pallas_call | solution.py:284
  60.2 0.4 collective-permute-start.15
  60.7 1.6 %collective-permute-done.15.got_ref = f32[64,2048]{1,0:T(8,128)S(1)} collective-permute-done((f32[64,2048]{1,0:T(8,128)S(1)}, f32[64,2048]{1,0:T(8,128)S(1)}, u32[]{:S(2)}, u32[]{:S(2)}) %collective-permute-start.15) | collective-permute-done | bytes 524320 | tf_op jit(solution)/shard_map/ppermute | solution.py:467
  62.2 0.1 fold_cores.1
  62.3 1.6 %collective-permute-start.16 = (f32[16,2048]{1,0:T(8,128)S(1)}, f32[16,2048]{1,0:T(8,128)S(1)}, u32[]{:S(2)}, u32[]{:S(2)}) collective-permute-start(f32[16,2048]{1,0:T(8,128)S(1)} %get-tuple-element.41), channel_id=1, source_target_pairs={{0,2},{2,0},{4,6},{6,4},{8,10},{10,8},{12,14},{14,12},{1,3},{3,1},... | collective-permute-start | bytes 393224 | tf_op jit(solution)/shard_map/ppermute | solution.py:464
  63.8 0.3 collective-permute-start.17
  64.2 1.7 %collective-permute-start.18 = (f32[16,2048]{1,0:T(8,128)S(1)}, f32[16,2048]{1,0:T(8,128)S(1)}, u32[]{:S(2)}, u32[]{:S(2)}) collective-permute-start(f32[16,2048]{1,0:T(8,128)S(1)} %get-tuple-element.43), channel_id=1, source_target_pairs={{0,6},{2,4},{4,2},{6,0},{8,14},{10,12},{12,10},{14,8},{1,7},{3,5},... | collective-permute-start | bytes 393224 | tf_op jit(solution)/shard_map/ppermute | solution.py:464
  65.8 0.0 copy-start
  65.8 7.0 %grad_gate.1 = bf16[1344,6144]{1,0:T(8,128)(2,1)} custom-call(bf16[1344,48]{1,0:T(8,128)(2,1)S(1)} %get-tuple-element.39.refs_0_, bf16[48,6144]{1,0:T(8,128)(2,1)S(1)} %get-tuple-element.40.refs_1_), custom_call_target="tpu_custom_call" | custom-call | flops 792723456 | bytes 16515072 | tf_op jit(solution)/shard_map/grad_gate/pallas_call | solution.py:362
  72.9 0.0 collective-permute-done.16.refs_1_
  72.9 0.0 collective-permute-done.17.refs_2_
  72.9 0.0 collective-permute-done.18.refs_3_
  72.9 1.7 %collective-permute-start.19 = (f32[8,2048]{1,0:T(8,128)S(1)}, f32[8,2048]{1,0:T(8,128)S(1)}, u32[]{:S(2)}, u32[]{:S(2)}) collective-permute-start(f32[8,2048]{1,0:T(8,128)S(1)} %get-tuple-element.50), channel_id=1, source_target_pairs={{0,8},{2,10},{4,12},{6,14},{8,0},{10,2},{12,4},{14,6},{1,9},{3,11}... | collective-permute-start | bytes 196616 | tf_op jit(solution)/shard_map/ppermute | solution.py:461
  74.6 7.0 %grad_up.1 = bf16[1344,6144]{1,0:T(8,128)(2,1)} custom-call(bf16[1344,48]{1,0:T(8,128)(2,1)S(1)} %get-tuple-element.49.refs_0_, bf16[48,6144]{1,0:T(8,128)(2,1)S(1)} %get-tuple-element.40.refs_1_), custom_call_target="tpu_custom_call" | custom-call | flops 792723456 | bytes 16515072 | tf_op jit(solution)/shard_map/grad_up/pallas_call | solution.py:362
  81.7 0.0 collective-permute-done.19.got_ref
  81.7 0.0 copy-done
  81.7 1.5 %finish_tokens.1 = (bf16[16,3072]{1,0:T(8,128)(2,1)}, f32[4,16]{1,0:T(4,128)}) custom-call(s32[1]{0:T(128)} %bitcast.e_ref, s32[4,16]{1,0:T(4,128)S(1)} %bitcast.6, f32[8,2048]{1,0:T(8,128)S(1)} %get-tuple-element.48.mine_ref, f32[8,2048]{1,0:T(8,128)S(1)} %collective-permute-done.19.got_ref), custom_call_target="tpu_custom_call" | custom-call | tf_op jit(solution)/shard_map/finish_tokens/pallas_call | solution.py:442
  (1 shorter events, 0.0 us)
Async XLA Ops:
  2.0 7.7 %collective-permute-start = (bf16[8,3968]{1,0:T(8,128)(2,1)S(1)}, bf16[8,3968]{1,0:T(8,128)(2,1)S(1)}, u32[]{:S(2)}, u32[]{:S(2)}) collective-permute-start(bf16[8,3968]{1,0:T(8,128)(2,1)S(1)} %get-tuple-element.32), channel_id=1, source_target_pairs={{0,8},{2,10},{4,12},{6,14},{8,0},{10,2},{12,4},{14,6},{1,9},{3,11}... | collective-permute-start | bytes 190472 | tf_op jit(solution)/shard_map/ppermute | solution.py:461
  6.1 3.6 %collective-permute-start.7 = (bf16[8,3968]{1,0:T(8,128)(2,1)S(1)}, bf16[8,3968]{1,0:T(8,128)(2,1)S(1)}, u32[]{:S(2)}, u32[]{:S(2)}) collective-permute-start(bf16[8,3968]{1,0:T(8,128)(2,1)S(1)} %get-tuple-element.31.refs_0_), channel_id=1, source_target_pairs={{0,1},{1,0},{2,3},{3,2},{4,5},{5,4},{6,7},{7,6},{8,9},{9,8},{10,11... | collective-permute-start | bytes 190472 | tf_op jit(solution)/shard_map/ppermute | solution.py:467
  6.1 6.1 %collective-permute-start.5 = (bf16[8,3968]{1,0:T(8,128)(2,1)S(1)}, bf16[8,3968]{1,0:T(8,128)(2,1)S(1)}, u32[]{:S(2)}, u32[]{:S(2)}) collective-permute-start(bf16[8,3968]{1,0:T(8,128)(2,1)S(1)} %get-tuple-element.31.refs_0_), channel_id=1, source_target_pairs={{0,6},{2,4},{4,2},{6,0},{8,14},{10,12},{12,10},{14,8},{1,7},{3,5},... | collective-permute-start | bytes 190472 | tf_op jit(solution)/shard_map/ppermute | solution.py:464
  8.6 4.8 %collective-permute-start.3 = (bf16[8,3968]{1,0:T(8,128)(2,1)S(1)}, bf16[8,3968]{1,0:T(8,128)(2,1)S(1)}, u32[]{:S(2)}, u32[]{:S(2)}) collective-permute-start(bf16[8,3968]{1,0:T(8,128)(2,1)S(1)} %get-tuple-element.31.refs_0_), channel_id=1, source_target_pairs={{0,4},{2,6},{4,0},{6,2},{8,12},{10,14},{12,8},{14,10},{1,5},{3,7},... | collective-permute-start | bytes 190472 | tf_op jit(solution)/shard_map/ppermute | solution.py:464
  9.1 5.9 %collective-permute-start.1 = (bf16[8,3968]{1,0:T(8,128)(2,1)S(1)}, bf16[8,3968]{1,0:T(8,128)(2,1)S(1)}, u32[]{:S(2)}, u32[]{:S(2)}) collective-permute-start(bf16[8,3968]{1,0:T(8,128)(2,1)S(1)} %get-tuple-element.31.refs_0_), channel_id=1, source_target_pairs={{0,2},{2,0},{4,6},{6,4},{8,10},{10,8},{12,14},{14,12},{1,3},{3,1},... | collective-permute-start | bytes 190472 | tf_op jit(solution)/shard_map/ppermute | solution.py:464
  9.7 5.2 %collective-permute-start.8 = (bf16[8,3968]{1,0:T(8,128)(2,1)S(1)}, bf16[8,3968]{1,0:T(8,128)(2,1)S(1)}, u32[]{:S(2)}, u32[]{:S(2)}) collective-permute-start(bf16[8,3968]{1,0:T(8,128)(2,1)S(1)} %collective-permute-done.refs_1_), channel_id=1, source_target_pairs={{0,1},{1,0},{2,3},{3,2},{4,5},{5,4},{6,7},{7,6},{8,9},{9,8},{10,11... | collective-permute-start | bytes 190472 | tf_op jit(solution)/shard_map/ppermute | solution.py:467
  9.7 5.8 %collective-permute-start.6 = (bf16[8,3968]{1,0:T(8,128)(2,1)S(1)}, bf16[8,3968]{1,0:T(8,128)(2,1)S(1)}, u32[]{:S(2)}, u32[]{:S(2)}) collective-permute-start(bf16[8,3968]{1,0:T(8,128)(2,1)S(1)} %collective-permute-done.refs_1_), channel_id=1, source_target_pairs={{0,6},{2,4},{4,2},{6,0},{8,14},{10,12},{12,10},{14,8},{1,7},{3,5},... | collective-permute-start | bytes 190472 | tf_op jit(solution)/shard_map/ppermute | solution.py:464
  12.2 4.2 %collective-permute-start.4 = (bf16[8,3968]{1,0:T(8,128)(2,1)S(1)}, bf16[8,3968]{1,0:T(8,128)(2,1)S(1)}, u32[]{:S(2)}, u32[]{:S(2)}) collective-permute-start(bf16[8,3968]{1,0:T(8,128)(2,1)S(1)} %collective-permute-done.refs_1_), channel_id=1, source_target_pairs={{0,4},{2,6},{4,0},{6,2},{8,12},{10,14},{12,8},{14,10},{1,5},{3,7},... | collective-permute-start | bytes 190472 | tf_op jit(solution)/shard_map/ppermute | solution.py:464
  13.4 4.2 %collective-permute-start.2 = (bf16[8,3968]{1,0:T(8,128)(2,1)S(1)}, bf16[8,3968]{1,0:T(8,128)(2,1)S(1)}, u32[]{:S(2)}, u32[]{:S(2)}) collective-permute-start(bf16[8,3968]{1,0:T(8,128)(2,1)S(1)} %collective-permute-done.refs_1_), channel_id=1, source_target_pairs={{0,2},{2,0},{4,6},{6,4},{8,10},{10,8},{12,14},{14,12},{1,3},{3,1},... | collective-permute-start | bytes 190472 | tf_op jit(solution)/shard_map/ppermute | solution.py:464
  14.9 2.8 %collective-permute-start.13 = (bf16[8,3968]{1,0:T(8,128)(2,1)S(1)}, bf16[8,3968]{1,0:T(8,128)(2,1)S(1)}, u32[]{:S(2)}, u32[]{:S(2)}) collective-permute-start(bf16[8,3968]{1,0:T(8,128)(2,1)S(1)} %collective-permute-done.5.refs_6_), channel_id=1, source_target_pairs={{0,1},{1,0},{2,3},{3,2},{4,5},{5,4},{6,7},{7,6},{8,9},{9,8},{10,11... | collective-permute-start | bytes 190472 | tf_op jit(solution)/shard_map/ppermute | solution.py:467
  14.9 3.3 %collective-permute-start.11 = (bf16[8,3968]{1,0:T(8,128)(2,1)S(1)}, bf16[8,3968]{1,0:T(8,128)(2,1)S(1)}, u32[]{:S(2)}, u32[]{:S(2)}) collective-permute-start(bf16[8,3968]{1,0:T(8,128)(2,1)S(1)} %collective-permute-done.3.refs_4_), channel_id=1, source_target_pairs={{0,1},{1,0},{2,3},{3,2},{4,5},{5,4},{6,7},{7,6},{8,9},{9,8},{10,11... | collective-permute-start | bytes 190472 | tf_op jit(solution)/shard_map/ppermute | solution.py:467
  15.5 2.8 %collective-permute-start.9 = (bf16[8,3968]{1,0:T(8,128)(2,1)S(1)}, bf16[8,3968]{1,0:T(8,128)(2,1)S(1)}, u32[]{:S(2)}, u32[]{:S(2)}) collective-permute-start(bf16[8,3968]{1,0:T(8,128)(2,1)S(1)} %collective-permute-done.1.refs_2_), channel_id=1, source_target_pairs={{0,1},{1,0},{2,3},{3,2},{4,5},{5,4},{6,7},{7,6},{8,9},{9,8},{10,11... | collective-permute-start | bytes 190472 | tf_op jit(solution)/shard_map/ppermute | solution.py:467
  16.4 1.8 %collective-permute-start.14 = (bf16[8,3968]{1,0:T(8,128)(2,1)S(1)}, bf16[8,3968]{1,0:T(8,128)(2,1)S(1)}, u32[]{:S(2)}, u32[]{:S(2)}) collective-permute-start(bf16[8,3968]{1,0:T(8,128)(2,1)S(1)} %collective-permute-done.6.refs_7_), channel_id=1, source_target_pairs={{0,1},{1,0},{2,3},{3,2},{4,5},{5,4},{6,7},{7,6},{8,9},{9,8},{10,11... | collective-permute-start | bytes 190472 | tf_op jit(solution)/shard_map/ppermute | solution.py:467
  17.7 1.3 %collective-permute-start.12 = (bf16[8,3968]{1,0:T(8,128)(2,1)S(1)}, bf16[8,3968]{1,0:T(8,128)(2,1)S(1)}, u32[]{:S(2)}, u32[]{:S(2)}) collective-permute-start(bf16[8,3968]{1,0:T(8,128)(2,1)S(1)} %collective-permute-done.4.refs_5_), channel_id=1, source_target_pairs={{0,1},{1,0},{2,3},{3,2},{4,5},{5,4},{6,7},{7,6},{8,9},{9,8},{10,11... | collective-permute-start | bytes 190472 | tf_op jit(solution)/shard_map/ppermute | solution.py:467
  17.7 1.4 %collective-permute-start.10 = (bf16[8,3968]{1,0:T(8,128)(2,1)S(1)}, bf16[8,3968]{1,0:T(8,128)(2,1)S(1)}, u32[]{:S(2)}, u32[]{:S(2)}) collective-permute-start(bf16[8,3968]{1,0:T(8,128)(2,1)S(1)} %collective-permute-done.2.refs_3_), channel_id=1, source_target_pairs={{0,1},{1,0},{2,3},{3,2},{4,5},{5,4},{6,7},{7,6},{8,9},{9,8},{10,11... | collective-permute-start | bytes 190472 | tf_op jit(solution)/shard_map/ppermute | solution.py:467
  60.2 2.0 %collective-permute-start.15 = (f32[64,2048]{1,0:T(8,128)S(1)}, f32[64,2048]{1,0:T(8,128)S(1)}, u32[]{:S(2)}, u32[]{:S(2)}) collective-permute-start(f32[64,2048]{1,0:T(8,128)S(1)} %get-tuple-element.36), channel_id=1, source_target_pairs={{0,1},{1,0},{2,3},{3,2},{4,5},{5,4},{6,7},{7,6},{8,9},{9,8},{10,11... | collective-permute-start | bytes 1572872 | tf_op jit(solution)/shard_map/ppermute | solution.py:467
  62.3 10.6 %collective-permute-start.16 = (f32[16,2048]{1,0:T(8,128)S(1)}, f32[16,2048]{1,0:T(8,128)S(1)}, u32[]{:S(2)}, u32[]{:S(2)}) collective-permute-start(f32[16,2048]{1,0:T(8,128)S(1)} %get-tuple-element.41), channel_id=1, source_target_pairs={{0,2},{2,0},{4,6},{6,4},{8,10},{10,8},{12,14},{14,12},{1,3},{3,1},... | collective-permute-start | bytes 393224 | tf_op jit(solution)/shard_map/ppermute | solution.py:464
  63.8 9.0 %collective-permute-start.17 = (f32[16,2048]{1,0:T(8,128)S(1)}, f32[16,2048]{1,0:T(8,128)S(1)}, u32[]{:S(2)}, u32[]{:S(2)}) collective-permute-start(f32[16,2048]{1,0:T(8,128)S(1)} %get-tuple-element.42), channel_id=1, source_target_pairs={{0,4},{2,6},{4,0},{6,2},{8,12},{10,14},{12,8},{14,10},{1,5},{3,7},... | collective-permute-start | bytes 393224 | tf_op jit(solution)/shard_map/ppermute | solution.py:464
  64.2 8.7 %collective-permute-start.18 = (f32[16,2048]{1,0:T(8,128)S(1)}, f32[16,2048]{1,0:T(8,128)S(1)}, u32[]{:S(2)}, u32[]{:S(2)}) collective-permute-start(f32[16,2048]{1,0:T(8,128)S(1)} %get-tuple-element.43), channel_id=1, source_target_pairs={{0,6},{2,4},{4,2},{6,0},{8,14},{10,12},{12,10},{14,8},{1,7},{3,5},... | collective-permute-start | bytes 393224 | tf_op jit(solution)/shard_map/ppermute | solution.py:464
  65.8 15.8 %copy-start = (s32[16,4]{0,1:T(4,128)S(1)}, s32[16,4]{0,1:T(4,128)}, u32[]{:S(2)}) copy-start(s32[16,4]{0,1:T(4,128)} %param.9) | copy-start | bytes 772
  72.9 8.7 %collective-permute-start.19 = (f32[8,2048]{1,0:T(8,128)S(1)}, f32[8,2048]{1,0:T(8,128)S(1)}, u32[]{:S(2)}, u32[]{:S(2)}) collective-permute-start(f32[8,2048]{1,0:T(8,128)S(1)} %get-tuple-element.50), channel_id=1, source_target_pairs={{0,8},{2,10},{4,12},{6,14},{8,0},{10,2},{12,4},{14,6},{1,9},{3,11}... | collective-permute-start | bytes 196616 | tf_op jit(solution)/shard_map/ppermute | solution.py:461

commit v8 on v7

--- a/solution.py
+++ b/solution.py
@@ -164,8 +164,12 @@
         slot = lax.rem(i, slots)
         return pltpu.make_async_copy(ring.at[slot], down_ref.at[:, columns(i)], sent.at[slot])
 
-    for n in range(2):
-        load(0, n).start()
+    def start(i):
+        load(i, 0).start()
+        load(i, 1).start()
+        load_down(i).start()
+
+    start(0)
     held[...] = jnp.zeros_like(held)
     factor[...] = jnp.zeros_like(factor)
     for n, ref in enumerate(mine):
@@ -173,47 +177,36 @@
     for side, out in enumerate((x_ref, g_ref)):
         for group, at in ((mine, t), (theirs, 1 - t)):
             assemble(group, held, out, pl.multiple_of(at * width, width), side)
-        if side == 0:
-            for i in range(1, min(ahead, steps)):
-                for n in range(2):
-                    load(i, n).start()
-
-    def add_to(out, i, w, x):
-        more = lax.dot_general(w, x, NT, preferred_element_type=F32)
-        out[...] = jnp.where(i == 0, more, out[...] + more)
+    for i in range(1, min(ahead, steps)):
+        start(i)
+
+    def three(i):
+        cols = columns(i)
+        x = x_ref[:, cols]
+        return (
+            lambda: lax.dot_general(wg_ref[:, cols], x, NT, preferred_element_type=F32),
+            lambda: lax.dot_general(wu_ref[:, cols], x, NT, preferred_element_type=F32),
+            lambda: lax.dot_general(ring[lax.rem(i, slots)], g_ref[:, cols], NT, preferred_element_type=F32),
+        )
+
+    sums = (h_ref, u_ref, da_ref)
+    waits = lambda i: (load(i, 0), load(i, 1), load_down(i))
+    for wait, dot, out in zip(waits(0), three(0), sums):
+        wait.wait()
+        out[...] = dot()
 
     def up_step(i, carry):
-        x = x_ref[:, columns(i)]
-        load(i, 0).wait()
-        add_to(h_ref, i, wg_ref[:, columns(i)], x)
-        load(i, 1).wait()
-
-        @pl.when(i + ahead < steps)
+        @pl.when(i + ahead - 1 < steps)
         def _():
-            for n in range(2):
-                load(i + ahead, n).start()
-
-        @pl.when(i + ahead >= steps)
-        def _():
-            load_down(i + ahead - steps).start()
-
-        add_to(u_ref, i, wu_ref[:, columns(i)], x)
+            start(i + ahead - 1)
+
+        for wait in waits(i):
+            wait.wait()
+        for dot, out in zip(three(i), sums):
+            out[...] += dot()
         return carry
 
-    lax.fori_loop(0, steps, up_step, 0)
-
-    def down_step(i, carry):
-        g = g_ref[:, columns(i)]
-        load_down(i).wait()
-
-        @pl.when(i + ahead < steps)
-        def _():
-            load_down(i + ahead).start()
-
-        add_to(da_ref, i, ring[lax.rem(i, slots)], g)
-        return carry
-
-    lax.fori_loop(0, steps, down_step, 0)
+    lax.fori_loop(1, steps, up_step, 0)
 
     weight = factor[...].T[:1, :]
 
@@ -235,12 +228,9 @@
         dur_ref[:, at] = du.T.astype(BF16)
         return total + jnp.sum(act * da, axis=0, keepdims=True)
 
-    whole = hidden // LANES
-    total = lax.fori_loop(
-        0, whole, lambda i, v: units(pl.multiple_of(i * LANES, LANES), LANES, v), jnp.zeros((1, rows), F32)
-    )
-    if hidden % LANES:
-        total = units(whole * LANES, hidden % LANES, total)
+    total = jnp.zeros((1, rows), F32)
+    for begin in range(0, hidden, LANES):
+        total = units(begin, min(LANES, hidden - begin), total)
     gates = jnp.broadcast_to(total, (LANES, rows)).T
     tile = tile_of(hidden, 448)
 
@@ -277,7 +267,7 @@
     rows = -(-pieces * CAP // 16) * 16
     chunk = chunk_of(width, 768)
     steps = depth // chunk
-    ahead = 2
+    ahead = 3
     slots = 4
     unit = jax.ShapeDtypeStruct((hidden, rows), BF16)
     packed = jax.ShapeDtypeStruct((pieces * SUBS, width // 2 + width // SUBS + LANES), F32)

time: 83.4 us -> 72.1 us (0.86)
  Pallas kernels: 58.2 us -> 46.9 us
    pallas_call x1, Pallas kernels: 41.1 us -> 29.8 us  [expert_units(): pl.pallas_call(functools.partial(experts_body, pieces, chunk, ahead), out...]
  transfers between devices with their start and end apart: 20 -> 20, of which waited for: 6 -> 6; matrix products, arithmetic and copies ran while one was open for 0% -> 0% of each run, Pallas kernels for 17% -> 20%
where the time goes in v8:
time: 72.1 us; the launch traced here: 71.9 us
  Pallas kernels  46.9 us (65%)
  starting transfers between devices  19.6 us (27%)
  waiting for transfers between devices  4.74 us (7%)
  between operations  0.74 us (1%)
    pallas_call x1, Pallas kernels, expert_units(): pl.pallas_call(functools.partial(experts_body, pieces, chunk, ahead), out...  29.8 us
    pallas_call x2, Pallas kernels, weight_grads(): pl.pallas_call(functools.partial(weights_body, count, chunk), out_shape=[...  14 us
    ppermute x9, starting transfers between devices, across(): return lax.ppermute(v, 'expert', [(i, i ^ d) for i in range(n_expert)])  12.3 us
    ppermute x2, starting transfers between devices, partner(): lax.ppermute(v, 'expert', [(i, (i + copies) % n_expert) for i in range(n_...  5.81 us
    ppermute x9, waiting for transfers between devices, other_core(): return lax.ppermute(v, 'tensor', [(0, 1), (1, 0)])  2.46 us
    ppermute x9, waiting for transfers between devices, across(): return lax.ppermute(v, 'expert', [(i, i ^ d) for i in range(n_expert)])  2.18 us
    pallas_call x1, Pallas kernels, finish(): pl.pallas_call(finish_body, out_shape=(jax.ShapeDtypeStruct((toks, width)...  1.54 us
    ppermute x9, starting transfers between devices, other_core(): return lax.ppermute(v, 'tensor', [(0, 1), (1, 0)])  1.51 us
  transfers between devices with their start and end apart: 20, of which 6 were waited for; matrix products, arithmetic and copies ran while one was open for 0% of the time, Pallas kernels for 20%

profile of v8, /device:TPU:0, one launch (start us, length us, event | category | flops | bytes accessed | tf_op | source)
XLA Modules:
  0.0 71.9 jit_solution(1462942629176111319)
XLA Ops:
  0.6 1.4 %pick_rows.1 = (bf16[8,3968]{1,0:T(8,128)(2,1)S(1)}, bf16[8,3968]{1,0:T(8,128)(2,1)S(1)}) custom-call(s32[1]{0:T(128)} %bitcast.e_ref, s32[4,16]{1,0:T(4,128)} %bitcast.5, bf16[4,16]{1,0:T(4,128)(2,1)} %bitcast.7, bf16[16,3072]{1,0:T(8,128)(2,1)} %tok_any.1, bf16[16,3072]{1,0:T(8,128)(2,1)} %grad_any.1), custom_call_target="tpu_custom_call" | custom-call | tf_op jit(solution)/shard_map/pick_rows/pallas_call | solution.py:93
  2.0 4.1 %collective-permute-start = (bf16[8,3968]{1,0:T(8,128)(2,1)S(1)}, bf16[8,3968]{1,0:T(8,128)(2,1)S(1)}, u32[]{:S(2)}, u32[]{:S(2)}) collective-permute-start(bf16[8,3968]{1,0:T(8,128)(2,1)S(1)} %get-tuple-element.32), channel_id=1, source_target_pairs={{0,8},{2,10},{4,12},{6,14},{8,0},{10,2},{12,4},{14,6},{1,9},{3,11}... | collective-permute-start | bytes 190472 | tf_op jit(solution)/shard_map/ppermute | solution.py:451
  6.1 0.0 collective-permute-start.7
  6.1 2.5 %collective-permute-start.5 = (bf16[8,3968]{1,0:T(8,128)(2,1)S(1)}, bf16[8,3968]{1,0:T(8,128)(2,1)S(1)}, u32[]{:S(2)}, u32[]{:S(2)}) collective-permute-start(bf16[8,3968]{1,0:T(8,128)(2,1)S(1)} %get-tuple-element.31.refs_0_), channel_id=1, source_target_pairs={{0,6},{2,4},{4,2},{6,0},{8,14},{10,12},{12,10},{14,8},{1,7},{3,5},... | collective-permute-start | bytes 190472 | tf_op jit(solution)/shard_map/ppermute | solution.py:454
  8.6 0.5 collective-permute-start.3
  9.1 0.5 collective-permute-start.1
  9.6 0.1 collective-permute-done.refs_1_
  9.7 0.0 collective-permute-start.8
  9.7 0.0 collective-permute-done.7.refs_8_
  9.7 2.5 %collective-permute-start.6 = (bf16[8,3968]{1,0:T(8,128)(2,1)S(1)}, bf16[8,3968]{1,0:T(8,128)(2,1)S(1)}, u32[]{:S(2)}, u32[]{:S(2)}) collective-permute-start(bf16[8,3968]{1,0:T(8,128)(2,1)S(1)} %collective-permute-done.refs_1_), channel_id=1, source_target_pairs={{0,6},{2,4},{4,2},{6,0},{8,14},{10,12},{12,10},{14,8},{1,7},{3,5},... | collective-permute-start | bytes 190472 | tf_op jit(solution)/shard_map/ppermute | solution.py:454
  12.2 0.0 collective-permute-done.5.refs_6_
  12.2 1.3 %collective-permute-start.4 = (bf16[8,3968]{1,0:T(8,128)(2,1)S(1)}, bf16[8,3968]{1,0:T(8,128)(2,1)S(1)}, u32[]{:S(2)}, u32[]{:S(2)}) collective-permute-start(bf16[8,3968]{1,0:T(8,128)(2,1)S(1)} %collective-permute-done.refs_1_), channel_id=1, source_target_pairs={{0,4},{2,6},{4,0},{6,2},{8,12},{10,14},{12,8},{14,10},{1,5},{3,7},... | collective-permute-start | bytes 190472 | tf_op jit(solution)/shard_map/ppermute | solution.py:454
  13.4 0.0 collective-permute-done.3.refs_4_
  13.4 1.5 %collective-permute-start.2 = (bf16[8,3968]{1,0:T(8,128)(2,1)S(1)}, bf16[8,3968]{1,0:T(8,128)(2,1)S(1)}, u32[]{:S(2)}, u32[]{:S(2)}) collective-permute-start(bf16[8,3968]{1,0:T(8,128)(2,1)S(1)} %collective-permute-done.refs_1_), channel_id=1, source_target_pairs={{0,2},{2,0},{4,6},{6,4},{8,10},{10,8},{12,14},{14,12},{1,3},{3,1},... | collective-permute-start | bytes 190472 | tf_op jit(solution)/shard_map/ppermute | solution.py:454
  14.9 0.0 collective-permute-done.1.refs_2_
  14.9 0.0 collective-permute-start.13
  14.9 0.0 collective-permute-done.8.refs_9_
  14.9 0.5 collective-permute-start.11
  15.5 0.0 collective-permute-done.6.refs_7_
  15.5 0.1 collective-permute-start.9
  15.5 0.9 %collective-permute-done.4.refs_5_ = bf16[8,3968]{1,0:T(8,128)(2,1)S(1)} collective-permute-done((bf16[8,3968]{1,0:T(8,128)(2,1)S(1)}, bf16[8,3968]{1,0:T(8,128)(2,1)S(1)}, u32[]{:S(2)}, u32[]{:S(2)}) %collective-permute-start.4) | collective-permute-done | bytes 63520 | tf_op jit(solution)/shard_map/ppermute | solution.py:454
  16.4 0.0 collective-permute-start.14
  16.4 1.3 %collective-permute-done.2.refs_3_ = bf16[8,3968]{1,0:T(8,128)(2,1)S(1)} collective-permute-done((bf16[8,3968]{1,0:T(8,128)(2,1)S(1)}, bf16[8,3968]{1,0:T(8,128)(2,1)S(1)}, u32[]{:S(2)}, u32[]{:S(2)}) %collective-permute-start.2) | collective-permute-done | bytes 63520 | tf_op jit(solution)/shard_map/ppermute | solution.py:454
  17.7 0.0 collective-permute-start.12
  17.7 0.0 collective-permute-done.13.refs_14_
  17.7 0.5 collective-permute-start.10
  18.2 0.0 collective-permute-done.11.refs_12_
  18.2 0.0 collective-permute-done.9.refs_10_
  18.2 0.0 collective-permute-done.14.refs_15_
  18.2 0.7 %collective-permute-done.12.refs_13_ = bf16[8,3968]{1,0:T(8,128)(2,1)S(1)} collective-permute-done((bf16[8,3968]{1,0:T(8,128)(2,1)S(1)}, bf16[8,3968]{1,0:T(8,128)(2,1)S(1)}, u32[]{:S(2)}, u32[]{:S(2)}) %collective-permute-start.12) | collective-permute-done | bytes 63520 | tf_op jit(solution)/shard_map/ppermute | solution.py:457
  18.9 0.2 collective-permute-done.10.refs_11_
  19.1 29.8 %expert_units.1 = (bf16[48,6144]{1,0:T(8,128)(2,1)S(1)}, bf16[1344,48]{1,0:T(8,128)(2,1)S(1)}, bf16[1344,48]{1,0:T(8,128)(2,1)S(1)}, f32[64,2048]{1,0:T(8,128)S(...) custom-call(s32[1]{0:T(128)} %bitcast.2.t_ref, bf16[8,3968]{1,0:T(8,128)(2,1)S(1)} %get-tuple-element.31.refs_0_, ...), custom_call_target="tpu_custom_call" | custom-call | flops 4756340736 | bytes 66060288 | tf_op jit(solution)/shard_map/expert_units/pallas_call | solution.py:274
  48.9 0.4 collective-permute-start.15
  49.4 1.6 %collective-permute-done.15.got_ref = f32[64,2048]{1,0:T(8,128)S(1)} collective-permute-done((f32[64,2048]{1,0:T(8,128)S(1)}, f32[64,2048]{1,0:T(8,128)S(1)}, u32[]{:S(2)}, u32[]{:S(2)}) %collective-permute-start.15) | collective-permute-done | bytes 524320 | tf_op jit(solution)/shard_map/ppermute | solution.py:457
  50.9 0.1 fold_cores.1
  51.0 1.5 %collective-permute-start.16 = (f32[16,2048]{1,0:T(8,128)S(1)}, f32[16,2048]{1,0:T(8,128)S(1)}, u32[]{:S(2)}, u32[]{:S(2)}) collective-permute-start(f32[16,2048]{1,0:T(8,128)S(1)} %get-tuple-element.41), channel_id=1, source_target_pairs={{0,2},{2,0},{4,6},{6,4},{8,10},{10,8},{12,14},{14,12},{1,3},{3,1},... | collective-permute-start | bytes 393224 | tf_op jit(solution)/shard_map/ppermute | solution.py:454
  52.5 0.3 collective-permute-start.17
  52.9 1.7 %collective-permute-start.18 = (f32[16,2048]{1,0:T(8,128)S(1)}, f32[16,2048]{1,0:T(8,128)S(1)}, u32[]{:S(2)}, u32[]{:S(2)}) collective-permute-start(f32[16,2048]{1,0:T(8,128)S(1)} %get-tuple-element.43), channel_id=1, source_target_pairs={{0,6},{2,4},{4,2},{6,0},{8,14},{10,12},{12,10},{14,8},{1,7},{3,5},... | collective-permute-start | bytes 393224 | tf_op jit(solution)/shard_map/ppermute | solution.py:454
  54.5 0.0 copy-start
  54.5 7.0 %grad_gate.1 = bf16[1344,6144]{1,0:T(8,128)(2,1)} custom-call(bf16[1344,48]{1,0:T(8,128)(2,1)S(1)} %get-tuple-element.39.refs_0_, bf16[48,6144]{1,0:T(8,128)(2,1)S(1)} %get-tuple-element.40.refs_1_), custom_call_target="tpu_custom_call" | custom-call | flops 792723456 | bytes 16515072 | tf_op jit(solution)/shard_map/grad_gate/pallas_call | solution.py:352
  61.6 0.0 collective-permute-done.16.refs_1_
  61.6 0.0 collective-permute-done.17.refs_2_
  61.6 0.0 collective-permute-done.18.refs_3_
  61.6 1.7 %collective-permute-start.19 = (f32[8,2048]{1,0:T(8,128)S(1)}, f32[8,2048]{1,0:T(8,128)S(1)}, u32[]{:S(2)}, u32[]{:S(2)}) collective-permute-start(f32[8,2048]{1,0:T(8,128)S(1)} %get-tuple-element.50), channel_id=1, source_target_pairs={{0,8},{2,10},{4,12},{6,14},{8,0},{10,2},{12,4},{14,6},{1,9},{3,11}... | collective-permute-start | bytes 196616 | tf_op jit(solution)/shard_map/ppermute | solution.py:451
  63.3 7.0 %grad_up.1 = bf16[1344,6144]{1,0:T(8,128)(2,1)} custom-call(bf16[1344,48]{1,0:T(8,128)(2,1)S(1)} %get-tuple-element.49.refs_0_, bf16[48,6144]{1,0:T(8,128)(2,1)S(1)} %get-tuple-element.40.refs_1_), custom_call_target="tpu_custom_call" | custom-call | flops 792723456 | bytes 16515072 | tf_op jit(solution)/shard_map/grad_up/pallas_call | solution.py:352
  70.4 0.0 collective-permute-done.19.got_ref
  70.4 0.0 copy-done
  70.4 1.5 %finish_tokens.1 = (bf16[16,3072]{1,0:T(8,128)(2,1)}, f32[4,16]{1,0:T(4,128)}) custom-call(s32[1]{0:T(128)} %bitcast.e_ref, s32[4,16]{1,0:T(4,128)S(1)} %bitcast.6, f32[8,2048]{1,0:T(8,128)S(1)} %get-tuple-element.48.mine_ref, f32[8,2048]{1,0:T(8,128)S(1)} %collective-permute-done.19.got_ref), custom_call_target="tpu_custom_call" | custom-call | tf_op jit(solution)/shard_map/finish_tokens/pallas_call | solution.py:432
  (1 shorter events, 0.0 us)
Async XLA Ops:
  2.0 7.7 %collective-permute-start = (bf16[8,3968]{1,0:T(8,128)(2,1)S(1)}, bf16[8,3968]{1,0:T(8,128)(2,1)S(1)}, u32[]{:S(2)}, u32[]{:S(2)}) collective-permute-start(bf16[8,3968]{1,0:T(8,128)(2,1)S(1)} %get-tuple-element.32), channel_id=1, source_target_pairs={{0,8},{2,10},{4,12},{6,14},{8,0},{10,2},{12,4},{14,6},{1,9},{3,11}... | collective-permute-start | bytes 190472 | tf_op jit(solution)/shard_map/ppermute | solution.py:451
  6.1 3.6 %collective-permute-start.7 = (bf16[8,3968]{1,0:T(8,128)(2,1)S(1)}, bf16[8,3968]{1,0:T(8,128)(2,1)S(1)}, u32[]{:S(2)}, u32[]{:S(2)}) collective-permute-start(bf16[8,3968]{1,0:T(8,128)(2,1)S(1)} %get-tuple-element.31.refs_0_), channel_id=1, source_target_pairs={{0,1},{1,0},{2,3},{3,2},{4,5},{5,4},{6,7},{7,6},{8,9},{9,8},{10,11... | collective-permute-start | bytes 190472 | tf_op jit(solution)/shard_map/ppermute | solution.py:457
  6.1 6.1 %collective-permute-start.5 = (bf16[8,3968]{1,0:T(8,128)(2,1)S(1)}, bf16[8,3968]{1,0:T(8,128)(2,1)S(1)}, u32[]{:S(2)}, u32[]{:S(2)}) collective-permute-start(bf16[8,3968]{1,0:T(8,128)(2,1)S(1)} %get-tuple-element.31.refs_0_), channel_id=1, source_target_pairs={{0,6},{2,4},{4,2},{6,0},{8,14},{10,12},{12,10},{14,8},{1,7},{3,5},... | collective-permute-start | bytes 190472 | tf_op jit(solution)/shard_map/ppermute | solution.py:454
  8.6 4.8 %collective-permute-start.3 = (bf16[8,3968]{1,0:T(8,128)(2,1)S(1)}, bf16[8,3968]{1,0:T(8,128)(2,1)S(1)}, u32[]{:S(2)}, u32[]{:S(2)}) collective-permute-start(bf16[8,3968]{1,0:T(8,128)(2,1)S(1)} %get-tuple-element.31.refs_0_), channel_id=1, source_target_pairs={{0,4},{2,6},{4,0},{6,2},{8,12},{10,14},{12,8},{14,10},{1,5},{3,7},... | collective-permute-start | bytes 190472 | tf_op jit(solution)/shard_map/ppermute | solution.py:454
  9.1 5.9 %collective-permute-start.1 = (bf16[8,3968]{1,0:T(8,128)(2,1)S(1)}, bf16[8,3968]{1,0:T(8,128)(2,1)S(1)}, u32[]{:S(2)}, u32[]{:S(2)}) collective-permute-start(bf16[8,3968]{1,0:T(8,128)(2,1)S(1)} %get-tuple-element.31.refs_0_), channel_id=1, source_target_pairs={{0,2},{2,0},{4,6},{6,4},{8,10},{10,8},{12,14},{14,12},{1,3},{3,1},... | collective-permute-start | bytes 190472 | tf_op jit(solution)/shard_map/ppermute | solution.py:454
  9.7 5.2 %collective-permute-start.8 = (bf16[8,3968]{1,0:T(8,128)(2,1)S(1)}, bf16[8,3968]{1,0:T(8,128)(2,1)S(1)}, u32[]{:S(2)}, u32[]{:S(2)}) collective-permute-start(bf16[8,3968]{1,0:T(8,128)(2,1)S(1)} %collective-permute-done.refs_1_), channel_id=1, source_target_pairs={{0,1},{1,0},{2,3},{3,2},{4,5},{5,4},{6,7},{7,6},{8,9},{9,8},{10,11... | collective-permute-start | bytes 190472 | tf_op jit(solution)/shard_map/ppermute | solution.py:457
  9.7 5.8 %collective-permute-start.6 = (bf16[8,3968]{1,0:T(8,128)(2,1)S(1)}, bf16[8,3968]{1,0:T(8,128)(2,1)S(1)}, u32[]{:S(2)}, u32[]{:S(2)}) collective-permute-start(bf16[8,3968]{1,0:T(8,128)(2,1)S(1)} %collective-permute-done.refs_1_), channel_id=1, source_target_pairs={{0,6},{2,4},{4,2},{6,0},{8,14},{10,12},{12,10},{14,8},{1,7},{3,5},... | collective-permute-start | bytes 190472 | tf_op jit(solution)/shard_map/ppermute | solution.py:454
  12.2 4.2 %collective-permute-start.4 = (bf16[8,3968]{1,0:T(8,128)(2,1)S(1)}, bf16[8,3968]{1,0:T(8,128)(2,1)S(1)}, u32[]{:S(2)}, u32[]{:S(2)}) collective-permute-start(bf16[8,3968]{1,0:T(8,128)(2,1)S(1)} %collective-permute-done.refs_1_), channel_id=1, source_target_pairs={{0,4},{2,6},{4,0},{6,2},{8,12},{10,14},{12,8},{14,10},{1,5},{3,7},... | collective-permute-start | bytes 190472 | tf_op jit(solution)/shard_map/ppermute | solution.py:454
  13.4 4.2 %collective-permute-start.2 = (bf16[8,3968]{1,0:T(8,128)(2,1)S(1)}, bf16[8,3968]{1,0:T(8,128)(2,1)S(1)}, u32[]{:S(2)}, u32[]{:S(2)}) collective-permute-start(bf16[8,3968]{1,0:T(8,128)(2,1)S(1)} %collective-permute-done.refs_1_), channel_id=1, source_target_pairs={{0,2},{2,0},{4,6},{6,4},{8,10},{10,8},{12,14},{14,12},{1,3},{3,1},... | collective-permute-start | bytes 190472 | tf_op jit(solution)/shard_map/ppermute | solution.py:454
  14.9 2.8 %collective-permute-start.13 = (bf16[8,3968]{1,0:T(8,128)(2,1)S(1)}, bf16[8,3968]{1,0:T(8,128)(2,1)S(1)}, u32[]{:S(2)}, u32[]{:S(2)}) collective-permute-start(bf16[8,3968]{1,0:T(8,128)(2,1)S(1)} %collective-permute-done.5.refs_6_), channel_id=1, source_target_pairs={{0,1},{1,0},{2,3},{3,2},{4,5},{5,4},{6,7},{7,6},{8,9},{9,8},{10,11... | collective-permute-start | bytes 190472 | tf_op jit(solution)/shard_map/ppermute | solution.py:457
  14.9 3.3 %collective-permute-start.11 = (bf16[8,3968]{1,0:T(8,128)(2,1)S(1)}, bf16[8,3968]{1,0:T(8,128)(2,1)S(1)}, u32[]{:S(2)}, u32[]{:S(2)}) collective-permute-start(bf16[8,3968]{1,0:T(8,128)(2,1)S(1)} %collective-permute-done.3.refs_4_), channel_id=1, source_target_pairs={{0,1},{1,0},{2,3},{3,2},{4,5},{5,4},{6,7},{7,6},{8,9},{9,8},{10,11... | collective-permute-start | bytes 190472 | tf_op jit(solution)/shard_map/ppermute | solution.py:457
  15.5 2.8 %collective-permute-start.9 = (bf16[8,3968]{1,0:T(8,128)(2,1)S(1)}, bf16[8,3968]{1,0:T(8,128)(2,1)S(1)}, u32[]{:S(2)}, u32[]{:S(2)}) collective-permute-start(bf16[8,3968]{1,0:T(8,128)(2,1)S(1)} %collective-permute-done.1.refs_2_), channel_id=1, source_target_pairs={{0,1},{1,0},{2,3},{3,2},{4,5},{5,4},{6,7},{7,6},{8,9},{9,8},{10,11... | collective-permute-start | bytes 190472 | tf_op jit(solution)/shard_map/ppermute | solution.py:457
  16.4 1.8 %collective-permute-start.14 = (bf16[8,3968]{1,0:T(8,128)(2,1)S(1)}, bf16[8,3968]{1,0:T(8,128)(2,1)S(1)}, u32[]{:S(2)}, u32[]{:S(2)}) collective-permute-start(bf16[8,3968]{1,0:T(8,128)(2,1)S(1)} %collective-permute-done.6.refs_7_), channel_id=1, source_target_pairs={{0,1},{1,0},{2,3},{3,2},{4,5},{5,4},{6,7},{7,6},{8,9},{9,8},{10,11... | collective-permute-start | bytes 190472 | tf_op jit(solution)/shard_map/ppermute | solution.py:457
  17.7 1.3 %collective-permute-start.12 = (bf16[8,3968]{1,0:T(8,128)(2,1)S(1)}, bf16[8,3968]{1,0:T(8,128)(2,1)S(1)}, u32[]{:S(2)}, u32[]{:S(2)}) collective-permute-start(bf16[8,3968]{1,0:T(8,128)(2,1)S(1)} %collective-permute-done.4.refs_5_), channel_id=1, source_target_pairs={{0,1},{1,0},{2,3},{3,2},{4,5},{5,4},{6,7},{7,6},{8,9},{9,8},{10,11... | collective-permute-start | bytes 190472 | tf_op jit(solution)/shard_map/ppermute | solution.py:457
  17.7 1.4 %collective-permute-start.10 = (bf16[8,3968]{1,0:T(8,128)(2,1)S(1)}, bf16[8,3968]{1,0:T(8,128)(2,1)S(1)}, u32[]{:S(2)}, u32[]{:S(2)}) collective-permute-start(bf16[8,3968]{1,0:T(8,128)(2,1)S(1)} %collective-permute-done.2.refs_3_), channel_id=1, source_target_pairs={{0,1},{1,0},{2,3},{3,2},{4,5},{5,4},{6,7},{7,6},{8,9},{9,8},{10,11... | collective-permute-start | bytes 190472 | tf_op jit(solution)/shard_map/ppermute | solution.py:457
  48.9 2.0 %collective-permute-start.15 = (f32[64,2048]{1,0:T(8,128)S(1)}, f32[64,2048]{1,0:T(8,128)S(1)}, u32[]{:S(2)}, u32[]{:S(2)}) collective-permute-start(f32[64,2048]{1,0:T(8,128)S(1)} %get-tuple-element.36), channel_id=1, source_target_pairs={{0,1},{1,0},{2,3},{3,2},{4,5},{5,4},{6,7},{7,6},{8,9},{9,8},{10,11... | collective-permute-start | bytes 1572872 | tf_op jit(solution)/shard_map/ppermute | solution.py:457
  51.0 10.6 %collective-permute-start.16 = (f32[16,2048]{1,0:T(8,128)S(1)}, f32[16,2048]{1,0:T(8,128)S(1)}, u32[]{:S(2)}, u32[]{:S(2)}) collective-permute-start(f32[16,2048]{1,0:T(8,128)S(1)} %get-tuple-element.41), channel_id=1, source_target_pairs={{0,2},{2,0},{4,6},{6,4},{8,10},{10,8},{12,14},{14,12},{1,3},{3,1},... | collective-permute-start | bytes 393224 | tf_op jit(solution)/shard_map/ppermute | solution.py:454
  52.5 9.1 %collective-permute-start.17 = (f32[16,2048]{1,0:T(8,128)S(1)}, f32[16,2048]{1,0:T(8,128)S(1)}, u32[]{:S(2)}, u32[]{:S(2)}) collective-permute-start(f32[16,2048]{1,0:T(8,128)S(1)} %get-tuple-element.42), channel_id=1, source_target_pairs={{0,4},{2,6},{4,0},{6,2},{8,12},{10,14},{12,8},{14,10},{1,5},{3,7},... | collective-permute-start | bytes 393224 | tf_op jit(solution)/shard_map/ppermute | solution.py:454
  52.9 8.7 %collective-permute-start.18 = (f32[16,2048]{1,0:T(8,128)S(1)}, f32[16,2048]{1,0:T(8,128)S(1)}, u32[]{:S(2)}, u32[]{:S(2)}) collective-permute-start(f32[16,2048]{1,0:T(8,128)S(1)} %get-tuple-element.43), channel_id=1, source_target_pairs={{0,6},{2,4},{4,2},{6,0},{8,14},{10,12},{12,10},{14,8},{1,7},{3,5},... | collective-permute-start | bytes 393224 | tf_op jit(solution)/shard_map/ppermute | solution.py:454
  54.5 15.8 %copy-start = (s32[16,4]{0,1:T(4,128)S(1)}, s32[16,4]{0,1:T(4,128)}, u32[]{:S(2)}) copy-start(s32[16,4]{0,1:T(4,128)} %param.9) | copy-start | bytes 772
  61.6 8.7 %collective-permute-start.19 = (f32[8,2048]{1,0:T(8,128)S(1)}, f32[8,2048]{1,0:T(8,128)S(1)}, u32[]{:S(2)}, u32[]{:S(2)}) collective-permute-start(f32[8,2048]{1,0:T(8,128)S(1)} %get-tuple-element.50), channel_id=1, source_target_pairs={{0,8},{2,10},{4,12},{6,14},{8,0},{10,2},{12,4},{14,6},{1,9},{3,11}... | collective-permute-start | bytes 196616 | tf_op jit(solution)/shard_map/ppermute | solution.py:451

commit v9 on v8

--- a/solution.py
+++ b/solution.py
@@ -123,12 +123,19 @@
     out[:, pl.ds(base, width)] = held[...].astype(BF16)
 
 
+def slot_of(n, pieces):
+    if n < 2:
+        return n
+    far = pieces // 2 - 1
+    return 2 * (n - 1) if n < 2 + far else 2 * (n - 1 - far) + 1
+
+
 def pack(part, gates, out, pieces):
     width = part.shape[1]
     half, eighth = width // 2, width // SUBS
     size = half + eighth
     for n in range(pieces):
-        at, to = n * CAP, n * SUBS
+        at, to = n * CAP, slot_of(n, pieces) * SUBS
         for h in range(2):
             out[to + h * WHOLE : to + (h + 1) * WHOLE, :half] = part[at : at + WHOLE, h * half : (h + 1) * half]
         for s in range(SUBS):
@@ -137,11 +144,28 @@
         out[to + CAP : to + SUBS, size:] = jnp.zeros((SUBS - CAP, LANES), F32)
 
 
+def stack_body(*refs):
+    for n, ref in enumerate(refs[:-1]):
+        refs[-1][n] = ref[...]
+
+
+def stack(pieces, name):
+    return pl.pallas_call(
+        stack_body,
+        out_shape=jax.ShapeDtypeStruct((len(pieces),) + pieces[0].shape, BF16),
+        in_specs=[VMEM] * len(pieces),
+        out_specs=VMEM,
+        compiler_params=pltpu.CompilerParams(vmem_limit_bytes=6 * MIB),
+        name=name,
+    )(*pieces)
+
+
 def experts_body(pieces, chunk, ahead, t_ref, *refs):
-    mine, theirs = refs[:pieces], refs[pieces : 2 * pieces]
+    mine, (early, late) = refs[:pieces], refs[pieces : pieces + 2]
+    theirs = [early.at[n] for n in range(early.shape[0])] + [late.at[n] for n in range(late.shape[0])]
     (wg_hbm, wu_hbm, wd_hbm, x_ref, dh_ref, du_ref, give_ref, keep_ref, down_ref,
      wg_ref, wu_ref, ring, g_ref, wt_ref, h_ref, u_ref, da_ref, dhr_ref, dur_ref, acc,
-     held, factor, landed, ring_landed, sent) = refs[2 * pieces :]
+     held, factor, landed, ring_landed, sent) = refs[pieces + 2 :]
     rows, depth = x_ref.shape
     hidden = wg_ref.shape[0]
     width = depth // 2
@@ -159,10 +183,6 @@
     def load_down(i):
         slot = lax.rem(i, slots)
         return pltpu.make_async_copy(wd_hbm.at[:, columns(i)], ring.at[slot], ring_landed.at[slot])
-
-    def store_down(i):
-        slot = lax.rem(i, slots)
-        return pltpu.make_async_copy(ring.at[slot], down_ref.at[:, columns(i)], sent.at[slot])
 
     def start(i):
         load(i, 0).start()
@@ -233,35 +253,27 @@
         total = units(begin, min(LANES, hidden - begin), total)
     gates = jnp.broadcast_to(total, (LANES, rows)).T
     tile = tile_of(hidden, 448)
-
-    def grad_step(i, carry):
-        slot = lax.rem(i, slots)
-        cols = columns(i)
-
-        @pl.when(i >= slots)
-        def _():
-            store_down(i - slots).wait()
-
-        g = g_ref[:, cols]
-        for at in range(0, hidden, tile):
-            ring[slot, at : at + tile, :] = jnp.dot(
-                wt_ref[at : at + tile, :], g, preferred_element_type=F32
-            ).astype(BF16)
-        store_down(i).start()
+    leaving = []
+    for i in range(steps):
+        cols = pl.ds(i * chunk, chunk)
         acc[:, cols] = jnp.dot(dhr_ref[...], wg_ref[:, cols], preferred_element_type=F32) + jnp.dot(
             dur_ref[...], wu_ref[:, cols], preferred_element_type=F32
         )
-        return carry
-
-    lax.fori_loop(0, steps, grad_step, 0)
+        room = wg_ref.at[:, pl.ds((i - 1) * chunk, chunk)] if i else ring.at[0]
+        for at in range(0, hidden, tile):
+            room[at : at + tile, :] = jnp.dot(
+                wt_ref[at : at + tile, :], g_ref[:, cols], preferred_element_type=F32
+            ).astype(BF16)
+        leaving.append(pltpu.make_async_copy(room, down_ref.at[:, cols], sent.at[i]))
+        leaving[-1].start()
     for at, out in ((1 - t, give_ref), (t, keep_ref)):
         held[...] = acc[:, pl.ds(pl.multiple_of(at * width, width), width)]
         pack(held, gates, out, pieces)
-    for i in range(max(0, steps - slots), steps):
-        store_down(i).wait()
-
-
-def expert_units(t, mine, theirs, w_gate, w_up, w_down, width):
+    for copy in leaving:
+        copy.wait()
+
+
+def expert_units(t, mine, early, late, w_gate, w_up, w_down, width):
     hidden, depth = w_gate.shape
     pieces = len(mine)
     rows = -(-pieces * CAP // 16) * 16
@@ -281,7 +293,7 @@
             packed,
             jax.ShapeDtypeStruct((hidden, depth), BF16),
         ),
-        in_specs=[SMEM] + [VMEM] * (2 * pieces) + [HBM] * 3,
+        in_specs=[SMEM] + [VMEM] * (pieces + 2) + [HBM] * 3,
         out_specs=[VMEM] * 5 + [HBM],
         scratch_shapes=[
             pltpu.VMEM((hidden, depth), BF16),
@@ -299,68 +311,50 @@
             pltpu.VMEM((rows, LANES), F32),
             pltpu.SemaphoreType.DMA((steps, 2)),
             pltpu.SemaphoreType.DMA((slots,)),
-            pltpu.SemaphoreType.DMA((slots,)),
+            pltpu.SemaphoreType.DMA((steps,)),
         ],
         compiler_params=pltpu.CompilerParams(vmem_limit_bytes=50 * MIB),
         cost_estimate=pl.CostEstimate(
             flops=12 * rows * hidden * depth, bytes_accessed=8 * hidden * depth, transcendentals=rows * hidden
         ),
         name="expert_units",
-    )(t, *mine, *theirs, w_gate, w_up, w_down)
-
-
-def weights_body(count, chunk, *refs):
-    lefts, x_ref, outs, (ring, sent) = refs[:count], refs[count], refs[count + 1 : 2 * count + 1], refs[2 * count + 1 :]
-    slots = ring.shape[1]
-    hidden = lefts[0].shape[0]
+    )(t, *mine, early, late, w_gate, w_up, w_down)
+
+
+def weights_body(chunk, left_ref, x_ref, out_ref, room, sent):
+    hidden = left_ref.shape[0]
     steps = x_ref.shape[1] // chunk
     tile = tile_of(hidden, 448)
-
-    def store(i, n):
-        cols = pl.ds(pl.multiple_of(i * chunk, chunk), chunk)
-        slot = lax.rem(i, slots)
-        return pltpu.make_async_copy(ring.at[n, slot], outs[n].at[:, cols], sent.at[n, slot])
-
-    def step(i, carry):
-        slot = lax.rem(i, slots)
-        x = x_ref[:, pl.ds(pl.multiple_of(i * chunk, chunk), chunk)]
-        for n in range(count):
-
-            @pl.when(i >= slots)
-            def _():
-                store(i - slots, n).wait()
-
-            for at in range(0, hidden, tile):
-                ring[n, slot, at : at + tile, :] = jnp.dot(
-                    lefts[n][at : at + tile, :], x, preferred_element_type=F32
-                ).astype(BF16)
-            store(i, n).start()
-        return carry
-
-    lax.fori_loop(0, steps, step, 0)
-    for i in range(max(0, steps - slots), steps):
-        for n in range(count):
-            store(i, n).wait()
-
-
-def weight_grads(lefts, right, name):
-    count = len(lefts)
-    hidden, rows = lefts[0].shape
+    leaving = []
+    for i in range(steps):
+        cols = pl.ds(i * chunk, chunk)
+        for at in range(0, hidden, tile):
+            room[i, at : at + tile, :] = jnp.dot(
+                left_ref[at : at + tile, :], x_ref[:, cols], preferred_element_type=F32
+            ).astype(BF16)
+        leaving.append(pltpu.make_async_copy(room.at[i], out_ref.at[:, cols], sent.at[i]))
+        leaving[-1].start()
+    for copy in leaving:
+        copy.wait()
+
+
+def weight_grad(left, right, name):
+    hidden, rows = left.shape
     depth = right.shape[1]
-    chunk = chunk_of(depth, 512)
-    slots = min(4, depth // chunk)
-    return pl.pallas_call(
-        functools.partial(weights_body, count, chunk),
-        out_shape=[jax.ShapeDtypeStruct((hidden, depth), BF16)] * count,
-        in_specs=[VMEM] * (count + 1),
-        out_specs=[HBM] * count,
-        scratch_shapes=[pltpu.VMEM((count, slots, hidden, chunk), BF16), pltpu.SemaphoreType.DMA((count, slots))],
-        compiler_params=pltpu.CompilerParams(vmem_limit_bytes=24 * MIB),
+    chunk = chunk_of(depth, 768)
+    steps = depth // chunk
+    return pl.pallas_call(
+        functools.partial(weights_body, chunk),
+        out_shape=jax.ShapeDtypeStruct((hidden, depth), BF16),
+        in_specs=[VMEM] * 2,
+        out_specs=HBM,
+        scratch_shapes=[pltpu.VMEM((steps, hidden, chunk), BF16), pltpu.SemaphoreType.DMA((steps,))],
+        compiler_params=pltpu.CompilerParams(vmem_limit_bytes=28 * MIB),
         cost_estimate=pl.CostEstimate(
-            flops=2 * count * rows * hidden * depth, bytes_accessed=2 * count * hidden * depth, transcendentals=0
+            flops=2 * rows * hidden * depth, bytes_accessed=2 * hidden * depth, transcendentals=0
         ),
         name=name,
-    )(*lefts, right)
+    )(left, right)
 
 
 def fold_body(copies, keep_ref, got_ref, *outs):
@@ -464,18 +458,24 @@
     got = partner(oth)
     first = {0: own} | {d: across(own, d) for d in far_first}
     second = {0: got} | {d: across(got, d) for d in far_first}
-    mine = [piece for d in range(copies) for piece in (first[d], second[d])]
-    theirs = [other_core(piece) for piece in mine]
-    x, dh, du, give, keep, grad_w_down = expert_units(t, mine, theirs, w_gate, w_up, w_down, width)
+    early = [own, got] + [first[d] for d in range(1, copies)]
+    late = [second[d] for d in range(1, copies)]
+    if late:
+        early, late[far_first[0] - 1] = lax.optimization_barrier((early, late[far_first[0] - 1]))
+    early_there = other_core(stack(early, "stack_early"))
+    late_there = other_core(stack(late, "stack_late"))
+    x, dh, du, give, keep, grad_w_down = expert_units(
+        t, early + late, early_there, late_there, w_gate, w_up, w_down, width
+    )
     blocks = list(fold(copies, keep, other_core(give)))
     arrived = {d: across(blocks[d], d) for d in far_first}
     dh, local = lax.optimization_barrier((dh, blocks[0]))
-    (grad_w_gate,) = weight_grads((dh,), x, "grad_gate")
+    grad_w_gate = weight_grad(dh, x, "grad_gate")
     grad_w_gate, arrived = lax.optimization_barrier((grad_w_gate, arrived))
     kept, others = merge([local] + [arrived[d] for d in range(1, copies)])
     back = partner(others)
     du, kept = lax.optimization_barrier((du, kept))
-    (grad_w_up,) = weight_grads((du,), x, "grad_up")
+    grad_w_up = weight_grad(du, x, "grad_up")
     grad_w_up, back = lax.optimization_barrier((grad_w_up, back))
     token_grad, gate_t = finish(e, ids_t, kept, back, width)
     return token_grad, gate_t.T, grad_w_gate, grad_w_up, grad_w_down

time: 72.1 us -> 75 us (1.040)
  waiting for transfers between devices: 4.74 us -> 8.58 us
  Pallas kernels: 46.9 us -> 45.8 us
    ppermute x9, waiting for transfers between devices: 2.18 us -> 5.39 us  [across(): return lax.ppermute(v, 'expert', [(i, i ^ d) for i in range(n_expert)])]
    ppermute x9 -> x3, starting transfers between devices: 1.51 us -> 0.35 us  [other_core(): return lax.ppermute(v, 'tensor', [(0, 1), (1, 0)])]
    ppermute x2, starting transfers between devices: 5.81 us -> 6.71 us  [partner(): lax.ppermute(v, 'expert', [(i, (i + copies) % n_expert) for i in range(n_...]
    pallas_call x2 -> x4, Pallas kernels: 14 us -> 13.3 us  [the longest x2 13.2 us: weight_grad(): pl.pallas_call(functools.partial(weights_body, chunk), out_shape=jax.Shap...]
    ppermute x9 -> x3, waiting for transfers between devices: 2.46 us -> 3.19 us  [other_core(): return lax.ppermute(v, 'tensor', [(0, 1), (1, 0)])]
  transfers between devices with their start and end apart: 20 -> 14, of which waited for: 6 -> 7; matrix products, arithmetic and copies ran while one was open for 0% -> 0% of each run, Pallas kernels for 20% -> 18%
where the time goes in v9:
time: 75 us; the launch traced here: 74.8 us
  Pallas kernels  45.8 us (61%)
  starting transfers between devices  19.7 us (26%)
  waiting for transfers between devices  8.58 us (11%)
  between operations  0.75 us (1%)
    pallas_call x1, Pallas kernels, expert_units(): pl.pallas_call(functools.partial(experts_body, pieces, chunk, ahead), out...  29.5 us
    pallas_call x2, Pallas kernels, weight_grad(): pl.pallas_call(functools.partial(weights_body, chunk), out_shape=jax.Shap...  13.2 us
    ppermute x9, starting transfers between devices, across(): return lax.ppermute(v, 'expert', [(i, i ^ d) for i in range(n_expert)])  12.7 us
    ppermute x2, starting transfers between devices, partner(): lax.ppermute(v, 'expert', [(i, (i + copies) % n_expert) for i in range(n_...  6.71 us
    ppermute x9, waiting for transfers between devices, across(): return lax.ppermute(v, 'expert', [(i, i ^ d) for i in range(n_expert)])  5.39 us
    ppermute x3, waiting for transfers between devices, other_core(): return lax.ppermute(v, 'tensor', [(0, 1), (1, 0)])  3.19 us
    pallas_call x1, Pallas kernels, finish(): pl.pallas_call(finish_body, out_shape=(jax.ShapeDtypeStruct((toks, width)...  1.54 us
  transfers between devices with their start and end apart: 14, of which 7 were waited for; matrix products, arithmetic and copies ran while one was open for 0% of the time, Pallas kernels for 18%

profile of v9, /device:TPU:0, one launch (start us, length us, event | category | flops | bytes accessed | tf_op | source)
XLA Modules:
  0.0 74.8 jit_solution(9104035045299002174)
XLA Ops:
  0.6 1.4 %pick_rows.1 = (bf16[8,3968]{1,0:T(8,128)(2,1)S(1)}, bf16[8,3968]{1,0:T(8,128)(2,1)S(1)}) custom-call(s32[1]{0:T(128)} %bitcast.e_ref, s32[4,16]{1,0:T(4,128)} %bitcast.5, bf16[4,16]{1,0:T(4,128)(2,1)} %bitcast.7, bf16[16,3072]{1,0:T(8,128)(2,1)} %tok_any.1, bf16[16,3072]{1,0:T(8,128)(2,1)} %grad_any.1), custom_call_target="tpu_custom_call" | custom-call | tf_op jit(solution)/shard_map/pick_rows/pallas_call | solution.py:93
  2.0 4.1 %collective-permute-start = (bf16[8,3968]{1,0:T(8,128)(2,1)S(1)}, bf16[8,3968]{1,0:T(8,128)(2,1)S(1)}, u32[]{:S(2)}, u32[]{:S(2)}) collective-permute-start(bf16[8,3968]{1,0:T(8,128)(2,1)S(1)} %get-tuple-element.38), channel_id=1, source_target_pairs={{0,8},{2,10},{4,12},{6,14},{8,0},{10,2},{12,4},{14,6},{1,9},{3,11}... | collective-permute-start | bytes 190472 | tf_op jit(solution)/shard_map/ppermute | solution.py:445
  6.1 2.5 %collective-permute-start.3 = (bf16[8,3968]{1,0:T(8,128)(2,1)S(1)}, bf16[8,3968]{1,0:T(8,128)(2,1)S(1)}, u32[]{:S(2)}, u32[]{:S(2)}) collective-permute-start(bf16[8,3968]{1,0:T(8,128)(2,1)S(1)} %get-tuple-element.39.refs_0_), channel_id=1, source_target_pairs={{0,6},{2,4},{4,2},{6,0},{8,14},{10,12},{12,10},{14,8},{1,7},{3,5},... | collective-permute-start | bytes 190472 | tf_op jit(solution)/shard_map/ppermute | solution.py:448
  8.6 0.4 collective-permute-start.2
  9.1 0.5 collective-permute-start.1
  9.6 0.0 collective-permute-done.refs_1_
  9.6 2.5 %collective-permute-start.4 = (bf16[8,3968]{1,0:T(8,128)(2,1)S(1)}, bf16[8,3968]{1,0:T(8,128)(2,1)S(1)}, u32[]{:S(2)}, u32[]{:S(2)}) collective-permute-start(bf16[8,3968]{1,0:T(8,128)(2,1)S(1)} %collective-permute-done.refs_1_), channel_id=1, source_target_pairs={{0,6},{2,4},{4,2},{6,0},{8,14},{10,12},{12,10},{14,8},{1,7},{3,5},... | collective-permute-start | bytes 190472 | tf_op jit(solution)/shard_map/ppermute | solution.py:448
  12.1 0.0 collective-permute-done.3.refs_4_
  12.1 1.1 %collective-permute-done.2.refs_3_ = bf16[8,3968]{1,0:T(8,128)(2,1)S(1)} collective-permute-done((bf16[8,3968]{1,0:T(8,128)(2,1)S(1)}, bf16[8,3968]{1,0:T(8,128)(2,1)S(1)}, u32[]{:S(2)}, u32[]{:S(2)}) %collective-permute-start.2) | collective-permute-done | bytes 63520 | tf_op jit(solution)/shard_map/ppermute | solution.py:448
  13.2 0.2 collective-permute-done.1.refs_2_
  13.5 1.3 %collective-permute-done.4.refs_2_.refs_7_ = bf16[8,3968]{1,0:T(8,128)(2,1)S(1)} collective-permute-done((bf16[8,3968]{1,0:T(8,128)(2,1)S(1)}, bf16[8,3968]{1,0:T(8,128)(2,1)S(1)}, u32[]{:S(2)}, u32[]{:S(2)}) %collective-permute-start.4) | collective-permute-done | bytes 63520 | tf_op jit(solution)/shard_map/ppermute | solution.py:448
  14.8 0.1 collective-permute-start.7
  14.9 1.6 %collective-permute-start.6 = (bf16[8,3968]{1,0:T(8,128)(2,1)S(1)}, bf16[8,3968]{1,0:T(8,128)(2,1)S(1)}, u32[]{:S(2)}, u32[]{:S(2)}) collective-permute-start(bf16[8,3968]{1,0:T(8,128)(2,1)S(1)} %collective-permute-done.refs_1_), channel_id=1, source_target_pairs={{0,4},{2,6},{4,0},{6,2},{8,12},{10,14},{12,8},{14,10},{1,5},{3,7},... | collective-permute-start | bytes 190472 | tf_op jit(solution)/shard_map/ppermute | solution.py:448
  16.5 1.5 %collective-permute-start.5 = (bf16[8,3968]{1,0:T(8,128)(2,1)S(1)}, bf16[8,3968]{1,0:T(8,128)(2,1)S(1)}, u32[]{:S(2)}, u32[]{:S(2)}) collective-permute-start(bf16[8,3968]{1,0:T(8,128)(2,1)S(1)} %collective-permute-done.refs_1_), channel_id=1, source_target_pairs={{0,2},{2,0},{4,6},{6,4},{8,10},{10,8},{12,14},{14,12},{1,3},{3,1},... | collective-permute-start | bytes 190472 | tf_op jit(solution)/shard_map/ppermute | solution.py:448
  18.0 1.3 %collective-permute-done.6.refs_1_.refs_6_ = bf16[8,3968]{1,0:T(8,128)(2,1)S(1)} collective-permute-done((bf16[8,3968]{1,0:T(8,128)(2,1)S(1)}, bf16[8,3968]{1,0:T(8,128)(2,1)S(1)}, u32[]{:S(2)}, u32[]{:S(2)}) %collective-permute-start.6) | collective-permute-done | bytes 63520 | tf_op jit(solution)/shard_map/ppermute | solution.py:448
  19.3 1.4 %collective-permute-done.5.refs_0_.refs_5_ = bf16[8,3968]{1,0:T(8,128)(2,1)S(1)} collective-permute-done((bf16[8,3968]{1,0:T(8,128)(2,1)S(1)}, bf16[8,3968]{1,0:T(8,128)(2,1)S(1)}, u32[]{:S(2)}, u32[]{:S(2)}) %collective-permute-start.5) | collective-permute-done | bytes 63520 | tf_op jit(solution)/shard_map/ppermute | solution.py:448
  20.8 0.1 collective-permute-start.8
  20.8 1.4 %collective-permute-done.8.refs_9_ = bf16[3,8,3968]{2,1,0:T(8,128)(2,1)S(1)} collective-permute-done((bf16[3,8,3968]{2,1,0:T(8,128)(2,1)S(1)}, bf16[3,8,3968]{2,1,0:T(8,128)(2,1)S(1)}, u32[]{:S(2)}, u32[]{:S(2)}) %collective-permute-start.8) | collective-permute-done | bytes 190496 | tf_op jit(solution)/shard_map/ppermute | solution.py:451
  22.3 0.0 collective-permute-done.7.refs_8_
  22.3 29.5 %expert_units.1 = (bf16[48,6144]{1,0:T(8,128)(2,1)S(1)}, bf16[1344,48]{1,0:T(8,128)(2,1)S(1)}, bf16[1344,48]{1,0:T(8,128)(2,1)S(1)}, f32[64,2048]{1,0:T(8,128)S(...) custom-call(s32[1]{0:T(128)} %bitcast.2.t_ref, bf16[8,3968]{1,0:T(8,128)(2,1)S(1)} %get-tuple-element.39.refs_0_, ...), custom_call_target="tpu_custom_call" | custom-call | flops 4756340736 | bytes 66060288 | tf_op jit(solution)/shard_map/expert_units/pallas_call | solution.py:286
  51.7 0.2 collective-permute-start.9
  51.9 1.8 %collective-permute-done.9.got_ref = f32[64,2048]{1,0:T(8,128)S(1)} collective-permute-done((f32[64,2048]{1,0:T(8,128)S(1)}, f32[64,2048]{1,0:T(8,128)S(1)}, u32[]{:S(2)}, u32[]{:S(2)}) %collective-permute-start.9) | collective-permute-done | bytes 524320 | tf_op jit(solution)/shard_map/ppermute | solution.py:451
  53.7 0.1 fold_cores.1
  53.8 1.6 %collective-permute-start.10 = (f32[16,2048]{1,0:T(8,128)S(1)}, f32[16,2048]{1,0:T(8,128)S(1)}, u32[]{:S(2)}, u32[]{:S(2)}) collective-permute-start(f32[16,2048]{1,0:T(8,128)S(1)} %get-tuple-element.53), channel_id=1, source_target_pairs={{0,2},{2,0},{4,6},{6,4},{8,10},{10,8},{12,14},{14,12},{1,3},{3,1},... | collective-permute-start | bytes 393224 | tf_op jit(solution)/shard_map/ppermute | solution.py:448
  55.3 0.5 collective-permute-start.11
  55.8 1.5 %collective-permute-start.12 = (f32[16,2048]{1,0:T(8,128)S(1)}, f32[16,2048]{1,0:T(8,128)S(1)}, u32[]{:S(2)}, u32[]{:S(2)}) collective-permute-start(f32[16,2048]{1,0:T(8,128)S(1)} %get-tuple-element.55), channel_id=1, source_target_pairs={{0,6},{2,4},{4,2},{6,0},{8,14},{10,12},{12,10},{14,8},{1,7},{3,5},... | collective-permute-start | bytes 393224 | tf_op jit(solution)/shard_map/ppermute | solution.py:448
  57.3 0.0 copy-start
  57.3 6.6 %grad_gate.1 = bf16[1344,6144]{1,0:T(8,128)(2,1)} custom-call(bf16[1344,48]{1,0:T(8,128)(2,1)S(1)} %get-tuple-element.51.left_ref, bf16[48,6144]{1,0:T(8,128)(2,1)S(1)} %get-tuple-element.52.x_ref), custom_call_target="tpu_custom_call" | custom-call | flops 792723456 | bytes 16515072 | tf_op jit(solution)/shard_map/grad_gate/pallas_call | solution.py:346
  64.0 0.0 collective-permute-done.10.refs_1_
  64.0 0.0 collective-permute-done.11.refs_2_
  64.0 0.0 collective-permute-done.12.refs_3_
  64.0 2.6 %collective-permute-start.13 = (f32[8,2048]{1,0:T(8,128)S(1)}, f32[8,2048]{1,0:T(8,128)S(1)}, u32[]{:S(2)}, u32[]{:S(2)}) collective-permute-start(f32[8,2048]{1,0:T(8,128)S(1)} %get-tuple-element.62), channel_id=1, source_target_pairs={{0,8},{2,10},{4,12},{6,14},{8,0},{10,2},{12,4},{14,6},{1,9},{3,11}... | collective-permute-start | bytes 196616 | tf_op jit(solution)/shard_map/ppermute | solution.py:445
  66.6 6.6 %grad_up.1 = bf16[1344,6144]{1,0:T(8,128)(2,1)} custom-call(bf16[1344,48]{1,0:T(8,128)(2,1)S(1)} %get-tuple-element.61.left_ref, bf16[48,6144]{1,0:T(8,128)(2,1)S(1)} %get-tuple-element.52.x_ref), custom_call_target="tpu_custom_call" | custom-call | flops 792723456 | bytes 16515072 | tf_op jit(solution)/shard_map/grad_up/pallas_call | solution.py:346
  73.3 0.0 collective-permute-done.13.got_ref
  73.3 0.0 copy-done
  73.3 1.5 %finish_tokens.1 = (bf16[16,3072]{1,0:T(8,128)(2,1)}, f32[4,16]{1,0:T(4,128)}) custom-call(s32[1]{0:T(128)} %bitcast.e_ref, s32[4,16]{1,0:T(4,128)S(1)} %bitcast.6, f32[8,2048]{1,0:T(8,128)S(1)} %get-tuple-element.60.mine_ref, f32[8,2048]{1,0:T(8,128)S(1)} %collective-permute-done.13.got_ref), custom_call_target="tpu_custom_call" | custom-call | tf_op jit(solution)/shard_map/finish_tokens/pallas_call | solution.py:426
  (3 shorter events, 0.1 us)
Async XLA Ops:
  2.0 7.6 %collective-permute-start = (bf16[8,3968]{1,0:T(8,128)(2,1)S(1)}, bf16[8,3968]{1,0:T(8,128)(2,1)S(1)}, u32[]{:S(2)}, u32[]{:S(2)}) collective-permute-start(bf16[8,3968]{1,0:T(8,128)(2,1)S(1)} %get-tuple-element.38), channel_id=1, source_target_pairs={{0,8},{2,10},{4,12},{6,14},{8,0},{10,2},{12,4},{14,6},{1,9},{3,11}... | collective-permute-start | bytes 190472 | tf_op jit(solution)/shard_map/ppermute | solution.py:445
  6.1 6.0 %collective-permute-start.3 = (bf16[8,3968]{1,0:T(8,128)(2,1)S(1)}, bf16[8,3968]{1,0:T(8,128)(2,1)S(1)}, u32[]{:S(2)}, u32[]{:S(2)}) collective-permute-start(bf16[8,3968]{1,0:T(8,128)(2,1)S(1)} %get-tuple-element.39.refs_0_), channel_id=1, source_target_pairs={{0,6},{2,4},{4,2},{6,0},{8,14},{10,12},{12,10},{14,8},{1,7},{3,5},... | collective-permute-start | bytes 190472 | tf_op jit(solution)/shard_map/ppermute | solution.py:448
  8.6 4.6 %collective-permute-start.2 = (bf16[8,3968]{1,0:T(8,128)(2,1)S(1)}, bf16[8,3968]{1,0:T(8,128)(2,1)S(1)}, u32[]{:S(2)}, u32[]{:S(2)}) collective-permute-start(bf16[8,3968]{1,0:T(8,128)(2,1)S(1)} %get-tuple-element.39.refs_0_), channel_id=1, source_target_pairs={{0,4},{2,6},{4,0},{6,2},{8,12},{10,14},{12,8},{14,10},{1,5},{3,7},... | collective-permute-start | bytes 190472 | tf_op jit(solution)/shard_map/ppermute | solution.py:448
  9.1 4.4 %collective-permute-start.1 = (bf16[8,3968]{1,0:T(8,128)(2,1)S(1)}, bf16[8,3968]{1,0:T(8,128)(2,1)S(1)}, u32[]{:S(2)}, u32[]{:S(2)}) collective-permute-start(bf16[8,3968]{1,0:T(8,128)(2,1)S(1)} %get-tuple-element.39.refs_0_), channel_id=1, source_target_pairs={{0,2},{2,0},{4,6},{6,4},{8,10},{10,8},{12,14},{14,12},{1,3},{3,1},... | collective-permute-start | bytes 190472 | tf_op jit(solution)/shard_map/ppermute | solution.py:448
  9.6 5.1 %collective-permute-start.4 = (bf16[8,3968]{1,0:T(8,128)(2,1)S(1)}, bf16[8,3968]{1,0:T(8,128)(2,1)S(1)}, u32[]{:S(2)}, u32[]{:S(2)}) collective-permute-start(bf16[8,3968]{1,0:T(8,128)(2,1)S(1)} %collective-permute-done.refs_1_), channel_id=1, source_target_pairs={{0,6},{2,4},{4,2},{6,0},{8,14},{10,12},{12,10},{14,8},{1,7},{3,5},... | collective-permute-start | bytes 190472 | tf_op jit(solution)/shard_map/ppermute | solution.py:448
  14.8 7.5 %collective-permute-start.7 = (bf16[5,8,3968]{2,1,0:T(8,128)(2,1)S(1)}, bf16[5,8,3968]{2,1,0:T(8,128)(2,1)S(1)}, u32[]{:S(2)}, u32[]{:S(2)}) collective-permute-start(bf16[5,8,3968]{2,1,0:T(8,128)(2,1)S(1)} %stack_early.1), channel_id=1, source_target_pairs={{0,1},{1,0},{2,3},{3,2},{4,5},{5,4},{6,7},{7,6},{8,9},{9,8},{10,11... | collective-permute-start | bytes 952328 | tf_op jit(solution)/shard_map/ppermute | solution.py:451
  14.9 4.5 %collective-permute-start.6 = (bf16[8,3968]{1,0:T(8,128)(2,1)S(1)}, bf16[8,3968]{1,0:T(8,128)(2,1)S(1)}, u32[]{:S(2)}, u32[]{:S(2)}) collective-permute-start(bf16[8,3968]{1,0:T(8,128)(2,1)S(1)} %collective-permute-done.refs_1_), channel_id=1, source_target_pairs={{0,4},{2,6},{4,0},{6,2},{8,12},{10,14},{12,8},{14,10},{1,5},{3,7},... | collective-permute-start | bytes 190472 | tf_op jit(solution)/shard_map/ppermute | solution.py:448
  16.5 4.2 %collective-permute-start.5 = (bf16[8,3968]{1,0:T(8,128)(2,1)S(1)}, bf16[8,3968]{1,0:T(8,128)(2,1)S(1)}, u32[]{:S(2)}, u32[]{:S(2)}) collective-permute-start(bf16[8,3968]{1,0:T(8,128)(2,1)S(1)} %collective-permute-done.refs_1_), channel_id=1, source_target_pairs={{0,2},{2,0},{4,6},{6,4},{8,10},{10,8},{12,14},{14,12},{1,3},{3,1},... | collective-permute-start | bytes 190472 | tf_op jit(solution)/shard_map/ppermute | solution.py:448
  20.8 1.5 %collective-permute-start.8 = (bf16[3,8,3968]{2,1,0:T(8,128)(2,1)S(1)}, bf16[3,8,3968]{2,1,0:T(8,128)(2,1)S(1)}, u32[]{:S(2)}, u32[]{:S(2)}) collective-permute-start(bf16[3,8,3968]{2,1,0:T(8,128)(2,1)S(1)} %stack_late.1), channel_id=1, source_target_pairs={{0,1},{1,0},{2,3},{3,2},{4,5},{5,4},{6,7},{7,6},{8,9},{9,8},{10,11... | collective-permute-start | bytes 571400 | tf_op jit(solution)/shard_map/ppermute | solution.py:451
  51.7 2.0 %collective-permute-start.9 = (f32[64,2048]{1,0:T(8,128)S(1)}, f32[64,2048]{1,0:T(8,128)S(1)}, u32[]{:S(2)}, u32[]{:S(2)}) collective-permute-start(f32[64,2048]{1,0:T(8,128)S(1)} %get-tuple-element.48), channel_id=1, source_target_pairs={{0,1},{1,0},{2,3},{3,2},{4,5},{5,4},{6,7},{7,6},{8,9},{9,8},{10,11... | collective-permute-start | bytes 1572872 | tf_op jit(solution)/shard_map/ppermute | solution.py:451
  53.8 10.2 %collective-permute-start.10 = (f32[16,2048]{1,0:T(8,128)S(1)}, f32[16,2048]{1,0:T(8,128)S(1)}, u32[]{:S(2)}, u32[]{:S(2)}) collective-permute-start(f32[16,2048]{1,0:T(8,128)S(1)} %get-tuple-element.53), channel_id=1, source_target_pairs={{0,2},{2,0},{4,6},{6,4},{8,10},{10,8},{12,14},{14,12},{1,3},{3,1},... | collective-permute-start | bytes 393224 | tf_op jit(solution)/shard_map/ppermute | solution.py:448
  55.3 8.6 %collective-permute-start.11 = (f32[16,2048]{1,0:T(8,128)S(1)}, f32[16,2048]{1,0:T(8,128)S(1)}, u32[]{:S(2)}, u32[]{:S(2)}) collective-permute-start(f32[16,2048]{1,0:T(8,128)S(1)} %get-tuple-element.54), channel_id=1, source_target_pairs={{0,4},{2,6},{4,0},{6,2},{8,12},{10,14},{12,8},{14,10},{1,5},{3,7},... | collective-permute-start | bytes 393224 | tf_op jit(solution)/shard_map/ppermute | solution.py:448
  55.8 8.2 %collective-permute-start.12 = (f32[16,2048]{1,0:T(8,128)S(1)}, f32[16,2048]{1,0:T(8,128)S(1)}, u32[]{:S(2)}, u32[]{:S(2)}) collective-permute-start(f32[16,2048]{1,0:T(8,128)S(1)} %get-tuple-element.55), channel_id=1, source_target_pairs={{0,6},{2,4},{4,2},{6,0},{8,14},{10,12},{12,10},{14,8},{1,7},{3,5},... | collective-permute-start | bytes 393224 | tf_op jit(solution)/shard_map/ppermute | solution.py:448
  57.3 16.0 %copy-start = (s32[16,4]{0,1:T(4,128)S(1)}, s32[16,4]{0,1:T(4,128)}, u32[]{:S(2)}) copy-start(s32[16,4]{0,1:T(4,128)} %param.9) | copy-start | bytes 772
  64.0 9.2 %collective-permute-start.13 = (f32[8,2048]{1,0:T(8,128)S(1)}, f32[8,2048]{1,0:T(8,128)S(1)}, u32[]{:S(2)}, u32[]{:S(2)}) collective-permute-start(f32[8,2048]{1,0:T(8,128)S(1)} %get-tuple-element.62), channel_id=1, source_target_pairs={{0,8},{2,10},{4,12},{6,14},{8,0},{10,2},{12,4},{14,6},{1,9},{3,11}... | collective-permute-start | bytes 196616 | tf_op jit(solution)/shard_map/ppermute | solution.py:445

commit v10 on v9

--- a/solution.py
+++ b/solution.py
@@ -15,6 +15,7 @@
 F32 = jnp.float32
 BF16 = jnp.bfloat16
 MIB = 1 << 20
+BLOCK = 384
 VMEM = pl.BlockSpec(memory_space=pltpu.VMEM)
 SMEM = pl.BlockSpec(memory_space=pltpu.SMEM)
 HBM = pl.BlockSpec(memory_space=pltpu.HBM)
@@ -109,6 +110,11 @@
     return max(n for n in range(LANES, most + 1, LANES) if width % n == 0)
 
 
+def place_of(step, chunks, chunk, t):
+    side = t if step < chunks else 1 - t
+    return pl.multiple_of(side * (chunks * chunk) + step % chunks * chunk, chunk)
+
+
 def assemble(pieces, held, out, base, side):
     width = held.shape[1]
     half, eighth = width // 2, width // SUBS
@@ -123,19 +129,12 @@
     out[:, pl.ds(base, width)] = held[...].astype(BF16)
 
 
-def slot_of(n, pieces):
-    if n < 2:
-        return n
-    far = pieces // 2 - 1
-    return 2 * (n - 1) if n < 2 + far else 2 * (n - 1 - far) + 1
-
-
 def pack(part, gates, out, pieces):
     width = part.shape[1]
     half, eighth = width // 2, width // SUBS
     size = half + eighth
     for n in range(pieces):
-        at, to = n * CAP, slot_of(n, pieces) * SUBS
+        at, to = n * CAP, n * SUBS
         for h in range(2):
             out[to + h * WHOLE : to + (h + 1) * WHOLE, :half] = part[at : at + WHOLE, h * half : (h + 1) * half]
         for s in range(SUBS):
@@ -161,11 +160,11 @@
 
 
 def experts_body(pieces, chunk, ahead, t_ref, *refs):
-    mine, (early, late) = refs[:pieces], refs[pieces : pieces + 2]
-    theirs = [early.at[n] for n in range(early.shape[0])] + [late.at[n] for n in range(late.shape[0])]
+    mine = refs[:pieces]
+    theirs = [refs[pieces].at[n] for n in range(pieces)]
     (wg_hbm, wu_hbm, wd_hbm, x_ref, dh_ref, du_ref, give_ref, keep_ref, down_ref,
-     wg_ref, wu_ref, ring, g_ref, wt_ref, h_ref, u_ref, da_ref, dhr_ref, dur_ref, acc,
-     held, factor, landed, ring_landed, sent) = refs[pieces + 2 :]
+     wg_ref, wu_ref, ring, g_ref, wt_ref, h_ref, u_ref, da_ref, dhr_ref, dur_ref, parts,
+     held, factor, landed, ring_landed, sent) = refs[pieces + 1 :]
     rows, depth = x_ref.shape
     hidden = wg_ref.shape[0]
     width = depth // 2
@@ -226,15 +225,12 @@
             out[...] += dot()
         return carry
 
-    lax.fori_loop(1, steps, up_step, 0)
+    lax.fori_loop(1, steps - 1, up_step, 0)
 
     weight = factor[...].T[:1, :]
 
-    def units(start, size, total):
-        at = pl.ds(start, size)
-        h = h_ref[at, :]
-        u = u_ref[at, :]
-        da = da_ref[at, :]
+    def units(begin, h, u, da):
+        at = pl.ds(begin, h.shape[0])
         sigma = 1.0 / (1.0 + jnp.exp(-h))
         silu = h * sigma
         act = silu * u
@@ -246,41 +242,59 @@
         du_ref[at, :] = du.astype(BF16)
         dhr_ref[:, at] = dh.T.astype(BF16)
         dur_ref[:, at] = du.T.astype(BF16)
-        return total + jnp.sum(act * da, axis=0, keepdims=True)
-
+        return jnp.sum(act * da, axis=0, keepdims=True)
+
+    last = steps - 1
+    cols = pl.ds(last * chunk, chunk)
+    for wait in waits(last):
+        wait.wait()
     total = jnp.zeros((1, rows), F32)
-    for begin in range(0, hidden, LANES):
-        total = units(begin, min(LANES, hidden - begin), total)
+    for begin in range(0, hidden, BLOCK):
+        end = min(begin + BLOCK, hidden)
+        h, u, da = (
+            out[begin:end, :] + lax.dot_general(w, v[:, cols], NT, preferred_element_type=F32)
+            for out, w, v in (
+                (h_ref, wg_ref[begin:end, cols], x_ref),
+                (u_ref, wu_ref[begin:end, cols], x_ref),
+                (da_ref, ring[last % slots, begin:end, :], g_ref),
+            )
+        )
+        for at in range(0, end - begin, LANES):
+            part = slice(at, min(at + LANES, end - begin))
+            total += units(begin + at, h[part], u[part], da[part])
     gates = jnp.broadcast_to(total, (LANES, rows)).T
     tile = tile_of(hidden, 448)
+    half = steps // 2
     leaving = []
     for i in range(steps):
-        cols = pl.ds(i * chunk, chunk)
-        acc[:, cols] = jnp.dot(dhr_ref[...], wg_ref[:, cols], preferred_element_type=F32) + jnp.dot(
-            dur_ref[...], wu_ref[:, cols], preferred_element_type=F32
-        )
-        room = wg_ref.at[:, pl.ds((i - 1) * chunk, chunk)] if i else ring.at[0]
+        side, c = divmod(i, half)
+        cols = pl.ds(place_of(i, half, chunk, 1 - t), chunk)
+        parts[side, :, c * chunk : (c + 1) * chunk] = jnp.dot(
+            dhr_ref[...], wg_ref[:, cols], preferred_element_type=F32
+        ) + jnp.dot(dur_ref[...], wu_ref[:, cols], preferred_element_type=F32)
+        if i >= slots:
+            leaving[i - slots].wait()
+        room = ring.at[i % slots]
         for at in range(0, hidden, tile):
             room[at : at + tile, :] = jnp.dot(
                 wt_ref[at : at + tile, :], g_ref[:, cols], preferred_element_type=F32
             ).astype(BF16)
         leaving.append(pltpu.make_async_copy(room, down_ref.at[:, cols], sent.at[i]))
         leaving[-1].start()
-    for at, out in ((1 - t, give_ref), (t, keep_ref)):
-        held[...] = acc[:, pl.ds(pl.multiple_of(at * width, width), width)]
-        pack(held, gates, out, pieces)
-    for copy in leaving:
+        if c == half - 1:
+            pack(parts.at[side], gates, (give_ref, keep_ref)[side], pieces)
+    for copy in leaving[-slots:]:
         copy.wait()
 
 
-def expert_units(t, mine, early, late, w_gate, w_up, w_down, width):
+def expert_units(t, mine, theirs, w_gate, w_up, w_down, width):
     hidden, depth = w_gate.shape
     pieces = len(mine)
     rows = -(-pieces * CAP // 16) * 16
     chunk = chunk_of(width, 768)
     steps = depth // chunk
     ahead = 3
-    slots = 4
+    slots = min(5, steps)
     unit = jax.ShapeDtypeStruct((hidden, rows), BF16)
     packed = jax.ShapeDtypeStruct((pieces * SUBS, width // 2 + width // SUBS + LANES), F32)
     return pl.pallas_call(
@@ -293,7 +307,7 @@
             packed,
             jax.ShapeDtypeStruct((hidden, depth), BF16),
         ),
-        in_specs=[SMEM] + [VMEM] * (pieces + 2) + [HBM] * 3,
+        in_specs=[SMEM] + [VMEM] * (pieces + 1) + [HBM] * 3,
         out_specs=[VMEM] * 5 + [HBM],
         scratch_shapes=[
             pltpu.VMEM((hidden, depth), BF16),
@@ -306,7 +320,7 @@
             pltpu.VMEM((hidden, rows), F32),
             pltpu.VMEM((rows, hidden), BF16),
             pltpu.VMEM((rows, hidden), BF16),
-            pltpu.VMEM((rows, depth), F32),
+            pltpu.VMEM((2, rows, width), F32),
             pltpu.VMEM((rows, width), F32),
             pltpu.VMEM((rows, LANES), F32),
             pltpu.SemaphoreType.DMA((steps, 2)),
@@ -318,7 +332,7 @@
             flops=12 * rows * hidden * depth, bytes_accessed=8 * hidden * depth, transcendentals=rows * hidden
         ),
         name="expert_units",
-    )(t, *mine, early, late, w_gate, w_up, w_down)
+    )(t, *mine, theirs, w_gate, w_up, w_down)
 
 
 def weights_body(chunk, left_ref, x_ref, out_ref, room, sent):
@@ -458,14 +472,10 @@
     got = partner(oth)
     first = {0: own} | {d: across(own, d) for d in far_first}
     second = {0: got} | {d: across(got, d) for d in far_first}
-    early = [own, got] + [first[d] for d in range(1, copies)]
-    late = [second[d] for d in range(1, copies)]
-    if late:
-        early, late[far_first[0] - 1] = lax.optimization_barrier((early, late[far_first[0] - 1]))
-    early_there = other_core(stack(early, "stack_early"))
-    late_there = other_core(stack(late, "stack_late"))
+    pieces = [piece for d in range(copies) for piece in (first[d], second[d])]
+    theirs = other_core(stack(pieces, "stack_pieces"))
     x, dh, du, give, keep, grad_w_down = expert_units(
-        t, early + late, early_there, late_there, w_gate, w_up, w_down, width
+        t, pieces, theirs, w_gate, w_up, w_down, width
     )
     blocks = list(fold(copies, keep, other_core(give)))
     arrived = {d: across(blocks[d], d) for d in far_first}

time: 75 us -> 72 us (0.960)
  starting transfers between devices: 19.7 us -> 17.5 us
  waiting for transfers between devices: 8.58 us -> 7.03 us
    ppermute x9, waiting for transfers between devices: 5.39 us -> 3.4 us  [across(): return lax.ppermute(v, 'expert', [(i, i ^ d) for i in range(n_expert)])]
    ppermute x9, starting transfers between devices: 12.7 us -> 10.8 us  [across(): return lax.ppermute(v, 'expert', [(i, i ^ d) for i in range(n_expert)])]
    ppermute x3 -> x2, waiting for transfers between devices: 3.19 us -> 3.62 us  [other_core(): return lax.ppermute(v, 'tensor', [(0, 1), (1, 0)])]
  transfers between devices with their start and end apart: 14 -> 13, of which waited for: 7 -> 6; matrix products, arithmetic and copies ran while one was open for 0% -> 0% of each run, Pallas kernels for 18% -> 19%
where the time goes in v10:
time: 72 us; the launch traced here: 71.8 us
  Pallas kernels  46.5 us (65%)
  starting transfers between devices  17.5 us (24%)
  waiting for transfers between devices  7.03 us (10%)
  between operations  0.75 us (1%)
    pallas_call x1, Pallas kernels, expert_units(): pl.pallas_call(functools.partial(experts_body, pieces, chunk, ahead), out...  30.2 us
    pallas_call x2, Pallas kernels, weight_grad(): pl.pallas_call(functools.partial(weights_body, chunk), out_shape=jax.Shap...  13.3 us
    ppermute x9, starting transfers between devices, across(): return lax.ppermute(v, 'expert', [(i, i ^ d) for i in range(n_expert)])  10.8 us
    ppermute x2, starting transfers between devices, partner(): lax.ppermute(v, 'expert', [(i, (i + copies) % n_expert) for i in range(n_...  6.37 us
    ppermute x2, waiting for transfers between devices, other_core(): return lax.ppermute(v, 'tensor', [(0, 1), (1, 0)])  3.62 us
    ppermute x9, waiting for transfers between devices, across(): return lax.ppermute(v, 'expert', [(i, i ^ d) for i in range(n_expert)])  3.4 us
    pallas_call x1, Pallas kernels, finish(): pl.pallas_call(finish_body, out_shape=(jax.ShapeDtypeStruct((toks, width)...  1.54 us
  transfers between devices with their start and end apart: 13, of which 6 were waited for; matrix products, arithmetic and copies ran while one was open for 0% of the time, Pallas kernels for 19%

profile of v10, /device:TPU:0, one launch (start us, length us, event | category | flops | bytes accessed | tf_op | source)
XLA Modules:
  0.0 71.8 jit_solution(6457241033446364841)
XLA Ops:
  0.6 1.4 %pick_rows.1 = (bf16[8,3968]{1,0:T(8,128)(2,1)S(1)}, bf16[8,3968]{1,0:T(8,128)(2,1)S(1)}) custom-call(s32[1]{0:T(128)} %bitcast.e_ref, s32[4,16]{1,0:T(4,128)} %bitcast.5, bf16[4,16]{1,0:T(4,128)(2,1)} %bitcast.7, bf16[16,3072]{1,0:T(8,128)(2,1)} %tok_any.1, bf16[16,3072]{1,0:T(8,128)(2,1)} %grad_any.1), custom_call_target="tpu_custom_call" | custom-call | tf_op jit(solution)/shard_map/pick_rows/pallas_call | solution.py:94
  2.0 4.1 %collective-permute-start = (bf16[8,3968]{1,0:T(8,128)(2,1)S(1)}, bf16[8,3968]{1,0:T(8,128)(2,1)S(1)}, u32[]{:S(2)}, u32[]{:S(2)}) collective-permute-start(bf16[8,3968]{1,0:T(8,128)(2,1)S(1)} %get-tuple-element.32), channel_id=1, source_target_pairs={{0,8},{2,10},{4,12},{6,14},{8,0},{10,2},{12,4},{14,6},{1,9},{3,11}... | collective-permute-start | bytes 190472 | tf_op jit(solution)/shard_map/ppermute | solution.py:459
  6.1 2.5 %collective-permute-start.5 = (bf16[8,3968]{1,0:T(8,128)(2,1)S(1)}, bf16[8,3968]{1,0:T(8,128)(2,1)S(1)}, u32[]{:S(2)}, u32[]{:S(2)}) collective-permute-start(bf16[8,3968]{1,0:T(8,128)(2,1)S(1)} %get-tuple-element.31.refs_0_), channel_id=1, source_target_pairs={{0,6},{2,4},{4,2},{6,0},{8,14},{10,12},{12,10},{14,8},{1,7},{3,5},... | collective-permute-start | bytes 190472 | tf_op jit(solution)/shard_map/ppermute | solution.py:462
  8.6 0.4 collective-permute-start.3
  9.1 0.5 collective-permute-start.1
  9.6 0.0 collective-permute-done.refs_1_
  9.6 2.5 %collective-permute-start.6 = (bf16[8,3968]{1,0:T(8,128)(2,1)S(1)}, bf16[8,3968]{1,0:T(8,128)(2,1)S(1)}, u32[]{:S(2)}, u32[]{:S(2)}) collective-permute-start(bf16[8,3968]{1,0:T(8,128)(2,1)S(1)} %collective-permute-done.refs_1_), channel_id=1, source_target_pairs={{0,6},{2,4},{4,2},{6,0},{8,14},{10,12},{12,10},{14,8},{1,7},{3,5},... | collective-permute-start | bytes 190472 | tf_op jit(solution)/shard_map/ppermute | solution.py:462
  12.1 0.4 collective-permute-start.4
  12.6 0.0 collective-permute-done.5.refs_6_
  12.6 0.8 %collective-permute-start.2 = (bf16[8,3968]{1,0:T(8,128)(2,1)S(1)}, bf16[8,3968]{1,0:T(8,128)(2,1)S(1)}, u32[]{:S(2)}, u32[]{:S(2)}) collective-permute-start(bf16[8,3968]{1,0:T(8,128)(2,1)S(1)} %collective-permute-done.refs_1_), channel_id=1, source_target_pairs={{0,2},{2,0},{4,6},{6,4},{8,10},{10,8},{12,14},{14,12},{1,3},{3,1},... | collective-permute-start | bytes 190472 | tf_op jit(solution)/shard_map/ppermute | solution.py:462
  13.4 0.0 collective-permute-done.3.refs_4_
  13.4 0.2 collective-permute-done.1.refs_2_
  13.6 1.2 %collective-permute-done.6.refs_7_ = bf16[8,3968]{1,0:T(8,128)(2,1)S(1)} collective-permute-done((bf16[8,3968]{1,0:T(8,128)(2,1)S(1)}, bf16[8,3968]{1,0:T(8,128)(2,1)S(1)}, u32[]{:S(2)}, u32[]{:S(2)}) %collective-permute-start.6) | collective-permute-done | bytes 63520 | tf_op jit(solution)/shard_map/ppermute | solution.py:462
  14.8 1.5 %collective-permute-done.4.refs_5_ = bf16[8,3968]{1,0:T(8,128)(2,1)S(1)} collective-permute-done((bf16[8,3968]{1,0:T(8,128)(2,1)S(1)}, bf16[8,3968]{1,0:T(8,128)(2,1)S(1)}, u32[]{:S(2)}, u32[]{:S(2)}) %collective-permute-start.4) | collective-permute-done | bytes 63520 | tf_op jit(solution)/shard_map/ppermute | solution.py:462
  16.4 0.4 collective-permute-done.2.refs_3_
  16.8 0.1 collective-permute-start.7
  16.9 1.9 %collective-permute-done.7.refs_8_ = bf16[8,8,3968]{2,1,0:T(8,128)(2,1)S(1)} collective-permute-done((bf16[8,8,3968]{2,1,0:T(8,128)(2,1)S(1)}, bf16[8,8,3968]{2,1,0:T(8,128)(2,1)S(1)}, u32[]{:S(2)}, u32[]{:S(2)}) %collective-permute-start.7) | collective-permute-done | bytes 507936 | tf_op jit(solution)/shard_map/ppermute | solution.py:465
  18.8 30.2 %expert_units.1 = (bf16[48,6144]{1,0:T(8,128)(2,1)S(1)}, bf16[1344,48]{1,0:T(8,128)(2,1)S(1)}, bf16[1344,48]{1,0:T(8,128)(2,1)S(1)}, f32[64,2048]{1,0:T(8,128)S(...) custom-call(s32[1]{0:T(128)} %bitcast.2.t_ref, bf16[8,3968]{1,0:T(8,128)(2,1)S(1)} %get-tuple-element.31.refs_0_, ...), custom_call_target="tpu_custom_call" | custom-call | flops 4756340736 | bytes 66060288 | tf_op jit(solution)/shard_map/expert_units/pallas_call | solution.py:300
  49.0 0.2 collective-permute-start.8
  49.2 1.8 %collective-permute-done.8.got_ref = f32[64,2048]{1,0:T(8,128)S(1)} collective-permute-done((f32[64,2048]{1,0:T(8,128)S(1)}, f32[64,2048]{1,0:T(8,128)S(1)}, u32[]{:S(2)}, u32[]{:S(2)}) %collective-permute-start.8) | collective-permute-done | bytes 524320 | tf_op jit(solution)/shard_map/ppermute | solution.py:465
  51.0 0.1 fold_cores.1
  51.0 0.9 %collective-permute-start.9 = (f32[16,2048]{1,0:T(8,128)S(1)}, f32[16,2048]{1,0:T(8,128)S(1)}, u32[]{:S(2)}, u32[]{:S(2)}) collective-permute-start(f32[16,2048]{1,0:T(8,128)S(1)} %get-tuple-element.41), channel_id=1, source_target_pairs={{0,2},{2,0},{4,6},{6,4},{8,10},{10,8},{12,14},{14,12},{1,3},{3,1},... | collective-permute-start | bytes 393224 | tf_op jit(solution)/shard_map/ppermute | solution.py:462
  52.0 1.3 %collective-permute-start.10 = (f32[16,2048]{1,0:T(8,128)S(1)}, f32[16,2048]{1,0:T(8,128)S(1)}, u32[]{:S(2)}, u32[]{:S(2)}) collective-permute-start(f32[16,2048]{1,0:T(8,128)S(1)} %get-tuple-element.42), channel_id=1, source_target_pairs={{0,4},{2,6},{4,0},{6,2},{8,12},{10,14},{12,8},{14,10},{1,5},{3,7},... | collective-permute-start | bytes 393224 | tf_op jit(solution)/shard_map/ppermute | solution.py:462
  53.2 1.4 %collective-permute-start.11 = (f32[16,2048]{1,0:T(8,128)S(1)}, f32[16,2048]{1,0:T(8,128)S(1)}, u32[]{:S(2)}, u32[]{:S(2)}) collective-permute-start(f32[16,2048]{1,0:T(8,128)S(1)} %get-tuple-element.43), channel_id=1, source_target_pairs={{0,6},{2,4},{4,2},{6,0},{8,14},{10,12},{12,10},{14,8},{1,7},{3,5},... | collective-permute-start | bytes 393224 | tf_op jit(solution)/shard_map/ppermute | solution.py:462
  54.6 0.0 copy-start
  54.6 6.7 %grad_gate.1 = bf16[1344,6144]{1,0:T(8,128)(2,1)} custom-call(bf16[1344,48]{1,0:T(8,128)(2,1)S(1)} %get-tuple-element.39.left_ref, bf16[48,6144]{1,0:T(8,128)(2,1)S(1)} %get-tuple-element.40.x_ref), custom_call_target="tpu_custom_call" | custom-call | flops 792723456 | bytes 16515072 | tf_op jit(solution)/shard_map/grad_gate/pallas_call | solution.py:360
  61.3 0.0 collective-permute-done.9.refs_1_
  61.3 0.0 collective-permute-done.10.refs_2_
  61.3 0.0 collective-permute-done.11.refs_3_
  61.3 2.3 %collective-permute-start.12 = (f32[8,2048]{1,0:T(8,128)S(1)}, f32[8,2048]{1,0:T(8,128)S(1)}, u32[]{:S(2)}, u32[]{:S(2)}) collective-permute-start(f32[8,2048]{1,0:T(8,128)S(1)} %get-tuple-element.50), channel_id=1, source_target_pairs={{0,8},{2,10},{4,12},{6,14},{8,0},{10,2},{12,4},{14,6},{1,9},{3,11}... | collective-permute-start | bytes 196616 | tf_op jit(solution)/shard_map/ppermute | solution.py:459
  63.6 6.6 %grad_up.1 = bf16[1344,6144]{1,0:T(8,128)(2,1)} custom-call(bf16[1344,48]{1,0:T(8,128)(2,1)S(1)} %get-tuple-element.49.left_ref, bf16[48,6144]{1,0:T(8,128)(2,1)S(1)} %get-tuple-element.40.x_ref), custom_call_target="tpu_custom_call" | custom-call | flops 792723456 | bytes 16515072 | tf_op jit(solution)/shard_map/grad_up/pallas_call | solution.py:360
  70.2 0.0 collective-permute-done.12.got_ref
  70.3 0.0 copy-done
  70.3 1.5 %finish_tokens.1 = (bf16[16,3072]{1,0:T(8,128)(2,1)}, f32[4,16]{1,0:T(4,128)}) custom-call(s32[1]{0:T(128)} %bitcast.e_ref, s32[4,16]{1,0:T(4,128)S(1)} %bitcast.6, f32[8,2048]{1,0:T(8,128)S(1)} %get-tuple-element.48.mine_ref, f32[8,2048]{1,0:T(8,128)S(1)} %collective-permute-done.12.got_ref), custom_call_target="tpu_custom_call" | custom-call | tf_op jit(solution)/shard_map/finish_tokens/pallas_call | solution.py:440
  (2 shorter events, 0.1 us)
Async XLA Ops:
  2.0 7.6 %collective-permute-start = (bf16[8,3968]{1,0:T(8,128)(2,1)S(1)}, bf16[8,3968]{1,0:T(8,128)(2,1)S(1)}, u32[]{:S(2)}, u32[]{:S(2)}) collective-permute-start(bf16[8,3968]{1,0:T(8,128)(2,1)S(1)} %get-tuple-element.32), channel_id=1, source_target_pairs={{0,8},{2,10},{4,12},{6,14},{8,0},{10,2},{12,4},{14,6},{1,9},{3,11}... | collective-permute-start | bytes 190472 | tf_op jit(solution)/shard_map/ppermute | solution.py:459
  6.1 6.4 %collective-permute-start.5 = (bf16[8,3968]{1,0:T(8,128)(2,1)S(1)}, bf16[8,3968]{1,0:T(8,128)(2,1)S(1)}, u32[]{:S(2)}, u32[]{:S(2)}) collective-permute-start(bf16[8,3968]{1,0:T(8,128)(2,1)S(1)} %get-tuple-element.31.refs_0_), channel_id=1, source_target_pairs={{0,6},{2,4},{4,2},{6,0},{8,14},{10,12},{12,10},{14,8},{1,7},{3,5},... | collective-permute-start | bytes 190472 | tf_op jit(solution)/shard_map/ppermute | solution.py:462
  8.6 4.8 %collective-permute-start.3 = (bf16[8,3968]{1,0:T(8,128)(2,1)S(1)}, bf16[8,3968]{1,0:T(8,128)(2,1)S(1)}, u32[]{:S(2)}, u32[]{:S(2)}) collective-permute-start(bf16[8,3968]{1,0:T(8,128)(2,1)S(1)} %get-tuple-element.31.refs_0_), channel_id=1, source_target_pairs={{0,4},{2,6},{4,0},{6,2},{8,12},{10,14},{12,8},{14,10},{1,5},{3,7},... | collective-permute-start | bytes 190472 | tf_op jit(solution)/shard_map/ppermute | solution.py:462
  9.1 4.6 %collective-permute-start.1 = (bf16[8,3968]{1,0:T(8,128)(2,1)S(1)}, bf16[8,3968]{1,0:T(8,128)(2,1)S(1)}, u32[]{:S(2)}, u32[]{:S(2)}) collective-permute-start(bf16[8,3968]{1,0:T(8,128)(2,1)S(1)} %get-tuple-element.31.refs_0_), channel_id=1, source_target_pairs={{0,2},{2,0},{4,6},{6,4},{8,10},{10,8},{12,14},{14,12},{1,3},{3,1},... | collective-permute-start | bytes 190472 | tf_op jit(solution)/shard_map/ppermute | solution.py:462
  9.6 5.2 %collective-permute-start.6 = (bf16[8,3968]{1,0:T(8,128)(2,1)S(1)}, bf16[8,3968]{1,0:T(8,128)(2,1)S(1)}, u32[]{:S(2)}, u32[]{:S(2)}) collective-permute-start(bf16[8,3968]{1,0:T(8,128)(2,1)S(1)} %collective-permute-done.refs_1_), channel_id=1, source_target_pairs={{0,6},{2,4},{4,2},{6,0},{8,14},{10,12},{12,10},{14,8},{1,7},{3,5},... | collective-permute-start | bytes 190472 | tf_op jit(solution)/shard_map/ppermute | solution.py:462
  12.1 4.2 %collective-permute-start.4 = (bf16[8,3968]{1,0:T(8,128)(2,1)S(1)}, bf16[8,3968]{1,0:T(8,128)(2,1)S(1)}, u32[]{:S(2)}, u32[]{:S(2)}) collective-permute-start(bf16[8,3968]{1,0:T(8,128)(2,1)S(1)} %collective-permute-done.refs_1_), channel_id=1, source_target_pairs={{0,4},{2,6},{4,0},{6,2},{8,12},{10,14},{12,8},{14,10},{1,5},{3,7},... | collective-permute-start | bytes 190472 | tf_op jit(solution)/shard_map/ppermute | solution.py:462
  12.6 4.2 %collective-permute-start.2 = (bf16[8,3968]{1,0:T(8,128)(2,1)S(1)}, bf16[8,3968]{1,0:T(8,128)(2,1)S(1)}, u32[]{:S(2)}, u32[]{:S(2)}) collective-permute-start(bf16[8,3968]{1,0:T(8,128)(2,1)S(1)} %collective-permute-done.refs_1_), channel_id=1, source_target_pairs={{0,2},{2,0},{4,6},{6,4},{8,10},{10,8},{12,14},{14,12},{1,3},{3,1},... | collective-permute-start | bytes 190472 | tf_op jit(solution)/shard_map/ppermute | solution.py:462
  16.8 2.0 %collective-permute-start.7 = (bf16[8,8,3968]{2,1,0:T(8,128)(2,1)S(1)}, bf16[8,8,3968]{2,1,0:T(8,128)(2,1)S(1)}, u32[]{:S(2)}, u32[]{:S(2)}) collective-permute-start(bf16[8,8,3968]{2,1,0:T(8,128)(2,1)S(1)} %stack_pieces.1), channel_id=1, source_target_pairs={{0,1},{1,0},{2,3},{3,2},{4,5},{5,4},{6,7},{7,6},{8,9},{9,8},{10,11... | collective-permute-start | bytes 1523720 | tf_op jit(solution)/shard_map/ppermute | solution.py:465
  49.0 2.0 %collective-permute-start.8 = (f32[64,2048]{1,0:T(8,128)S(1)}, f32[64,2048]{1,0:T(8,128)S(1)}, u32[]{:S(2)}, u32[]{:S(2)}) collective-permute-start(f32[64,2048]{1,0:T(8,128)S(1)} %get-tuple-element.36), channel_id=1, source_target_pairs={{0,1},{1,0},{2,3},{3,2},{4,5},{5,4},{6,7},{7,6},{8,9},{9,8},{10,11... | collective-permute-start | bytes 1572872 | tf_op jit(solution)/shard_map/ppermute | solution.py:465
  51.0 10.2 %collective-permute-start.9 = (f32[16,2048]{1,0:T(8,128)S(1)}, f32[16,2048]{1,0:T(8,128)S(1)}, u32[]{:S(2)}, u32[]{:S(2)}) collective-permute-start(f32[16,2048]{1,0:T(8,128)S(1)} %get-tuple-element.41), channel_id=1, source_target_pairs={{0,2},{2,0},{4,6},{6,4},{8,10},{10,8},{12,14},{14,12},{1,3},{3,1},... | collective-permute-start | bytes 393224 | tf_op jit(solution)/shard_map/ppermute | solution.py:462
  52.0 9.3 %collective-permute-start.10 = (f32[16,2048]{1,0:T(8,128)S(1)}, f32[16,2048]{1,0:T(8,128)S(1)}, u32[]{:S(2)}, u32[]{:S(2)}) collective-permute-start(f32[16,2048]{1,0:T(8,128)S(1)} %get-tuple-element.42), channel_id=1, source_target_pairs={{0,4},{2,6},{4,0},{6,2},{8,12},{10,14},{12,8},{14,10},{1,5},{3,7},... | collective-permute-start | bytes 393224 | tf_op jit(solution)/shard_map/ppermute | solution.py:462
  53.2 8.1 %collective-permute-start.11 = (f32[16,2048]{1,0:T(8,128)S(1)}, f32[16,2048]{1,0:T(8,128)S(1)}, u32[]{:S(2)}, u32[]{:S(2)}) collective-permute-start(f32[16,2048]{1,0:T(8,128)S(1)} %get-tuple-element.43), channel_id=1, source_target_pairs={{0,6},{2,4},{4,2},{6,0},{8,14},{10,12},{12,10},{14,8},{1,7},{3,5},... | collective-permute-start | bytes 393224 | tf_op jit(solution)/shard_map/ppermute | solution.py:462
  54.6 15.7 %copy-start = (s32[16,4]{0,1:T(4,128)S(1)}, s32[16,4]{0,1:T(4,128)}, u32[]{:S(2)}) copy-start(s32[16,4]{0,1:T(4,128)} %param.9) | copy-start | bytes 772
  61.3 8.9 %collective-permute-start.12 = (f32[8,2048]{1,0:T(8,128)S(1)}, f32[8,2048]{1,0:T(8,128)S(1)}, u32[]{:S(2)}, u32[]{:S(2)}) collective-permute-start(f32[8,2048]{1,0:T(8,128)S(1)} %get-tuple-element.50), channel_id=1, source_target_pairs={{0,8},{2,10},{4,12},{6,14},{8,0},{10,2},{12,4},{14,6},{1,9},{3,11}... | collective-permute-start | bytes 196616 | tf_op jit(solution)/shard_map/ppermute | solution.py:459

commit v11 on v9

--- a/solution.py
+++ b/solution.py
@@ -15,6 +15,8 @@
 F32 = jnp.float32
 BF16 = jnp.bfloat16
 MIB = 1 << 20
+GATE_CHUNKS = 2
+UP_CHUNKS = 4
 VMEM = pl.BlockSpec(memory_space=pltpu.VMEM)
 SMEM = pl.BlockSpec(memory_space=pltpu.SMEM)
 HBM = pl.BlockSpec(memory_space=pltpu.HBM)
@@ -123,19 +125,12 @@
     out[:, pl.ds(base, width)] = held[...].astype(BF16)
 
 
-def slot_of(n, pieces):
-    if n < 2:
-        return n
-    far = pieces // 2 - 1
-    return 2 * (n - 1) if n < 2 + far else 2 * (n - 1 - far) + 1
-
-
 def pack(part, gates, out, pieces):
     width = part.shape[1]
     half, eighth = width // 2, width // SUBS
     size = half + eighth
     for n in range(pieces):
-        at, to = n * CAP, slot_of(n, pieces) * SUBS
+        at, to = n * CAP, n * SUBS
         for h in range(2):
             out[to + h * WHOLE : to + (h + 1) * WHOLE, :half] = part[at : at + WHOLE, h * half : (h + 1) * half]
         for s in range(SUBS):
@@ -161,11 +156,11 @@
 
 
 def experts_body(pieces, chunk, ahead, t_ref, *refs):
-    mine, (early, late) = refs[:pieces], refs[pieces : pieces + 2]
-    theirs = [early.at[n] for n in range(early.shape[0])] + [late.at[n] for n in range(late.shape[0])]
-    (wg_hbm, wu_hbm, wd_hbm, x_ref, dh_ref, du_ref, give_ref, keep_ref, down_ref,
+    mine = refs[:pieces]
+    theirs = [refs[pieces].at[n] for n in range(pieces)]
+    (wg_hbm, wu_hbm, wd_hbm, x_ref, dh_ref, du_ref, give_ref, keep_ref, down_ref, gate_ref, up_ref,
      wg_ref, wu_ref, ring, g_ref, wt_ref, h_ref, u_ref, da_ref, dhr_ref, dur_ref, acc,
-     held, factor, landed, ring_landed, sent) = refs[pieces + 2 :]
+     held, factor, landed, ring_landed, sent) = refs[pieces + 1 :]
     rows, depth = x_ref.shape
     hidden = wg_ref.shape[0]
     width = depth // 2
@@ -259,13 +254,19 @@
         acc[:, cols] = jnp.dot(dhr_ref[...], wg_ref[:, cols], preferred_element_type=F32) + jnp.dot(
             dur_ref[...], wu_ref[:, cols], preferred_element_type=F32
         )
-        room = wg_ref.at[:, pl.ds((i - 1) * chunk, chunk)] if i else ring.at[0]
-        for at in range(0, hidden, tile):
-            room[at : at + tile, :] = jnp.dot(
-                wt_ref[at : at + tile, :], g_ref[:, cols], preferred_element_type=F32
-            ).astype(BF16)
-        leaving.append(pltpu.make_async_copy(room, down_ref.at[:, cols], sent.at[i]))
-        leaving[-1].start()
+        before = pl.ds((i - 1) * chunk, chunk)
+        jobs = [(wt_ref, g_ref, wg_ref.at[:, before] if i else ring.at[0], down_ref)]
+        if i < UP_CHUNKS:
+            jobs.append((du_ref, x_ref, wu_ref.at[:, before] if i else ring.at[1], up_ref))
+        if i < GATE_CHUNKS:
+            jobs.append((dh_ref, x_ref, ring.at[2 + i], gate_ref))
+        for left, right, room, out in jobs:
+            for at in range(0, hidden, tile):
+                room[at : at + tile, :] = jnp.dot(
+                    left[at : at + tile, :], right[:, cols], preferred_element_type=F32
+                ).astype(BF16)
+            leaving.append(pltpu.make_async_copy(room, out.at[:, cols], sent.at[len(leaving)]))
+            leaving[-1].start()
     for at, out in ((1 - t, give_ref), (t, keep_ref)):
         held[...] = acc[:, pl.ds(pl.multiple_of(at * width, width), width)]
         pack(held, gates, out, pieces)
@@ -273,7 +274,7 @@
         copy.wait()
 
 
-def expert_units(t, mine, early, late, w_gate, w_up, w_down, width):
+def expert_units(t, mine, theirs, w_gate, w_up, w_down, width):
     hidden, depth = w_gate.shape
     pieces = len(mine)
     rows = -(-pieces * CAP // 16) * 16
@@ -291,10 +292,10 @@
             unit,
             packed,
             packed,
-            jax.ShapeDtypeStruct((hidden, depth), BF16),
-        ),
-        in_specs=[SMEM] + [VMEM] * (pieces + 2) + [HBM] * 3,
-        out_specs=[VMEM] * 5 + [HBM],
+        )
+        + (jax.ShapeDtypeStruct((hidden, depth), BF16),) * 3,
+        in_specs=[SMEM] + [VMEM] * (pieces + 1) + [HBM] * 3,
+        out_specs=[VMEM] * 5 + [HBM] * 3,
         scratch_shapes=[
             pltpu.VMEM((hidden, depth), BF16),
             pltpu.VMEM((hidden, depth), BF16),
@@ -311,23 +312,22 @@
             pltpu.VMEM((rows, LANES), F32),
             pltpu.SemaphoreType.DMA((steps, 2)),
             pltpu.SemaphoreType.DMA((slots,)),
-            pltpu.SemaphoreType.DMA((steps,)),
+            pltpu.SemaphoreType.DMA((steps + UP_CHUNKS + GATE_CHUNKS,)),
         ],
         compiler_params=pltpu.CompilerParams(vmem_limit_bytes=50 * MIB),
         cost_estimate=pl.CostEstimate(
             flops=12 * rows * hidden * depth, bytes_accessed=8 * hidden * depth, transcendentals=rows * hidden
         ),
         name="expert_units",
-    )(t, *mine, early, late, w_gate, w_up, w_down)
-
-
-def weights_body(chunk, left_ref, x_ref, out_ref, room, sent):
+    )(t, *mine, theirs, w_gate, w_up, w_down)
+
+
+def weights_body(chunk, begun, left_ref, x_ref, _, out_ref, room, sent):
     hidden = left_ref.shape[0]
-    steps = x_ref.shape[1] // chunk
     tile = tile_of(hidden, 448)
     leaving = []
-    for i in range(steps):
-        cols = pl.ds(i * chunk, chunk)
+    for i in range(room.shape[0]):
+        cols = pl.ds((begun + i) * chunk, chunk)
         for at in range(0, hidden, tile):
             room[i, at : at + tile, :] = jnp.dot(
                 left_ref[at : at + tile, :], x_ref[:, cols], preferred_element_type=F32
@@ -338,23 +338,24 @@
         copy.wait()
 
 
-def weight_grad(left, right, name):
+def weight_grad(left, right, part, begun, name):
     hidden, rows = left.shape
     depth = right.shape[1]
-    chunk = chunk_of(depth, 768)
-    steps = depth // chunk
-    return pl.pallas_call(
-        functools.partial(weights_body, chunk),
+    chunk = chunk_of(depth // 2, 768)
+    steps = depth // chunk - begun
+    return pl.pallas_call(
+        functools.partial(weights_body, chunk, begun),
         out_shape=jax.ShapeDtypeStruct((hidden, depth), BF16),
-        in_specs=[VMEM] * 2,
+        in_specs=[VMEM] * 2 + [HBM],
         out_specs=HBM,
+        input_output_aliases={2: 0},
         scratch_shapes=[pltpu.VMEM((steps, hidden, chunk), BF16), pltpu.SemaphoreType.DMA((steps,))],
         compiler_params=pltpu.CompilerParams(vmem_limit_bytes=28 * MIB),
         cost_estimate=pl.CostEstimate(
-            flops=2 * rows * hidden * depth, bytes_accessed=2 * hidden * depth, transcendentals=0
+            flops=2 * rows * hidden * steps * chunk, bytes_accessed=2 * hidden * steps * chunk, transcendentals=0
         ),
         name=name,
-    )(left, right)
+    )(left, right, part)
 
 
 def fold_body(copies, keep_ref, got_ref, *outs):
@@ -458,24 +459,20 @@
     got = partner(oth)
     first = {0: own} | {d: across(own, d) for d in far_first}
     second = {0: got} | {d: across(got, d) for d in far_first}
-    early = [own, got] + [first[d] for d in range(1, copies)]
-    late = [second[d] for d in range(1, copies)]
-    if late:
-        early, late[far_first[0] - 1] = lax.optimization_barrier((early, late[far_first[0] - 1]))
-    early_there = other_core(stack(early, "stack_early"))
-    late_there = other_core(stack(late, "stack_late"))
-    x, dh, du, give, keep, grad_w_down = expert_units(
-        t, early + late, early_there, late_there, w_gate, w_up, w_down, width
+    pieces = [piece for d in range(copies) for piece in (first[d], second[d])]
+    theirs = other_core(stack(pieces, "stack_pieces"))
+    x, dh, du, give, keep, grad_w_down, gate_begun, up_begun = expert_units(
+        t, pieces, theirs, w_gate, w_up, w_down, width
     )
     blocks = list(fold(copies, keep, other_core(give)))
     arrived = {d: across(blocks[d], d) for d in far_first}
     dh, local = lax.optimization_barrier((dh, blocks[0]))
-    grad_w_gate = weight_grad(dh, x, "grad_gate")
+    grad_w_gate = weight_grad(dh, x, gate_begun, GATE_CHUNKS, "grad_gate")
     grad_w_gate, arrived = lax.optimization_barrier((grad_w_gate, arrived))
     kept, others = merge([local] + [arrived[d] for d in range(1, copies)])
     back = partner(others)
     du, kept = lax.optimization_barrier((du, kept))
-    grad_w_up = weight_grad(du, x, "grad_up")
+    grad_w_up = weight_grad(du, x, up_begun, UP_CHUNKS, "grad_up")
     grad_w_up, back = lax.optimization_barrier((grad_w_up, back))
     token_grad, gate_t = finish(e, ids_t, kept, back, width)
     return token_grad, gate_t.T, grad_w_gate, grad_w_up, grad_w_down

time: 75 us -> 71.5 us (0.953)
  starting transfers between devices: 19.7 us -> 17.6 us
  waiting for transfers between devices: 8.58 us -> 7.69 us
    pallas_call x2, Pallas kernels: 13.2 us -> 9.47 us  [weight_grad(): pl.pallas_call(functools.partial(weights_body, chunk, begun), out_shape=j...]
    pallas_call x1, Pallas kernels: 29.5 us -> 32.8 us  [expert_units(): pl.pallas_call(functools.partial(experts_body, pieces, chunk, ahead), out...]
    ppermute x9, starting transfers between devices: 12.7 us -> 10.8 us  [across(): return lax.ppermute(v, 'expert', [(i, i ^ d) for i in range(n_expert)])]
    ppermute x9, waiting for transfers between devices: 5.39 us -> 4.04 us  [across(): return lax.ppermute(v, 'expert', [(i, i ^ d) for i in range(n_expert)])]
    ppermute x3 -> x2, waiting for transfers between devices: 3.19 us -> 3.65 us  [other_core(): return lax.ppermute(v, 'tensor', [(0, 1), (1, 0)])]
  transfers between devices with their start and end apart: 14 -> 13, of which waited for: 7 -> 7; matrix products, arithmetic and copies ran while one was open for 0% -> 0% of each run, Pallas kernels for 18% -> 13%
where the time goes in v11:
time: 71.5 us; the launch traced here: 71.4 us
  Pallas kernels  45.3 us (63%)
  starting transfers between devices  17.6 us (25%)
  waiting for transfers between devices  7.69 us (11%)
  between operations  0.74 us (1%)
    pallas_call x1, Pallas kernels, expert_units(): pl.pallas_call(functools.partial(experts_body, pieces, chunk, ahead), out...  32.8 us
    ppermute x9, starting transfers between devices, across(): return lax.ppermute(v, 'expert', [(i, i ^ d) for i in range(n_expert)])  10.8 us
    pallas_call x2, Pallas kernels, weight_grad(): pl.pallas_call(functools.partial(weights_body, chunk, begun), out_shape=j...  9.47 us
    ppermute x2, starting transfers between devices, partner(): lax.ppermute(v, 'expert', [(i, (i + copies) % n_expert) for i in range(n_...  6.5 us
    ppermute x9, waiting for transfers between devices, across(): return lax.ppermute(v, 'expert', [(i, i ^ d) for i in range(n_expert)])  4.04 us
    ppermute x2, waiting for transfers between devices, other_core(): return lax.ppermute(v, 'tensor', [(0, 1), (1, 0)])  3.65 us
    pallas_call x1, Pallas kernels, finish(): pl.pallas_call(finish_body, out_shape=(jax.ShapeDtypeStruct((toks, width)...  1.54 us
  transfers between devices with their start and end apart: 13, of which 7 were waited for; matrix products, arithmetic and copies ran while one was open for 0% of the time, Pallas kernels for 13%

profile of v11, /device:TPU:0, one launch (start us, length us, event | category | flops | bytes accessed | tf_op | source)
XLA Modules:
  0.0 71.4 jit_solution(4117419306157709145)
XLA Ops:
  0.6 1.4 %pick_rows.1 = (bf16[8,3968]{1,0:T(8,128)(2,1)S(1)}, bf16[8,3968]{1,0:T(8,128)(2,1)S(1)}) custom-call(s32[1]{0:T(128)} %bitcast.e_ref, s32[4,16]{1,0:T(4,128)} %bitcast.5, bf16[4,16]{1,0:T(4,128)(2,1)} %bitcast.7, bf16[16,3072]{1,0:T(8,128)(2,1)} %tok_any.1, bf16[16,3072]{1,0:T(8,128)(2,1)} %grad_any.1), custom_call_target="tpu_custom_call" | custom-call | tf_op jit(solution)/shard_map/pick_rows/pallas_call | solution.py:95
  2.0 4.1 %collective-permute-start = (bf16[8,3968]{1,0:T(8,128)(2,1)S(1)}, bf16[8,3968]{1,0:T(8,128)(2,1)S(1)}, u32[]{:S(2)}, u32[]{:S(2)}) collective-permute-start(bf16[8,3968]{1,0:T(8,128)(2,1)S(1)} %get-tuple-element.34), channel_id=1, source_target_pairs={{0,8},{2,10},{4,12},{6,14},{8,0},{10,2},{12,4},{14,6},{1,9},{3,11}... | collective-permute-start | bytes 190472 | tf_op jit(solution)/shard_map/ppermute | solution.py:446
  6.1 2.5 %collective-permute-start.5 = (bf16[8,3968]{1,0:T(8,128)(2,1)S(1)}, bf16[8,3968]{1,0:T(8,128)(2,1)S(1)}, u32[]{:S(2)}, u32[]{:S(2)}) collective-permute-start(bf16[8,3968]{1,0:T(8,128)(2,1)S(1)} %get-tuple-element.33.refs_0_), channel_id=1, source_target_pairs={{0,6},{2,4},{4,2},{6,0},{8,14},{10,12},{12,10},{14,8},{1,7},{3,5},... | collective-permute-start | bytes 190472 | tf_op jit(solution)/shard_map/ppermute | solution.py:449
  8.6 0.4 collective-permute-start.3
  9.1 0.5 collective-permute-start.1
  9.6 0.0 collective-permute-done.refs_1_
  9.6 2.5 %collective-permute-start.6 = (bf16[8,3968]{1,0:T(8,128)(2,1)S(1)}, bf16[8,3968]{1,0:T(8,128)(2,1)S(1)}, u32[]{:S(2)}, u32[]{:S(2)}) collective-permute-start(bf16[8,3968]{1,0:T(8,128)(2,1)S(1)} %collective-permute-done.refs_1_), channel_id=1, source_target_pairs={{0,6},{2,4},{4,2},{6,0},{8,14},{10,12},{12,10},{14,8},{1,7},{3,5},... | collective-permute-start | bytes 190472 | tf_op jit(solution)/shard_map/ppermute | solution.py:449
  12.1 0.4 collective-permute-start.4
  12.6 0.0 collective-permute-done.5.refs_6_
  12.6 0.8 %collective-permute-start.2 = (bf16[8,3968]{1,0:T(8,128)(2,1)S(1)}, bf16[8,3968]{1,0:T(8,128)(2,1)S(1)}, u32[]{:S(2)}, u32[]{:S(2)}) collective-permute-start(bf16[8,3968]{1,0:T(8,128)(2,1)S(1)} %collective-permute-done.refs_1_), channel_id=1, source_target_pairs={{0,2},{2,0},{4,6},{6,4},{8,10},{10,8},{12,14},{14,12},{1,3},{3,1},... | collective-permute-start | bytes 190472 | tf_op jit(solution)/shard_map/ppermute | solution.py:449
  13.4 0.0 collective-permute-done.3.refs_4_
  13.4 0.2 collective-permute-done.1.refs_2_
  13.6 1.2 %collective-permute-done.6.refs_7_ = bf16[8,3968]{1,0:T(8,128)(2,1)S(1)} collective-permute-done((bf16[8,3968]{1,0:T(8,128)(2,1)S(1)}, bf16[8,3968]{1,0:T(8,128)(2,1)S(1)}, u32[]{:S(2)}, u32[]{:S(2)}) %collective-permute-start.6) | collective-permute-done | bytes 63520 | tf_op jit(solution)/shard_map/ppermute | solution.py:449
  14.8 1.5 %collective-permute-done.4.refs_5_ = bf16[8,3968]{1,0:T(8,128)(2,1)S(1)} collective-permute-done((bf16[8,3968]{1,0:T(8,128)(2,1)S(1)}, bf16[8,3968]{1,0:T(8,128)(2,1)S(1)}, u32[]{:S(2)}, u32[]{:S(2)}) %collective-permute-start.4) | collective-permute-done | bytes 63520 | tf_op jit(solution)/shard_map/ppermute | solution.py:449
  16.4 0.4 collective-permute-done.2.refs_3_
  16.8 0.1 collective-permute-start.7
  16.9 1.9 %collective-permute-done.7.refs_8_ = bf16[8,8,3968]{2,1,0:T(8,128)(2,1)S(1)} collective-permute-done((bf16[8,8,3968]{2,1,0:T(8,128)(2,1)S(1)}, bf16[8,8,3968]{2,1,0:T(8,128)(2,1)S(1)}, u32[]{:S(2)}, u32[]{:S(2)}) %collective-permute-start.7) | collective-permute-done | bytes 507936 | tf_op jit(solution)/shard_map/ppermute | solution.py:452
  18.8 32.8 %expert_units.1 = (bf16[48,6144]{1,0:T(8,128)(2,1)S(1)}, bf16[1344,48]{1,0:T(8,128)(2,1)S(1)}, bf16[1344,48]{1,0:T(8,128)(2,1)S(1)}, f32[64,2048]{1,0:T(8,128)S(...) custom-call(s32[1]{0:T(128)} %bitcast.2.t_ref, ...), custom_call_target="tpu_custom_call" | custom-call | flops 4756340736 | bytes 66060288 | tf_op jit(solution)/shard_map/expert_units/pallas_call | solution.py:287
  51.6 0.2 collective-permute-start.8
  51.8 1.8 %collective-permute-done.8.got_ref = f32[64,2048]{1,0:T(8,128)S(1)} collective-permute-done((f32[64,2048]{1,0:T(8,128)S(1)}, f32[64,2048]{1,0:T(8,128)S(1)}, u32[]{:S(2)}, u32[]{:S(2)}) %collective-permute-start.8) | collective-permute-done | bytes 524320 | tf_op jit(solution)/shard_map/ppermute | solution.py:452
  53.6 0.1 fold_cores.1
  53.7 0.9 %collective-permute-start.9 = (f32[16,2048]{1,0:T(8,128)S(1)}, f32[16,2048]{1,0:T(8,128)S(1)}, u32[]{:S(2)}, u32[]{:S(2)}) collective-permute-start(f32[16,2048]{1,0:T(8,128)S(1)} %get-tuple-element.44), channel_id=1, source_target_pairs={{0,2},{2,0},{4,6},{6,4},{8,10},{10,8},{12,14},{14,12},{1,3},{3,1},... | collective-permute-start | bytes 393224 | tf_op jit(solution)/shard_map/ppermute | solution.py:449
  54.6 1.3 %collective-permute-start.10 = (f32[16,2048]{1,0:T(8,128)S(1)}, f32[16,2048]{1,0:T(8,128)S(1)}, u32[]{:S(2)}, u32[]{:S(2)}) collective-permute-start(f32[16,2048]{1,0:T(8,128)S(1)} %get-tuple-element.45), channel_id=1, source_target_pairs={{0,4},{2,6},{4,0},{6,2},{8,12},{10,14},{12,8},{14,10},{1,5},{3,7},... | collective-permute-start | bytes 393224 | tf_op jit(solution)/shard_map/ppermute | solution.py:449
  55.8 1.4 %collective-permute-start.11 = (f32[16,2048]{1,0:T(8,128)S(1)}, f32[16,2048]{1,0:T(8,128)S(1)}, u32[]{:S(2)}, u32[]{:S(2)}) collective-permute-start(f32[16,2048]{1,0:T(8,128)S(1)} %get-tuple-element.46), channel_id=1, source_target_pairs={{0,6},{2,4},{4,2},{6,0},{8,14},{10,12},{12,10},{14,8},{1,7},{3,5},... | collective-permute-start | bytes 393224 | tf_op jit(solution)/shard_map/ppermute | solution.py:449
  57.2 5.4 %grad_gate.1 = bf16[1344,6144]{1,0:T(8,128)(2,1)} custom-call(bf16[1344,48]{1,0:T(8,128)(2,1)S(1)} %get-tuple-element.41.left_ref, bf16[48,6144]{1,0:T(8,128)(2,1)S(1)} %get-tuple-element.42.x_ref, bf16[1344,6144]{1,0:T(8,128)(2,1)} %get-tuple-element.43._), custom_call_target="tpu_custom_call", output_to_operand_aliasing={{}: (2, {})} | custom-call | flops 594542592 | bytes 12386304 | tf_op jit(solution)/shard_map/grad_gate/pallas_call | solution.py:346
  62.6 0.0 collective-permute-done.9.refs_1_
  62.6 0.0 collective-permute-done.10.refs_2_
  62.6 0.6 collective-permute-done.11.refs_3_
  63.3 2.4 %collective-permute-start.12 = (f32[8,2048]{1,0:T(8,128)S(1)}, f32[8,2048]{1,0:T(8,128)S(1)}, u32[]{:S(2)}, u32[]{:S(2)}) collective-permute-start(f32[8,2048]{1,0:T(8,128)S(1)} %get-tuple-element.54), channel_id=1, source_target_pairs={{0,8},{2,10},{4,12},{6,14},{8,0},{10,2},{12,4},{14,6},{1,9},{3,11}... | collective-permute-start | bytes 196616 | tf_op jit(solution)/shard_map/ppermute | solution.py:446
  65.7 0.0 copy-start
  65.7 4.1 %grad_up.1 = bf16[1344,6144]{1,0:T(8,128)(2,1)} custom-call(bf16[1344,48]{1,0:T(8,128)(2,1)S(1)} %get-tuple-element.52.left_ref, bf16[48,6144]{1,0:T(8,128)(2,1)S(1)} %get-tuple-element.42.x_ref, bf16[1344,6144]{1,0:T(8,128)(2,1)} %get-tuple-element.53._), custom_call_target="tpu_custom_call", output_to_operand_aliasing={{}: (2, {})} | custom-call | flops 396361728 | bytes 8257536 | tf_op jit(solution)/shard_map/grad_up/pallas_call | solution.py:346
  69.8 0.0 collective-permute-done.12.got_ref
  69.8 0.0 copy-done
  69.8 1.5 %finish_tokens.1 = (bf16[16,3072]{1,0:T(8,128)(2,1)}, f32[4,16]{1,0:T(4,128)}) custom-call(s32[1]{0:T(128)} %bitcast.e_ref, s32[4,16]{1,0:T(4,128)S(1)} %bitcast.6, f32[8,2048]{1,0:T(8,128)S(1)} %get-tuple-element.51.mine_ref, f32[8,2048]{1,0:T(8,128)S(1)} %collective-permute-done.12.got_ref), custom_call_target="tpu_custom_call" | custom-call | tf_op jit(solution)/shard_map/finish_tokens/pallas_call | solution.py:427
  (2 shorter events, 0.1 us)
Async XLA Ops:
  2.0 7.6 %collective-permute-start = (bf16[8,3968]{1,0:T(8,128)(2,1)S(1)}, bf16[8,3968]{1,0:T(8,128)(2,1)S(1)}, u32[]{:S(2)}, u32[]{:S(2)}) collective-permute-start(bf16[8,3968]{1,0:T(8,128)(2,1)S(1)} %get-tuple-element.34), channel_id=1, source_target_pairs={{0,8},{2,10},{4,12},{6,14},{8,0},{10,2},{12,4},{14,6},{1,9},{3,11}... | collective-permute-start | bytes 190472 | tf_op jit(solution)/shard_map/ppermute | solution.py:446
  6.1 6.4 %collective-permute-start.5 = (bf16[8,3968]{1,0:T(8,128)(2,1)S(1)}, bf16[8,3968]{1,0:T(8,128)(2,1)S(1)}, u32[]{:S(2)}, u32[]{:S(2)}) collective-permute-start(bf16[8,3968]{1,0:T(8,128)(2,1)S(1)} %get-tuple-element.33.refs_0_), channel_id=1, source_target_pairs={{0,6},{2,4},{4,2},{6,0},{8,14},{10,12},{12,10},{14,8},{1,7},{3,5},... | collective-permute-start | bytes 190472 | tf_op jit(solution)/shard_map/ppermute | solution.py:449
  8.6 4.8 %collective-permute-start.3 = (bf16[8,3968]{1,0:T(8,128)(2,1)S(1)}, bf16[8,3968]{1,0:T(8,128)(2,1)S(1)}, u32[]{:S(2)}, u32[]{:S(2)}) collective-permute-start(bf16[8,3968]{1,0:T(8,128)(2,1)S(1)} %get-tuple-element.33.refs_0_), channel_id=1, source_target_pairs={{0,4},{2,6},{4,0},{6,2},{8,12},{10,14},{12,8},{14,10},{1,5},{3,7},... | collective-permute-start | bytes 190472 | tf_op jit(solution)/shard_map/ppermute | solution.py:449
  9.1 4.6 %collective-permute-start.1 = (bf16[8,3968]{1,0:T(8,128)(2,1)S(1)}, bf16[8,3968]{1,0:T(8,128)(2,1)S(1)}, u32[]{:S(2)}, u32[]{:S(2)}) collective-permute-start(bf16[8,3968]{1,0:T(8,128)(2,1)S(1)} %get-tuple-element.33.refs_0_), channel_id=1, source_target_pairs={{0,2},{2,0},{4,6},{6,4},{8,10},{10,8},{12,14},{14,12},{1,3},{3,1},... | collective-permute-start | bytes 190472 | tf_op jit(solution)/shard_map/ppermute | solution.py:449
  9.6 5.2 %collective-permute-start.6 = (bf16[8,3968]{1,0:T(8,128)(2,1)S(1)}, bf16[8,3968]{1,0:T(8,128)(2,1)S(1)}, u32[]{:S(2)}, u32[]{:S(2)}) collective-permute-start(bf16[8,3968]{1,0:T(8,128)(2,1)S(1)} %collective-permute-done.refs_1_), channel_id=1, source_target_pairs={{0,6},{2,4},{4,2},{6,0},{8,14},{10,12},{12,10},{14,8},{1,7},{3,5},... | collective-permute-start | bytes 190472 | tf_op jit(solution)/shard_map/ppermute | solution.py:449
  12.1 4.2 %collective-permute-start.4 = (bf16[8,3968]{1,0:T(8,128)(2,1)S(1)}, bf16[8,3968]{1,0:T(8,128)(2,1)S(1)}, u32[]{:S(2)}, u32[]{:S(2)}) collective-permute-start(bf16[8,3968]{1,0:T(8,128)(2,1)S(1)} %collective-permute-done.refs_1_), channel_id=1, source_target_pairs={{0,4},{2,6},{4,0},{6,2},{8,12},{10,14},{12,8},{14,10},{1,5},{3,7},... | collective-permute-start | bytes 190472 | tf_op jit(solution)/shard_map/ppermute | solution.py:449
  12.6 4.2 %collective-permute-start.2 = (bf16[8,3968]{1,0:T(8,128)(2,1)S(1)}, bf16[8,3968]{1,0:T(8,128)(2,1)S(1)}, u32[]{:S(2)}, u32[]{:S(2)}) collective-permute-start(bf16[8,3968]{1,0:T(8,128)(2,1)S(1)} %collective-permute-done.refs_1_), channel_id=1, source_target_pairs={{0,2},{2,0},{4,6},{6,4},{8,10},{10,8},{12,14},{14,12},{1,3},{3,1},... | collective-permute-start | bytes 190472 | tf_op jit(solution)/shard_map/ppermute | solution.py:449
  16.8 2.0 %collective-permute-start.7 = (bf16[8,8,3968]{2,1,0:T(8,128)(2,1)S(1)}, bf16[8,8,3968]{2,1,0:T(8,128)(2,1)S(1)}, u32[]{:S(2)}, u32[]{:S(2)}) collective-permute-start(bf16[8,8,3968]{2,1,0:T(8,128)(2,1)S(1)} %stack_pieces.1), channel_id=1, source_target_pairs={{0,1},{1,0},{2,3},{3,2},{4,5},{5,4},{6,7},{7,6},{8,9},{9,8},{10,11... | collective-permute-start | bytes 1523720 | tf_op jit(solution)/shard_map/ppermute | solution.py:452
  51.6 2.0 %collective-permute-start.8 = (f32[64,2048]{1,0:T(8,128)S(1)}, f32[64,2048]{1,0:T(8,128)S(1)}, u32[]{:S(2)}, u32[]{:S(2)}) collective-permute-start(f32[64,2048]{1,0:T(8,128)S(1)} %get-tuple-element.38), channel_id=1, source_target_pairs={{0,1},{1,0},{2,3},{3,2},{4,5},{5,4},{6,7},{7,6},{8,9},{9,8},{10,11... | collective-permute-start | bytes 1572872 | tf_op jit(solution)/shard_map/ppermute | solution.py:452
  53.7 8.9 %collective-permute-start.9 = (f32[16,2048]{1,0:T(8,128)S(1)}, f32[16,2048]{1,0:T(8,128)S(1)}, u32[]{:S(2)}, u32[]{:S(2)}) collective-permute-start(f32[16,2048]{1,0:T(8,128)S(1)} %get-tuple-element.44), channel_id=1, source_target_pairs={{0,2},{2,0},{4,6},{6,4},{8,10},{10,8},{12,14},{14,12},{1,3},{3,1},... | collective-permute-start | bytes 393224 | tf_op jit(solution)/shard_map/ppermute | solution.py:449
  54.6 8.0 %collective-permute-start.10 = (f32[16,2048]{1,0:T(8,128)S(1)}, f32[16,2048]{1,0:T(8,128)S(1)}, u32[]{:S(2)}, u32[]{:S(2)}) collective-permute-start(f32[16,2048]{1,0:T(8,128)S(1)} %get-tuple-element.45), channel_id=1, source_target_pairs={{0,4},{2,6},{4,0},{6,2},{8,12},{10,14},{12,8},{14,10},{1,5},{3,7},... | collective-permute-start | bytes 393224 | tf_op jit(solution)/shard_map/ppermute | solution.py:449
  55.8 7.4 %collective-permute-start.11 = (f32[16,2048]{1,0:T(8,128)S(1)}, f32[16,2048]{1,0:T(8,128)S(1)}, u32[]{:S(2)}, u32[]{:S(2)}) collective-permute-start(f32[16,2048]{1,0:T(8,128)S(1)} %get-tuple-element.46), channel_id=1, source_target_pairs={{0,6},{2,4},{4,2},{6,0},{8,14},{10,12},{12,10},{14,8},{1,7},{3,5},... | collective-permute-start | bytes 393224 | tf_op jit(solution)/shard_map/ppermute | solution.py:449
  63.3 6.5 %collective-permute-start.12 = (f32[8,2048]{1,0:T(8,128)S(1)}, f32[8,2048]{1,0:T(8,128)S(1)}, u32[]{:S(2)}, u32[]{:S(2)}) collective-permute-start(f32[8,2048]{1,0:T(8,128)S(1)} %get-tuple-element.54), channel_id=1, source_target_pairs={{0,8},{2,10},{4,12},{6,14},{8,0},{10,2},{12,4},{14,6},{1,9},{3,11}... | collective-permute-start | bytes 196616 | tf_op jit(solution)/shard_map/ppermute | solution.py:446
  65.7 4.1 %copy-start = (s32[16,4]{0,1:T(4,128)S(1)}, s32[16,4]{0,1:T(4,128)}, u32[]{:S(2)}) copy-start(s32[16,4]{0,1:T(4,128)} %param.9) | copy-start | bytes 772

commit v12 on v11

--- a/solution.py
+++ b/solution.py
@@ -15,7 +15,7 @@
 F32 = jnp.float32
 BF16 = jnp.bfloat16
 MIB = 1 << 20
-GATE_CHUNKS = 2
+GATE_CHUNKS = 1
 UP_CHUNKS = 4
 VMEM = pl.BlockSpec(memory_space=pltpu.VMEM)
 SMEM = pl.BlockSpec(memory_space=pltpu.SMEM)
@@ -159,7 +159,7 @@
     mine = refs[:pieces]
     theirs = [refs[pieces].at[n] for n in range(pieces)]
     (wg_hbm, wu_hbm, wd_hbm, x_ref, dh_ref, du_ref, give_ref, keep_ref, down_ref, gate_ref, up_ref,
-     wg_ref, wu_ref, ring, g_ref, wt_ref, h_ref, u_ref, da_ref, dhr_ref, dur_ref, acc,
+     wg_ref, wu_ref, ring, stage, g_ref, wt_ref, h_ref, u_ref, da_ref, dhr_ref, dur_ref, acc,
      held, factor, landed, ring_landed, sent) = refs[pieces + 1 :]
     rows, depth = x_ref.shape
     hidden = wg_ref.shape[0]
@@ -182,7 +182,6 @@
     def start(i):
         load(i, 0).start()
         load(i, 1).start()
-        load_down(i).start()
 
     start(0)
     held[...] = jnp.zeros_like(held)
@@ -195,82 +194,96 @@
     for i in range(1, min(ahead, steps)):
         start(i)
 
-    def three(i):
+    def add_up(i):
         cols = columns(i)
         x = x_ref[:, cols]
-        return (
-            lambda: lax.dot_general(wg_ref[:, cols], x, NT, preferred_element_type=F32),
-            lambda: lax.dot_general(wu_ref[:, cols], x, NT, preferred_element_type=F32),
-            lambda: lax.dot_general(ring[lax.rem(i, slots)], g_ref[:, cols], NT, preferred_element_type=F32),
-        )
-
-    sums = (h_ref, u_ref, da_ref)
-    waits = lambda i: (load(i, 0), load(i, 1), load_down(i))
-    for wait, dot, out in zip(waits(0), three(0), sums):
-        wait.wait()
-        out[...] = dot()
+        for n in range(2):
+            load(i, n).wait()
+        for w, out in ((wg_ref, h_ref), (wu_ref, u_ref)):
+            more = lax.dot_general(w[:, cols], x, NT, preferred_element_type=F32)
+            out[...] = jnp.where(i == 0, more, out[...] + more)
 
     def up_step(i, carry):
-        @pl.when(i + ahead - 1 < steps)
+        @pl.when(i + ahead < steps)
         def _():
-            start(i + ahead - 1)
-
-        for wait in waits(i):
-            wait.wait()
-        for dot, out in zip(three(i), sums):
-            out[...] += dot()
+            start(i + ahead)
+
+        @pl.when(jnp.logical_and(i + ahead >= steps, i + ahead - steps < slots))
+        def _():
+            load_down(i + ahead - steps).start()
+
+        add_up(i)
         return carry
 
-    lax.fori_loop(1, steps, up_step, 0)
+    lax.fori_loop(0, steps, up_step, 0)
+    for i in range(min(ahead, steps, slots), min(slots, steps)):
+        load_down(i).start()
 
     weight = factor[...].T[:1, :]
 
-    def units(start, size, total):
-        at = pl.ds(start, size)
-        h = h_ref[at, :]
-        u = u_ref[at, :]
-        da = da_ref[at, :]
+    spans = [(begin, min(begin + LANES, hidden)) for begin in range(0, hidden, LANES)]
+    for begin, end in spans:
+        h = h_ref[begin:end, :]
+        silu = h * (1.0 / (1.0 + jnp.exp(-h)))
+        wt_ref[begin:end, :] = (weight * (silu * u_ref[begin:end, :])).astype(BF16)
+
+    tile = tile_of(hidden, 448)
+    leaving = []
+
+    def leave(left, right, room, out, cols):
+        for at in range(0, hidden, tile):
+            room[at : at + tile, :] = jnp.dot(
+                left[at : at + tile, :], right[:, cols], preferred_element_type=F32
+            ).astype(BF16)
+        leaving.append(pltpu.make_async_copy(room, out.at[:, cols], sent.at[len(leaving)]))
+        leaving[-1].start()
+
+    staged = stage.shape[0]
+    for i in range(steps):
+        cols = pl.ds(i * chunk, chunk)
+        load_down(i).wait()
+        if i >= staged:
+            leaving[i - staged].wait()
+        more = lax.dot_general(ring[i % slots], g_ref[:, cols], NT, preferred_element_type=F32)
+        da_ref[...] = da_ref[...] + more if i else more
+        leave(wt_ref, g_ref, stage.at[i % staged], down_ref, cols)
+        if i + slots < steps:
+            load_down(i + slots).start()
+
+    total = jnp.zeros((1, rows), F32)
+    for begin, end in spans:
+        h = h_ref[begin:end, :]
+        u = u_ref[begin:end, :]
+        da = da_ref[begin:end, :]
         sigma = 1.0 / (1.0 + jnp.exp(-h))
         silu = h * sigma
         act = silu * u
         scaled = weight * da
-        wt_ref[at, :] = (weight * act).astype(BF16)
         dh = scaled * u * sigma * (1.0 + h * (1.0 - sigma))
         du = scaled * silu
-        dh_ref[at, :] = dh.astype(BF16)
-        du_ref[at, :] = du.astype(BF16)
-        dhr_ref[:, at] = dh.T.astype(BF16)
-        dur_ref[:, at] = du.T.astype(BF16)
-        return total + jnp.sum(act * da, axis=0, keepdims=True)
-
-    total = jnp.zeros((1, rows), F32)
-    for begin in range(0, hidden, LANES):
-        total = units(begin, min(LANES, hidden - begin), total)
+        dh_ref[begin:end, :] = dh.astype(BF16)
+        du_ref[begin:end, :] = du.astype(BF16)
+        dhr_ref[:, begin:end] = dh.T.astype(BF16)
+        dur_ref[:, begin:end] = du.T.astype(BF16)
+        total += jnp.sum(act * da, axis=0, keepdims=True)
     gates = jnp.broadcast_to(total, (LANES, rows)).T
-    tile = tile_of(hidden, 448)
-    leaving = []
+    for copy in leaving[steps - min(staged, steps) :]:
+        copy.wait()
+    gone = len(leaving)
     for i in range(steps):
         cols = pl.ds(i * chunk, chunk)
         acc[:, cols] = jnp.dot(dhr_ref[...], wg_ref[:, cols], preferred_element_type=F32) + jnp.dot(
             dur_ref[...], wu_ref[:, cols], preferred_element_type=F32
         )
         before = pl.ds((i - 1) * chunk, chunk)
-        jobs = [(wt_ref, g_ref, wg_ref.at[:, before] if i else ring.at[0], down_ref)]
         if i < UP_CHUNKS:
-            jobs.append((du_ref, x_ref, wu_ref.at[:, before] if i else ring.at[1], up_ref))
+            leave(du_ref, x_ref, wu_ref.at[:, before] if i else stage.at[0], up_ref, cols)
         if i < GATE_CHUNKS:
-            jobs.append((dh_ref, x_ref, ring.at[2 + i], gate_ref))
-        for left, right, room, out in jobs:
-            for at in range(0, hidden, tile):
-                room[at : at + tile, :] = jnp.dot(
-                    left[at : at + tile, :], right[:, cols], preferred_element_type=F32
-                ).astype(BF16)
-            leaving.append(pltpu.make_async_copy(room, out.at[:, cols], sent.at[len(leaving)]))
-            leaving[-1].start()
+            leave(dh_ref, x_ref, wg_ref.at[:, before] if i else stage.at[1], gate_ref, cols)
     for at, out in ((1 - t, give_ref), (t, keep_ref)):
         held[...] = acc[:, pl.ds(pl.multiple_of(at * width, width), width)]
         pack(held, gates, out, pieces)
-    for copy in leaving:
+    for copy in leaving[gone:]:
         copy.wait()
 
 
@@ -281,7 +294,7 @@
     chunk = chunk_of(width, 768)
     steps = depth // chunk
     ahead = 3
-    slots = 4
+    slots = min(3, steps)
     unit = jax.ShapeDtypeStruct((hidden, rows), BF16)
     packed = jax.ShapeDtypeStruct((pieces * SUBS, width // 2 + width // SUBS + LANES), F32)
     return pl.pallas_call(
@@ -300,6 +313,7 @@
             pltpu.VMEM((hidden, depth), BF16),
             pltpu.VMEM((hidden, depth), BF16),
             pltpu.VMEM((slots, hidden, chunk), BF16),
+            pltpu.VMEM((2, hidden, chunk), BF16),
             pltpu.VMEM((rows, depth), BF16),
             pltpu.VMEM((hidden, rows), BF16),
             pltpu.VMEM((hidden, rows), F32),

time: 71.5 us -> 72 us (level)
  Pallas kernels: 45.3 us -> 46.3 us
  transfers between devices with their start and end apart: 13 -> 13, of which waited for: 7 -> 7; matrix products, arithmetic and copies ran while one was open for 0% -> 0% of each run, Pallas kernels for 13% -> 14%
where the time goes in v12:
time: 72 us; the launch traced here: 71.8 us
  Pallas kernels  46.3 us (64%)
  starting transfers between devices  17.5 us (24%)
  waiting for transfers between devices  7.25 us (10%)
  between operations  0.74 us (1%)
    pallas_call x1, Pallas kernels, expert_units(): pl.pallas_call(functools.partial(experts_body, pieces, chunk, ahead), out...  33.3 us
    ppermute x9, starting transfers between devices, across(): return lax.ppermute(v, 'expert', [(i, i ^ d) for i in range(n_expert)])  10.8 us
    pallas_call x2, Pallas kernels, weight_grad(): pl.pallas_call(functools.partial(weights_body, chunk, begun), out_shape=j...  10 us
    ppermute x2, starting transfers between devices, partner(): lax.ppermute(v, 'expert', [(i, (i + copies) % n_expert) for i in range(n_...  6.53 us
    ppermute x2, waiting for transfers between devices, other_core(): return lax.ppermute(v, 'tensor', [(0, 1), (1, 0)])  3.77 us
    ppermute x9, waiting for transfers between devices, across(): return lax.ppermute(v, 'expert', [(i, i ^ d) for i in range(n_expert)])  3.48 us
    pallas_call x1, Pallas kernels, finish(): pl.pallas_call(finish_body, out_shape=(jax.ShapeDtypeStruct((toks, width)...  1.55 us
  transfers between devices with their start and end apart: 13, of which 7 were waited for; matrix products, arithmetic and copies ran while one was open for 0% of the time, Pallas kernels for 14%

profile of v12, /device:TPU:0, one launch (start us, length us, event | category | flops | bytes accessed | tf_op | source)
XLA Modules:
  0.0 71.8 jit_solution(8583215947352218089)
XLA Ops:
  0.6 1.4 %pick_rows.1 = (bf16[8,3968]{1,0:T(8,128)(2,1)S(1)}, bf16[8,3968]{1,0:T(8,128)(2,1)S(1)}) custom-call(s32[1]{0:T(128)} %bitcast.e_ref, s32[4,16]{1,0:T(4,128)} %bitcast.5, bf16[4,16]{1,0:T(4,128)(2,1)} %bitcast.7, bf16[16,3072]{1,0:T(8,128)(2,1)} %tok_any.1, bf16[16,3072]{1,0:T(8,128)(2,1)} %grad_any.1), custom_call_target="tpu_custom_call" | custom-call | tf_op jit(solution)/shard_map/pick_rows/pallas_call | solution.py:95
  2.0 4.1 %collective-permute-start = (bf16[8,3968]{1,0:T(8,128)(2,1)S(1)}, bf16[8,3968]{1,0:T(8,128)(2,1)S(1)}, u32[]{:S(2)}, u32[]{:S(2)}) collective-permute-start(bf16[8,3968]{1,0:T(8,128)(2,1)S(1)} %get-tuple-element.34), channel_id=1, source_target_pairs={{0,8},{2,10},{4,12},{6,14},{8,0},{10,2},{12,4},{14,6},{1,9},{3,11}... | collective-permute-start | bytes 190472 | tf_op jit(solution)/shard_map/ppermute | solution.py:460
  6.1 2.5 %collective-permute-start.5 = (bf16[8,3968]{1,0:T(8,128)(2,1)S(1)}, bf16[8,3968]{1,0:T(8,128)(2,1)S(1)}, u32[]{:S(2)}, u32[]{:S(2)}) collective-permute-start(bf16[8,3968]{1,0:T(8,128)(2,1)S(1)} %get-tuple-element.33.refs_0_), channel_id=1, source_target_pairs={{0,6},{2,4},{4,2},{6,0},{8,14},{10,12},{12,10},{14,8},{1,7},{3,5},... | collective-permute-start | bytes 190472 | tf_op jit(solution)/shard_map/ppermute | solution.py:463
  8.6 0.4 collective-permute-start.3
  9.1 0.5 collective-permute-start.1
  9.6 0.0 collective-permute-done.refs_1_
  9.6 2.5 %collective-permute-start.6 = (bf16[8,3968]{1,0:T(8,128)(2,1)S(1)}, bf16[8,3968]{1,0:T(8,128)(2,1)S(1)}, u32[]{:S(2)}, u32[]{:S(2)}) collective-permute-start(bf16[8,3968]{1,0:T(8,128)(2,1)S(1)} %collective-permute-done.refs_1_), channel_id=1, source_target_pairs={{0,6},{2,4},{4,2},{6,0},{8,14},{10,12},{12,10},{14,8},{1,7},{3,5},... | collective-permute-start | bytes 190472 | tf_op jit(solution)/shard_map/ppermute | solution.py:463
  12.1 0.4 collective-permute-start.4
  12.6 0.0 collective-permute-done.5.refs_6_
  12.6 0.8 %collective-permute-start.2 = (bf16[8,3968]{1,0:T(8,128)(2,1)S(1)}, bf16[8,3968]{1,0:T(8,128)(2,1)S(1)}, u32[]{:S(2)}, u32[]{:S(2)}) collective-permute-start(bf16[8,3968]{1,0:T(8,128)(2,1)S(1)} %collective-permute-done.refs_1_), channel_id=1, source_target_pairs={{0,2},{2,0},{4,6},{6,4},{8,10},{10,8},{12,14},{14,12},{1,3},{3,1},... | collective-permute-start | bytes 190472 | tf_op jit(solution)/shard_map/ppermute | solution.py:463
  13.4 0.0 collective-permute-done.3.refs_4_
  13.4 0.2 collective-permute-done.1.refs_2_
  13.6 1.2 %collective-permute-done.6.refs_7_ = bf16[8,3968]{1,0:T(8,128)(2,1)S(1)} collective-permute-done((bf16[8,3968]{1,0:T(8,128)(2,1)S(1)}, bf16[8,3968]{1,0:T(8,128)(2,1)S(1)}, u32[]{:S(2)}, u32[]{:S(2)}) %collective-permute-start.6) | collective-permute-done | bytes 63520 | tf_op jit(solution)/shard_map/ppermute | solution.py:463
  14.8 1.5 %collective-permute-done.4.refs_5_ = bf16[8,3968]{1,0:T(8,128)(2,1)S(1)} collective-permute-done((bf16[8,3968]{1,0:T(8,128)(2,1)S(1)}, bf16[8,3968]{1,0:T(8,128)(2,1)S(1)}, u32[]{:S(2)}, u32[]{:S(2)}) %collective-permute-start.4) | collective-permute-done | bytes 63520 | tf_op jit(solution)/shard_map/ppermute | solution.py:463
  16.4 0.4 collective-permute-done.2.refs_3_
  16.8 0.1 collective-permute-start.7
  16.9 1.9 %collective-permute-done.7.refs_8_ = bf16[8,8,3968]{2,1,0:T(8,128)(2,1)S(1)} collective-permute-done((bf16[8,8,3968]{2,1,0:T(8,128)(2,1)S(1)}, bf16[8,8,3968]{2,1,0:T(8,128)(2,1)S(1)}, u32[]{:S(2)}, u32[]{:S(2)}) %collective-permute-start.7) | collective-permute-done | bytes 507936 | tf_op jit(solution)/shard_map/ppermute | solution.py:466
  18.8 33.3 %expert_units.1 = (bf16[48,6144]{1,0:T(8,128)(2,1)S(1)}, bf16[1344,48]{1,0:T(8,128)(2,1)S(1)}, bf16[1344,48]{1,0:T(8,128)(2,1)S(1)}, f32[64,2048]{1,0:T(8,128)S(...) custom-call(s32[1]{0:T(128)} %bitcast.2.t_ref, ...), custom_call_target="tpu_custom_call" | custom-call | flops 4756340736 | bytes 66060288 | tf_op jit(solution)/shard_map/expert_units/pallas_call | solution.py:300
  52.1 0.1 collective-permute-start.8
  52.1 1.9 %collective-permute-done.8.got_ref = f32[64,2048]{1,0:T(8,128)S(1)} collective-permute-done((f32[64,2048]{1,0:T(8,128)S(1)}, f32[64,2048]{1,0:T(8,128)S(1)}, u32[]{:S(2)}, u32[]{:S(2)}) %collective-permute-start.8) | collective-permute-done | bytes 524320 | tf_op jit(solution)/shard_map/ppermute | solution.py:466
  54.0 0.1 fold_cores.1
  54.1 0.9 %collective-permute-start.9 = (f32[16,2048]{1,0:T(8,128)S(1)}, f32[16,2048]{1,0:T(8,128)S(1)}, u32[]{:S(2)}, u32[]{:S(2)}) collective-permute-start(f32[16,2048]{1,0:T(8,128)S(1)} %get-tuple-element.44), channel_id=1, source_target_pairs={{0,2},{2,0},{4,6},{6,4},{8,10},{10,8},{12,14},{14,12},{1,3},{3,1},... | collective-permute-start | bytes 393224 | tf_op jit(solution)/shard_map/ppermute | solution.py:463
  55.0 1.1 %collective-permute-start.10 = (f32[16,2048]{1,0:T(8,128)S(1)}, f32[16,2048]{1,0:T(8,128)S(1)}, u32[]{:S(2)}, u32[]{:S(2)}) collective-permute-start(f32[16,2048]{1,0:T(8,128)S(1)} %get-tuple-element.45), channel_id=1, source_target_pairs={{0,4},{2,6},{4,0},{6,2},{8,12},{10,14},{12,8},{14,10},{1,5},{3,7},... | collective-permute-start | bytes 393224 | tf_op jit(solution)/shard_map/ppermute | solution.py:463
  56.1 1.6 %collective-permute-start.11 = (f32[16,2048]{1,0:T(8,128)S(1)}, f32[16,2048]{1,0:T(8,128)S(1)}, u32[]{:S(2)}, u32[]{:S(2)}) collective-permute-start(f32[16,2048]{1,0:T(8,128)S(1)} %get-tuple-element.46), channel_id=1, source_target_pairs={{0,6},{2,4},{4,2},{6,0},{8,14},{10,12},{12,10},{14,8},{1,7},{3,5},... | collective-permute-start | bytes 393224 | tf_op jit(solution)/shard_map/ppermute | solution.py:463
  57.7 5.9 %grad_gate.1 = bf16[1344,6144]{1,0:T(8,128)(2,1)} custom-call(bf16[1344,48]{1,0:T(8,128)(2,1)S(1)} %get-tuple-element.41.left_ref, bf16[48,6144]{1,0:T(8,128)(2,1)S(1)} %get-tuple-element.42.x_ref, bf16[1344,6144]{1,0:T(8,128)(2,1)} %get-tuple-element.43._), custom_call_target="tpu_custom_call", output_to_operand_aliasing={{}: (2, {})} | custom-call | flops 693633024 | bytes 14450688 | tf_op jit(solution)/shard_map/grad_gate/pallas_call | solution.py:360
  63.6 0.0 collective-permute-done.9.refs_1_
  63.6 0.0 collective-permute-done.10.refs_2_
  63.6 0.1 collective-permute-done.11.refs_3_
  63.7 2.4 %collective-permute-start.12 = (f32[8,2048]{1,0:T(8,128)S(1)}, f32[8,2048]{1,0:T(8,128)S(1)}, u32[]{:S(2)}, u32[]{:S(2)}) collective-permute-start(f32[8,2048]{1,0:T(8,128)S(1)} %get-tuple-element.54), channel_id=1, source_target_pairs={{0,8},{2,10},{4,12},{6,14},{8,0},{10,2},{12,4},{14,6},{1,9},{3,11}... | collective-permute-start | bytes 196616 | tf_op jit(solution)/shard_map/ppermute | solution.py:460
  66.2 0.0 copy-start
  66.2 4.1 %grad_up.1 = bf16[1344,6144]{1,0:T(8,128)(2,1)} custom-call(bf16[1344,48]{1,0:T(8,128)(2,1)S(1)} %get-tuple-element.52.left_ref, bf16[48,6144]{1,0:T(8,128)(2,1)S(1)} %get-tuple-element.42.x_ref, bf16[1344,6144]{1,0:T(8,128)(2,1)} %get-tuple-element.53._), custom_call_target="tpu_custom_call", output_to_operand_aliasing={{}: (2, {})} | custom-call | flops 396361728 | bytes 8257536 | tf_op jit(solution)/shard_map/grad_up/pallas_call | solution.py:360
  70.3 0.0 collective-permute-done.12.got_ref
  70.3 0.0 copy-done
  70.3 1.5 %finish_tokens.1 = (bf16[16,3072]{1,0:T(8,128)(2,1)}, f32[4,16]{1,0:T(4,128)}) custom-call(s32[1]{0:T(128)} %bitcast.e_ref, s32[4,16]{1,0:T(4,128)S(1)} %bitcast.6, f32[8,2048]{1,0:T(8,128)S(1)} %get-tuple-element.51.mine_ref, f32[8,2048]{1,0:T(8,128)S(1)} %collective-permute-done.12.got_ref), custom_call_target="tpu_custom_call" | custom-call | tf_op jit(solution)/shard_map/finish_tokens/pallas_call | solution.py:441
  (2 shorter events, 0.1 us)
Async XLA Ops:
  2.0 7.6 %collective-permute-start = (bf16[8,3968]{1,0:T(8,128)(2,1)S(1)}, bf16[8,3968]{1,0:T(8,128)(2,1)S(1)}, u32[]{:S(2)}, u32[]{:S(2)}) collective-permute-start(bf16[8,3968]{1,0:T(8,128)(2,1)S(1)} %get-tuple-element.34), channel_id=1, source_target_pairs={{0,8},{2,10},{4,12},{6,14},{8,0},{10,2},{12,4},{14,6},{1,9},{3,11}... | collective-permute-start | bytes 190472 | tf_op jit(solution)/shard_map/ppermute | solution.py:460
  6.1 6.4 %collective-permute-start.5 = (bf16[8,3968]{1,0:T(8,128)(2,1)S(1)}, bf16[8,3968]{1,0:T(8,128)(2,1)S(1)}, u32[]{:S(2)}, u32[]{:S(2)}) collective-permute-start(bf16[8,3968]{1,0:T(8,128)(2,1)S(1)} %get-tuple-element.33.refs_0_), channel_id=1, source_target_pairs={{0,6},{2,4},{4,2},{6,0},{8,14},{10,12},{12,10},{14,8},{1,7},{3,5},... | collective-permute-start | bytes 190472 | tf_op jit(solution)/shard_map/ppermute | solution.py:463
  8.6 4.8 %collective-permute-start.3 = (bf16[8,3968]{1,0:T(8,128)(2,1)S(1)}, bf16[8,3968]{1,0:T(8,128)(2,1)S(1)}, u32[]{:S(2)}, u32[]{:S(2)}) collective-permute-start(bf16[8,3968]{1,0:T(8,128)(2,1)S(1)} %get-tuple-element.33.refs_0_), channel_id=1, source_target_pairs={{0,4},{2,6},{4,0},{6,2},{8,12},{10,14},{12,8},{14,10},{1,5},{3,7},... | collective-permute-start | bytes 190472 | tf_op jit(solution)/shard_map/ppermute | solution.py:463
  9.1 4.6 %collective-permute-start.1 = (bf16[8,3968]{1,0:T(8,128)(2,1)S(1)}, bf16[8,3968]{1,0:T(8,128)(2,1)S(1)}, u32[]{:S(2)}, u32[]{:S(2)}) collective-permute-start(bf16[8,3968]{1,0:T(8,128)(2,1)S(1)} %get-tuple-element.33.refs_0_), channel_id=1, source_target_pairs={{0,2},{2,0},{4,6},{6,4},{8,10},{10,8},{12,14},{14,12},{1,3},{3,1},... | collective-permute-start | bytes 190472 | tf_op jit(solution)/shard_map/ppermute | solution.py:463
  9.6 5.2 %collective-permute-start.6 = (bf16[8,3968]{1,0:T(8,128)(2,1)S(1)}, bf16[8,3968]{1,0:T(8,128)(2,1)S(1)}, u32[]{:S(2)}, u32[]{:S(2)}) collective-permute-start(bf16[8,3968]{1,0:T(8,128)(2,1)S(1)} %collective-permute-done.refs_1_), channel_id=1, source_target_pairs={{0,6},{2,4},{4,2},{6,0},{8,14},{10,12},{12,10},{14,8},{1,7},{3,5},... | collective-permute-start | bytes 190472 | tf_op jit(solution)/shard_map/ppermute | solution.py:463
  12.1 4.2 %collective-permute-start.4 = (bf16[8,3968]{1,0:T(8,128)(2,1)S(1)}, bf16[8,3968]{1,0:T(8,128)(2,1)S(1)}, u32[]{:S(2)}, u32[]{:S(2)}) collective-permute-start(bf16[8,3968]{1,0:T(8,128)(2,1)S(1)} %collective-permute-done.refs_1_), channel_id=1, source_target_pairs={{0,4},{2,6},{4,0},{6,2},{8,12},{10,14},{12,8},{14,10},{1,5},{3,7},... | collective-permute-start | bytes 190472 | tf_op jit(solution)/shard_map/ppermute | solution.py:463
  12.6 4.2 %collective-permute-start.2 = (bf16[8,3968]{1,0:T(8,128)(2,1)S(1)}, bf16[8,3968]{1,0:T(8,128)(2,1)S(1)}, u32[]{:S(2)}, u32[]{:S(2)}) collective-permute-start(bf16[8,3968]{1,0:T(8,128)(2,1)S(1)} %collective-permute-done.refs_1_), channel_id=1, source_target_pairs={{0,2},{2,0},{4,6},{6,4},{8,10},{10,8},{12,14},{14,12},{1,3},{3,1},... | collective-permute-start | bytes 190472 | tf_op jit(solution)/shard_map/ppermute | solution.py:463
  16.8 2.0 %collective-permute-start.7 = (bf16[8,8,3968]{2,1,0:T(8,128)(2,1)S(1)}, bf16[8,8,3968]{2,1,0:T(8,128)(2,1)S(1)}, u32[]{:S(2)}, u32[]{:S(2)}) collective-permute-start(bf16[8,8,3968]{2,1,0:T(8,128)(2,1)S(1)} %stack_pieces.1), channel_id=1, source_target_pairs={{0,1},{1,0},{2,3},{3,2},{4,5},{5,4},{6,7},{7,6},{8,9},{9,8},{10,11... | collective-permute-start | bytes 1523720 | tf_op jit(solution)/shard_map/ppermute | solution.py:466
  52.1 2.0 %collective-permute-start.8 = (f32[64,2048]{1,0:T(8,128)S(1)}, f32[64,2048]{1,0:T(8,128)S(1)}, u32[]{:S(2)}, u32[]{:S(2)}) collective-permute-start(f32[64,2048]{1,0:T(8,128)S(1)} %get-tuple-element.38), channel_id=1, source_target_pairs={{0,1},{1,0},{2,3},{3,2},{4,5},{5,4},{6,7},{7,6},{8,9},{9,8},{10,11... | collective-permute-start | bytes 1572872 | tf_op jit(solution)/shard_map/ppermute | solution.py:466
  54.1 9.5 %collective-permute-start.9 = (f32[16,2048]{1,0:T(8,128)S(1)}, f32[16,2048]{1,0:T(8,128)S(1)}, u32[]{:S(2)}, u32[]{:S(2)}) collective-permute-start(f32[16,2048]{1,0:T(8,128)S(1)} %get-tuple-element.44), channel_id=1, source_target_pairs={{0,2},{2,0},{4,6},{6,4},{8,10},{10,8},{12,14},{14,12},{1,3},{3,1},... | collective-permute-start | bytes 393224 | tf_op jit(solution)/shard_map/ppermute | solution.py:463
  55.0 8.6 %collective-permute-start.10 = (f32[16,2048]{1,0:T(8,128)S(1)}, f32[16,2048]{1,0:T(8,128)S(1)}, u32[]{:S(2)}, u32[]{:S(2)}) collective-permute-start(f32[16,2048]{1,0:T(8,128)S(1)} %get-tuple-element.45), channel_id=1, source_target_pairs={{0,4},{2,6},{4,0},{6,2},{8,12},{10,14},{12,8},{14,10},{1,5},{3,7},... | collective-permute-start | bytes 393224 | tf_op jit(solution)/shard_map/ppermute | solution.py:463
  56.1 7.6 %collective-permute-start.11 = (f32[16,2048]{1,0:T(8,128)S(1)}, f32[16,2048]{1,0:T(8,128)S(1)}, u32[]{:S(2)}, u32[]{:S(2)}) collective-permute-start(f32[16,2048]{1,0:T(8,128)S(1)} %get-tuple-element.46), channel_id=1, source_target_pairs={{0,6},{2,4},{4,2},{6,0},{8,14},{10,12},{12,10},{14,8},{1,7},{3,5},... | collective-permute-start | bytes 393224 | tf_op jit(solution)/shard_map/ppermute | solution.py:463
  63.7 6.5 %collective-permute-start.12 = (f32[8,2048]{1,0:T(8,128)S(1)}, f32[8,2048]{1,0:T(8,128)S(1)}, u32[]{:S(2)}, u32[]{:S(2)}) collective-permute-start(f32[8,2048]{1,0:T(8,128)S(1)} %get-tuple-element.54), channel_id=1, source_target_pairs={{0,8},{2,10},{4,12},{6,14},{8,0},{10,2},{12,4},{14,6},{1,9},{3,11}... | collective-permute-start | bytes 196616 | tf_op jit(solution)/shard_map/ppermute | solution.py:460
  66.2 4.1 %copy-start = (s32[16,4]{0,1:T(4,128)S(1)}, s32[16,4]{0,1:T(4,128)}, u32[]{:S(2)}) copy-start(s32[16,4]{0,1:T(4,128)} %param.9) | copy-start | bytes 772

commit v13 on v11

--- a/solution.py
+++ b/solution.py
@@ -15,7 +15,7 @@
 F32 = jnp.float32
 BF16 = jnp.bfloat16
 MIB = 1 << 20
-GATE_CHUNKS = 2
+GATE_CHUNKS = 1
 UP_CHUNKS = 4
 VMEM = pl.BlockSpec(memory_space=pltpu.VMEM)
 SMEM = pl.BlockSpec(memory_space=pltpu.SMEM)
@@ -155,7 +155,7 @@
     )(*pieces)
 
 
-def experts_body(pieces, chunk, ahead, t_ref, *refs):
+def experts_body(pieces, chunk, t_ref, *refs):
     mine = refs[:pieces]
     theirs = [refs[pieces].at[n] for n in range(pieces)]
     (wg_hbm, wu_hbm, wd_hbm, x_ref, dh_ref, du_ref, give_ref, keep_ref, down_ref, gate_ref, up_ref,
@@ -192,7 +192,7 @@
     for side, out in enumerate((x_ref, g_ref)):
         for group, at in ((mine, t), (theirs, 1 - t)):
             assemble(group, held, out, pl.multiple_of(at * width, width), side)
-    for i in range(1, min(ahead, steps)):
+    for i in range(1, min(3, steps)):
         start(i)
 
     def three(i):
@@ -210,18 +210,27 @@
         wait.wait()
         out[...] = dot()
 
-    def up_step(i, carry):
-        @pl.when(i + ahead - 1 < steps)
-        def _():
-            start(i + ahead - 1)
-
+    def pair_step(j, carry):
+        i = 1 + 2 * j
+        for n in (i + 2, i + 3):
+
+            @pl.when(n < steps)
+            def _():
+                start(n)
+
+        for wait in waits(i) + waits(i + 1):
+            wait.wait()
+        for dot, other, out in zip(three(i), three(i + 1), sums):
+            out[...] += dot() + other()
+        return carry
+
+    pairs = (steps - 1) // 2
+    lax.fori_loop(0, pairs, pair_step, 0)
+    for i in range(1 + 2 * pairs, steps):
         for wait in waits(i):
             wait.wait()
         for dot, out in zip(three(i), sums):
             out[...] += dot()
-        return carry
-
-    lax.fori_loop(1, steps, up_step, 0)
 
     weight = factor[...].T[:1, :]
 
@@ -280,12 +289,11 @@
     rows = -(-pieces * CAP // 16) * 16
     chunk = chunk_of(width, 768)
     steps = depth // chunk
-    ahead = 3
     slots = 4
     unit = jax.ShapeDtypeStruct((hidden, rows), BF16)
     packed = jax.ShapeDtypeStruct((pieces * SUBS, width // 2 + width // SUBS + LANES), F32)
     return pl.pallas_call(
-        functools.partial(experts_body, pieces, chunk, ahead),
+        functools.partial(experts_body, pieces, chunk),
         out_shape=(
             jax.ShapeDtypeStruct((rows, depth), BF16),
             unit,

time: 71.5 us -> 73.5 us (1.028)
  Pallas kernels: 45.3 us -> 47.9 us
    pallas_call x1, Pallas kernels: 32.8 us -> 34.8 us  [expert_units(): pl.pallas_call(functools.partial(experts_body, pieces, chunk), out_shape=...]
  transfers between devices with their start and end apart: 13 -> 13, of which waited for: 7 -> 7; matrix products, arithmetic and copies ran while one was open for 0% -> 0% of each run, Pallas kernels for 13% -> 14%
where the time goes in v13:
time: 73.5 us; the launch traced here: 73.3 us
  Pallas kernels  47.9 us (65%)
  starting transfers between devices  17.6 us (24%)
  waiting for transfers between devices  7.13 us (10%)
  between operations  0.74 us (1%)
    pallas_call x1, Pallas kernels, expert_units(): pl.pallas_call(functools.partial(experts_body, pieces, chunk), out_shape=...  34.8 us
    ppermute x9, starting transfers between devices, across(): return lax.ppermute(v, 'expert', [(i, i ^ d) for i in range(n_expert)])  10.8 us
    pallas_call x2, Pallas kernels, weight_grad(): pl.pallas_call(functools.partial(weights_body, chunk, begun), out_shape=j...  10 us
    ppermute x2, starting transfers between devices, partner(): lax.ppermute(v, 'expert', [(i, (i + copies) % n_expert) for i in range(n_...  6.48 us
    ppermute x2, waiting for transfers between devices, other_core(): return lax.ppermute(v, 'tensor', [(0, 1), (1, 0)])  3.62 us
    ppermute x9, waiting for transfers between devices, across(): return lax.ppermute(v, 'expert', [(i, i ^ d) for i in range(n_expert)])  3.5 us
    pallas_call x1, Pallas kernels, finish(): pl.pallas_call(finish_body, out_shape=(jax.ShapeDtypeStruct((toks, width)...  1.55 us
  transfers between devices with their start and end apart: 13, of which 7 were waited for; matrix products, arithmetic and copies ran while one was open for 0% of the time, Pallas kernels for 14%

profile of v13, /device:TPU:0, one launch (start us, length us, event | category | flops | bytes accessed | tf_op | source)
XLA Modules:
  0.0 73.3 jit_solution(732788219665378257)
XLA Ops:
  0.6 1.4 %pick_rows.1 = (bf16[8,3968]{1,0:T(8,128)(2,1)S(1)}, bf16[8,3968]{1,0:T(8,128)(2,1)S(1)}) custom-call(s32[1]{0:T(128)} %bitcast.e_ref, s32[4,16]{1,0:T(4,128)} %bitcast.5, bf16[4,16]{1,0:T(4,128)(2,1)} %bitcast.7, bf16[16,3072]{1,0:T(8,128)(2,1)} %tok_any.1, bf16[16,3072]{1,0:T(8,128)(2,1)} %grad_any.1), custom_call_target="tpu_custom_call" | custom-call | tf_op jit(solution)/shard_map/pick_rows/pallas_call | solution.py:95
  2.0 4.1 %collective-permute-start = (bf16[8,3968]{1,0:T(8,128)(2,1)S(1)}, bf16[8,3968]{1,0:T(8,128)(2,1)S(1)}, u32[]{:S(2)}, u32[]{:S(2)}) collective-permute-start(bf16[8,3968]{1,0:T(8,128)(2,1)S(1)} %get-tuple-element.34), channel_id=1, source_target_pairs={{0,8},{2,10},{4,12},{6,14},{8,0},{10,2},{12,4},{14,6},{1,9},{3,11}... | collective-permute-start | bytes 190472 | tf_op jit(solution)/shard_map/ppermute | solution.py:454
  6.1 2.5 %collective-permute-start.5 = (bf16[8,3968]{1,0:T(8,128)(2,1)S(1)}, bf16[8,3968]{1,0:T(8,128)(2,1)S(1)}, u32[]{:S(2)}, u32[]{:S(2)}) collective-permute-start(bf16[8,3968]{1,0:T(8,128)(2,1)S(1)} %get-tuple-element.33.refs_0_), channel_id=1, source_target_pairs={{0,6},{2,4},{4,2},{6,0},{8,14},{10,12},{12,10},{14,8},{1,7},{3,5},... | collective-permute-start | bytes 190472 | tf_op jit(solution)/shard_map/ppermute | solution.py:457
  8.6 0.4 collective-permute-start.3
  9.1 0.5 collective-permute-start.1
  9.6 0.0 collective-permute-done.refs_1_
  9.6 2.5 %collective-permute-start.6 = (bf16[8,3968]{1,0:T(8,128)(2,1)S(1)}, bf16[8,3968]{1,0:T(8,128)(2,1)S(1)}, u32[]{:S(2)}, u32[]{:S(2)}) collective-permute-start(bf16[8,3968]{1,0:T(8,128)(2,1)S(1)} %collective-permute-done.refs_1_), channel_id=1, source_target_pairs={{0,6},{2,4},{4,2},{6,0},{8,14},{10,12},{12,10},{14,8},{1,7},{3,5},... | collective-permute-start | bytes 190472 | tf_op jit(solution)/shard_map/ppermute | solution.py:457
  12.1 0.4 collective-permute-start.4
  12.6 0.0 collective-permute-done.5.refs_6_
  12.6 0.8 %collective-permute-start.2 = (bf16[8,3968]{1,0:T(8,128)(2,1)S(1)}, bf16[8,3968]{1,0:T(8,128)(2,1)S(1)}, u32[]{:S(2)}, u32[]{:S(2)}) collective-permute-start(bf16[8,3968]{1,0:T(8,128)(2,1)S(1)} %collective-permute-done.refs_1_), channel_id=1, source_target_pairs={{0,2},{2,0},{4,6},{6,4},{8,10},{10,8},{12,14},{14,12},{1,3},{3,1},... | collective-permute-start | bytes 190472 | tf_op jit(solution)/shard_map/ppermute | solution.py:457
  13.4 0.0 collective-permute-done.3.refs_4_
  13.4 0.2 collective-permute-done.1.refs_2_
  13.6 1.2 %collective-permute-done.6.refs_7_ = bf16[8,3968]{1,0:T(8,128)(2,1)S(1)} collective-permute-done((bf16[8,3968]{1,0:T(8,128)(2,1)S(1)}, bf16[8,3968]{1,0:T(8,128)(2,1)S(1)}, u32[]{:S(2)}, u32[]{:S(2)}) %collective-permute-start.6) | collective-permute-done | bytes 63520 | tf_op jit(solution)/shard_map/ppermute | solution.py:457
  14.8 1.5 %collective-permute-done.4.refs_5_ = bf16[8,3968]{1,0:T(8,128)(2,1)S(1)} collective-permute-done((bf16[8,3968]{1,0:T(8,128)(2,1)S(1)}, bf16[8,3968]{1,0:T(8,128)(2,1)S(1)}, u32[]{:S(2)}, u32[]{:S(2)}) %collective-permute-start.4) | collective-permute-done | bytes 63520 | tf_op jit(solution)/shard_map/ppermute | solution.py:457
  16.4 0.4 collective-permute-done.2.refs_3_
  16.8 0.1 collective-permute-start.7
  16.9 1.9 %collective-permute-done.7.refs_8_ = bf16[8,8,3968]{2,1,0:T(8,128)(2,1)S(1)} collective-permute-done((bf16[8,8,3968]{2,1,0:T(8,128)(2,1)S(1)}, bf16[8,8,3968]{2,1,0:T(8,128)(2,1)S(1)}, u32[]{:S(2)}, u32[]{:S(2)}) %collective-permute-start.7) | collective-permute-done | bytes 507936 | tf_op jit(solution)/shard_map/ppermute | solution.py:460
  18.8 34.8 %expert_units.1 = (bf16[48,6144]{1,0:T(8,128)(2,1)S(1)}, bf16[1344,48]{1,0:T(8,128)(2,1)S(1)}, bf16[1344,48]{1,0:T(8,128)(2,1)S(1)}, f32[64,2048]{1,0:T(8,128)S(...) custom-call(s32[1]{0:T(128)} %bitcast.2.t_ref, ...), custom_call_target="tpu_custom_call" | custom-call | flops 4756340736 | bytes 66060288 | tf_op jit(solution)/shard_map/expert_units/pallas_call | solution.py:295
  53.6 0.2 collective-permute-start.8
  53.8 1.8 %collective-permute-done.8.got_ref = f32[64,2048]{1,0:T(8,128)S(1)} collective-permute-done((f32[64,2048]{1,0:T(8,128)S(1)}, f32[64,2048]{1,0:T(8,128)S(1)}, u32[]{:S(2)}, u32[]{:S(2)}) %collective-permute-start.8) | collective-permute-done | bytes 524320 | tf_op jit(solution)/shard_map/ppermute | solution.py:460
  55.6 0.1 fold_cores.1
  55.6 0.9 %collective-permute-start.9 = (f32[16,2048]{1,0:T(8,128)S(1)}, f32[16,2048]{1,0:T(8,128)S(1)}, u32[]{:S(2)}, u32[]{:S(2)}) collective-permute-start(f32[16,2048]{1,0:T(8,128)S(1)} %get-tuple-element.44), channel_id=1, source_target_pairs={{0,2},{2,0},{4,6},{6,4},{8,10},{10,8},{12,14},{14,12},{1,3},{3,1},... | collective-permute-start | bytes 393224 | tf_op jit(solution)/shard_map/ppermute | solution.py:457
  56.5 1.2 %collective-permute-start.10 = (f32[16,2048]{1,0:T(8,128)S(1)}, f32[16,2048]{1,0:T(8,128)S(1)}, u32[]{:S(2)}, u32[]{:S(2)}) collective-permute-start(f32[16,2048]{1,0:T(8,128)S(1)} %get-tuple-element.45), channel_id=1, source_target_pairs={{0,4},{2,6},{4,0},{6,2},{8,12},{10,14},{12,8},{14,10},{1,5},{3,7},... | collective-permute-start | bytes 393224 | tf_op jit(solution)/shard_map/ppermute | solution.py:457
  57.8 1.4 %collective-permute-start.11 = (f32[16,2048]{1,0:T(8,128)S(1)}, f32[16,2048]{1,0:T(8,128)S(1)}, u32[]{:S(2)}, u32[]{:S(2)}) collective-permute-start(f32[16,2048]{1,0:T(8,128)S(1)} %get-tuple-element.46), channel_id=1, source_target_pairs={{0,6},{2,4},{4,2},{6,0},{8,14},{10,12},{12,10},{14,8},{1,7},{3,5},... | collective-permute-start | bytes 393224 | tf_op jit(solution)/shard_map/ppermute | solution.py:457
  59.2 5.9 %grad_gate.1 = bf16[1344,6144]{1,0:T(8,128)(2,1)} custom-call(bf16[1344,48]{1,0:T(8,128)(2,1)S(1)} %get-tuple-element.41.left_ref, bf16[48,6144]{1,0:T(8,128)(2,1)S(1)} %get-tuple-element.42.x_ref, bf16[1344,6144]{1,0:T(8,128)(2,1)} %get-tuple-element.43._), custom_call_target="tpu_custom_call", output_to_operand_aliasing={{}: (2, {})} | custom-call | flops 693633024 | bytes 14450688 | tf_op jit(solution)/shard_map/grad_gate/pallas_call | solution.py:354
  65.1 0.0 collective-permute-done.9.refs_1_
  65.1 0.0 collective-permute-done.10.refs_2_
  65.1 0.1 collective-permute-done.11.refs_3_
  65.3 2.4 %collective-permute-start.12 = (f32[8,2048]{1,0:T(8,128)S(1)}, f32[8,2048]{1,0:T(8,128)S(1)}, u32[]{:S(2)}, u32[]{:S(2)}) collective-permute-start(f32[8,2048]{1,0:T(8,128)S(1)} %get-tuple-element.54), channel_id=1, source_target_pairs={{0,8},{2,10},{4,12},{6,14},{8,0},{10,2},{12,4},{14,6},{1,9},{3,11}... | collective-permute-start | bytes 196616 | tf_op jit(solution)/shard_map/ppermute | solution.py:454
  67.6 0.0 copy-start
  67.7 4.1 %grad_up.1 = bf16[1344,6144]{1,0:T(8,128)(2,1)} custom-call(bf16[1344,48]{1,0:T(8,128)(2,1)S(1)} %get-tuple-element.52.left_ref, bf16[48,6144]{1,0:T(8,128)(2,1)S(1)} %get-tuple-element.42.x_ref, bf16[1344,6144]{1,0:T(8,128)(2,1)} %get-tuple-element.53._), custom_call_target="tpu_custom_call", output_to_operand_aliasing={{}: (2, {})} | custom-call | flops 396361728 | bytes 8257536 | tf_op jit(solution)/shard_map/grad_up/pallas_call | solution.py:354
  71.8 0.0 collective-permute-done.12.got_ref
  71.8 0.0 copy-done
  71.8 1.5 %finish_tokens.1 = (bf16[16,3072]{1,0:T(8,128)(2,1)}, f32[4,16]{1,0:T(4,128)}) custom-call(s32[1]{0:T(128)} %bitcast.e_ref, s32[4,16]{1,0:T(4,128)S(1)} %bitcast.6, f32[8,2048]{1,0:T(8,128)S(1)} %get-tuple-element.51.mine_ref, f32[8,2048]{1,0:T(8,128)S(1)} %collective-permute-done.12.got_ref), custom_call_target="tpu_custom_call" | custom-call | tf_op jit(solution)/shard_map/finish_tokens/pallas_call | solution.py:435
  (2 shorter events, 0.1 us)
Async XLA Ops:
  2.0 7.6 %collective-permute-start = (bf16[8,3968]{1,0:T(8,128)(2,1)S(1)}, bf16[8,3968]{1,0:T(8,128)(2,1)S(1)}, u32[]{:S(2)}, u32[]{:S(2)}) collective-permute-start(bf16[8,3968]{1,0:T(8,128)(2,1)S(1)} %get-tuple-element.34), channel_id=1, source_target_pairs={{0,8},{2,10},{4,12},{6,14},{8,0},{10,2},{12,4},{14,6},{1,9},{3,11}... | collective-permute-start | bytes 190472 | tf_op jit(solution)/shard_map/ppermute | solution.py:454
  6.1 6.4 %collective-permute-start.5 = (bf16[8,3968]{1,0:T(8,128)(2,1)S(1)}, bf16[8,3968]{1,0:T(8,128)(2,1)S(1)}, u32[]{:S(2)}, u32[]{:S(2)}) collective-permute-start(bf16[8,3968]{1,0:T(8,128)(2,1)S(1)} %get-tuple-element.33.refs_0_), channel_id=1, source_target_pairs={{0,6},{2,4},{4,2},{6,0},{8,14},{10,12},{12,10},{14,8},{1,7},{3,5},... | collective-permute-start | bytes 190472 | tf_op jit(solution)/shard_map/ppermute | solution.py:457
  8.6 4.8 %collective-permute-start.3 = (bf16[8,3968]{1,0:T(8,128)(2,1)S(1)}, bf16[8,3968]{1,0:T(8,128)(2,1)S(1)}, u32[]{:S(2)}, u32[]{:S(2)}) collective-permute-start(bf16[8,3968]{1,0:T(8,128)(2,1)S(1)} %get-tuple-element.33.refs_0_), channel_id=1, source_target_pairs={{0,4},{2,6},{4,0},{6,2},{8,12},{10,14},{12,8},{14,10},{1,5},{3,7},... | collective-permute-start | bytes 190472 | tf_op jit(solution)/shard_map/ppermute | solution.py:457
  9.1 4.6 %collective-permute-start.1 = (bf16[8,3968]{1,0:T(8,128)(2,1)S(1)}, bf16[8,3968]{1,0:T(8,128)(2,1)S(1)}, u32[]{:S(2)}, u32[]{:S(2)}) collective-permute-start(bf16[8,3968]{1,0:T(8,128)(2,1)S(1)} %get-tuple-element.33.refs_0_), channel_id=1, source_target_pairs={{0,2},{2,0},{4,6},{6,4},{8,10},{10,8},{12,14},{14,12},{1,3},{3,1},... | collective-permute-start | bytes 190472 | tf_op jit(solution)/shard_map/ppermute | solution.py:457
  9.6 5.2 %collective-permute-start.6 = (bf16[8,3968]{1,0:T(8,128)(2,1)S(1)}, bf16[8,3968]{1,0:T(8,128)(2,1)S(1)}, u32[]{:S(2)}, u32[]{:S(2)}) collective-permute-start(bf16[8,3968]{1,0:T(8,128)(2,1)S(1)} %collective-permute-done.refs_1_), channel_id=1, source_target_pairs={{0,6},{2,4},{4,2},{6,0},{8,14},{10,12},{12,10},{14,8},{1,7},{3,5},... | collective-permute-start | bytes 190472 | tf_op jit(solution)/shard_map/ppermute | solution.py:457
  12.1 4.2 %collective-permute-start.4 = (bf16[8,3968]{1,0:T(8,128)(2,1)S(1)}, bf16[8,3968]{1,0:T(8,128)(2,1)S(1)}, u32[]{:S(2)}, u32[]{:S(2)}) collective-permute-start(bf16[8,3968]{1,0:T(8,128)(2,1)S(1)} %collective-permute-done.refs_1_), channel_id=1, source_target_pairs={{0,4},{2,6},{4,0},{6,2},{8,12},{10,14},{12,8},{14,10},{1,5},{3,7},... | collective-permute-start | bytes 190472 | tf_op jit(solution)/shard_map/ppermute | solution.py:457
  12.6 4.2 %collective-permute-start.2 = (bf16[8,3968]{1,0:T(8,128)(2,1)S(1)}, bf16[8,3968]{1,0:T(8,128)(2,1)S(1)}, u32[]{:S(2)}, u32[]{:S(2)}) collective-permute-start(bf16[8,3968]{1,0:T(8,128)(2,1)S(1)} %collective-permute-done.refs_1_), channel_id=1, source_target_pairs={{0,2},{2,0},{4,6},{6,4},{8,10},{10,8},{12,14},{14,12},{1,3},{3,1},... | collective-permute-start | bytes 190472 | tf_op jit(solution)/shard_map/ppermute | solution.py:457
  16.8 2.0 %collective-permute-start.7 = (bf16[8,8,3968]{2,1,0:T(8,128)(2,1)S(1)}, bf16[8,8,3968]{2,1,0:T(8,128)(2,1)S(1)}, u32[]{:S(2)}, u32[]{:S(2)}) collective-permute-start(bf16[8,8,3968]{2,1,0:T(8,128)(2,1)S(1)} %stack_pieces.1), channel_id=1, source_target_pairs={{0,1},{1,0},{2,3},{3,2},{4,5},{5,4},{6,7},{7,6},{8,9},{9,8},{10,11... | collective-permute-start | bytes 1523720 | tf_op jit(solution)/shard_map/ppermute | solution.py:460
  53.6 2.0 %collective-permute-start.8 = (f32[64,2048]{1,0:T(8,128)S(1)}, f32[64,2048]{1,0:T(8,128)S(1)}, u32[]{:S(2)}, u32[]{:S(2)}) collective-permute-start(f32[64,2048]{1,0:T(8,128)S(1)} %get-tuple-element.38), channel_id=1, source_target_pairs={{0,1},{1,0},{2,3},{3,2},{4,5},{5,4},{6,7},{7,6},{8,9},{9,8},{10,11... | collective-permute-start | bytes 1572872 | tf_op jit(solution)/shard_map/ppermute | solution.py:460
  55.6 9.5 %collective-permute-start.9 = (f32[16,2048]{1,0:T(8,128)S(1)}, f32[16,2048]{1,0:T(8,128)S(1)}, u32[]{:S(2)}, u32[]{:S(2)}) collective-permute-start(f32[16,2048]{1,0:T(8,128)S(1)} %get-tuple-element.44), channel_id=1, source_target_pairs={{0,2},{2,0},{4,6},{6,4},{8,10},{10,8},{12,14},{14,12},{1,3},{3,1},... | collective-permute-start | bytes 393224 | tf_op jit(solution)/shard_map/ppermute | solution.py:457
  56.5 8.6 %collective-permute-start.10 = (f32[16,2048]{1,0:T(8,128)S(1)}, f32[16,2048]{1,0:T(8,128)S(1)}, u32[]{:S(2)}, u32[]{:S(2)}) collective-permute-start(f32[16,2048]{1,0:T(8,128)S(1)} %get-tuple-element.45), channel_id=1, source_target_pairs={{0,4},{2,6},{4,0},{6,2},{8,12},{10,14},{12,8},{14,10},{1,5},{3,7},... | collective-permute-start | bytes 393224 | tf_op jit(solution)/shard_map/ppermute | solution.py:457
  57.8 7.5 %collective-permute-start.11 = (f32[16,2048]{1,0:T(8,128)S(1)}, f32[16,2048]{1,0:T(8,128)S(1)}, u32[]{:S(2)}, u32[]{:S(2)}) collective-permute-start(f32[16,2048]{1,0:T(8,128)S(1)} %get-tuple-element.46), channel_id=1, source_target_pairs={{0,6},{2,4},{4,2},{6,0},{8,14},{10,12},{12,10},{14,8},{1,7},{3,5},... | collective-permute-start | bytes 393224 | tf_op jit(solution)/shard_map/ppermute | solution.py:457
  65.3 6.5 %collective-permute-start.12 = (f32[8,2048]{1,0:T(8,128)S(1)}, f32[8,2048]{1,0:T(8,128)S(1)}, u32[]{:S(2)}, u32[]{:S(2)}) collective-permute-start(f32[8,2048]{1,0:T(8,128)S(1)} %get-tuple-element.54), channel_id=1, source_target_pairs={{0,8},{2,10},{4,12},{6,14},{8,0},{10,2},{12,4},{14,6},{1,9},{3,11}... | collective-permute-start | bytes 196616 | tf_op jit(solution)/shard_map/ppermute | solution.py:454
  67.6 4.1 %copy-start = (s32[16,4]{0,1:T(4,128)S(1)}, s32[16,4]{0,1:T(4,128)}, u32[]{:S(2)}) copy-start(s32[16,4]{0,1:T(4,128)} %param.9) | copy-start | bytes 772

commit v14 on v11

--- a/solution.py
+++ b/solution.py
@@ -15,8 +15,8 @@
 F32 = jnp.float32
 BF16 = jnp.bfloat16
 MIB = 1 << 20
-GATE_CHUNKS = 2
-UP_CHUNKS = 4
+GATE_CHUNKS = 1
+UP_CHUNKS = 5
 VMEM = pl.BlockSpec(memory_space=pltpu.VMEM)
 SMEM = pl.BlockSpec(memory_space=pltpu.SMEM)
 HBM = pl.BlockSpec(memory_space=pltpu.HBM)
@@ -410,13 +410,11 @@
     data = jnp.concatenate([mine_ref[...], got_ref[...]], axis=0)
     tn = (((0,), (0,)), ((), ()))
     exact = dict(precision=lax.Precision.HIGHEST, preferred_element_type=F32)
-    halves = [
-        lax.dot_general(jnp.where(sub // WHOLE == h, main, 0.0), data[:, :half], tn, **exact) for h in range(2)
-    ]
     for s in range(SUBS):
-        last = lax.dot_general(jnp.where(sub == s, tail, 0.0), data[:, half : half + eighth], tn, **exact)
         h, at = divmod(s * eighth, half)
-        tok_ref[:, s * eighth : (s + 1) * eighth] = (halves[h][:, at : at + eighth] + last).astype(BF16)
+        left = jnp.concatenate([jnp.where(sub // WHOLE == h, main, 0.0), jnp.where(sub == s, tail, 0.0)], axis=0)
+        right = jnp.concatenate([data[:, at : at + eighth], data[:, half : half + eighth]], axis=0)
+        tok_ref[:, s * eighth : (s + 1) * eighth] = lax.dot_general(left, right, tn, **exact).astype(BF16)
     term = plain * data[:, half + eighth : half + eighth + 1]
     for k, hit in enumerate(hits):
         gate_ref[k : k + 1, :] = jnp.sum(jnp.where(hit, term, 0.0), axis=0, keepdims=True)

time: 71.5 us -> 70.6 us (0.987)
  no operation moved by 1% of the time
where the time goes in v14:
time: 70.6 us; the launch traced here: 70.4 us
  Pallas kernels  44.9 us (64%)
  starting transfers between devices  17.6 us (25%)
  waiting for transfers between devices  7.12 us (10%)
  between operations  0.74 us (1%)
    pallas_call x1, Pallas kernels, expert_units(): pl.pallas_call(functools.partial(experts_body, pieces, chunk, ahead), out...  32.9 us
    ppermute x9, starting transfers between devices, across(): return lax.ppermute(v, 'expert', [(i, i ^ d) for i in range(n_expert)])  10.8 us
    pallas_call x2, Pallas kernels, weight_grad(): pl.pallas_call(functools.partial(weights_body, chunk, begun), out_shape=j...  9.3 us
    ppermute x2, starting transfers between devices, partner(): lax.ppermute(v, 'expert', [(i, (i + copies) % n_expert) for i in range(n_...  6.49 us
    ppermute x2, waiting for transfers between devices, other_core(): return lax.ppermute(v, 'tensor', [(0, 1), (1, 0)])  3.65 us
    ppermute x9, waiting for transfers between devices, across(): return lax.ppermute(v, 'expert', [(i, i ^ d) for i in range(n_expert)])  3.47 us
  transfers between devices with their start and end apart: 13, of which 7 were waited for; matrix products, arithmetic and copies ran while one was open for 0% of the time, Pallas kernels for 13%

profile of v14, /device:TPU:0, one launch (start us, length us, event | category | flops | bytes accessed | tf_op | source)
XLA Modules:
  0.0 70.4 jit_solution(3511441838464413291)
XLA Ops:
  0.6 1.4 %pick_rows.1 = (bf16[8,3968]{1,0:T(8,128)(2,1)S(1)}, bf16[8,3968]{1,0:T(8,128)(2,1)S(1)}) custom-call(s32[1]{0:T(128)} %bitcast.e_ref, s32[4,16]{1,0:T(4,128)} %bitcast.5, bf16[4,16]{1,0:T(4,128)(2,1)} %bitcast.7, bf16[16,3072]{1,0:T(8,128)(2,1)} %tok_any.1, bf16[16,3072]{1,0:T(8,128)(2,1)} %grad_any.1), custom_call_target="tpu_custom_call" | custom-call | tf_op jit(solution)/shard_map/pick_rows/pallas_call | solution.py:95
  2.0 4.1 %collective-permute-start = (bf16[8,3968]{1,0:T(8,128)(2,1)S(1)}, bf16[8,3968]{1,0:T(8,128)(2,1)S(1)}, u32[]{:S(2)}, u32[]{:S(2)}) collective-permute-start(bf16[8,3968]{1,0:T(8,128)(2,1)S(1)} %get-tuple-element.34), channel_id=1, source_target_pairs={{0,8},{2,10},{4,12},{6,14},{8,0},{10,2},{12,4},{14,6},{1,9},{3,11}... | collective-permute-start | bytes 190472 | tf_op jit(solution)/shard_map/ppermute | solution.py:444
  6.1 2.5 %collective-permute-start.5 = (bf16[8,3968]{1,0:T(8,128)(2,1)S(1)}, bf16[8,3968]{1,0:T(8,128)(2,1)S(1)}, u32[]{:S(2)}, u32[]{:S(2)}) collective-permute-start(bf16[8,3968]{1,0:T(8,128)(2,1)S(1)} %get-tuple-element.33.refs_0_), channel_id=1, source_target_pairs={{0,6},{2,4},{4,2},{6,0},{8,14},{10,12},{12,10},{14,8},{1,7},{3,5},... | collective-permute-start | bytes 190472 | tf_op jit(solution)/shard_map/ppermute | solution.py:447
  8.6 0.4 collective-permute-start.3
  9.1 0.5 collective-permute-start.1
  9.6 0.0 collective-permute-done.refs_1_
  9.6 2.5 %collective-permute-start.6 = (bf16[8,3968]{1,0:T(8,128)(2,1)S(1)}, bf16[8,3968]{1,0:T(8,128)(2,1)S(1)}, u32[]{:S(2)}, u32[]{:S(2)}) collective-permute-start(bf16[8,3968]{1,0:T(8,128)(2,1)S(1)} %collective-permute-done.refs_1_), channel_id=1, source_target_pairs={{0,6},{2,4},{4,2},{6,0},{8,14},{10,12},{12,10},{14,8},{1,7},{3,5},... | collective-permute-start | bytes 190472 | tf_op jit(solution)/shard_map/ppermute | solution.py:447
  12.1 0.4 collective-permute-start.4
  12.6 0.0 collective-permute-done.5.refs_6_
  12.6 0.8 %collective-permute-start.2 = (bf16[8,3968]{1,0:T(8,128)(2,1)S(1)}, bf16[8,3968]{1,0:T(8,128)(2,1)S(1)}, u32[]{:S(2)}, u32[]{:S(2)}) collective-permute-start(bf16[8,3968]{1,0:T(8,128)(2,1)S(1)} %collective-permute-done.refs_1_), channel_id=1, source_target_pairs={{0,2},{2,0},{4,6},{6,4},{8,10},{10,8},{12,14},{14,12},{1,3},{3,1},... | collective-permute-start | bytes 190472 | tf_op jit(solution)/shard_map/ppermute | solution.py:447
  13.4 0.0 collective-permute-done.3.refs_4_
  13.4 0.2 collective-permute-done.1.refs_2_
  13.6 1.2 %collective-permute-done.6.refs_7_ = bf16[8,3968]{1,0:T(8,128)(2,1)S(1)} collective-permute-done((bf16[8,3968]{1,0:T(8,128)(2,1)S(1)}, bf16[8,3968]{1,0:T(8,128)(2,1)S(1)}, u32[]{:S(2)}, u32[]{:S(2)}) %collective-permute-start.6) | collective-permute-done | bytes 63520 | tf_op jit(solution)/shard_map/ppermute | solution.py:447
  14.8 1.5 %collective-permute-done.4.refs_5_ = bf16[8,3968]{1,0:T(8,128)(2,1)S(1)} collective-permute-done((bf16[8,3968]{1,0:T(8,128)(2,1)S(1)}, bf16[8,3968]{1,0:T(8,128)(2,1)S(1)}, u32[]{:S(2)}, u32[]{:S(2)}) %collective-permute-start.4) | collective-permute-done | bytes 63520 | tf_op jit(solution)/shard_map/ppermute | solution.py:447
  16.4 0.4 collective-permute-done.2.refs_3_
  16.8 0.1 collective-permute-start.7
  16.9 1.9 %collective-permute-done.7.refs_8_ = bf16[8,8,3968]{2,1,0:T(8,128)(2,1)S(1)} collective-permute-done((bf16[8,8,3968]{2,1,0:T(8,128)(2,1)S(1)}, bf16[8,8,3968]{2,1,0:T(8,128)(2,1)S(1)}, u32[]{:S(2)}, u32[]{:S(2)}) %collective-permute-start.7) | collective-permute-done | bytes 507936 | tf_op jit(solution)/shard_map/ppermute | solution.py:450
  18.8 32.9 %expert_units.1 = (bf16[48,6144]{1,0:T(8,128)(2,1)S(1)}, bf16[1344,48]{1,0:T(8,128)(2,1)S(1)}, bf16[1344,48]{1,0:T(8,128)(2,1)S(1)}, f32[64,2048]{1,0:T(8,128)S(...) custom-call(s32[1]{0:T(128)} %bitcast.2.t_ref, ...), custom_call_target="tpu_custom_call" | custom-call | flops 4756340736 | bytes 66060288 | tf_op jit(solution)/shard_map/expert_units/pallas_call | solution.py:287
  51.7 0.2 collective-permute-start.8
  51.9 1.8 %collective-permute-done.8.got_ref = f32[64,2048]{1,0:T(8,128)S(1)} collective-permute-done((f32[64,2048]{1,0:T(8,128)S(1)}, f32[64,2048]{1,0:T(8,128)S(1)}, u32[]{:S(2)}, u32[]{:S(2)}) %collective-permute-start.8) | collective-permute-done | bytes 524320 | tf_op jit(solution)/shard_map/ppermute | solution.py:450
  53.7 0.1 fold_cores.1
  53.7 0.9 %collective-permute-start.9 = (f32[16,2048]{1,0:T(8,128)S(1)}, f32[16,2048]{1,0:T(8,128)S(1)}, u32[]{:S(2)}, u32[]{:S(2)}) collective-permute-start(f32[16,2048]{1,0:T(8,128)S(1)} %get-tuple-element.44), channel_id=1, source_target_pairs={{0,2},{2,0},{4,6},{6,4},{8,10},{10,8},{12,14},{14,12},{1,3},{3,1},... | collective-permute-start | bytes 393224 | tf_op jit(solution)/shard_map/ppermute | solution.py:447
  54.6 1.3 %collective-permute-start.10 = (f32[16,2048]{1,0:T(8,128)S(1)}, f32[16,2048]{1,0:T(8,128)S(1)}, u32[]{:S(2)}, u32[]{:S(2)}) collective-permute-start(f32[16,2048]{1,0:T(8,128)S(1)} %get-tuple-element.45), channel_id=1, source_target_pairs={{0,4},{2,6},{4,0},{6,2},{8,12},{10,14},{12,8},{14,10},{1,5},{3,7},... | collective-permute-start | bytes 393224 | tf_op jit(solution)/shard_map/ppermute | solution.py:447
  55.9 1.4 %collective-permute-start.11 = (f32[16,2048]{1,0:T(8,128)S(1)}, f32[16,2048]{1,0:T(8,128)S(1)}, u32[]{:S(2)}, u32[]{:S(2)}) collective-permute-start(f32[16,2048]{1,0:T(8,128)S(1)} %get-tuple-element.46), channel_id=1, source_target_pairs={{0,6},{2,4},{4,2},{6,0},{8,14},{10,12},{12,10},{14,8},{1,7},{3,5},... | collective-permute-start | bytes 393224 | tf_op jit(solution)/shard_map/ppermute | solution.py:447
  57.3 5.9 %grad_gate.1 = bf16[1344,6144]{1,0:T(8,128)(2,1)} custom-call(bf16[1344,48]{1,0:T(8,128)(2,1)S(1)} %get-tuple-element.41.left_ref, bf16[48,6144]{1,0:T(8,128)(2,1)S(1)} %get-tuple-element.42.x_ref, bf16[1344,6144]{1,0:T(8,128)(2,1)} %get-tuple-element.43._), custom_call_target="tpu_custom_call", output_to_operand_aliasing={{}: (2, {})} | custom-call | flops 693633024 | bytes 14450688 | tf_op jit(solution)/shard_map/grad_gate/pallas_call | solution.py:346
  63.2 0.0 collective-permute-done.9.refs_1_
  63.3 0.0 collective-permute-done.10.refs_2_
  63.3 0.1 collective-permute-done.11.refs_3_
  63.4 2.4 %collective-permute-start.12 = (f32[8,2048]{1,0:T(8,128)S(1)}, f32[8,2048]{1,0:T(8,128)S(1)}, u32[]{:S(2)}, u32[]{:S(2)}) collective-permute-start(f32[8,2048]{1,0:T(8,128)S(1)} %get-tuple-element.54), channel_id=1, source_target_pairs={{0,8},{2,10},{4,12},{6,14},{8,0},{10,2},{12,4},{14,6},{1,9},{3,11}... | collective-permute-start | bytes 196616 | tf_op jit(solution)/shard_map/ppermute | solution.py:444
  65.7 0.0 copy-start
  65.7 3.4 %grad_up.1 = bf16[1344,6144]{1,0:T(8,128)(2,1)} custom-call(bf16[1344,48]{1,0:T(8,128)(2,1)S(1)} %get-tuple-element.52.left_ref, bf16[48,6144]{1,0:T(8,128)(2,1)S(1)} %get-tuple-element.42.x_ref, bf16[1344,6144]{1,0:T(8,128)(2,1)} %get-tuple-element.53._), custom_call_target="tpu_custom_call", output_to_operand_aliasing={{}: (2, {})} | custom-call | flops 297271296 | bytes 6193152 | tf_op jit(solution)/shard_map/grad_up/pallas_call | solution.py:346
  69.1 0.0 collective-permute-done.12.got_ref
  69.1 0.0 copy-done
  69.1 1.3 %finish_tokens.1 = (bf16[16,3072]{1,0:T(8,128)(2,1)}, f32[4,16]{1,0:T(4,128)}) custom-call(s32[1]{0:T(128)} %bitcast.e_ref, s32[4,16]{1,0:T(4,128)S(1)} %bitcast.6, f32[8,2048]{1,0:T(8,128)S(1)} %get-tuple-element.51.mine_ref, f32[8,2048]{1,0:T(8,128)S(1)} %collective-permute-done.12.got_ref), custom_call_target="tpu_custom_call" | custom-call | tf_op jit(solution)/shard_map/finish_tokens/pallas_call | solution.py:425
  (2 shorter events, 0.1 us)
Async XLA Ops:
  2.0 7.6 %collective-permute-start = (bf16[8,3968]{1,0:T(8,128)(2,1)S(1)}, bf16[8,3968]{1,0:T(8,128)(2,1)S(1)}, u32[]{:S(2)}, u32[]{:S(2)}) collective-permute-start(bf16[8,3968]{1,0:T(8,128)(2,1)S(1)} %get-tuple-element.34), channel_id=1, source_target_pairs={{0,8},{2,10},{4,12},{6,14},{8,0},{10,2},{12,4},{14,6},{1,9},{3,11}... | collective-permute-start | bytes 190472 | tf_op jit(solution)/shard_map/ppermute | solution.py:444
  6.1 6.4 %collective-permute-start.5 = (bf16[8,3968]{1,0:T(8,128)(2,1)S(1)}, bf16[8,3968]{1,0:T(8,128)(2,1)S(1)}, u32[]{:S(2)}, u32[]{:S(2)}) collective-permute-start(bf16[8,3968]{1,0:T(8,128)(2,1)S(1)} %get-tuple-element.33.refs_0_), channel_id=1, source_target_pairs={{0,6},{2,4},{4,2},{6,0},{8,14},{10,12},{12,10},{14,8},{1,7},{3,5},... | collective-permute-start | bytes 190472 | tf_op jit(solution)/shard_map/ppermute | solution.py:447
  8.6 4.8 %collective-permute-start.3 = (bf16[8,3968]{1,0:T(8,128)(2,1)S(1)}, bf16[8,3968]{1,0:T(8,128)(2,1)S(1)}, u32[]{:S(2)}, u32[]{:S(2)}) collective-permute-start(bf16[8,3968]{1,0:T(8,128)(2,1)S(1)} %get-tuple-element.33.refs_0_), channel_id=1, source_target_pairs={{0,4},{2,6},{4,0},{6,2},{8,12},{10,14},{12,8},{14,10},{1,5},{3,7},... | collective-permute-start | bytes 190472 | tf_op jit(solution)/shard_map/ppermute | solution.py:447
  9.1 4.6 %collective-permute-start.1 = (bf16[8,3968]{1,0:T(8,128)(2,1)S(1)}, bf16[8,3968]{1,0:T(8,128)(2,1)S(1)}, u32[]{:S(2)}, u32[]{:S(2)}) collective-permute-start(bf16[8,3968]{1,0:T(8,128)(2,1)S(1)} %get-tuple-element.33.refs_0_), channel_id=1, source_target_pairs={{0,2},{2,0},{4,6},{6,4},{8,10},{10,8},{12,14},{14,12},{1,3},{3,1},... | collective-permute-start | bytes 190472 | tf_op jit(solution)/shard_map/ppermute | solution.py:447
  9.6 5.2 %collective-permute-start.6 = (bf16[8,3968]{1,0:T(8,128)(2,1)S(1)}, bf16[8,3968]{1,0:T(8,128)(2,1)S(1)}, u32[]{:S(2)}, u32[]{:S(2)}) collective-permute-start(bf16[8,3968]{1,0:T(8,128)(2,1)S(1)} %collective-permute-done.refs_1_), channel_id=1, source_target_pairs={{0,6},{2,4},{4,2},{6,0},{8,14},{10,12},{12,10},{14,8},{1,7},{3,5},... | collective-permute-start | bytes 190472 | tf_op jit(solution)/shard_map/ppermute | solution.py:447
  12.1 4.2 %collective-permute-start.4 = (bf16[8,3968]{1,0:T(8,128)(2,1)S(1)}, bf16[8,3968]{1,0:T(8,128)(2,1)S(1)}, u32[]{:S(2)}, u32[]{:S(2)}) collective-permute-start(bf16[8,3968]{1,0:T(8,128)(2,1)S(1)} %collective-permute-done.refs_1_), channel_id=1, source_target_pairs={{0,4},{2,6},{4,0},{6,2},{8,12},{10,14},{12,8},{14,10},{1,5},{3,7},... | collective-permute-start | bytes 190472 | tf_op jit(solution)/shard_map/ppermute | solution.py:447
  12.6 4.2 %collective-permute-start.2 = (bf16[8,3968]{1,0:T(8,128)(2,1)S(1)}, bf16[8,3968]{1,0:T(8,128)(2,1)S(1)}, u32[]{:S(2)}, u32[]{:S(2)}) collective-permute-start(bf16[8,3968]{1,0:T(8,128)(2,1)S(1)} %collective-permute-done.refs_1_), channel_id=1, source_target_pairs={{0,2},{2,0},{4,6},{6,4},{8,10},{10,8},{12,14},{14,12},{1,3},{3,1},... | collective-permute-start | bytes 190472 | tf_op jit(solution)/shard_map/ppermute | solution.py:447
  16.8 2.0 %collective-permute-start.7 = (bf16[8,8,3968]{2,1,0:T(8,128)(2,1)S(1)}, bf16[8,8,3968]{2,1,0:T(8,128)(2,1)S(1)}, u32[]{:S(2)}, u32[]{:S(2)}) collective-permute-start(bf16[8,8,3968]{2,1,0:T(8,128)(2,1)S(1)} %stack_pieces.1), channel_id=1, source_target_pairs={{0,1},{1,0},{2,3},{3,2},{4,5},{5,4},{6,7},{7,6},{8,9},{9,8},{10,11... | collective-permute-start | bytes 1523720 | tf_op jit(solution)/shard_map/ppermute | solution.py:450
  51.7 2.0 %collective-permute-start.8 = (f32[64,2048]{1,0:T(8,128)S(1)}, f32[64,2048]{1,0:T(8,128)S(1)}, u32[]{:S(2)}, u32[]{:S(2)}) collective-permute-start(f32[64,2048]{1,0:T(8,128)S(1)} %get-tuple-element.38), channel_id=1, source_target_pairs={{0,1},{1,0},{2,3},{3,2},{4,5},{5,4},{6,7},{7,6},{8,9},{9,8},{10,11... | collective-permute-start | bytes 1572872 | tf_op jit(solution)/shard_map/ppermute | solution.py:450
  53.7 9.5 %collective-permute-start.9 = (f32[16,2048]{1,0:T(8,128)S(1)}, f32[16,2048]{1,0:T(8,128)S(1)}, u32[]{:S(2)}, u32[]{:S(2)}) collective-permute-start(f32[16,2048]{1,0:T(8,128)S(1)} %get-tuple-element.44), channel_id=1, source_target_pairs={{0,2},{2,0},{4,6},{6,4},{8,10},{10,8},{12,14},{14,12},{1,3},{3,1},... | collective-permute-start | bytes 393224 | tf_op jit(solution)/shard_map/ppermute | solution.py:447
  54.6 8.6 %collective-permute-start.10 = (f32[16,2048]{1,0:T(8,128)S(1)}, f32[16,2048]{1,0:T(8,128)S(1)}, u32[]{:S(2)}, u32[]{:S(2)}) collective-permute-start(f32[16,2048]{1,0:T(8,128)S(1)} %get-tuple-element.45), channel_id=1, source_target_pairs={{0,4},{2,6},{4,0},{6,2},{8,12},{10,14},{12,8},{14,10},{1,5},{3,7},... | collective-permute-start | bytes 393224 | tf_op jit(solution)/shard_map/ppermute | solution.py:447
  55.9 7.4 %collective-permute-start.11 = (f32[16,2048]{1,0:T(8,128)S(1)}, f32[16,2048]{1,0:T(8,128)S(1)}, u32[]{:S(2)}, u32[]{:S(2)}) collective-permute-start(f32[16,2048]{1,0:T(8,128)S(1)} %get-tuple-element.46), channel_id=1, source_target_pairs={{0,6},{2,4},{4,2},{6,0},{8,14},{10,12},{12,10},{14,8},{1,7},{3,5},... | collective-permute-start | bytes 393224 | tf_op jit(solution)/shard_map/ppermute | solution.py:447
  63.4 5.8 %collective-permute-start.12 = (f32[8,2048]{1,0:T(8,128)S(1)}, f32[8,2048]{1,0:T(8,128)S(1)}, u32[]{:S(2)}, u32[]{:S(2)}) collective-permute-start(f32[8,2048]{1,0:T(8,128)S(1)} %get-tuple-element.54), channel_id=1, source_target_pairs={{0,8},{2,10},{4,12},{6,14},{8,0},{10,2},{12,4},{14,6},{1,9},{3,11}... | collective-permute-start | bytes 196616 | tf_op jit(solution)/shard_map/ppermute | solution.py:444
  65.7 3.4 %copy-start = (s32[16,4]{0,1:T(4,128)S(1)}, s32[16,4]{0,1:T(4,128)}, u32[]{:S(2)}) copy-start(s32[16,4]{0,1:T(4,128)} %param.9) | copy-start | bytes 772
